TPU v7x, 32 devices: a whole 2x2x4 slice. The times are simulated.
32 devices in a mesh: group: 2 (over x), slab: 4 (over y, core), inner: 4 (over z).
Axes of the slice: x: 2, y: 2, z: 4, core: 2. Of those that a mesh axis runs over, the one named last changes fastest.
Arguments:
- populations: float32 [19, 32, 32, 256], P(None, ('group', 'slab'), 'inner'), parts along dimension 1, may hold values from 0 to 1, as said below
- relaxation: float32 [32, 32, 256], P(('group', 'slab'), 'inner'), parts along dimension 0, may hold values from 0.7 to 1.8
- node_flags: int32 [32, 32, 256], P(('group', 'slab'), 'inner'), parts along dimension 0, may hold values from 0 to 3, as said below
- displacement: float32 [3, 65536], P(None, ('group', 'slab', 'inner')), parts along dimension 1, may hold values from -0.04 to 0.04
- elements: int32 [3, 131072], P(None, ('group', 'slab', 'inner')), parts along dimension 1, may hold values from 0 to 4095, as said below
- shape_inverse: float32 [3, 131072], P(None, ('group', 'slab', 'inner')), parts along dimension 1, may hold values from -0.5 to 2
- stiffness: float32 [131072], P(('group', 'slab', 'inner')), parts along dimension 0, may hold values from 5 to 50
- block_source: int32 [8, 4, 8], P(('group', 'slab'), 'inner'), parts along dimension 0, may hold values from 0 to 63
- block_target: int32 [8, 4, 8], P(('group', 'slab'), 'inner'), parts along dimension 0, may hold values from 0 to 3, as said below
- block_node: int32 [8, 4, 8], P(('group', 'slab'), 'inner'), parts along dimension 0, may hold values from 0 to 15
- block_count: int32 [8, 4], P(('group', 'slab'), 'inner'), parts along dimension 0, may hold values from 4 to 8, as said below
Outputs:
- populations_out: float32 [19, 32, 32, 256], P(None, ('group', 'slab'), 'inner'), parts along dimension 1
- wall_force: float32 [3, 65536], P(None, ('group', 'slab', 'inner')), parts along dimension 1
- wall_motion: float32 [8, 4, 8, 3, 128], P(('group', 'slab'), 'inner'), parts along dimension 0
There are 2 independent parts, one for each index of `group`. A program takes and returns all parts, laid end to end along the dimension named above; each array names one. Nothing has to cross between parts.
Inputs may be any that keep to these rules, and one draw needn't show every extreme that they name: `node_flags`: 0 fluid, 1 wall, 2 inlet, 3 outlet; the planes y = 0 and y = 31 are wall, x = 0 is inlet and x = 15 outlet except wall cells. Positive populations. `elements`: numbers below 4096 on devices of the last slab index below 2048. `block_target`: at most 3 of one device's blocks name one inner index, and every device names some inner index exactly 3 times among its live blocks. `block_count`: some device has 8 live blocks and some has half as many.
All inputs are finite; a program needn't handle non-finite values.
Results may differ from a plain program's by a relative error of at most 0.0003.
Values sent between devices are 32-bit elements; how exact they have to be, the bound alone decides.
No kernel may reach another device: no remote copies, remote signals or barrier semaphores. Data moves between devices by JAX's collectives and lax.ppermute only.
A program may use at most 64 MiB of HBM per device.

v0:
```python
import jax
import jax.numpy as jnp
from jax import lax
from jax.sharding import PartitionSpec as P

BLK = 128


VELOCITIES = (
    (0, 0, 0),
    (1, 0, 0),
    (-1, 0, 0),
    (0, 1, 0),
    (0, -1, 0),
    (0, 0, 1),
    (0, 0, -1),
    (1, 1, 0),
    (-1, -1, 0),
    (1, -1, 0),
    (-1, 1, 0),
    (1, 0, 1),
    (-1, 0, -1),
    (1, 0, -1),
    (-1, 0, 1),
    (0, 1, 1),
    (0, -1, -1),
    (0, 1, -1),
    (0, -1, 1),
)
WEIGHTS = (1.0 / 3.0,) + (1.0 / 18.0,) * 6 + (1.0 / 36.0,) * 12
OPPOSITE = (0, 2, 1, 4, 3, 6, 5, 8, 7, 10, 9, 12, 11, 14, 13, 16, 15, 18, 17)
INLET_SPEED = 0.04
LOAD_SCALE = 25.0
COMPLIANCE = 0.5
LAME_RATIO = 2.0


def extended(shard, sides, width):
    for axis, dim in sides:
        count, length = (lax.axis_size(axis), shard.shape[dim])
        up = [(i, (i + 1) % count) for i in range(count - 1)]
        down = [(j, i) for i, j in up]
        last = lax.slice_in_dim(shard, length - width, length, axis=dim)
        initial = lax.slice_in_dim(shard, 0, width, axis=dim)
        before = lax.ppermute(last, axis, up)
        after = lax.ppermute(initial, axis, down)
        shard = jnp.concatenate([before, shard, after], axis=dim)
    return shard


def from_behind(block, axis, distance):
    devices = range(lax.axis_size(axis))
    route = [(i - distance, i) for i in devices if i - distance in devices]
    return lax.ppermute(block, axis, route)


def moments(values):
    density = jnp.sum(values, axis=0)
    flows = []
    for axis_num in range(3):
        total = None
        for velocity in range(19):
            factor = VELOCITIES[velocity][axis_num]
            if factor != 0:
                term = values[velocity] if factor > 0 else -values[velocity]
                total = term if total is None else total + term
        flows.append(total)
    return (density, flows[0], flows[1], flows[2])


def equilibrium(density, vel_x, vel_y, vel_z):
    speed_sq = vel_x * vel_x + vel_y * vel_y + vel_z * vel_z
    result = []
    for velocity in range(19):
        project = 0.0
        for factor, component in zip(VELOCITIES[velocity], (vel_x, vel_y, vel_z)):
            if factor != 0:
                project = project + factor * component
        result.append(
            WEIGHTS[velocity]
            * density
            * (1.0 + 3.0 * project + 4.5 * project * project - 1.5 * speed_sq)
        )
    return jnp.stack(result)


def collide(values, relaxation, node_flags):
    density, flow_x, flow_y, flow_z = moments(values)
    vel_x = flow_x / density
    vel_y = flow_y / density
    vel_z = flow_z / density
    balance = equilibrium(density, vel_x, vel_y, vel_z)
    relaxed = values - relaxation[None] * (values - balance)
    bounced = jnp.stack([values[other] for other in OPPOSITE])
    unity = jnp.ones_like(density)
    nothing = jnp.zeros_like(density)
    inflow = equilibrium(unity, jnp.full_like(density, INLET_SPEED), nothing, nothing)
    outflow = equilibrium(unity, vel_x, vel_y, vel_z)
    kinds = node_flags[None]
    collided = jnp.where(
        kinds == 0, relaxed, jnp.where(kinds == 1, bounced, jnp.where(kinds == 2, inflow, outflow))
    )
    return collided


def pull(padded, rows_x, rows_y):
    moved = []
    for velocity in range(19):
        step_x, step_y, step_z = VELOCITIES[velocity]
        piece = padded[
            velocity, 1 - step_x : 1 - step_x + rows_x, 1 - step_y : 1 - step_y + rows_y, :
        ]
        moved.append(jnp.roll(piece, step_z, axis=2))
    return jnp.stack(moved)


def element_forces(first, second, third, shape_inverse, stiffness):
    diag_a = shape_inverse[0]
    skew_b = shape_inverse[1]
    diag_c = shape_inverse[2]
    edge_one = second - first
    edge_two = third - first
    grad_one = diag_a * edge_one
    grad_two = skew_b * edge_one + diag_c * edge_two
    column_one = jnp.stack([grad_one[0] + 1.0, grad_one[1], grad_one[2]])
    column_two = jnp.stack([grad_two[0], grad_two[1] + 1.0, grad_two[2]])
    metric_aa = jnp.sum(column_one * column_one, axis=0)
    metric_ab = jnp.sum(column_one * column_two, axis=0)
    metric_bb = jnp.sum(column_two * column_two, axis=0)
    determinant = metric_aa * metric_bb - metric_ab * metric_ab
    inverse_aa = metric_bb / determinant
    inverse_ab = -metric_ab / determinant
    inverse_bb = metric_aa / determinant
    pulled_one = column_one * inverse_aa + column_two * inverse_ab
    pulled_two = column_one * inverse_ab + column_two * inverse_bb
    log_volume = 0.5 * jnp.log(determinant)
    stress_one = stiffness * (column_one - pulled_one + LAME_RATIO * log_volume * pulled_one)
    stress_two = stiffness * (column_two - pulled_two + LAME_RATIO * log_volume * pulled_two)
    force_one = diag_a * stress_one + skew_b * stress_two
    force_two = diag_c * stress_two
    return (-(force_one + force_two), force_one, force_two)


def block_view(residual, node_blocks):
    return residual.reshape(3, node_blocks, BLK).transpose(1, 0, 2)


def shards(
    populations,
    relaxation,
    node_flags,
    displacement,
    elements,
    shape_inverse,
    stiffness,
    block_source,
    block_target,
    block_node,
    block_count,
):
    planes = populations.shape[1]
    columns = populations.shape[2]
    values = populations
    for sweep in range(2):
        collided = collide(values, relaxation, node_flags)
        padded = extended(collided, (("slab", 1), ("inner", 2)), 1)
        values = pull(padded, planes, columns)
    density, flow_x, flow_y, flow_z = moments(values)
    loads = LOAD_SCALE * jnp.stack([flow_x, flow_y + (density - 1.0) / 3.0, flow_z])
    loads = loads.reshape(3, -1, BLK)
    blocks = jnp.transpose(jnp.take(loads, block_source[0, 0], axis=1), (1, 0, 2))
    node_dev = displacement.shape[1]
    node_blocks = node_dev // BLK
    next_nodes = from_behind(displacement, "slab", -1)
    table = jnp.concatenate([displacement, next_nodes], axis=1)
    nodal = element_forces(
        table[:, elements[0]],
        table[:, elements[1]],
        table[:, elements[2]],
        shape_inverse,
        stiffness,
    )
    node_forces = jnp.zeros((3, 2 * node_dev), jnp.float32)
    for corner in range(3):
        node_forces = node_forces.at[:, elements[corner]].add(nodal[corner])
    internal = node_forces[:, :node_dev] + from_behind(node_forces[:, node_dev:], "slab", 1)
    cycle_size = lax.axis_size("inner")
    live_count = block_count[0, 0]
    target = block_target[0, 0]
    node_ids = block_node[0, 0]
    slots_here = target.shape[0]
    active = jnp.arange(slots_here, dtype=jnp.int32) < live_count
    highest = lax.Precision.HIGHEST
    keys = target * node_blocks + node_ids
    owners = jnp.arange(cycle_size * node_blocks, dtype=jnp.int32)
    choose = ((keys[None, :] == owners[:, None]) & active[None, :]).astype(jnp.float32)
    spread = jnp.einsum("sk,kab->sab", choose, blocks, precision=highest)
    received = lax.psum_scatter(
        spread.reshape(cycle_size, node_blocks, 3, BLK), "inner", scatter_dimension=0, tiled=True
    )[0]
    external = received.transpose(1, 0, 2).reshape(3, node_dev)
    residual = external - internal
    everyone = lax.all_gather(block_view(residual, node_blocks)[None], "inner", axis=0, tiled=True)
    motion = jnp.einsum("sk,sab->kab", choose, everyone.reshape(-1, 3, BLK), precision=highest)
    motion = COMPLIANCE * motion
    return (values, residual, motion[None, None])


def solution(mesh):
    return jax.shard_map(
        shards,
        mesh=mesh,
        in_specs=(
            P(None, ("group", "slab"), "inner", None),
            P(("group", "slab"), "inner", None),
            P(("group", "slab"), "inner", None),
            P(None, ("group", "slab", "inner")),
            P(None, ("group", "slab", "inner")),
            P(None, ("group", "slab", "inner")),
            P(("group", "slab", "inner")),
            P(("group", "slab"), "inner", None),
            P(("group", "slab"), "inner", None),
            P(("group", "slab"), "inner", None),
            P(("group", "slab"), "inner"),
        ),
        out_specs=(
            P(None, ("group", "slab"), "inner", None),
            P(None, ("group", "slab", "inner")),
            P(("group", "slab"), "inner", None, None, None),
        ),
        check_vma=False,
    )
```

profile of v0, /device:TPU:0, one launch (start us, length us, event | category | flops | bytes accessed | tf_op | source)
XLA Modules:
  0.0 266.0 jit_solution(10868186532150341859)
XLA Ops:
  7.2 0.8 constant_dynamic-update-slice_fusion.37
  8.0 1.1 reduce_sum.838
  9.1 1.2 constant_dynamic-update-slice_fusion.18
  11.6 0.3 select_select_fusion.1
  11.9 0.7 fusion.104
  12.6 1.3 collective-permute-start.1
  13.9 3.7 %collective-permute-start = (f32[19,1,8,256]{3,2,1,0:T(8,128)}, f32[19,1,8,256]{3,2,1,0:T(8,128)}, u32[]{:S(2)}, u32[]{:S(2)}) collective-permute-start(f32[19,1,8,256]{3,2,1,0:T(8,128)} %get-tuple-element.89), channel_id=1, source_target_pairs={{0,4},{4,8},{8,12},{1,5},{5,9},{9,13},{2,6},{6,10},{10,14},{3,7},{... | collective-permute-start | bytes 466952 | tf_op jit(solution)/shard_map/ppermute | solution.py:45
  17.6 1.3 collective-permute-start.8
  18.9 0.5 compare_and_fusion
  19.5 0.6 fusion.105
  20.2 0.6 broadcast_clamp_fusion.2
  20.8 0.6 broadcast_clamp_fusion
  21.4 0.5 add_bitcast_fusion.1
  21.9 0.6 pad_clamp_fusion
  23.2 0.6 pad_maximum_fusion.6
  23.8 1.5 copy.125
  25.3 15.5 %gather_fusion.1 = f32[4096,3]{1,0:T(8,128)} fusion(f32[3,4096]{0,1:T(8,128)S(1)} %copy.125, s32[4096]{0:T(1024)} %broadcast_clamp_fusion.2), kind=kCustom, calls=%fused_computation.1 | custom fusion | bytes 114688 | tf_op jit(solution)/shard_map/gather | solution.py:178
  40.8 2.8 %copy.127 = f32[4096,3]{0,1:T(4,128)} copy(f32[4096,3]{1,0:T(8,128)} %gather_fusion.1) | data formatting | bytes 98304 | tf_op jit(solution)/shard_map/gather | solution.py:178
  43.6 15.5 %gather_fusion.2 = f32[4096,3]{1,0:T(8,128)} fusion(f32[3,4096]{0,1:T(8,128)S(1)} %copy.125, s32[4096]{0:T(1024)} %get-tuple-element.255), kind=kCustom, calls=%fused_computation.2 | custom fusion | bytes 114688 | tf_op jit(solution)/shard_map/gather | solution.py:177
  59.1 2.8 %copy.128 = f32[4096,3]{0,1:T(4,128)} copy(f32[4096,3]{1,0:T(8,128)} %gather_fusion.2) | data formatting | bytes 98304 | tf_op jit(solution)/shard_map/gather | solution.py:177
  61.9 15.5 %gather_fusion.3 = f32[4096,3]{1,0:T(8,128)} fusion(f32[3,4096]{0,1:T(8,128)S(1)} %copy.125, s32[4096]{0:T(1024)} %get-tuple-element.254), kind=kCustom, calls=%fused_computation.3 | custom fusion | bytes 114688 | tf_op jit(solution)/shard_map/gather | solution.py:179
  77.5 2.2 copy.130
  79.9 0.2 multiply_reduce_fusion.2
  80.1 0.7 multiply_bitcast_fusion.1
  80.9 0.8 negate_bitcast_fusion
  81.6 2.0 copy.132
  83.6 23.2 %scatter_custom_fusion = f32[3,4096]{0,1:T(8,128)S(1)} fusion(s32[4096]{0:T(1024)} %bitcast.394, f32[4096,3]{1,0:T(8,128)} %copy.132, f32[]{:T(128)} %constant.29.clone.1), kind=kCustom, calls=%fused_computation.10 | custom fusion | flops 12288 | bytes 49664 | tf_op jit(solution)/shard_map/scatter-add | solution.py:185
  106.8 2.8 %copy.133 = f32[4096,3]{1,0:T(8,128)} copy(f32[4096,3]{0,1:T(4,128)} %bitcast.379) | data formatting | bytes 98304 | tf_op jit(solution)/shard_map/add | solution.py:139
  109.6 2.8 %copy.134 = f32[4096,3]{1,0:T(8,128)} copy(f32[4096,3]{0,1:T(4,128)} %get-tuple-element.28) | data formatting | bytes 98304 | tf_op jit(solution)/shard_map/mul | solution.py:140
  112.4 23.4 %scatter_fusion = f32[3,4096]{0,1:T(8,128)S(1)} fusion(f32[3,4096]{0,1:T(8,128)S(1)} %scatter_custom_fusion, s32[4096]{0:T(1024)S(1)} %bitcast.384, f32[4096,3]{1,0:T(8,128)} %copy.133), kind=kCustom, calls=%fused_computation.5 | custom fusion | flops 12288 | bytes 163840 | tf_op jit(solution)/shard_map/scatter-add | solution.py:185
  135.8 23.4 %scatter_fusion.1 = f32[3,4096]{0,1:T(8,128)S(1)} fusion(f32[3,4096]{0,1:T(8,128)S(1)} %scatter_fusion, s32[4096]{0:T(1024)S(1)} %bitcast.386, f32[4096,3]{1,0:T(8,128)} %copy.134), kind=kCustom, calls=%fused_computation.6 | custom fusion | flops 12288 | bytes 163840 | tf_op jit(solution)/shard_map/scatter-add | solution.py:185
  159.3 0.7 slice_bitcast_fusion.3
  160.4 1.1 pad_maximum_fusion.5
  161.5 4.9 %collective-permute-start.2 = (f32[19,6,1,256]{3,2,1,0:T(1,128)S(1)}, f32[19,6,1,256]{3,2,1,0:T(1,128)S(1)}, u32[]{:S(2)}, u32[]{:S(2)}) collective-permute-start(f32[19,6,1,256]{3,2,1,0:T(1,128)S(1)} %get-tuple-element.69), channel_id=1, source_target_pairs={{0,1},{1,2},{2,3},{4,5},{5,6},{6,7},{8,9},{9,10},{10,11},{12,13},{... | collective-permute-start | bytes 350216 | tf_op jit(solution)/shard_map/ppermute | solution.py:45
  166.5 1.5 collective-permute-start.3
  168.1 1.8 collective-permute-done.2
  169.9 4.5 %collective-permute-done.3 = f32[19,6,1,256]{3,2,1,0:T(1,128)S(1)} collective-permute-done((f32[19,6,1,256]{3,2,1,0:T(1,128)S(1)}, f32[19,6,1,256]{3,2,1,0:T(1,128)S(1)}, u32[]{:S(2)}, u32[]{:S(2)}) %collective-permute-start.3) | collective-permute-done | bytes 116768 | tf_op jit(solution)/shard_map/ppermute | solution.py:46
  174.3 0.7 maximum_bitcast_fusion.5
  175.5 1.0 constant_dynamic-update-slice_fusion.107
  178.6 0.3 select_select_fusion
  178.9 1.3 collective-permute-start.5
  180.2 3.0 %collective-permute-start.4 = (f32[19,1,8,256]{3,2,1,0:T(8,128)S(1)}, f32[19,1,8,256]{3,2,1,0:T(8,128)S(1)}, u32[]{:S(2)}, u32[]{:S(2)}) collective-permute-start(f32[19,1,8,256]{3,2,1,0:T(8,128)S(1)} %get-tuple-element.81), channel_id=1, source_target_pairs={{0,4},{4,8},{8,12},{1,5},{5,9},{9,13},{2,6},{6,10},{10,14},{3,7},{... | collective-permute-start | bytes 466952 | tf_op jit(solution)/shard_map/ppermute | solution.py:45
  183.3 1.4 fusion.102
  184.7 1.6 copy.135
  186.3 3.1 %collective-permute-start.9 = (f32[3,2048]{1,0:T(4,128)S(1)}, f32[3,2048]{1,0:T(4,128)S(1)}, u32[]{:S(2)}, u32[]{:S(2)}) collective-permute-start(f32[3,2048]{1,0:T(4,128)S(1)} %copy.135), channel_id=1, source_target_pairs={{0,4},{4,8},{8,12},{1,5},{5,9},{9,13},{2,6},{6,10},{10,14},{3,7},{... | collective-permute-start | bytes 73736 | tf_op jit(solution)/shard_map/ppermute | solution.py:54
  189.4 0.6 dynamic-slice
  190.0 1.6 copy.136
  191.6 0.4 copy.137
  192.5 1.3 collective-permute-start.7
  193.8 4.6 %collective-permute-start.6 = (f32[19,6,1,256]{3,2,1,0:T(1,128)S(1)}, f32[19,6,1,256]{3,2,1,0:T(1,128)S(1)}, u32[]{:S(2)}, u32[]{:S(2)}) collective-permute-start(f32[19,6,1,256]{3,2,1,0:T(1,128)S(1)} %get-tuple-element.66), channel_id=1, source_target_pairs={{0,1},{1,2},{2,3},{4,5},{5,6},{6,7},{8,9},{9,10},{10,11},{12,13},{... | collective-permute-start | bytes 350216 | tf_op jit(solution)/shard_map/ppermute | solution.py:45
  198.4 1.5 collective-permute-done.7
  200.0 1.2 collective-permute-done.6
  201.8 0.2 multiply_add_fusion.1
  202.7 0.8 copy-done.17
  203.9 0.7 gather_fusion
  204.7 1.0 fusion.89
  205.7 0.7 constant_dynamic-update-slice_fusion.146
  206.4 35.4 %all-reduce.3.cloned.1.call-done = f32[4,16,3,128]{3,1,0,2:T(8,128)} async-done(((f32[4,16,3,128]{3,1,0,2:T(8,128)}), f32[4,16,3,128]{3,1,0,2:T(8,128)}) %all-reduce.3.cloned.1.call-update) | async-done | bytes 98320
  241.8 1.4 dynamic-slice_bitcast_fusion
  243.2 0.4 copy.124
  243.7 0.9 copy.139
  244.6 0.3 copy.140
  244.9 13.4 %all-gather = f32[64,3,128]{2,0,1:T(8,128)S(1)} all-gather(f32[16,3,128]{2,0,1:T(8,128)S(1)} %bitcast.392), channel_id=2, replica_groups=mesh['group'=2,'slab'=4,'inner'=4] {'inner'}, dimensions={0}, use_global_device_ids=true | all-gather | bytes 122880 | tf_op jit(solution)/shard_map/all_gather | solution.py:203
  258.3 0.8 fusion
  (243 shorter events, 6.1 us)
Async XLA Ops:
  7.2 234.6 %all-reduce.3.cloned.1.call-start = ((), (), s32[]{:S(2)}) async-start(), calls=%async_computation | async-start | bytes 196608
  9.1 1.8 copy-start
  10.6 0.9 copy-start.15
  10.6 0.9 copy-start.5
  11.4 1.2 copy-start.7
  11.5 1.2 copy-start.9
  11.5 6.1 %copy-start.16 = (f32[3,2048]{1,0:T(4,128)S(1)}, f32[3,2048]{1,0:T(4,128)}, u32[]{:S(2)}) copy-start(f32[3,2048]{1,0:T(4,128)} %param.14) | copy-start | bytes 73732
  11.5 7.4 %copy-start.19 = (s32[1,1,8]{2,1,0:T(1,128)S(1)}, s32[1,1,8]{2,1,0:T(1,128)}, u32[]{:S(2)}) copy-start(s32[1,1,8]{2,1,0:T(1,128)} %param.18) | copy-start | bytes 100
  11.5 7.9 %copy-start.13 = (s32[3,4096]{1,0:T(4,128)S(1)}, s32[3,4096]{1,0:T(4,128)}, u32[]{:S(2)}) copy-start(s32[3,4096]{1,0:T(4,128)} %param.15) | copy-start | bytes 147460
  11.5 8.0 %copy-start.14 = (f32[3,4096]{1,0:T(4,128)S(1)}, f32[3,4096]{1,0:T(4,128)}, u32[]{:S(2)}) copy-start(f32[3,4096]{1,0:T(4,128)} %param.16) | copy-start | bytes 147460
  11.5 9.9 %copy-start.20 = (s32[1,1,8]{2,1,0:T(1,128)S(1)}, s32[1,1,8]{2,1,0:T(1,128)}, u32[]{:S(2)}) copy-start(s32[1,1,8]{2,1,0:T(1,128)} %param.20) | copy-start | bytes 100
  11.5 9.8 %copy-start.21 = (s32[1,1,8]{2,1,0:T(1,128)S(1)}, s32[1,1,8]{2,1,0:T(1,128)}, u32[]{:S(2)}) copy-start(s32[1,1,8]{2,1,0:T(1,128)} %param.19) | copy-start | bytes 100
  12.6 146.7 %collective-permute-start.1 = (f32[19,1,8,256]{3,2,1,0:T(8,128)}, f32[19,1,8,256]{3,2,1,0:T(8,128)S(1)}, u32[]{:S(2)}, u32[]{:S(2)}) collective-permute-start(f32[19,1,8,256]{3,2,1,0:T(8,128)} %get-tuple-element.90), channel_id=1, source_target_pairs={{4,0},{8,4},{12,8},{5,1},{9,5},{13,9},{6,2},{10,6},{14,10},{7,3},{... | collective-permute-start | bytes 466952 | tf_op jit(solution)/shard_map/ppermute | solution.py:46
  13.9 145.4 %collective-permute-start = (f32[19,1,8,256]{3,2,1,0:T(8,128)}, f32[19,1,8,256]{3,2,1,0:T(8,128)}, u32[]{:S(2)}, u32[]{:S(2)}) collective-permute-start(f32[19,1,8,256]{3,2,1,0:T(8,128)} %get-tuple-element.89), channel_id=1, source_target_pairs={{0,4},{4,8},{8,12},{1,5},{5,9},{9,13},{2,6},{6,10},{10,14},{3,7},{... | collective-permute-start | bytes 466952 | tf_op jit(solution)/shard_map/ppermute | solution.py:45
  17.6 5.6 %collective-permute-start.8 = (f32[3,2048]{1,0:T(4,128)S(1)}, f32[3,2048]{1,0:T(4,128)S(1)}, u32[]{:S(2)}, u32[]{:S(2)}) collective-permute-start(f32[3,2048]{1,0:T(4,128)S(1)} %copy-done.16), channel_id=1, source_target_pairs={{4,0},{8,4},{12,8},{5,1},{9,5},{13,9},{6,2},{10,6},{14,10},{7,3},{... | collective-permute-start | bytes 73736 | tf_op jit(solution)/shard_map/ppermute | solution.py:54
  19.5 3.7 %copy-start.12 = (s32[4096,1]{0,1:T(1,128)}, s32[4096,1]{0,1:T(1,128)S(1)}, u32[]{:S(2)}) copy-start(s32[4096,1]{0,1:T(1,128)S(1)} %get-tuple-element.124) | copy-start | bytes 49156
  77.4 2.3 copy-start.1
  77.4 2.3 copy-start.2
  77.4 2.3 copy-start.3
  77.4 2.3 copy-start.4
  77.4 2.7 %copy-start.11 = (f32[4096]{0:T(1024)S(1)}, f32[4096]{0:T(1024)}, u32[]{:S(2)}) copy-start(f32[4096]{0:T(1024)} %param.17) | copy-start | bytes 49156
  161.5 8.3 %collective-permute-start.2 = (f32[19,6,1,256]{3,2,1,0:T(1,128)S(1)}, f32[19,6,1,256]{3,2,1,0:T(1,128)S(1)}, u32[]{:S(2)}, u32[]{:S(2)}) collective-permute-start(f32[19,6,1,256]{3,2,1,0:T(1,128)S(1)} %get-tuple-element.69), channel_id=1, source_target_pairs={{0,1},{1,2},{2,3},{4,5},{5,6},{6,7},{8,9},{9,10},{10,11},{12,13},{... | collective-permute-start | bytes 350216 | tf_op jit(solution)/shard_map/ppermute | solution.py:45
  166.5 7.8 %collective-permute-start.3 = (f32[19,6,1,256]{3,2,1,0:T(1,128)S(1)}, f32[19,6,1,256]{3,2,1,0:T(1,128)S(1)}, u32[]{:S(2)}, u32[]{:S(2)}) collective-permute-start(f32[19,6,1,256]{3,2,1,0:T(1,128)S(1)} %get-tuple-element.70), channel_id=1, source_target_pairs={{1,0},{2,1},{3,2},{5,4},{6,5},{7,6},{9,8},{10,9},{11,10},{13,12},{... | collective-permute-start | bytes 350216 | tf_op jit(solution)/shard_map/ppermute | solution.py:46
  177.7 0.8 copy-start.6
  177.7 0.8 copy-start.8
  177.7 0.8 copy-start.10
  178.9 13.0 %collective-permute-start.5 = (f32[19,1,8,256]{3,2,1,0:T(8,128)S(1)}, f32[19,1,8,256]{3,2,1,0:T(8,128)S(1)}, u32[]{:S(2)}, u32[]{:S(2)}) collective-permute-start(f32[19,1,8,256]{3,2,1,0:T(8,128)S(1)} %get-tuple-element.82), channel_id=1, source_target_pairs={{4,0},{8,4},{12,8},{5,1},{9,5},{13,9},{6,2},{10,6},{14,10},{7,3},{... | collective-permute-start | bytes 466952 | tf_op jit(solution)/shard_map/ppermute | solution.py:46
  180.2 9.2 %copy-start.23 = (u32[32]{0:T(128)S(1)}, u32[32]{0:T(128)}, u32[]{:S(2)}) copy-start(u32[32]{0:T(128)} %constant.92) | copy-start | bytes 388
  180.2 11.7 %collective-permute-start.4 = (f32[19,1,8,256]{3,2,1,0:T(8,128)S(1)}, f32[19,1,8,256]{3,2,1,0:T(8,128)S(1)}, u32[]{:S(2)}, u32[]{:S(2)}) collective-permute-start(f32[19,1,8,256]{3,2,1,0:T(8,128)S(1)} %get-tuple-element.81), channel_id=1, source_target_pairs={{0,4},{4,8},{8,12},{1,5},{5,9},{9,13},{2,6},{6,10},{10,14},{3,7},{... | collective-permute-start | bytes 466952 | tf_op jit(solution)/shard_map/ppermute | solution.py:45
  186.3 5.3 %collective-permute-start.9 = (f32[3,2048]{1,0:T(4,128)S(1)}, f32[3,2048]{1,0:T(4,128)S(1)}, u32[]{:S(2)}, u32[]{:S(2)}) collective-permute-start(f32[3,2048]{1,0:T(4,128)S(1)} %copy.135), channel_id=1, source_target_pairs={{0,4},{4,8},{8,12},{1,5},{5,9},{9,13},{2,6},{6,10},{10,14},{3,7},{... | collective-permute-start | bytes 73736 | tf_op jit(solution)/shard_map/ppermute | solution.py:54
  192.5 7.5 %collective-permute-start.7 = (f32[19,6,1,256]{3,2,1,0:T(1,128)S(1)}, f32[19,6,1,256]{3,2,1,0:T(1,128)S(1)}, u32[]{:S(2)}, u32[]{:S(2)}) collective-permute-start(f32[19,6,1,256]{3,2,1,0:T(1,128)S(1)} %get-tuple-element.65), channel_id=1, source_target_pairs={{1,0},{2,1},{3,2},{5,4},{6,5},{7,6},{9,8},{10,9},{11,10},{13,12},{... | collective-permute-start | bytes 350216 | tf_op jit(solution)/shard_map/ppermute | solution.py:46
  193.8 7.4 %collective-permute-start.6 = (f32[19,6,1,256]{3,2,1,0:T(1,128)S(1)}, f32[19,6,1,256]{3,2,1,0:T(1,128)S(1)}, u32[]{:S(2)}, u32[]{:S(2)}) collective-permute-start(f32[19,6,1,256]{3,2,1,0:T(1,128)S(1)} %get-tuple-element.66), channel_id=1, source_target_pairs={{0,1},{1,2},{2,3},{4,5},{5,6},{6,7},{8,9},{9,10},{10,11},{12,13},{... | collective-permute-start | bytes 350216 | tf_op jit(solution)/shard_map/ppermute | solution.py:45
  201.8 2.9 %copy-start.18 = (pred[8]{0:T(512)(128)(4,1)S(1)}, pred[8]{0:T(512)(128)(4,1)}, u32[]{:S(2)}) copy-start(pred[8]{0:T(512)(128)(4,1)} %compare_and_fusion) | copy-start | bytes 28
  201.8 3.0 %copy-start.22 = (s32[8]{0:T(128)S(1)}, s32[8]{0:T(128)}, u32[]{:S(2)}) copy-start(s32[8]{0:T(128)} %add_bitcast_fusion.1) | copy-start | bytes 100
  202.7 0.8 copy-start.17
Sparse Core Ops, SparseCore 0:
  205.8 35.9 all-reduce.2
where the time goes:
time: 268 us; the launch traced here: 266 us
  other arithmetic  86.4 us (32%)
  local copies, waits for them, and re-layouts  77.8 us (29%)
  waiting for transfers between devices  44.4 us (17%)
  starting transfers between devices  26 us (10%)
  between operations  16.2 us (6%)
  blocking collectives  13.4 us (5%)
    scatter-add x3, other arithmetic, shards(): node_forces = node_forces.at[:, elements[corner]].add(nodal[corner])  70 us
    unnamed x2, waiting for transfers between devices  35.4 us
    gather x2, local copies, waits for them, and re-layouts, shards(): table[:, elements[1]]  18.3 us
    gather x2, local copies, waits for them, and re-layouts, shards(): table[:, elements[0]]  18.3 us
    gather x2, local copies, waits for them, and re-layouts, shards(): table[:, elements[2]]  17.7 us
    ppermute x4, starting transfers between devices, extended(): before = lax.ppermute(last, axis, up)  16.2 us
    all_gather x1, blocking collectives, shards(): lax.all_gather(block_view(residual, node_blocks)[None], 'inner', axis=0,...  13.4 us
    ppermute x4, waiting for transfers between devices, extended(): after = lax.ppermute(initial, axis, down)  6.01 us
  transfers between devices with their start and end apart: 11, of which 5 were waited for; matrix products, arithmetic and copies ran while one was open for 55% of the time, Pallas kernels for 0%

commit v1 on v0

v1 whole, which is shorter than its diff:
```python
import functools

import jax
import jax.numpy as jnp
from jax import lax
from jax.experimental import pallas as pl
from jax.experimental.pallas import tpu as pltpu
from jax.sharding import PartitionSpec as P

BLK = 128
VELOCITIES = (
    (0, 0, 0),
    (1, 0, 0),
    (-1, 0, 0),
    (0, 1, 0),
    (0, -1, 0),
    (0, 0, 1),
    (0, 0, -1),
    (1, 1, 0),
    (-1, -1, 0),
    (1, -1, 0),
    (-1, 1, 0),
    (1, 0, 1),
    (-1, 0, -1),
    (1, 0, -1),
    (-1, 0, 1),
    (0, 1, 1),
    (0, -1, -1),
    (0, 1, -1),
    (0, -1, 1),
)
WEIGHTS = (1.0 / 3.0,) + (1.0 / 18.0,) * 6 + (1.0 / 36.0,) * 12
OPPOSITE = (0, 2, 1, 4, 3, 6, 5, 8, 7, 10, 9, 12, 11, 14, 13, 16, 15, 18, 17)
INLET_SPEED = 0.04
LOAD_SCALE = 25.0
COMPLIANCE = 0.5
LAME_RATIO = 2.0
Q = 19
FLAG_SLOT = 19
RATE_SLOT = 20
SLOTS = 21
F32 = jnp.float32
VMEM_BYTES = 48 * 1024 * 1024


def moments(values):
    sums = [values[q] + values[q + 1] for q in range(1, Q, 2)]
    diffs = [values[q] - values[q + 1] for q in range(1, Q, 2)]
    density = values[0]
    for term in sums:
        density = density + term
    flows = []
    for axis in range(3):
        total = None
        for k, q in enumerate(range(1, Q, 2)):
            factor = VELOCITIES[q][axis]
            if factor == 0:
                continue
            if total is None:
                total = diffs[k] if factor > 0 else -diffs[k]
            else:
                total = total + diffs[k] if factor > 0 else total - diffs[k]
        flows.append(total)
    return density, flows[0], flows[1], flows[2]


def collide(values, rate, kind):
    density, flow_x, flow_y, flow_z = moments(values)
    inverse = 1.0 / density
    wall = kind == 1
    inlet = kind == 2
    fluid = kind == 0
    vel = (
        jnp.where(inlet, INLET_SPEED, flow_x * inverse),
        jnp.where(inlet, 0.0, flow_y * inverse),
        jnp.where(inlet, 0.0, flow_z * inverse),
    )
    scale = jnp.where(fluid, density, 1.0)
    rate = jnp.where(fluid, rate, 1.0)
    base = 1.0 - 1.5 * (vel[0] * vel[0] + vel[1] * vel[1] + vel[2] * vel[2])
    weighted = {w: w * scale for w in set(WEIGHTS)}
    out = [None] * Q
    relaxed = values[0] + rate * (weighted[WEIGHTS[0]] * base - values[0])
    out[0] = jnp.where(wall, values[0], relaxed)
    for q in range(1, Q, 2):
        project = None
        for factor, component in zip(VELOCITIES[q], vel):
            if factor == 0:
                continue
            if project is None:
                project = component
            else:
                project = project + component if factor > 0 else project - component
        even = base + 4.5 * (project * project)
        odd = 3.0 * project
        w = weighted[WEIGHTS[q]]
        forward = values[q] + rate * (w * (even + odd) - values[q])
        backward = values[q + 1] + rate * (w * (even - odd) - values[q + 1])
        out[q] = jnp.where(wall, values[q + 1], forward)
        out[q + 1] = jnp.where(wall, values[q], backward)
    return out


def roll_by(block, step, axis):
    if step == 0:
        return block
    return pltpu.roll(block, step % block.shape[axis], axis)


def face_slots(axis, sign):
    picks = []
    for q in range(Q):
        if VELOCITIES[q][axis] * sign >= 0:
            picks.append((q, 0))
        else:
            picks.append((OPPOSITE[q], 1))
    return picks


def first_kernel(pops, rate, flags, c1, up, down):
    planes = pops.shape[1]

    def plane(x, carry):
        values = [pops[q, x] for q in range(Q)]
        result = collide(values, rate[x], flags[x])
        for q in range(Q):
            c1[q, x] = roll_by(result[q], VELOCITIES[q][2], 1)
        return carry

    lax.fori_loop(0, planes, plane, 0)
    for slot, (q, depth) in enumerate(face_slots(0, 1)):
        up[slot] = c1[q, planes - 1 - depth]
    for slot, (q, depth) in enumerate(face_slots(0, -1)):
        down[slot] = c1[q, depth]
    up[FLAG_SLOT] = flags[planes - 1].astype(F32)
    up[RATE_SLOT] = rate[planes - 1]
    down[FLAG_SLOT] = flags[0].astype(F32)
    down[RATE_SLOT] = rate[0]


def pack_kernel(c1, rate, flags, below, above, top, bottom):
    planes = c1.shape[1]
    last = c1.shape[2] - 1
    for out, sign in ((top, 1), (bottom, -1)):
        for slot, (q, depth) in enumerate(face_slots(1, sign)):
            y = last - depth if sign > 0 else depth
            row = slice(y, y + 1)
            out[slot, 0:1] = below[OPPOSITE[q], row]
            out[slot, 1:2] = below[q, row]
            for x in range(planes):
                out[slot, x + 2 : x + 3] = c1[q, x, row]
            out[slot, planes + 2 : planes + 3] = above[q, row]
            out[slot, planes + 3 : planes + 4] = above[OPPOSITE[q], row]
        y = last if sign > 0 else 0
        row = slice(y, y + 1)
        for slot in (FLAG_SLOT, RATE_SLOT):
            out[slot, 0:1] = below[slot, row]
            out[slot, 1:2] = below[slot, row]
            for x in range(planes):
                if slot == FLAG_SLOT:
                    out[slot, x + 2 : x + 3] = flags[x, row].astype(F32)
                else:
                    out[slot, x + 2 : x + 3] = rate[x, row]
            out[slot, planes + 2 : planes + 3] = above[slot, row]
            out[slot, planes + 3 : planes + 4] = above[slot, row]


def second_kernel(
    block_source,
    block_target,
    block_node,
    block_count,
    c1,
    rate,
    flags,
    below,
    above,
    top,
    bottom,
    behind,
    ahead,
    internal_own,
    internal_other,
    out,
    message,
    extended,
    kinds,
    rates,
    second,
    edge_low,
    edge_high,
    loads,
):
    planes, rows, length = c1.shape[1:]
    half = length // BLK
    slots = block_source.shape[2]
    slab = lax.axis_index("slab")
    inner = lax.axis_index("inner")
    slab_end = lax.axis_size("slab") - 1
    inner_end = lax.axis_size("inner") - 1

    for q in range(Q):
        for x in range(planes):
            extended[q, x + 2] = c1[q, x]
        extended[q, 1] = below[q]
        extended[q, planes + 2] = above[q]
        if VELOCITIES[q][0] > 0:
            extended[q, 0] = below[OPPOSITE[q]]
        if VELOCITIES[q][0] < 0:
            extended[q, planes + 3] = above[OPPOSITE[q]]
    kinds[0] = below[FLAG_SLOT]
    rates[0] = below[RATE_SLOT]
    kinds[planes + 1] = above[FLAG_SLOT]
    rates[planes + 1] = above[RATE_SLOT]
    for x in range(planes):
        kinds[x + 1] = flags[x].astype(F32)
        rates[x + 1] = rate[x]

    sub = lax.broadcasted_iota(jnp.int32, (rows, length), 0)
    is_first = sub == 0
    is_last = sub == rows - 1

    def plane_one(at, carry):
        values = []
        for q in range(Q):
            step_x, step_y, _ = VELOCITIES[q]
            block = extended[q, at + 1 - step_x]
            if step_y > 0:
                edge = behind[q, pl.ds(at + 1 - step_x, 1)]
                block = jnp.where(is_first, edge, roll_by(block, 1, 0))
            if step_y < 0:
                edge = ahead[q, pl.ds(at + 1 - step_x, 1)]
                block = jnp.where(is_last, edge, roll_by(block, -1, 0))
            values.append(block)
        result = collide(values, rates[at], kinds[at])
        for q in range(Q):
            second[q, at] = roll_by(result[q], VELOCITIES[q][2], 1)
        return carry

    lax.fori_loop(0, planes + 2, plane_one, 0)

    @pl.when(slab == 0)
    def _():
        for q in range(Q):
            if VELOCITIES[q][0] > 0:
                second[q, 0] = jnp.zeros((rows, length), F32)

    @pl.when(slab == slab_end)
    def _():
        for q in range(Q):
            if VELOCITIES[q][0] < 0:
                second[q, planes + 1] = jnp.zeros((rows, length), F32)

    across = lax.broadcasted_iota(jnp.int32, (planes + 4, length), 0)
    hidden = ((across <= 1) & (slab == 0)) | ((across >= planes + 2) & (slab == slab_end))
    for sign, received, sent, edge, outside in (
        (1, behind, bottom, edge_low, inner == 0),
        (-1, ahead, top, edge_high, inner == inner_end),
    ):
        values = []
        for q in range(Q):
            step_x, step_y, _ = VELOCITIES[q]
            if step_y == 0:
                block = received[q]
            elif step_y == sign:
                block = received[OPPOSITE[q]]
            else:
                block = sent[q]
            values.append(roll_by(block, step_x, 0))
        result = collide(values, received[RATE_SLOT], received[FLAG_SLOT])
        place = 0
        for q in range(Q):
            if VELOCITIES[q][1] == sign:
                kept = jnp.where(hidden | outside, 0.0, result[q])
                edge[place] = roll_by(kept, VELOCITIES[q][2], 1)
                place += 1

    def plane_two(x, carry):
        values = []
        places = {1: 0, -1: 0}
        for q in range(Q):
            step_x, step_y, _ = VELOCITIES[q]
            block = second[q, x + 1 - step_x]
            if step_y > 0:
                edge = edge_low[places[1], pl.ds(x + 2 - step_x, 1)]
                places[1] += 1
                block = jnp.where(is_first, edge, roll_by(block, 1, 0))
            if step_y < 0:
                edge = edge_high[places[-1], pl.ds(x + 2 - step_x, 1)]
                places[-1] += 1
                block = jnp.where(is_last, edge, roll_by(block, -1, 0))
            values.append(block)
            out[q, x] = block
        density, flow_x, flow_y, flow_z = moments(values)
        parts = (
            LOAD_SCALE * flow_x,
            LOAD_SCALE * (flow_y + (density - 1.0) / 3.0),
            LOAD_SCALE * flow_z,
        )
        for part in range(3):
            for piece in range(half):
                loads[x * half + piece, part] = parts[part][:, piece * BLK : (piece + 1) * BLK]
        return carry

    lax.fori_loop(0, planes, plane_two, 0)

    node_blocks = internal_own.shape[1]
    live = block_count[0, 0]
    for k in range(slots):
        run = block_source[0, 0, k]
        x = run // (rows * half)
        left = run - x * (rows * half)
        y = left // half
        piece = left - y * half
        for part in range(3):
            message[4 * k + part : 4 * k + part + 1] = loads[x * half + piece, part, pl.ds(y, 1)]
        key = jnp.where(k < live, block_target[0, 0, k] * node_blocks + block_node[0, 0, k], -1)
        message[4 * k + 3 : 4 * k + 4] = jnp.broadcast_to(key, (1, BLK)).astype(F32)
    for part in range(3):
        start = 4 * slots + part * node_blocks
        message[start : start + node_blocks] = internal_own[part] + internal_other[part]


def shell_kernel(
    elements,
    displacement,
    next_nodes,
    shape_inverse,
    stiffness,
    own,
    other,
    ids,
    shapes,
    forces,
):
    node_dev = displacement.shape[1]
    node_blocks = node_dev // BLK
    runs = elements.shape[1] // BLK
    groups = runs // 8
    for j in range(runs):
        lanes = slice(j * BLK, (j + 1) * BLK)
        for row in range(3):
            ids[row, j : j + 1] = elements[row : row + 1, lanes]
            shapes[row, j : j + 1] = shape_inverse[row : row + 1, lanes]

    def compute(group, carry):
        rows = pl.ds(pl.multiple_of(group * 8, 8), 8)
        low = [ids[corner, rows] & (BLK - 1) for corner in range(3)]
        high = [ids[corner, rows] >> 7 for corner in range(3)]
        nodes = [[jnp.zeros((8, BLK), F32)] * 3 for _ in range(3)]
        for block in range(2 * node_blocks):
            source = displacement if block < node_blocks else next_nodes
            start = (block % node_blocks) * BLK
            table = [
                jnp.broadcast_to(source[part : part + 1, start : start + BLK], (8, BLK))
                for part in range(3)
            ]
            for corner in range(3):
                here = high[corner] == block
                for part in range(3):
                    picked = jnp.take_along_axis(
                        table[part], low[corner], axis=1, mode="promise_in_bounds"
                    )
                    nodes[corner][part] = jnp.where(here, picked, nodes[corner][part])
        diag_a = shapes[0, rows]
        skew_b = shapes[1, rows]
        diag_c = shapes[2, rows]
        stiff = stiffness[rows]
        first, second, third = nodes
        edge_one = [second[p] - first[p] for p in range(3)]
        edge_two = [third[p] - first[p] for p in range(3)]
        one = [diag_a * edge_one[p] for p in range(3)]
        two = [skew_b * edge_one[p] + diag_c * edge_two[p] for p in range(3)]
        one[0] = one[0] + 1.0
        two[1] = two[1] + 1.0
        aa = one[0] * one[0] + one[1] * one[1] + one[2] * one[2]
        ab = one[0] * two[0] + one[1] * two[1] + one[2] * two[2]
        bb = two[0] * two[0] + two[1] * two[1] + two[2] * two[2]
        determinant = aa * bb - ab * ab
        inverse_aa = bb / determinant
        inverse_ab = -ab / determinant
        inverse_bb = aa / determinant
        pressure = LAME_RATIO * (0.5 * jnp.log(determinant))
        for p in range(3):
            pulled_one = one[p] * inverse_aa + two[p] * inverse_ab
            pulled_two = one[p] * inverse_ab + two[p] * inverse_bb
            stress_one = stiff * (one[p] - pulled_one + pressure * pulled_one)
            stress_two = stiff * (two[p] - pulled_two + pressure * pulled_two)
            force_one = diag_a * stress_one + skew_b * stress_two
            force_two = diag_c * stress_two
            for corner, force in enumerate((-(force_one + force_two), force_one, force_two)):
                rest = force
                for part in range(3):
                    piece = rest.astype(jnp.bfloat16).astype(F32)
                    rest = rest - piece
                    forces[part * 3 + p, corner, rows] = piece
        return carry

    lax.fori_loop(0, groups, compute, 0)

    slots = 2 * node_blocks
    slot_ids = lax.broadcasted_iota(jnp.int32, (slots, BLK), 0)
    lane_ids = lax.broadcasted_iota(jnp.int32, (BLK, BLK), 0)

    def spread(group, total):
        corner = group // groups
        base = (group - corner * groups) * 8
        left = [[] for _ in range(9)]
        right = []
        for j in range(8):
            row = pl.ds(base + j, 1)
            numbers = ids[corner, row]
            here = slot_ids == (numbers >> 7)
            right.append(jnp.where(lane_ids == (numbers & (BLK - 1)), 1.0, 0.0).astype(jnp.bfloat16))
            for part in range(9):
                left[part].append(
                    jnp.where(here, forces[part, corner, row], 0.0).astype(jnp.bfloat16)
                )
        tall = jnp.concatenate([jnp.concatenate(part, axis=1) for part in left], axis=0)
        wide = jnp.concatenate(right, axis=1)
        return total + lax.dot_general(
            tall, wide, (((1,), (1,)), ((), ())), preferred_element_type=F32
        )

    total = lax.fori_loop(0, 3 * groups, spread, jnp.zeros((9 * slots, BLK), F32))
    for p in range(3):
        summed = (
            total[p * slots : (p + 1) * slots]
            + total[(3 + p) * slots : (4 + p) * slots]
            + total[(6 + p) * slots : (7 + p) * slots]
        )
        own[p] = summed[:node_blocks]
        other[p] = summed[node_blocks:]


def final_kernel(*refs):
    messages = refs[:-3]
    residual, motion, keys = refs[-3:]
    slots = keys.shape[0]
    node_blocks = residual.shape[1] // BLK
    count = len(messages)
    inner = lax.axis_index("inner")
    mine = messages[0]
    for k in range(slots):
        keys[k : k + 1] = mine[4 * k + 3 : 4 * k + 4]
    wanted = keys[...]
    node_ids = lax.broadcasted_iota(jnp.int32, (node_blocks, BLK), 0)
    own_ids = (node_ids + inner * node_blocks).astype(F32)
    external = [jnp.zeros((node_blocks, BLK), F32)] * 3
    moved = [jnp.zeros((slots, BLK), F32)] * 3
    for message in messages:
        for k in range(slots):
            key = message[4 * k + 3 : 4 * k + 4]
            here = own_ids == key
            same = wanted == key
            for part in range(3):
                row = message[4 * k + part : 4 * k + part + 1]
                external[part] = external[part] + jnp.where(here, row, 0.0)
                moved[part] = moved[part] + jnp.where(same, row, 0.0)
    for distance, message in enumerate(messages):
        sender = lax.rem(inner - distance + count, count)
        for b in range(node_blocks):
            key = jnp.broadcast_to(sender * node_blocks + b, (1, BLK)).astype(F32)
            same = wanted == key
            for part in range(3):
                at = 4 * slots + part * node_blocks + b
                moved[part] = moved[part] - jnp.where(same, message[at : at + 1], 0.0)
    live = wanted >= 0.0
    for part in range(3):
        start = 4 * slots + part * node_blocks
        left = external[part] - mine[start : start + node_blocks]
        for b in range(node_blocks):
            residual[part : part + 1, b * BLK : (b + 1) * BLK] = left[b : b + 1]
        shown = jnp.where(live, COMPLIANCE * moved[part], 0.0)
        for k in range(slots):
            motion[0, 0, k, part : part + 1] = shown[k : k + 1]


def call(kernel, outs, scratch=(), scalars=0, inputs=0):
    return pl.pallas_call(
        kernel,
        out_shape=outs,
        in_specs=[pl.BlockSpec(memory_space=pltpu.SMEM)] * scalars
        + [pl.BlockSpec(memory_space=pltpu.VMEM)] * inputs,
        out_specs=jax.tree.map(lambda _: pl.BlockSpec(memory_space=pltpu.VMEM), outs),
        scratch_shapes=list(scratch),
        compiler_params=pltpu.CompilerParams(vmem_limit_bytes=VMEM_BYTES),
    )


def shift(block, axis, step):
    count = lax.axis_size(axis)
    route = [(i, i + step) for i in range(count) if 0 <= i + step < count]
    return lax.ppermute(block, axis, route)


def around(block, axis, step):
    count = lax.axis_size(axis)
    return lax.ppermute(block, axis, [(i, (i + step) % count) for i in range(count)])


def shards(
    populations,
    relaxation,
    node_flags,
    displacement,
    elements,
    shape_inverse,
    stiffness,
    block_source,
    block_target,
    block_node,
    block_count,
):
    planes, rows, length = populations.shape[1:]
    half = length // BLK
    node_dev = displacement.shape[1]
    node_blocks = node_dev // BLK
    runs = stiffness.shape[0] // BLK
    slots = block_source.shape[2]
    count = lax.axis_size("inner")
    shape = lambda *dims: jax.ShapeDtypeStruct(dims, F32)

    next_nodes = shift(displacement, "slab", -1)
    face = shape(SLOTS, rows, length)
    c1, up, down = call(first_kernel, (shape(*populations.shape), face, face), inputs=3)(
        populations, relaxation, node_flags
    )
    below = shift(up, "slab", 1)
    above = shift(down, "slab", -1)
    own, other = call(
        shell_kernel,
        (shape(3, node_blocks, BLK), shape(3, node_blocks, BLK)),
        scratch=(
            pltpu.VMEM((3, runs, BLK), jnp.int32),
            pltpu.VMEM((3, runs, BLK), F32),
            pltpu.VMEM((9, 3, runs, BLK), F32),
        ),
        inputs=5,
    )(elements, displacement, next_nodes, shape_inverse, stiffness.reshape(runs, BLK))
    arrived = shift(other, "slab", 1)
    side = shape(SLOTS, planes + 4, length)
    top, bottom = call(pack_kernel, (side, side), inputs=5)(
        c1, relaxation, node_flags, below, above
    )
    behind = shift(top, "inner", 1)
    ahead = shift(bottom, "inner", -1)
    lines = 4 * slots + 3 * node_blocks
    values, message = call(
        second_kernel,
        (shape(*populations.shape), shape(lines, BLK)),
        scratch=(
            pltpu.VMEM((Q, planes + 4, rows, length), F32),
            pltpu.VMEM((planes + 2, rows, length), F32),
            pltpu.VMEM((planes + 2, rows, length), F32),
            pltpu.VMEM((Q, planes + 2, rows, length), F32),
            pltpu.VMEM((5, planes + 4, length), F32),
            pltpu.VMEM((5, planes + 4, length), F32),
            pltpu.VMEM((planes * half, 3, rows, BLK), F32),
        ),
        scalars=4,
        inputs=11,
    )(
        block_source,
        block_target,
        block_node,
        block_count,
        c1,
        relaxation,
        node_flags,
        below,
        above,
        top,
        bottom,
        behind,
        ahead,
        own,
        arrived,
    )
    messages = [message] + [around(message, "inner", step) for step in range(1, count)]
    residual, motion = call(
        final_kernel,
        (shape(3, node_dev), shape(1, 1, slots, 3, BLK)),
        scratch=(pltpu.VMEM((slots, BLK), F32),),
        inputs=count,
    )(*messages)
    return values, residual, motion


def solution(mesh):
    return jax.shard_map(
        shards,
        mesh=mesh,
        in_specs=(
            P(None, ("group", "slab"), "inner", None),
            P(("group", "slab"), "inner", None),
            P(("group", "slab"), "inner", None),
            P(None, ("group", "slab", "inner")),
            P(None, ("group", "slab", "inner")),
            P(None, ("group", "slab", "inner")),
            P(("group", "slab", "inner")),
            P(("group", "slab"), "inner", None),
            P(("group", "slab"), "inner", None),
            P(("group", "slab"), "inner", None),
            P(("group", "slab"), "inner"),
        ),
        out_specs=(
            P(None, ("group", "slab"), "inner", None),
            P(None, ("group", "slab", "inner")),
            P(("group", "slab"), "inner", None, None, None),
        ),
        check_vma=False,
    )
```

time: 268 us -> 50.5 us (0.19)
  other arithmetic: 86.4 us -> 0 us
  local copies, waits for them, and re-layouts: 77.8 us -> 3.71 us
  waiting for transfers between devices: 44.4 us -> 14 us
  between operations: 16.2 us -> 1.42 us
  blocking collectives: 13.4 us -> 0 us
  Pallas kernels: 0 us -> 11.2 us
  starting transfers between devices: 26 us -> 19.7 us
    scatter-add x3 -> x0, other arithmetic: 70 us -> none  [shards(): node_forces = node_forces.at[:, elements[corner]].add(nodal[corner])]
    gather x7 -> x0, local copies, waits for them, and re-layouts: 55.1 us -> none  [the longest x2 18.3 us: shards(): table[:, elements[1]]]
    unnamed x2 -> x0, waiting for transfers between devices: 35.4 us -> none
    all_gather x1 -> x0, blocking collectives: 13.4 us -> none  [shards(): lax.all_gather(block_view(residual, node_blocks)[None], 'inner', axis=0,...]
    pallas_call x0 -> x5, Pallas kernels: none -> 11.2 us  [the longest x1 6.92 us: shards(): call(shell_kernel, (shape(3, node_blocks, BLK), shape(3, node_blocks, BLK...]
    slice x41 -> x0, local copies, waits for them, and re-layouts: 7.29 us -> none  [the longest x2 2.98 us: shards(): node_forces[:, node_dev:]]
    ppermute x10 -> x9, starting transfers between devices: 26 us -> 19.7 us  [the longest x6 14.3 us: shift(): return lax.ppermute(block, axis, route)]
    ppermute x10 -> x9, waiting for transfers between devices: 9.02 us -> 14 us  [the longest x6 9.22 us: shift(): return lax.ppermute(block, axis, route)]
  transfers between devices with their start and end apart: 11 -> 9, of which waited for: 5 -> 6; matrix products, arithmetic and copies ran while one was open for 55% -> 0% of each run, Pallas kernels for 0% -> 14%
where the time goes in v1:
time: 50.5 us; the launch traced here: 50 us
  starting transfers between devices  19.7 us (39%)
  waiting for transfers between devices  14 us (28%)
  Pallas kernels  11.2 us (22%)
  local copies, waits for them, and re-layouts  3.71 us (7%)
  between operations  1.42 us (3%)
    ppermute x6, starting transfers between devices, shift(): return lax.ppermute(block, axis, route)  14.3 us
    ppermute x6, waiting for transfers between devices, shift(): return lax.ppermute(block, axis, route)  9.22 us
    pallas_call x1, Pallas kernels, shards(): call(shell_kernel, (shape(3, node_blocks, BLK), shape(3, node_blocks, BLK...  6.92 us
    ppermute x3, starting transfers between devices, around(): lax.ppermute(block, axis, [(i, (i + step) % count) for i in range(count)])  5.4 us
    ppermute x3, waiting for transfers between devices, around(): lax.ppermute(block, axis, [(i, (i + step) % count) for i in range(count)])  4.79 us
    unnamed x23, local copies, waits for them, and re-layouts  3.71 us
    pallas_call x1, Pallas kernels, shards(): call(second_kernel, (shape(*populations.shape), shape(lines, BLK)), scrat...  2.72 us
  transfers between devices with their start and end apart: 9, of which 6 were waited for; matrix products, arithmetic and copies ran while one was open for 0% of the time, Pallas kernels for 14%

profile of v1, /device:TPU:0, one launch (start us, length us, event | category | flops | bytes accessed | tf_op | source)
XLA Modules:
  0.0 50.0 jit_solution(4379240252917511209)
XLA Ops:
  0.6 0.0 copy-start
  0.6 1.1 %copy-done = f32[19,4,8,256]{3,2,1,0:T(8,128)S(1)} copy-done((f32[19,4,8,256]{3,2,1,0:T(8,128)S(1)}, f32[19,4,8,256]{3,2,1,0:T(8,128)}, u32[]{:S(2)}) %copy-start) | copy-done | bytes 622616
  1.7 0.0 copy-start.1
  1.7 0.8 %copy-done.1 = f32[4,8,256]{2,1,0:T(8,128)S(1)} copy-done((f32[4,8,256]{2,1,0:T(8,128)S(1)}, f32[4,8,256]{2,1,0:T(8,128)}, u32[]{:S(2)}) %copy-start.1) | copy-done | bytes 32792
  2.5 0.0 copy-start.2
  2.5 0.8 %copy-done.2 = s32[4,8,256]{2,1,0:T(8,128)S(1)} copy-done((s32[4,8,256]{2,1,0:T(8,128)S(1)}, s32[4,8,256]{2,1,0:T(8,128)}, u32[]{:S(2)}) %copy-start.2) | copy-done | bytes 32792
  3.2 0.6 %shard_map.130 = (f32[19,4,8,256]{3,2,1,0:T(8,128)S(1)}, f32[21,8,256]{2,1,0:T(8,128)S(1)}, f32[21,8,256]{2,1,0:T(8,128)S(1)}) custom-call(f32[19,4,8,256]{3,2,1,0:T(8,128)S(1)} %copy-done, f32[4,8,256]{2,1,0:T(8,128)S(1)} %copy-done.1, s32[4,8,256]{2,1,0:T(8,128)S(1)} %copy-done.2), custom_call_target="tpu_custom_call" | custom-call | tf_op jit(solution)/shard_map/pallas_call | solution.py:526
  3.8 2.4 %collective-permute-start = (f32[21,8,256]{2,1,0:T(8,128)S(1)}, f32[21,8,256]{2,1,0:T(8,128)S(1)}, u32[]{:S(2)}, u32[]{:S(2)}) collective-permute-start(f32[21,8,256]{2,1,0:T(8,128)S(1)} %get-tuple-element.15), channel_id=1, source_target_pairs={{0,4},{4,8},{8,12},{1,5},{5,9},{9,13},{2,6},{6,10},{10,14},{3,7},{... | collective-permute-start | bytes 516104 | tf_op jit(solution)/shard_map/ppermute | solution.py:494
  6.2 1.3 %collective-permute-start.1 = (f32[21,8,256]{2,1,0:T(8,128)S(1)}, f32[21,8,256]{2,1,0:T(8,128)S(1)}, u32[]{:S(2)}, u32[]{:S(2)}) collective-permute-start(f32[21,8,256]{2,1,0:T(8,128)S(1)} %get-tuple-element.16), channel_id=1, source_target_pairs={{4,0},{8,4},{12,8},{5,1},{9,5},{13,9},{6,2},{10,6},{14,10},{7,3},{... | collective-permute-start | bytes 516104 | tf_op jit(solution)/shard_map/ppermute | solution.py:494
  7.5 0.0 collective-permute-done.below
  7.5 4.1 %collective-permute-done.1.above = f32[21,8,256]{2,1,0:T(8,128)S(1)} collective-permute-done((f32[21,8,256]{2,1,0:T(8,128)S(1)}, f32[21,8,256]{2,1,0:T(8,128)S(1)}, u32[]{:S(2)}, u32[]{:S(2)}) %collective-permute-start.1) | collective-permute-done | bytes 172064 | tf_op jit(solution)/shard_map/ppermute | solution.py:494
  11.6 0.0 copy-start.6
  11.6 0.0 copy-start.4
  11.6 0.0 copy-start.5
  11.6 0.0 copy-start.7
  11.6 0.2 shard_map.131
  11.8 3.5 %collective-permute-start.2 = (f32[21,8,256]{2,1,0:T(8,128)S(1)}, f32[21,8,256]{2,1,0:T(8,128)S(1)}, u32[]{:S(2)}, u32[]{:S(2)}) collective-permute-start(f32[21,8,256]{2,1,0:T(8,128)S(1)} %get-tuple-element.17.top), channel_id=1, source_target_pairs={{0,1},{1,2},{2,3},{4,5},{5,6},{6,7},{8,9},{9,10},{10,11},{12,13},{... | collective-permute-start | bytes 516104 | tf_op jit(solution)/shard_map/ppermute | solution.py:494
  15.3 1.3 %collective-permute-start.3 = (f32[21,8,256]{2,1,0:T(8,128)S(1)}, f32[21,8,256]{2,1,0:T(8,128)S(1)}, u32[]{:S(2)}, u32[]{:S(2)}) collective-permute-start(f32[21,8,256]{2,1,0:T(8,128)S(1)} %get-tuple-element.18.bottom), channel_id=1, source_target_pairs={{1,0},{2,1},{3,2},{5,4},{6,5},{7,6},{9,8},{10,9},{11,10},{13,12},{... | collective-permute-start | bytes 516104 | tf_op jit(solution)/shard_map/ppermute | solution.py:494
  16.6 0.0 copy-done.6
  16.6 1.3 %collective-permute-start.4 = (f32[3,2048]{1,0:T(4,128)S(1)}, f32[3,2048]{1,0:T(4,128)S(1)}, u32[]{:S(2)}, u32[]{:S(2)}) collective-permute-start(f32[3,2048]{1,0:T(4,128)S(1)} %copy-done.6), channel_id=1, source_target_pairs={{4,0},{8,4},{12,8},{5,1},{9,5},{13,9},{6,2},{10,6},{14,10},{7,3},{... | collective-permute-start | bytes 73736 | tf_op jit(solution)/shard_map/ppermute | solution.py:494
  17.9 4.9 %collective-permute-done.4.next_nodes = f32[3,2048]{1,0:T(4,128)S(1)} collective-permute-done((f32[3,2048]{1,0:T(4,128)S(1)}, f32[3,2048]{1,0:T(4,128)S(1)}, u32[]{:S(2)}, u32[]{:S(2)}) %collective-permute-start.4) | collective-permute-done | bytes 24608 | tf_op jit(solution)/shard_map/ppermute | solution.py:494
  22.9 0.0 copy-done.4
  22.9 0.0 copy-done.5
  22.9 0.0 copy-done.7
  22.9 0.0 copy-start.3
  22.9 6.9 %shard_map.132 = (f32[3,16,128]{2,1,0:T(8,128)S(1)}, f32[3,16,128]{2,1,0:T(8,128)S(1)}) custom-call(s32[3,4096]{1,0:T(4,128)S(1)} %copy-done.4, f32[3,2048]{1,0:T(4,128)S(1)} %copy-done.6, f32[3,2048]{1,0:T(4,128)S(1)} %collective-permute-done.4.next_nodes, f32[3,4096]{1,0:T(4,128)S(1)} %copy-done.5, f32[32,128]{1,0:T(8,128)S(1)} %bitcast.1), custom_call_target="tpu_custom_call" | custom-call | tf_op jit(solution)/shard_map/pallas_call | solution.py:531
  29.8 4.5 %collective-permute-start.5 = (f32[3,16,128]{2,1,0:T(8,128)S(1)}, f32[3,16,128]{2,1,0:T(8,128)S(1)}, u32[]{:S(2)}, u32[]{:S(2)}) collective-permute-start(f32[3,16,128]{2,1,0:T(8,128)S(1)} %get-tuple-element.20), channel_id=1, source_target_pairs={{0,4},{4,8},{8,12},{1,5},{5,9},{9,13},{2,6},{6,10},{10,14},{3,7},{... | collective-permute-start | bytes 73736 | tf_op jit(solution)/shard_map/ppermute | solution.py:494
  35.0 0.0 copy-start.8
  35.0 0.0 copy-start.9
  35.0 0.0 copy-start.10
  35.0 0.1 collective-permute-done.5.internal_other
  35.2 0.0 collective-permute-done.2.behind
  35.2 0.0 collective-permute-done.3.ahead
  35.2 0.0 copy-done.3
  35.2 0.5 copy-done.8
  35.7 0.0 copy-done.9
  35.7 0.0 copy-done.10
  35.7 2.7 %shard_map.133 = (f32[19,4,8,256]{3,2,1,0:T(8,128)}, f32[80,128]{1,0:T(8,128)S(1)}) custom-call(s32[1,1,8]{2,1,0:T(1,128)S(1)} %copy-done.8, s32[1,1,8]{2,1,0:T(1,128)S(1)} %copy-done.9, s32[1,1,8]{2,1,0:T(1,128)S(1)} %copy-done.10, s32[1,1]{1,0:T(1,128)S(6)} %copy.15.block_count, f32[19,4,8,256]{3,2,1,0:T(8,128)S(1)} %get-tuple-element.14.c1, ...), custom_call_target="tpu_custom_call" | custom-call | tf_op jit(solution)/shard_map/pallas_call | solution.py:549
  38.4 4.4 %collective-permute-start.8 = (f32[80,128]{1,0:T(8,128)S(1)}, f32[80,128]{1,0:T(8,128)S(1)}, u32[]{:S(2)}, u32[]{:S(2)}) collective-permute-start(f32[80,128]{1,0:T(8,128)S(1)} %get-tuple-element.22.refs_0_), channel_id=1, source_target_pairs={{0,3},{1,0},{2,1},{3,2},{4,7},{5,4},{6,5},{7,6},{8,11},{9,8},{10,9... | collective-permute-start | bytes 122888 | tf_op jit(solution)/shard_map/ppermute | solution.py:499
  42.8 0.0 collective-permute-start.7
  42.8 1.0 %collective-permute-start.6 = (f32[80,128]{1,0:T(8,128)S(1)}, f32[80,128]{1,0:T(8,128)S(1)}, u32[]{:S(2)}, u32[]{:S(2)}) collective-permute-start(f32[80,128]{1,0:T(8,128)S(1)} %get-tuple-element.22.refs_0_), channel_id=1, source_target_pairs={{0,1},{1,2},{2,3},{3,0},{4,5},{5,6},{6,7},{7,4},{8,9},{9,10},{10,1... | collective-permute-start | bytes 122888 | tf_op jit(solution)/shard_map/ppermute | solution.py:499
  43.8 0.9 %collective-permute-done.8.refs_3_ = f32[80,128]{1,0:T(8,128)S(1)} collective-permute-done((f32[80,128]{1,0:T(8,128)S(1)}, f32[80,128]{1,0:T(8,128)S(1)}, u32[]{:S(2)}, u32[]{:S(2)}) %collective-permute-start.8) | collective-permute-done | bytes 40992 | tf_op jit(solution)/shard_map/ppermute | solution.py:499
  44.7 3.1 %collective-permute-done.7.refs_2_ = f32[80,128]{1,0:T(8,128)S(1)} collective-permute-done((f32[80,128]{1,0:T(8,128)S(1)}, f32[80,128]{1,0:T(8,128)S(1)}, u32[]{:S(2)}, u32[]{:S(2)}) %collective-permute-start.7) | collective-permute-done | bytes 40992 | tf_op jit(solution)/shard_map/ppermute | solution.py:499
  47.8 0.8 %collective-permute-done.6.refs_1_ = f32[80,128]{1,0:T(8,128)S(1)} collective-permute-done((f32[80,128]{1,0:T(8,128)S(1)}, f32[80,128]{1,0:T(8,128)S(1)}, u32[]{:S(2)}, u32[]{:S(2)}) %collective-permute-start.6) | collective-permute-done | bytes 40992 | tf_op jit(solution)/shard_map/ppermute | solution.py:499
  48.6 0.8 %shard_map.134 = (f32[3,2048]{1,0:T(4,128)}, f32[1,1,8,3,128]{4,3,2,1,0:T(4,128)S(1)}) custom-call(f32[80,128]{1,0:T(8,128)S(1)} %get-tuple-element.22.refs_0_, f32[80,128]{1,0:T(8,128)S(1)} %collective-permute-done.6.refs_1_, f32[80,128]{1,0:T(8,128)S(1)} %collective-permute-done.7.refs_2_, f32[80,128]{1,0:T(8,128)S(1)} %collective-permute-done.8.refs_3_), custom_call_target="tpu_custom_call" | custom-call | tf_op jit(solution)/shard_map/pallas_call | solution.py:581
  49.4 0.6 %copy.14 = f32[1,1,8,3,128]{4,2,3,1,0:T(8,128)} copy(f32[1,1,8,3,128]{4,3,2,1,0:T(4,128)S(1)} %get-tuple-element.27) | data formatting | bytes 24576
Async XLA Ops:
  0.6 1.1 %copy-start = (f32[19,4,8,256]{3,2,1,0:T(8,128)S(1)}, f32[19,4,8,256]{3,2,1,0:T(8,128)}, u32[]{:S(2)}) copy-start(f32[19,4,8,256]{3,2,1,0:T(8,128)} %pops.1) | copy-start | bytes 1867780
  1.7 0.8 %copy-start.1 = (f32[4,8,256]{2,1,0:T(8,128)S(1)}, f32[4,8,256]{2,1,0:T(8,128)}, u32[]{:S(2)}) copy-start(f32[4,8,256]{2,1,0:T(8,128)} %rate.5) | copy-start | bytes 98308
  2.5 0.8 %copy-start.2 = (s32[4,8,256]{2,1,0:T(8,128)S(1)}, s32[4,8,256]{2,1,0:T(8,128)}, u32[]{:S(2)}) copy-start(s32[4,8,256]{2,1,0:T(8,128)} %flags.5) | copy-start | bytes 98308
  3.8 3.7 %collective-permute-start = (f32[21,8,256]{2,1,0:T(8,128)S(1)}, f32[21,8,256]{2,1,0:T(8,128)S(1)}, u32[]{:S(2)}, u32[]{:S(2)}) collective-permute-start(f32[21,8,256]{2,1,0:T(8,128)S(1)} %get-tuple-element.15), channel_id=1, source_target_pairs={{0,4},{4,8},{8,12},{1,5},{5,9},{9,13},{2,6},{6,10},{10,14},{3,7},{... | collective-permute-start | bytes 516104 | tf_op jit(solution)/shard_map/ppermute | solution.py:494
  6.2 5.4 %collective-permute-start.1 = (f32[21,8,256]{2,1,0:T(8,128)S(1)}, f32[21,8,256]{2,1,0:T(8,128)S(1)}, u32[]{:S(2)}, u32[]{:S(2)}) collective-permute-start(f32[21,8,256]{2,1,0:T(8,128)S(1)} %get-tuple-element.16), channel_id=1, source_target_pairs={{4,0},{8,4},{12,8},{5,1},{9,5},{13,9},{6,2},{10,6},{14,10},{7,3},{... | collective-permute-start | bytes 516104 | tf_op jit(solution)/shard_map/ppermute | solution.py:494
  11.6 5.0 %copy-start.6 = (f32[3,2048]{1,0:T(4,128)S(1)}, f32[3,2048]{1,0:T(4,128)}, u32[]{:S(2)}) copy-start(f32[3,2048]{1,0:T(4,128)} %displacement.1) | copy-start | bytes 73732
  11.6 11.2 %copy-start.4 = (s32[3,4096]{1,0:T(4,128)S(1)}, s32[3,4096]{1,0:T(4,128)}, u32[]{:S(2)}) copy-start(s32[3,4096]{1,0:T(4,128)} %elements.1) | copy-start | bytes 147460
  11.6 11.2 %copy-start.5 = (f32[3,4096]{1,0:T(4,128)S(1)}, f32[3,4096]{1,0:T(4,128)}, u32[]{:S(2)}) copy-start(f32[3,4096]{1,0:T(4,128)} %shape_inverse.1) | copy-start | bytes 147460
  11.6 11.2 %copy-start.7 = (f32[4096]{0:T(1024)S(1)}, f32[4096]{0:T(1024)}, u32[]{:S(2)}) copy-start(f32[4096]{0:T(1024)} %param.17) | copy-start | bytes 49156
  11.8 23.4 %collective-permute-start.2 = (f32[21,8,256]{2,1,0:T(8,128)S(1)}, f32[21,8,256]{2,1,0:T(8,128)S(1)}, u32[]{:S(2)}, u32[]{:S(2)}) collective-permute-start(f32[21,8,256]{2,1,0:T(8,128)S(1)} %get-tuple-element.17.top), channel_id=1, source_target_pairs={{0,1},{1,2},{2,3},{4,5},{5,6},{6,7},{8,9},{9,10},{10,11},{12,13},{... | collective-permute-start | bytes 516104 | tf_op jit(solution)/shard_map/ppermute | solution.py:494
  15.3 19.9 %collective-permute-start.3 = (f32[21,8,256]{2,1,0:T(8,128)S(1)}, f32[21,8,256]{2,1,0:T(8,128)S(1)}, u32[]{:S(2)}, u32[]{:S(2)}) collective-permute-start(f32[21,8,256]{2,1,0:T(8,128)S(1)} %get-tuple-element.18.bottom), channel_id=1, source_target_pairs={{1,0},{2,1},{3,2},{5,4},{6,5},{7,6},{9,8},{10,9},{11,10},{13,12},{... | collective-permute-start | bytes 516104 | tf_op jit(solution)/shard_map/ppermute | solution.py:494
  16.6 6.2 %collective-permute-start.4 = (f32[3,2048]{1,0:T(4,128)S(1)}, f32[3,2048]{1,0:T(4,128)S(1)}, u32[]{:S(2)}, u32[]{:S(2)}) collective-permute-start(f32[3,2048]{1,0:T(4,128)S(1)} %copy-done.6), channel_id=1, source_target_pairs={{4,0},{8,4},{12,8},{5,1},{9,5},{13,9},{6,2},{10,6},{14,10},{7,3},{... | collective-permute-start | bytes 73736 | tf_op jit(solution)/shard_map/ppermute | solution.py:494
  22.9 12.3 %copy-start.3 = (s32[4,8,256]{2,1,0:T(8,128)S(1)}, s32[4,8,256]{2,1,0:T(8,128)}, u32[]{:S(2)}) copy-start(s32[4,8,256]{2,1,0:T(8,128)} %flags.5) | copy-start | bytes 98308
  29.8 5.4 %collective-permute-start.5 = (f32[3,16,128]{2,1,0:T(8,128)S(1)}, f32[3,16,128]{2,1,0:T(8,128)S(1)}, u32[]{:S(2)}, u32[]{:S(2)}) collective-permute-start(f32[3,16,128]{2,1,0:T(8,128)S(1)} %get-tuple-element.20), channel_id=1, source_target_pairs={{0,4},{4,8},{8,12},{1,5},{5,9},{9,13},{2,6},{6,10},{10,14},{3,7},{... | collective-permute-start | bytes 73736 | tf_op jit(solution)/shard_map/ppermute | solution.py:494
  35.0 0.7 %copy-start.8 = (s32[1,1,8]{2,1,0:T(1,128)S(1)}, s32[1,1,8]{2,1,0:T(1,128)}, u32[]{:S(2)}) copy-start(s32[1,1,8]{2,1,0:T(1,128)} %block_source.1) | copy-start | bytes 100
  35.0 0.7 %copy-start.9 = (s32[1,1,8]{2,1,0:T(1,128)S(1)}, s32[1,1,8]{2,1,0:T(1,128)}, u32[]{:S(2)}) copy-start(s32[1,1,8]{2,1,0:T(1,128)} %block_target.1) | copy-start | bytes 100
  35.0 0.7 %copy-start.10 = (s32[1,1,8]{2,1,0:T(1,128)S(1)}, s32[1,1,8]{2,1,0:T(1,128)}, u32[]{:S(2)}) copy-start(s32[1,1,8]{2,1,0:T(1,128)} %block_node.1) | copy-start | bytes 100
  38.4 6.3 %collective-permute-start.8 = (f32[80,128]{1,0:T(8,128)S(1)}, f32[80,128]{1,0:T(8,128)S(1)}, u32[]{:S(2)}, u32[]{:S(2)}) collective-permute-start(f32[80,128]{1,0:T(8,128)S(1)} %get-tuple-element.22.refs_0_), channel_id=1, source_target_pairs={{0,3},{1,0},{2,1},{3,2},{4,7},{5,4},{6,5},{7,6},{8,11},{9,8},{10,9... | collective-permute-start | bytes 122888 | tf_op jit(solution)/shard_map/ppermute | solution.py:499
  42.8 5.0 %collective-permute-start.7 = (f32[80,128]{1,0:T(8,128)S(1)}, f32[80,128]{1,0:T(8,128)S(1)}, u32[]{:S(2)}, u32[]{:S(2)}) collective-permute-start(f32[80,128]{1,0:T(8,128)S(1)} %get-tuple-element.22.refs_0_), channel_id=1, source_target_pairs={{0,2},{1,3},{2,0},{3,1},{4,6},{5,7},{6,4},{7,5},{8,10},{9,11},{10,... | collective-permute-start | bytes 122888 | tf_op jit(solution)/shard_map/ppermute | solution.py:499
  42.8 5.8 %collective-permute-start.6 = (f32[80,128]{1,0:T(8,128)S(1)}, f32[80,128]{1,0:T(8,128)S(1)}, u32[]{:S(2)}, u32[]{:S(2)}) collective-permute-start(f32[80,128]{1,0:T(8,128)S(1)} %get-tuple-element.22.refs_0_), channel_id=1, source_target_pairs={{0,1},{1,2},{2,3},{3,0},{4,5},{5,6},{6,7},{7,4},{8,9},{9,10},{10,1... | collective-permute-start | bytes 122888 | tf_op jit(solution)/shard_map/ppermute | solution.py:499

commit v2 on v1

--- a/solution.py
+++ b/solution.py
@@ -39,6 +39,9 @@
 FLAG_SLOT = 19
 RATE_SLOT = 20
 SLOTS = 21
+FORCE_SLOT = SLOTS + 6
+MESSAGE_SLOTS = FORCE_SLOT + 3
+PIECES = 2
 F32 = jnp.float32
 VMEM_BYTES = 48 * 1024 * 1024
 
@@ -117,52 +120,122 @@
     return picks
 
 
-def first_kernel(pops, rate, flags, c1, up, down):
-    planes = pops.shape[1]
+def mirror(q, axis):
+    flipped = tuple(-c if k == axis else c for k, c in enumerate(VELOCITIES[q]))
+    return VELOCITIES.index(flipped)
+
+
+def corner_rows(sign_x, sign_y):
+    rows = []
+    for q, depth in face_slots(0, sign_x):
+        if VELOCITIES[q][1] * sign_y >= 0:
+            rows.append((q, depth))
+        else:
+            rows.append((OPPOSITE[mirror(q, 1)], depth))
+    return rows
+
+
+def first_kernel(pops_hbm, rate_hbm, flags_hbm, c1, fixed, near, far, pops, rate, flags, sems):
+    planes, rows = c1.shape[1], c1.shape[2]
+    inner = lax.axis_index("inner")
+    even = lax.rem(inner, 2) == 0
+    copies = [
+        pltpu.make_async_copy(rate_hbm, rate, sems.at[planes]),
+        pltpu.make_async_copy(flags_hbm, flags, sems.at[planes + 1]),
+    ]
+    loads = [
+        pltpu.make_async_copy(pops_hbm.at[:, x], pops.at[x], sems.at[x]) for x in range(planes)
+    ]
+    for copy in loads[:1] + copies + loads[1:]:
+        copy.start()
+    for copy in copies:
+        copy.wait()
 
     def plane(x, carry):
-        values = [pops[q, x] for q in range(Q)]
-        result = collide(values, rate[x], flags[x])
+        pltpu.make_async_copy(pops_hbm.at[:, x], pops.at[x], sems.at[x]).wait()
+        kind = flags[x]
+        values = [pops[x, q] for q in range(Q)]
+        result = collide(values, rate[x], kind)
         for q in range(Q):
             c1[q, x] = roll_by(result[q], VELOCITIES[q][2], 1)
+        fixed[0, x] = kind.astype(F32)
+        fixed[1, x] = rate[x]
         return carry
 
     lax.fori_loop(0, planes, plane, 0)
-    for slot, (q, depth) in enumerate(face_slots(0, 1)):
-        up[slot] = c1[q, planes - 1 - depth]
-    for slot, (q, depth) in enumerate(face_slots(0, -1)):
-        down[slot] = c1[q, depth]
-    up[FLAG_SLOT] = flags[planes - 1].astype(F32)
-    up[RATE_SLOT] = rate[planes - 1]
-    down[FLAG_SLOT] = flags[0].astype(F32)
-    down[RATE_SLOT] = rate[0]
-
-
-def pack_kernel(c1, rate, flags, below, above, top, bottom):
-    planes = c1.shape[1]
-    last = c1.shape[2] - 1
-    for out, sign in ((top, 1), (bottom, -1)):
-        for slot, (q, depth) in enumerate(face_slots(1, sign)):
-            y = last - depth if sign > 0 else depth
-            row = slice(y, y + 1)
-            out[slot, 0:1] = below[OPPOSITE[q], row]
-            out[slot, 1:2] = below[q, row]
-            for x in range(planes):
-                out[slot, x + 2 : x + 3] = c1[q, x, row]
-            out[slot, planes + 2 : planes + 3] = above[q, row]
-            out[slot, planes + 3 : planes + 4] = above[OPPOSITE[q], row]
-        y = last if sign > 0 else 0
-        row = slice(y, y + 1)
-        for slot in (FLAG_SLOT, RATE_SLOT):
-            out[slot, 0:1] = below[slot, row]
-            out[slot, 1:2] = below[slot, row]
-            for x in range(planes):
-                if slot == FLAG_SLOT:
-                    out[slot, x + 2 : x + 3] = flags[x, row].astype(F32)
-                else:
-                    out[slot, x + 2 : x + 3] = rate[x, row]
-            out[slot, planes + 2 : planes + 3] = above[slot, row]
-            out[slot, planes + 3 : planes + 4] = above[slot, row]
+
+    def pack(out, sign, outside):
+        def line(x, carry):
+            for slot, (q, depth) in enumerate(face_slots(1, sign)):
+                y = rows - 1 - depth if sign > 0 else depth
+                out[slot, pl.ds(x, 1)] = c1[q, x, y : y + 1]
+            y = rows - 1 if sign > 0 else 0
+            for k, slot in enumerate((FLAG_SLOT, RATE_SLOT)):
+                out[slot, pl.ds(x, 1)] = fixed[k, x, y : y + 1]
+            return carry
+
+        lax.fori_loop(0, planes, line, 0)
+
+        @pl.when(outside)
+        def _():
+            out[...] = jnp.zeros(out.shape, F32)
+
+    first_row, last_row = inner == 0, inner == lax.axis_size("inner") - 1
+
+    @pl.when(even)
+    def _():
+        pack(near, 1, last_row)
+        pack(far, -1, first_row)
+
+    @pl.when(jnp.logical_not(even))
+    def _():
+        pack(near, -1, first_row)
+        pack(far, 1, last_row)
+
+
+def gather_both(near, far, both, axis):
+    odd = lax.rem(lax.axis_index(axis), 2)
+    for slot in range(both.shape[1]):
+        both[1 - odd, slot] = near[slot]
+        both[odd, slot] = far[slot]
+
+
+def pack_kernel(c1, fixed, near, far, other, up_or_down, down_or_up, both):
+    planes, rows = c1.shape[1], c1.shape[2]
+    gather_both(near, far, both, "inner")
+    slab = lax.axis_index("slab")
+    even = lax.rem(slab, 2) == 0
+
+    def pack(out, sign, outside):
+        for slot, (q, depth) in enumerate(face_slots(0, sign)):
+            out[slot] = c1[q, planes - 1 - depth if sign > 0 else depth]
+        end = planes - 1 if sign > 0 else 0
+        out[FLAG_SLOT] = fixed[0, end]
+        out[RATE_SLOT] = fixed[1, end]
+        for side, sign_y in enumerate((1, -1)):
+            picks = corner_rows(sign, sign_y) + [(FLAG_SLOT, 0), (RATE_SLOT, 0)]
+            for row, (slot, depth) in enumerate(picks):
+                x = planes - 1 - depth if sign > 0 else depth
+                at = SLOTS + 3 * side + row // 8
+                out[at, row % 8 : row % 8 + 1] = both[side, slot, x : x + 1]
+        for part in range(3):
+            out[FORCE_SLOT + part] = other[part]
+
+        @pl.when(outside)
+        def _():
+            out[...] = jnp.zeros(out.shape, F32)
+
+    first_plane, last_plane = slab == 0, slab == lax.axis_size("slab") - 1
+
+    @pl.when(even)
+    def _():
+        pack(up_or_down, 1, last_plane)
+        pack(down_or_up, -1, first_plane)
+
+    @pl.when(jnp.logical_not(even))
+    def _():
+        pack(up_or_down, -1, first_plane)
+        pack(down_or_up, 1, last_plane)
 
 
 def second_kernel(
@@ -171,73 +244,98 @@
     block_node,
     block_count,
     c1,
-    rate,
-    flags,
-    below,
-    above,
-    top,
-    bottom,
-    behind,
-    ahead,
+    fixed,
+    near_y,
+    far_y,
+    near_x,
+    far_x,
     internal_own,
-    internal_other,
     out,
     message,
+    both_y,
+    both_x,
     extended,
-    kinds,
-    rates,
+    walls,
+    crossing,
     second,
-    edge_low,
-    edge_high,
+    edges,
     loads,
 ):
     planes, rows, length = c1.shape[1:]
     half = length // BLK
     slots = block_source.shape[2]
+    wide = planes + 4
     slab = lax.axis_index("slab")
     inner = lax.axis_index("inner")
     slab_end = lax.axis_size("slab") - 1
     inner_end = lax.axis_size("inner") - 1
+    gather_both(near_y, far_y, both_y, "inner")
+    gather_both(near_x, far_x, both_x, "slab")
 
     for q in range(Q):
         for x in range(planes):
             extended[q, x + 2] = c1[q, x]
-        extended[q, 1] = below[q]
-        extended[q, planes + 2] = above[q]
+        extended[q, 1] = both_x[0, q]
+        extended[q, planes + 2] = both_x[1, q]
         if VELOCITIES[q][0] > 0:
-            extended[q, 0] = below[OPPOSITE[q]]
+            extended[q, 0] = both_x[0, OPPOSITE[q]]
         if VELOCITIES[q][0] < 0:
-            extended[q, planes + 3] = above[OPPOSITE[q]]
-    kinds[0] = below[FLAG_SLOT]
-    rates[0] = below[RATE_SLOT]
-    kinds[planes + 1] = above[FLAG_SLOT]
-    rates[planes + 1] = above[RATE_SLOT]
-    for x in range(planes):
-        kinds[x + 1] = flags[x].astype(F32)
-        rates[x + 1] = rate[x]
+            extended[q, planes + 3] = both_x[1, OPPOSITE[q]]
+
+    for side, sign in enumerate((1, -1)):
+        y = 0 if sign > 0 else rows - 1
+        own_row = slice(y, y + 1)
+        place = 0
+        for slot in range(SLOTS):
+            walls[side, slot, 2 : planes + 2] = both_y[side, slot]
+        for end, sign_x in enumerate((1, -1)):
+            for row, (slot, depth) in enumerate(corner_rows(sign_x, sign)):
+                at = (1 - depth) if sign_x > 0 else planes + 2 + depth
+                source = SLOTS + 3 * side + row // 8
+                walls[side, slot, at : at + 1] = both_x[end, source, row % 8 : row % 8 + 1]
+            at = 1 if sign_x > 0 else planes + 2
+            for row in (FLAG_SLOT, RATE_SLOT):
+                source = SLOTS + 3 * side + row // 8
+                walls[side, row, at : at + 1] = both_x[end, source, row % 8 : row % 8 + 1]
+        for q in range(Q):
+            if VELOCITIES[q][1] != -sign:
+                continue
+            for x in range(wide):
+                crossing[side, place, x : x + 1] = extended[q, x, own_row]
+            place += 1
 
     sub = lax.broadcasted_iota(jnp.int32, (rows, length), 0)
     is_first = sub == 0
     is_last = sub == rows - 1
 
-    def plane_one(at, carry):
+    def with_edge(block, step_y, edge):
+        if step_y > 0:
+            return jnp.where(is_first, edge, roll_by(block, 1, 0))
+        return jnp.where(is_last, edge, roll_by(block, -1, 0))
+
+    def store_plane(at, rate, kind):
         values = []
         for q in range(Q):
             step_x, step_y, _ = VELOCITIES[q]
             block = extended[q, at + 1 - step_x]
-            if step_y > 0:
-                edge = behind[q, pl.ds(at + 1 - step_x, 1)]
-                block = jnp.where(is_first, edge, roll_by(block, 1, 0))
-            if step_y < 0:
-                edge = ahead[q, pl.ds(at + 1 - step_x, 1)]
-                block = jnp.where(is_last, edge, roll_by(block, -1, 0))
+            if step_y != 0:
+                edge = walls[0 if step_y > 0 else 1, q, pl.ds(at + 1 - step_x, 1)]
+                block = with_edge(block, step_y, edge)
             values.append(block)
-        result = collide(values, rates[at], kinds[at])
+        result = collide(values, rate, kind)
         for q in range(Q):
             second[q, at] = roll_by(result[q], VELOCITIES[q][2], 1)
+
+    def inside_plane(x, carry):
+        store_plane(x + 1, fixed[1, x], fixed[0, x])
         return carry
 
-    lax.fori_loop(0, planes + 2, plane_one, 0)
+    def outside_plane(end, carry):
+        store_plane(end * (planes + 1), both_x[end, RATE_SLOT], both_x[end, FLAG_SLOT])
+        return carry
+
+    lax.fori_loop(0, planes, inside_plane, 0)
+    lax.fori_loop(0, 2, outside_plane, 0)
 
     @pl.when(slab == 0)
     def _():
@@ -251,28 +349,27 @@
             if VELOCITIES[q][0] < 0:
                 second[q, planes + 1] = jnp.zeros((rows, length), F32)
 
-    across = lax.broadcasted_iota(jnp.int32, (planes + 4, length), 0)
+    across = lax.broadcasted_iota(jnp.int32, (wide, length), 0)
     hidden = ((across <= 1) & (slab == 0)) | ((across >= planes + 2) & (slab == slab_end))
-    for sign, received, sent, edge, outside in (
-        (1, behind, bottom, edge_low, inner == 0),
-        (-1, ahead, top, edge_high, inner == inner_end),
-    ):
+    for side, sign, outside in ((0, 1, inner == 0), (1, -1, inner == inner_end)):
         values = []
+        place = 0
         for q in range(Q):
             step_x, step_y, _ = VELOCITIES[q]
             if step_y == 0:
-                block = received[q]
+                block = walls[side, q]
             elif step_y == sign:
-                block = received[OPPOSITE[q]]
+                block = walls[side, OPPOSITE[q]]
             else:
-                block = sent[q]
+                block = crossing[side, place]
+                place += 1
             values.append(roll_by(block, step_x, 0))
-        result = collide(values, received[RATE_SLOT], received[FLAG_SLOT])
+        result = collide(values, walls[side, RATE_SLOT], walls[side, FLAG_SLOT])
         place = 0
         for q in range(Q):
             if VELOCITIES[q][1] == sign:
                 kept = jnp.where(hidden | outside, 0.0, result[q])
-                edge[place] = roll_by(kept, VELOCITIES[q][2], 1)
+                edges[side, place] = roll_by(kept, VELOCITIES[q][2], 1)
                 place += 1
 
     def plane_two(x, carry):
@@ -281,14 +378,10 @@
         for q in range(Q):
             step_x, step_y, _ = VELOCITIES[q]
             block = second[q, x + 1 - step_x]
-            if step_y > 0:
-                edge = edge_low[places[1], pl.ds(x + 2 - step_x, 1)]
-                places[1] += 1
-                block = jnp.where(is_first, edge, roll_by(block, 1, 0))
-            if step_y < 0:
-                edge = edge_high[places[-1], pl.ds(x + 2 - step_x, 1)]
-                places[-1] += 1
-                block = jnp.where(is_last, edge, roll_by(block, -1, 0))
+            if step_y != 0:
+                edge = edges[0 if step_y > 0 else 1, places[step_y], pl.ds(x + 2 - step_x, 1)]
+                places[step_y] += 1
+                block = with_edge(block, step_y, edge)
             values.append(block)
             out[q, x] = block
         density, flow_x, flow_y, flow_z = moments(values)
@@ -318,20 +411,16 @@
         message[4 * k + 3 : 4 * k + 4] = jnp.broadcast_to(key, (1, BLK)).astype(F32)
     for part in range(3):
         start = 4 * slots + part * node_blocks
-        message[start : start + node_blocks] = internal_own[part] + internal_other[part]
-
-
-def shell_kernel(
-    elements,
-    displacement,
-    next_nodes,
-    shape_inverse,
-    stiffness,
-    own,
-    other,
-    ids,
-    shapes,
-    forces,
+        for piece in range(half):
+            at = piece * rows
+            message[start + at : start + at + rows] = (
+                internal_own[part, at : at + rows]
+                + both_x[0, FORCE_SLOT + part, :, piece * BLK : (piece + 1) * BLK]
+            )
+
+
+def element_kernel(
+    elements, displacement, next_nodes, shape_inverse, stiffness, low_ids, high_ids, forces, shapes
 ):
     node_dev = displacement.shape[1]
     node_blocks = node_dev // BLK
@@ -340,13 +429,15 @@
     for j in range(runs):
         lanes = slice(j * BLK, (j + 1) * BLK)
         for row in range(3):
-            ids[row, j : j + 1] = elements[row : row + 1, lanes]
+            number = elements[row : row + 1, lanes]
+            low_ids[row, j : j + 1] = number & (BLK - 1)
+            high_ids[row, j : j + 1] = number >> 7
             shapes[row, j : j + 1] = shape_inverse[row : row + 1, lanes]
 
     def compute(group, carry):
         rows = pl.ds(pl.multiple_of(group * 8, 8), 8)
-        low = [ids[corner, rows] & (BLK - 1) for corner in range(3)]
-        high = [ids[corner, rows] >> 7 for corner in range(3)]
+        low = [low_ids[corner, rows] for corner in range(3)]
+        high = [high_ids[corner, rows] for corner in range(3)]
         nodes = [[jnp.zeros((8, BLK), F32)] * 3 for _ in range(3)]
         for block in range(2 * node_blocks):
             source = displacement if block < node_blocks else next_nodes
@@ -390,7 +481,7 @@
             force_two = diag_c * stress_two
             for corner, force in enumerate((-(force_one + force_two), force_one, force_two)):
                 rest = force
-                for part in range(3):
+                for part in range(PIECES):
                     piece = rest.astype(jnp.bfloat16).astype(F32)
                     rest = rest - piece
                     forces[part * 3 + p, corner, rows] = piece
@@ -398,6 +489,10 @@
 
     lax.fori_loop(0, groups, compute, 0)
 
+
+def spread_kernel(low_ids, high_ids, forces, own, other):
+    node_blocks = own.shape[1]
+    groups = low_ids.shape[1] // 8
     slots = 2 * node_blocks
     slot_ids = lax.broadcasted_iota(jnp.int32, (slots, BLK), 0)
     lane_ids = lax.broadcasted_iota(jnp.int32, (BLK, BLK), 0)
@@ -405,14 +500,13 @@
     def spread(group, total):
         corner = group // groups
         base = (group - corner * groups) * 8
-        left = [[] for _ in range(9)]
+        left = [[] for _ in range(3 * PIECES)]
         right = []
         for j in range(8):
             row = pl.ds(base + j, 1)
-            numbers = ids[corner, row]
-            here = slot_ids == (numbers >> 7)
-            right.append(jnp.where(lane_ids == (numbers & (BLK - 1)), 1.0, 0.0).astype(jnp.bfloat16))
-            for part in range(9):
+            here = slot_ids == high_ids[corner, row]
+            right.append(jnp.where(lane_ids == low_ids[corner, row], 1.0, 0.0).astype(jnp.bfloat16))
+            for part in range(3 * PIECES):
                 left[part].append(
                     jnp.where(here, forces[part, corner, row], 0.0).astype(jnp.bfloat16)
                 )
@@ -422,23 +516,27 @@
             tall, wide, (((1,), (1,)), ((), ())), preferred_element_type=F32
         )
 
-    total = lax.fori_loop(0, 3 * groups, spread, jnp.zeros((9 * slots, BLK), F32))
+    total = lax.fori_loop(0, 3 * groups, spread, jnp.zeros((3 * PIECES * slots, BLK), F32))
+    half = other.shape[2] // BLK
+    rows = other.shape[1]
     for p in range(3):
-        summed = (
-            total[p * slots : (p + 1) * slots]
-            + total[(3 + p) * slots : (4 + p) * slots]
-            + total[(6 + p) * slots : (7 + p) * slots]
-        )
+        summed = total[p * slots : (p + 1) * slots]
+        for part in range(1, PIECES):
+            start = (3 * part + p) * slots
+            summed = summed + total[start : start + slots]
         own[p] = summed[:node_blocks]
-        other[p] = summed[node_blocks:]
-
-
-def final_kernel(*refs):
-    messages = refs[:-3]
-    residual, motion, keys = refs[-3:]
+        for piece in range(half):
+            at = node_blocks + piece * rows
+            other[p, :, piece * BLK : (piece + 1) * BLK] = summed[at : at + rows]
+
+
+def final_kernel(count, *refs):
+    messages = refs[:count]
+    values, out_hbm, residual, motion, keys, sem = refs[count:]
+    store = pltpu.make_async_copy(values, out_hbm, sem)
+    store.start()
     slots = keys.shape[0]
     node_blocks = residual.shape[1] // BLK
-    count = len(messages)
     inner = lax.axis_index("inner")
     mine = messages[0]
     for k in range(slots):
@@ -471,21 +569,24 @@
         left = external[part] - mine[start : start + node_blocks]
         for b in range(node_blocks):
             residual[part : part + 1, b * BLK : (b + 1) * BLK] = left[b : b + 1]
-        shown = jnp.where(live, COMPLIANCE * moved[part], 0.0)
-        for k in range(slots):
-            motion[0, 0, k, part : part + 1] = shown[k : k + 1]
-
-
-def call(kernel, outs, scratch=(), scalars=0, inputs=0):
+        motion[part] = jnp.where(live, COMPLIANCE * moved[part], 0.0)
+    store.wait()
+
+
+def call(kernel, outs, operands, spaces, scratch=(), out_spaces=None, micros=1.0):
+    spec = lambda space: pl.BlockSpec(memory_space=space)
+    out_spaces = out_spaces or (pltpu.VMEM,) * len(outs)
     return pl.pallas_call(
         kernel,
         out_shape=outs,
-        in_specs=[pl.BlockSpec(memory_space=pltpu.SMEM)] * scalars
-        + [pl.BlockSpec(memory_space=pltpu.VMEM)] * inputs,
-        out_specs=jax.tree.map(lambda _: pl.BlockSpec(memory_space=pltpu.VMEM), outs),
+        in_specs=[spec(space) for space in spaces],
+        out_specs=tuple(spec(space) for space in out_spaces),
         scratch_shapes=list(scratch),
         compiler_params=pltpu.CompilerParams(vmem_limit_bytes=VMEM_BYTES),
-    )
+        cost_estimate=pl.CostEstimate(
+            flops=0, bytes_accessed=int(micros * 3.6e6), transcendentals=0
+        ),
+    )(*operands)
 
 
 def shift(block, axis, step):
@@ -497,6 +598,17 @@
 def around(block, axis, step):
     count = lax.axis_size(axis)
     return lax.ppermute(block, axis, [(i, (i + step) % count) for i in range(count)])
+
+
+def swap(near, far, axis):
+    count = lax.axis_size(axis)
+    outcome = []
+    for block, start in ((near, 0), (far, 1)):
+        partner = list(range(count))
+        for i in range(start, count - 1, 2):
+            partner[i], partner[i + 1] = i + 1, i
+        outcome.append(lax.ppermute(block, axis, list(enumerate(partner))))
+    return outcome
 
 
 def shards(
@@ -520,71 +632,92 @@
     slots = block_source.shape[2]
     count = lax.axis_size("inner")
     shape = lambda *dims: jax.ShapeDtypeStruct(dims, F32)
+    whole = shape(*populations.shape)
+    vmem, hbm, smem = pltpu.VMEM, pltpu.HBM, pltpu.SMEM
 
     next_nodes = shift(displacement, "slab", -1)
-    face = shape(SLOTS, rows, length)
-    c1, up, down = call(first_kernel, (shape(*populations.shape), face, face), inputs=3)(
-        populations, relaxation, node_flags
+    face_y = shape(SLOTS, planes, length)
+    c1, fixed, near, far = call(
+        first_kernel,
+        (whole, shape(2, planes, rows, length), face_y, face_y),
+        (populations, relaxation, node_flags),
+        (hbm,) * 3,
+        scratch=(
+            pltpu.VMEM((planes, Q, rows, length), F32),
+            pltpu.VMEM((planes, rows, length), F32),
+            pltpu.VMEM((planes, rows, length), jnp.int32),
+            pltpu.SemaphoreType.DMA((planes + 2,)),
+        ),
+        micros=1.5,
     )
-    below = shift(up, "slab", 1)
-    above = shift(down, "slab", -1)
+    near_y, far_y = swap(near, far, "inner")
+    numbers = jax.ShapeDtypeStruct((3, runs, BLK), jnp.int32)
+    low_ids, high_ids, forces = call(
+        element_kernel,
+        (numbers, numbers, shape(3 * PIECES, 3, runs, BLK)),
+        (elements, displacement, next_nodes, shape_inverse, stiffness.reshape(runs, BLK)),
+        (vmem,) * 5,
+        scratch=(pltpu.VMEM((3, runs, BLK), F32),),
+        micros=3.0,
+    )
     own, other = call(
-        shell_kernel,
-        (shape(3, node_blocks, BLK), shape(3, node_blocks, BLK)),
-        scratch=(
-            pltpu.VMEM((3, runs, BLK), jnp.int32),
-            pltpu.VMEM((3, runs, BLK), F32),
-            pltpu.VMEM((9, 3, runs, BLK), F32),
-        ),
-        inputs=5,
-    )(elements, displacement, next_nodes, shape_inverse, stiffness.reshape(runs, BLK))
-    arrived = shift(other, "slab", 1)
-    side = shape(SLOTS, planes + 4, length)
-    top, bottom = call(pack_kernel, (side, side), inputs=5)(
-        c1, relaxation, node_flags, below, above
+        spread_kernel,
+        (shape(3, node_blocks, BLK), shape(3, node_blocks // half, length)),
+        (low_ids, high_ids, forces),
+        (vmem,) * 3,
+        micros=3.0,
     )
-    behind = shift(top, "inner", 1)
-    ahead = shift(bottom, "inner", -1)
+    face_x = shape(MESSAGE_SLOTS, rows, length)
+    near, far = call(
+        pack_kernel,
+        (face_x, face_x),
+        (c1, fixed, near_y, far_y, other),
+        (vmem,) * 5,
+        scratch=(pltpu.VMEM((2, SLOTS, planes, length), F32),),
+        micros=0.3,
+    )
+    near_x, far_x = swap(near, far, "slab")
     lines = 4 * slots + 3 * node_blocks
     values, message = call(
         second_kernel,
-        (shape(*populations.shape), shape(lines, BLK)),
+        (whole, shape(lines, BLK)),
+        (
+            block_source,
+            block_target,
+            block_node,
+            block_count,
+            c1,
+            fixed,
+            near_y,
+            far_y,
+            near_x,
+            far_x,
+            own,
+        ),
+        (smem,) * 4 + (vmem,) * 7,
         scratch=(
+            pltpu.VMEM((2, SLOTS, planes, length), F32),
+            pltpu.VMEM((2, MESSAGE_SLOTS, rows, length), F32),
             pltpu.VMEM((Q, planes + 4, rows, length), F32),
-            pltpu.VMEM((planes + 2, rows, length), F32),
-            pltpu.VMEM((planes + 2, rows, length), F32),
+            pltpu.VMEM((2, SLOTS, planes + 4, length), F32),
+            pltpu.VMEM((2, 5, planes + 4, length), F32),
             pltpu.VMEM((Q, planes + 2, rows, length), F32),
-            pltpu.VMEM((5, planes + 4, length), F32),
-            pltpu.VMEM((5, planes + 4, length), F32),
+            pltpu.VMEM((2, 5, planes + 4, length), F32),
             pltpu.VMEM((planes * half, 3, rows, BLK), F32),
         ),
-        scalars=4,
-        inputs=11,
-    )(
-        block_source,
-        block_target,
-        block_node,
-        block_count,
-        c1,
-        relaxation,
-        node_flags,
-        below,
-        above,
-        top,
-        bottom,
-        behind,
-        ahead,
-        own,
-        arrived,
+        micros=2.5,
     )
     messages = [message] + [around(message, "inner", step) for step in range(1, count)]
-    residual, motion = call(
-        final_kernel,
-        (shape(3, node_dev), shape(1, 1, slots, 3, BLK)),
-        scratch=(pltpu.VMEM((slots, BLK), F32),),
-        inputs=count,
-    )(*messages)
-    return values, residual, motion
+    populations_out, residual, motion = call(
+        functools.partial(final_kernel, count),
+        (whole, shape(3, node_dev), shape(3, slots, BLK)),
+        (*messages, values),
+        (vmem,) * (count + 1),
+        out_spaces=(hbm, vmem, vmem),
+        scratch=(pltpu.VMEM((slots, BLK), F32), pltpu.SemaphoreType.DMA(())),
+        micros=0.8,
+    )
+    return populations_out, residual, motion.transpose(1, 0, 2)[None, None]
 
 
 def solution(mesh):

time: 50.5 us -> 40.9 us (0.81)
  the two profiles are of different devices: /device:TPU:0 before, /device:TPU:1 now
where the time goes in v2:
time: 40.9 us; the launch traced here: 40.5 us
  starting transfers between devices  13.3 us (33%)
  waiting for transfers between devices  12.3 us (30%)
  Pallas kernels  10.8 us (26%)
  local copies, waits for them, and re-layouts  2.62 us (6%)
  between operations  1.43 us (3%)
    pallas_call x6, Pallas kernels, call(): pl.pallas_call(kernel, out_shape=outs, in_specs=[spec(space) for space in...  10.8 us
    ppermute x3, starting transfers between devices, around(): lax.ppermute(block, axis, [(i, (i + step) % count) for i in range(count)])  5.65 us
    ppermute x4, waiting for transfers between devices, swap(): outcome.append(lax.ppermute(block, axis, list(enumerate(partner))))  4.9 us
    ppermute x4, starting transfers between devices, swap(): outcome.append(lax.ppermute(block, axis, list(enumerate(partner))))  4.83 us
    ppermute x3, waiting for transfers between devices, around(): lax.ppermute(block, axis, [(i, (i + step) % count) for i in range(count)])  4.65 us
    ppermute x1, starting transfers between devices, shift(): return lax.ppermute(block, axis, route)  2.86 us
    ppermute x1, waiting for transfers between devices, shift(): return lax.ppermute(block, axis, route)  2.71 us
    unnamed x20, local copies, waits for them, and re-layouts  2.62 us
  transfers between devices with their start and end apart: 8, of which 5 were waited for; matrix products, arithmetic and copies ran while one was open for 0% of the time, Pallas kernels for 16%

profile of v2, /device:TPU:1, one launch (start us, length us, event | category | flops | bytes accessed | tf_op | source)
XLA Modules:
  0.0 40.5 jit_solution(7045247643127743713)
XLA Ops:
  0.6 0.0 copy-start
  0.6 1.1 %copy-done = f32[19,4,8,256]{3,2,1,0:T(8,128)S(1)} copy-done((f32[19,4,8,256]{3,2,1,0:T(8,128)S(1)}, f32[19,4,8,256]{3,2,1,0:T(8,128)}, u32[]{:S(2)}) %copy-start) | copy-done | bytes 622616
  1.7 0.0 copy-start.4
  1.7 0.8 %copy-done.4 = f32[4,8,256]{2,1,0:T(8,128)S(1)} copy-done((f32[4,8,256]{2,1,0:T(8,128)S(1)}, f32[4,8,256]{2,1,0:T(8,128)}, u32[]{:S(2)}) %copy-start.4) | copy-done | bytes 32792
  2.5 0.0 copy-start.5
  2.5 0.8 %copy-done.5 = s32[4,8,256]{2,1,0:T(8,128)S(1)} copy-done((s32[4,8,256]{2,1,0:T(8,128)S(1)}, s32[4,8,256]{2,1,0:T(8,128)}, u32[]{:S(2)}) %copy-start.5) | copy-done | bytes 32792
  3.2 0.0 copy-start.3
  3.2 0.0 copy-start.1
  3.2 0.0 copy-start.2
  3.2 0.0 copy-start.6
  3.2 1.0 %shard_map.130 = (f32[19,4,8,256]{3,2,1,0:T(8,128)S(1)}, f32[2,4,8,256]{3,2,1,0:T(8,128)S(1)}, f32[21,4,256]{2,1,0:T(4,128)S(1)}, f32[21,4,256]{2,1,0:T(4,128)S(1)}) custom-call(f32[19,4,8,256]{3,2,1,0:T(8,128)S(1)} %copy-done, f32[4,8,256]{2,1,0:T(8,128)S(1)} %copy-done.4, s32[4,8,256]{2,1,0:T(8,128)S(1)} %copy-done.5), custom_call_target="tpu_custom_call" | custom-call | bytes 5400000 | tf_op jit(solution)/shard_map/pallas_call | solution.py:579
  4.2 2.2 %collective-permute-start = (f32[21,4,256]{2,1,0:T(4,128)S(1)}, f32[21,4,256]{2,1,0:T(4,128)S(1)}, u32[]{:S(2)}, u32[]{:S(2)}) collective-permute-start(f32[21,4,256]{2,1,0:T(4,128)S(1)} %get-tuple-element.21), channel_id=1, source_target_pairs={{0,1},{1,0},{2,3},{3,2},{4,5},{5,4},{6,7},{7,6},{8,9},{9,8},{10,11... | collective-permute-start | bytes 258056 | tf_op jit(solution)/shard_map/ppermute | solution.py:610
  6.4 0.7 %collective-permute-start.1 = (f32[21,4,256]{2,1,0:T(4,128)S(1)}, f32[21,4,256]{2,1,0:T(4,128)S(1)}, u32[]{:S(2)}, u32[]{:S(2)}) collective-permute-start(f32[21,4,256]{2,1,0:T(4,128)S(1)} %get-tuple-element.22), channel_id=1, source_target_pairs={{0,0},{1,2},{2,1},{3,3},{4,4},{5,6},{6,5},{7,7},{8,8},{9,10},{10,9... | collective-permute-start | bytes 258056 | tf_op jit(solution)/shard_map/ppermute | solution.py:610
  7.1 0.0 copy-done.3
  7.1 2.9 %collective-permute-start.2 = (f32[3,2048]{1,0:T(4,128)S(1)}, f32[3,2048]{1,0:T(4,128)S(1)}, u32[]{:S(2)}, u32[]{:S(2)}) collective-permute-start(f32[3,2048]{1,0:T(4,128)S(1)} %copy-done.3), channel_id=1, source_target_pairs={{4,0},{8,4},{12,8},{5,1},{9,5},{13,9},{6,2},{10,6},{14,10},{7,3},{... | collective-permute-start | bytes 73736 | tf_op jit(solution)/shard_map/ppermute | solution.py:595
  9.9 2.7 %collective-permute-done.2.next_nodes = f32[3,2048]{1,0:T(4,128)S(1)} collective-permute-done((f32[3,2048]{1,0:T(4,128)S(1)}, f32[3,2048]{1,0:T(4,128)S(1)}, u32[]{:S(2)}, u32[]{:S(2)}) %collective-permute-start.2) | collective-permute-done | bytes 24608 | tf_op jit(solution)/shard_map/ppermute | solution.py:595
  12.6 0.0 copy-done.1
  12.7 0.0 copy-done.2
  12.7 0.0 copy-done.6
  12.7 3.0 %shard_map.131 = (s32[3,32,128]{2,1,0:T(8,128)S(1)}, s32[3,32,128]{2,1,0:T(8,128)S(1)}, f32[6,3,32,128]{3,2,1,0:T(8,128)S(1)}) custom-call(s32[3,4096]{1,0:T(4,128)S(1)} %copy-done.1, f32[3,2048]{1,0:T(4,128)S(1)} %copy-done.3, f32[3,2048]{1,0:T(4,128)S(1)} %collective-permute-done.2.next_nodes, f32[3,4096]{1,0:T(4,128)S(1)} %copy-done.2, f32[32,128]{1,0:T(8,128)S(1)} %bitcast.4), custom_call_target="tpu_custom_call" | custom-call | bytes 10800000 | tf_op jit(solution)/shard_map/pallas_call | solution.py:579
  15.7 3.3 %shard_map.132 = (f32[3,16,128]{2,1,0:T(8,128)S(1)}, f32[3,8,256]{2,1,0:T(8,128)S(1)}) custom-call(s32[3,32,128]{2,1,0:T(8,128)S(1)} %get-tuple-element.23.low_ids, s32[3,32,128]{2,1,0:T(8,128)S(1)} %get-tuple-element.24.high_ids, f32[6,3,32,128]{3,2,1,0:T(8,128)S(1)} %get-tuple-element.25.forces), custom_call_target="tpu_custom_call" | custom-call | bytes 10800000 | tf_op jit(solution)/shard_map/pallas_call | solution.py:579
  19.0 0.0 collective-permute-done.near.near_y
  19.0 0.0 collective-permute-done.1.far.far_y
  19.0 0.1 shard_map.133
  19.1 0.1 collective-permute-start.3
  19.2 1.9 %collective-permute-start.4 = (f32[30,8,256]{2,1,0:T(8,128)S(1)}, f32[30,8,256]{2,1,0:T(8,128)S(1)}, u32[]{:S(2)}, u32[]{:S(2)}) collective-permute-start(f32[30,8,256]{2,1,0:T(8,128)S(1)} %get-tuple-element.28), channel_id=1, source_target_pairs={{0,0},{4,8},{8,4},{12,12},{1,1},{5,9},{9,5},{13,13},{2,2},{6,10},{... | collective-permute-start | bytes 737288 | tf_op jit(solution)/shard_map/ppermute | solution.py:610
  21.7 0.0 copy-start.7
  21.8 0.0 copy-start.8
  21.8 0.0 copy-start.9
  21.8 0.0 collective-permute-done.3.near_x
  21.8 4.9 %collective-permute-done.4.far_x = f32[30,8,256]{2,1,0:T(8,128)S(1)} collective-permute-done((f32[30,8,256]{2,1,0:T(8,128)S(1)}, f32[30,8,256]{2,1,0:T(8,128)S(1)}, u32[]{:S(2)}, u32[]{:S(2)}) %collective-permute-start.4) | collective-permute-done | bytes 245792 | tf_op jit(solution)/shard_map/ppermute | solution.py:610
  26.7 0.0 copy-done.7
  26.7 0.0 copy-done.8
  26.7 0.0 copy-done.9
  26.7 2.0 %shard_map.134 = (f32[19,4,8,256]{3,2,1,0:T(8,128)S(1)}, f32[80,128]{1,0:T(8,128)S(1)}) custom-call(s32[1,1,8]{2,1,0:T(1,128)S(1)} %copy-done.7, s32[1,1,8]{2,1,0:T(1,128)S(1)} %copy-done.8, s32[1,1,8]{2,1,0:T(1,128)S(1)} %copy-done.9, s32[1,1]{1,0:T(1,128)S(6)} %copy.14.block_count, f32[19,4,8,256]{3,2,1,0:T(8,128)S(1)} %get-tuple-element.19.c1, ...), custom_call_target="tpu_custom_call" | custom-call | bytes 9000000 | tf_op jit(solution)/shard_map/pallas_call | solution.py:579
  28.7 2.2 %collective-permute-start.7 = (f32[80,128]{1,0:T(8,128)S(1)}, f32[80,128]{1,0:T(8,128)S(1)}, u32[]{:S(2)}, u32[]{:S(2)}) collective-permute-start(f32[80,128]{1,0:T(8,128)S(1)} %get-tuple-element.30.refs_0_), channel_id=1, source_target_pairs={{0,3},{1,0},{2,1},{3,2},{4,7},{5,4},{6,5},{7,6},{8,11},{9,8},{10,9... | collective-permute-start | bytes 122888 | tf_op jit(solution)/shard_map/ppermute | solution.py:600
  31.0 3.4 %collective-permute-start.6 = (f32[80,128]{1,0:T(8,128)S(1)}, f32[80,128]{1,0:T(8,128)S(1)}, u32[]{:S(2)}, u32[]{:S(2)}) collective-permute-start(f32[80,128]{1,0:T(8,128)S(1)} %get-tuple-element.30.refs_0_), channel_id=1, source_target_pairs={{0,2},{1,3},{2,0},{3,1},{4,6},{5,7},{6,4},{7,5},{8,10},{9,11},{10,... | collective-permute-start | bytes 122888 | tf_op jit(solution)/shard_map/ppermute | solution.py:600
  34.4 0.0 collective-permute-start.5
  34.4 0.6 %collective-permute-done.7.refs_3_ = f32[80,128]{1,0:T(8,128)S(1)} collective-permute-done((f32[80,128]{1,0:T(8,128)S(1)}, f32[80,128]{1,0:T(8,128)S(1)}, u32[]{:S(2)}, u32[]{:S(2)}) %collective-permute-start.7) | collective-permute-done | bytes 40992 | tf_op jit(solution)/shard_map/ppermute | solution.py:600
  35.0 1.2 %collective-permute-done.6.refs_2_ = f32[80,128]{1,0:T(8,128)S(1)} collective-permute-done((f32[80,128]{1,0:T(8,128)S(1)}, f32[80,128]{1,0:T(8,128)S(1)}, u32[]{:S(2)}, u32[]{:S(2)}) %collective-permute-start.6) | collective-permute-done | bytes 40992 | tf_op jit(solution)/shard_map/ppermute | solution.py:600
  36.2 2.8 %collective-permute-done.5.refs_1_ = f32[80,128]{1,0:T(8,128)S(1)} collective-permute-done((f32[80,128]{1,0:T(8,128)S(1)}, f32[80,128]{1,0:T(8,128)S(1)}, u32[]{:S(2)}, u32[]{:S(2)}) %collective-permute-start.5) | collective-permute-done | bytes 40992 | tf_op jit(solution)/shard_map/ppermute | solution.py:600
  39.0 1.4 %shard_map.135 = (f32[19,4,8,256]{3,2,1,0:T(8,128)}, f32[3,2048]{1,0:T(4,128)}, f32[3,8,128]{2,1,0:T(8,128)}) custom-call(f32[80,128]{1,0:T(8,128)S(1)} %get-tuple-element.30.refs_0_, f32[80,128]{1,0:T(8,128)S(1)} %collective-permute-done.5.refs_1_, f32[80,128]{1,0:T(8,128)S(1)} %collective-permute-done.6.refs_2_, ...), custom_call_target="tpu_custom_call" | custom-call | bytes 2880000 | tf_op jit(solution)/shard_map/pallas_call | solution.py:579
Async XLA Ops:
  0.6 1.1 %copy-start = (f32[19,4,8,256]{3,2,1,0:T(8,128)S(1)}, f32[19,4,8,256]{3,2,1,0:T(8,128)}, u32[]{:S(2)}) copy-start(f32[19,4,8,256]{3,2,1,0:T(8,128)} %pops_hbm.1) | copy-start | bytes 1867780
  1.7 0.8 %copy-start.4 = (f32[4,8,256]{2,1,0:T(8,128)S(1)}, f32[4,8,256]{2,1,0:T(8,128)}, u32[]{:S(2)}) copy-start(f32[4,8,256]{2,1,0:T(8,128)} %rate_hbm.1) | copy-start | bytes 98308
  2.5 0.8 %copy-start.5 = (s32[4,8,256]{2,1,0:T(8,128)S(1)}, s32[4,8,256]{2,1,0:T(8,128)}, u32[]{:S(2)}) copy-start(s32[4,8,256]{2,1,0:T(8,128)} %flags_hbm.1) | copy-start | bytes 98308
  3.2 3.8 %copy-start.3 = (f32[3,2048]{1,0:T(4,128)S(1)}, f32[3,2048]{1,0:T(4,128)}, u32[]{:S(2)}) copy-start(f32[3,2048]{1,0:T(4,128)} %displacement.1) | copy-start | bytes 73732
  3.2 9.4 %copy-start.1 = (s32[3,4096]{1,0:T(4,128)S(1)}, s32[3,4096]{1,0:T(4,128)}, u32[]{:S(2)}) copy-start(s32[3,4096]{1,0:T(4,128)} %elements.1) | copy-start | bytes 147460
  3.2 9.4 %copy-start.2 = (f32[3,4096]{1,0:T(4,128)S(1)}, f32[3,4096]{1,0:T(4,128)}, u32[]{:S(2)}) copy-start(f32[3,4096]{1,0:T(4,128)} %shape_inverse.1) | copy-start | bytes 147460
  3.2 9.4 %copy-start.6 = (f32[4096]{0:T(1024)S(1)}, f32[4096]{0:T(1024)}, u32[]{:S(2)}) copy-start(f32[4096]{0:T(1024)} %param.17) | copy-start | bytes 49156
  4.2 14.8 %collective-permute-start = (f32[21,4,256]{2,1,0:T(4,128)S(1)}, f32[21,4,256]{2,1,0:T(4,128)S(1)}, u32[]{:S(2)}, u32[]{:S(2)}) collective-permute-start(f32[21,4,256]{2,1,0:T(4,128)S(1)} %get-tuple-element.21), channel_id=1, source_target_pairs={{0,1},{1,0},{2,3},{3,2},{4,5},{5,4},{6,7},{7,6},{8,9},{9,8},{10,11... | collective-permute-start | bytes 258056 | tf_op jit(solution)/shard_map/ppermute | solution.py:610
  6.4 12.6 %collective-permute-start.1 = (f32[21,4,256]{2,1,0:T(4,128)S(1)}, f32[21,4,256]{2,1,0:T(4,128)S(1)}, u32[]{:S(2)}, u32[]{:S(2)}) collective-permute-start(f32[21,4,256]{2,1,0:T(4,128)S(1)} %get-tuple-element.22), channel_id=1, source_target_pairs={{0,0},{1,2},{2,1},{3,3},{4,4},{5,6},{6,5},{7,7},{8,8},{9,10},{10,9... | collective-permute-start | bytes 258056 | tf_op jit(solution)/shard_map/ppermute | solution.py:610
  7.1 5.6 %collective-permute-start.2 = (f32[3,2048]{1,0:T(4,128)S(1)}, f32[3,2048]{1,0:T(4,128)S(1)}, u32[]{:S(2)}, u32[]{:S(2)}) collective-permute-start(f32[3,2048]{1,0:T(4,128)S(1)} %copy-done.3), channel_id=1, source_target_pairs={{4,0},{8,4},{12,8},{5,1},{9,5},{13,9},{6,2},{10,6},{14,10},{7,3},{... | collective-permute-start | bytes 73736 | tf_op jit(solution)/shard_map/ppermute | solution.py:595
  19.1 2.7 %collective-permute-start.3 = (f32[30,8,256]{2,1,0:T(8,128)S(1)}, f32[30,8,256]{2,1,0:T(8,128)S(1)}, u32[]{:S(2)}, u32[]{:S(2)}) collective-permute-start(f32[30,8,256]{2,1,0:T(8,128)S(1)} %get-tuple-element.27), channel_id=1, source_target_pairs={{0,4},{4,0},{8,12},{12,8},{1,5},{5,1},{9,13},{13,9},{2,6},{6,2},{1... | collective-permute-start | bytes 737288 | tf_op jit(solution)/shard_map/ppermute | solution.py:610
  19.2 7.5 %collective-permute-start.4 = (f32[30,8,256]{2,1,0:T(8,128)S(1)}, f32[30,8,256]{2,1,0:T(8,128)S(1)}, u32[]{:S(2)}, u32[]{:S(2)}) collective-permute-start(f32[30,8,256]{2,1,0:T(8,128)S(1)} %get-tuple-element.28), channel_id=1, source_target_pairs={{0,0},{4,8},{8,4},{12,12},{1,1},{5,9},{9,5},{13,13},{2,2},{6,10},{... | collective-permute-start | bytes 737288 | tf_op jit(solution)/shard_map/ppermute | solution.py:610
  21.7 4.9 %copy-start.7 = (s32[1,1,8]{2,1,0:T(1,128)S(1)}, s32[1,1,8]{2,1,0:T(1,128)}, u32[]{:S(2)}) copy-start(s32[1,1,8]{2,1,0:T(1,128)} %block_source.1) | copy-start | bytes 100
  21.8 4.9 %copy-start.8 = (s32[1,1,8]{2,1,0:T(1,128)S(1)}, s32[1,1,8]{2,1,0:T(1,128)}, u32[]{:S(2)}) copy-start(s32[1,1,8]{2,1,0:T(1,128)} %block_target.1) | copy-start | bytes 100
  21.8 4.9 %copy-start.9 = (s32[1,1,8]{2,1,0:T(1,128)S(1)}, s32[1,1,8]{2,1,0:T(1,128)}, u32[]{:S(2)}) copy-start(s32[1,1,8]{2,1,0:T(1,128)} %block_node.1) | copy-start | bytes 100
  28.7 6.3 %collective-permute-start.7 = (f32[80,128]{1,0:T(8,128)S(1)}, f32[80,128]{1,0:T(8,128)S(1)}, u32[]{:S(2)}, u32[]{:S(2)}) collective-permute-start(f32[80,128]{1,0:T(8,128)S(1)} %get-tuple-element.30.refs_0_), channel_id=1, source_target_pairs={{0,3},{1,0},{2,1},{3,2},{4,7},{5,4},{6,5},{7,6},{8,11},{9,8},{10,9... | collective-permute-start | bytes 122888 | tf_op jit(solution)/shard_map/ppermute | solution.py:600
  31.0 5.2 %collective-permute-start.6 = (f32[80,128]{1,0:T(8,128)S(1)}, f32[80,128]{1,0:T(8,128)S(1)}, u32[]{:S(2)}, u32[]{:S(2)}) collective-permute-start(f32[80,128]{1,0:T(8,128)S(1)} %get-tuple-element.30.refs_0_), channel_id=1, source_target_pairs={{0,2},{1,3},{2,0},{3,1},{4,6},{5,7},{6,4},{7,5},{8,10},{9,11},{10,... | collective-permute-start | bytes 122888 | tf_op jit(solution)/shard_map/ppermute | solution.py:600
  34.4 4.7 %collective-permute-start.5 = (f32[80,128]{1,0:T(8,128)S(1)}, f32[80,128]{1,0:T(8,128)S(1)}, u32[]{:S(2)}, u32[]{:S(2)}) collective-permute-start(f32[80,128]{1,0:T(8,128)S(1)} %get-tuple-element.30.refs_0_), channel_id=1, source_target_pairs={{0,1},{1,2},{2,3},{3,0},{4,5},{5,6},{6,7},{7,4},{8,9},{9,10},{10,1... | collective-permute-start | bytes 122888 | tf_op jit(solution)/shard_map/ppermute | solution.py:600

commit v3 on v2

--- a/solution.py
+++ b/solution.py
@@ -135,10 +135,8 @@
     return rows
 
 
-def first_kernel(pops_hbm, rate_hbm, flags_hbm, c1, fixed, near, far, pops, rate, flags, sems):
-    planes, rows = c1.shape[1], c1.shape[2]
-    inner = lax.axis_index("inner")
-    even = lax.rem(inner, 2) == 0
+def first_kernel(pops_hbm, rate_hbm, flags_hbm, c1, fixed, pops, rate, flags, sems):
+    planes = c1.shape[1]
     copies = [
         pltpu.make_async_copy(rate_hbm, rate, sems.at[planes]),
         pltpu.make_async_copy(flags_hbm, flags, sems.at[planes + 1]),
@@ -163,6 +161,13 @@
         return carry
 
     lax.fori_loop(0, planes, plane, 0)
+
+
+def side_kernel(c1, fixed, next_nodes, near, far):
+    del next_nodes
+    planes, rows = c1.shape[1], c1.shape[2]
+    inner = lax.axis_index("inner")
+    even = lax.rem(inner, 2) == 0
 
     def pack(out, sign, outside):
         def line(x, carry):
@@ -420,24 +425,25 @@
 
 
 def element_kernel(
-    elements, displacement, next_nodes, shape_inverse, stiffness, low_ids, high_ids, forces, shapes
+    elements, displacement, next_nodes, shape_inverse, stiffness, low_ids, high_ids, forces, shapes,
+    numbers, corners,
 ):
     node_dev = displacement.shape[1]
     node_blocks = node_dev // BLK
     runs = elements.shape[1] // BLK
-    groups = runs // 8
     for j in range(runs):
         lanes = slice(j * BLK, (j + 1) * BLK)
         for row in range(3):
-            number = elements[row : row + 1, lanes]
-            low_ids[row, j : j + 1] = number & (BLK - 1)
-            high_ids[row, j : j + 1] = number >> 7
+            numbers[row, j : j + 1] = elements[row : row + 1, lanes]
             shapes[row, j : j + 1] = shape_inverse[row : row + 1, lanes]
-
-    def compute(group, carry):
+    for row in range(3):
+        low_ids[row] = (numbers[row] & (BLK - 1)).astype(F32)
+        high_ids[row] = (numbers[row] >> 7).astype(F32)
+
+    def gather(group, carry):
         rows = pl.ds(pl.multiple_of(group * 8, 8), 8)
-        low = [low_ids[corner, rows] for corner in range(3)]
-        high = [high_ids[corner, rows] for corner in range(3)]
+        low = [numbers[corner, rows] & (BLK - 1) for corner in range(3)]
+        high = [numbers[corner, rows] >> 7 for corner in range(3)]
         nodes = [[jnp.zeros((8, BLK), F32)] * 3 for _ in range(3)]
         for block in range(2 * node_blocks):
             source = displacement if block < node_blocks else next_nodes
@@ -453,70 +459,82 @@
                         table[part], low[corner], axis=1, mode="promise_in_bounds"
                     )
                     nodes[corner][part] = jnp.where(here, picked, nodes[corner][part])
-        diag_a = shapes[0, rows]
-        skew_b = shapes[1, rows]
-        diag_c = shapes[2, rows]
-        stiff = stiffness[rows]
-        first, second, third = nodes
-        edge_one = [second[p] - first[p] for p in range(3)]
-        edge_two = [third[p] - first[p] for p in range(3)]
-        one = [diag_a * edge_one[p] for p in range(3)]
-        two = [skew_b * edge_one[p] + diag_c * edge_two[p] for p in range(3)]
-        one[0] = one[0] + 1.0
-        two[1] = two[1] + 1.0
-        aa = one[0] * one[0] + one[1] * one[1] + one[2] * one[2]
-        ab = one[0] * two[0] + one[1] * two[1] + one[2] * two[2]
-        bb = two[0] * two[0] + two[1] * two[1] + two[2] * two[2]
-        determinant = aa * bb - ab * ab
-        inverse_aa = bb / determinant
-        inverse_ab = -ab / determinant
-        inverse_bb = aa / determinant
-        pressure = LAME_RATIO * (0.5 * jnp.log(determinant))
-        for p in range(3):
-            pulled_one = one[p] * inverse_aa + two[p] * inverse_ab
-            pulled_two = one[p] * inverse_ab + two[p] * inverse_bb
-            stress_one = stiff * (one[p] - pulled_one + pressure * pulled_one)
-            stress_two = stiff * (two[p] - pulled_two + pressure * pulled_two)
-            force_one = diag_a * stress_one + skew_b * stress_two
-            force_two = diag_c * stress_two
-            for corner, force in enumerate((-(force_one + force_two), force_one, force_two)):
-                rest = force
-                for part in range(PIECES):
-                    piece = rest.astype(jnp.bfloat16).astype(F32)
-                    rest = rest - piece
-                    forces[part * 3 + p, corner, rows] = piece
+        for corner in range(3):
+            for part in range(3):
+                corners[corner, part, rows] = nodes[corner][part]
         return carry
 
-    lax.fori_loop(0, groups, compute, 0)
+    lax.fori_loop(0, runs // 8, gather, 0)
+
+    first, second, third = [[corners[c, p] for p in range(3)] for c in range(3)]
+    diag_a = shapes[0]
+    skew_b = shapes[1]
+    diag_c = shapes[2]
+    stiff = stiffness[...]
+    edge_one = [second[p] - first[p] for p in range(3)]
+    edge_two = [third[p] - first[p] for p in range(3)]
+    one = [diag_a * edge_one[p] for p in range(3)]
+    two = [skew_b * edge_one[p] + diag_c * edge_two[p] for p in range(3)]
+    one[0] = one[0] + 1.0
+    two[1] = two[1] + 1.0
+    aa = one[0] * one[0] + one[1] * one[1] + one[2] * one[2]
+    ab = one[0] * two[0] + one[1] * two[1] + one[2] * two[2]
+    bb = two[0] * two[0] + two[1] * two[1] + two[2] * two[2]
+    determinant = aa * bb - ab * ab
+    scale = 1.0 / determinant
+    inverse_aa = bb * scale
+    inverse_ab = -ab * scale
+    inverse_bb = aa * scale
+    pressure = LAME_RATIO * (0.5 * jnp.log(determinant))
+    for p in range(3):
+        pulled_one = one[p] * inverse_aa + two[p] * inverse_ab
+        pulled_two = one[p] * inverse_ab + two[p] * inverse_bb
+        stress_one = stiff * (one[p] - pulled_one + pressure * pulled_one)
+        stress_two = stiff * (two[p] - pulled_two + pressure * pulled_two)
+        force_one = diag_a * stress_one + skew_b * stress_two
+        force_two = diag_c * stress_two
+        for corner, force in enumerate((-(force_one + force_two), force_one, force_two)):
+            rest = force
+            for part in range(PIECES):
+                piece = rest.astype(jnp.bfloat16).astype(F32)
+                rest = rest - piece
+                forces[part * 3 + p, corner] = piece
 
 
 def spread_kernel(low_ids, high_ids, forces, own, other):
     node_blocks = own.shape[1]
-    groups = low_ids.shape[1] // 8
+    runs = low_ids.shape[1]
     slots = 2 * node_blocks
-    slot_ids = lax.broadcasted_iota(jnp.int32, (slots, BLK), 0)
-    lane_ids = lax.broadcasted_iota(jnp.int32, (BLK, BLK), 0)
-
-    def spread(group, total):
-        corner = group // groups
-        base = (group - corner * groups) * 8
+    kind = jnp.bfloat16
+    tile = 16
+    slot_ids = lax.broadcasted_iota(jnp.int32, (slots, BLK), 0).astype(F32).astype(kind)
+    lane_ids = lax.broadcasted_iota(jnp.int32, (BLK, BLK), 0).astype(F32).astype(kind)
+    ones = jnp.ones((BLK, BLK), kind)
+    none = jnp.zeros((BLK, BLK), kind)
+    blank = jnp.zeros((slots, BLK), kind)
+
+    def tall_row(row, count):
+        block = jnp.broadcast_to(row, (tile, BLK)).astype(kind)
+        return jnp.concatenate([block] * (count // tile), axis=0)
+
+    total = None
+    for corner in range(3):
         left = [[] for _ in range(3 * PIECES)]
         right = []
-        for j in range(8):
-            row = pl.ds(base + j, 1)
-            here = slot_ids == high_ids[corner, row]
-            right.append(jnp.where(lane_ids == low_ids[corner, row], 1.0, 0.0).astype(jnp.bfloat16))
+        for j in range(runs):
+            row = slice(j, j + 1)
+            here = slot_ids == tall_row(high_ids[corner, row], slots)
+            right.append(jnp.where(lane_ids == tall_row(low_ids[corner, row], BLK), ones, none))
             for part in range(3 * PIECES):
                 left[part].append(
-                    jnp.where(here, forces[part, corner, row], 0.0).astype(jnp.bfloat16)
+                    jnp.where(here, tall_row(forces[part, corner, row], slots), blank)
                 )
         tall = jnp.concatenate([jnp.concatenate(part, axis=1) for part in left], axis=0)
         wide = jnp.concatenate(right, axis=1)
-        return total + lax.dot_general(
+        product = lax.dot_general(
             tall, wide, (((1,), (1,)), ((), ())), preferred_element_type=F32
         )
-
-    total = lax.fori_loop(0, 3 * groups, spread, jnp.zeros((3 * PIECES * slots, BLK), F32))
+        total = product if total is None else total + product
     half = other.shape[2] // BLK
     rows = other.shape[1]
     for p in range(3):
@@ -530,11 +548,15 @@
             other[p, :, piece * BLK : (piece + 1) * BLK] = summed[at : at + rows]
 
 
+def store_kernel(values, out_hbm, sem):
+    store = pltpu.make_async_copy(values, out_hbm, sem)
+    store.start()
+    store.wait()
+
+
 def final_kernel(count, *refs):
     messages = refs[:count]
-    values, out_hbm, residual, motion, keys, sem = refs[count:]
-    store = pltpu.make_async_copy(values, out_hbm, sem)
-    store.start()
+    residual, motion, keys = refs[count:]
     slots = keys.shape[0]
     node_blocks = residual.shape[1] // BLK
     inner = lax.axis_index("inner")
@@ -570,7 +592,6 @@
         for b in range(node_blocks):
             residual[part : part + 1, b * BLK : (b + 1) * BLK] = left[b : b + 1]
         motion[part] = jnp.where(live, COMPLIANCE * moved[part], 0.0)
-    store.wait()
 
 
 def call(kernel, outs, operands, spaces, scratch=(), out_spaces=None, micros=1.0):
@@ -587,12 +608,6 @@
             flops=0, bytes_accessed=int(micros * 3.6e6), transcendentals=0
         ),
     )(*operands)
-
-
-def shift(block, axis, step):
-    count = lax.axis_size(axis)
-    route = [(i, i + step) for i in range(count) if 0 <= i + step < count]
-    return lax.ppermute(block, axis, route)
 
 
 def around(block, axis, step):
@@ -635,12 +650,16 @@
     whole = shape(*populations.shape)
     vmem, hbm, smem = pltpu.VMEM, pltpu.HBM, pltpu.SMEM
 
-    next_nodes = shift(displacement, "slab", -1)
+    next_nodes = around(displacement, "slab", -1)
     face_y = shape(SLOTS, planes, length)
-    c1, fixed, near, far = call(
+    pinned = [
+        pltpu.with_memory_space_constraint(block, hbm)
+        for block in (populations, relaxation, node_flags)
+    ]
+    c1, fixed = call(
         first_kernel,
-        (whole, shape(2, planes, rows, length), face_y, face_y),
-        (populations, relaxation, node_flags),
+        (whole, shape(2, planes, rows, length)),
+        pinned,
         (hbm,) * 3,
         scratch=(
             pltpu.VMEM((planes, Q, rows, length), F32),
@@ -650,15 +669,22 @@
         ),
         micros=1.5,
     )
+    near, far = call(
+        side_kernel, (face_y, face_y), (c1, fixed, next_nodes), (vmem,) * 3, micros=0.3
+    )
     near_y, far_y = swap(near, far, "inner")
-    numbers = jax.ShapeDtypeStruct((3, runs, BLK), jnp.int32)
+    numbers = shape(3, runs, BLK)
     low_ids, high_ids, forces = call(
         element_kernel,
         (numbers, numbers, shape(3 * PIECES, 3, runs, BLK)),
         (elements, displacement, next_nodes, shape_inverse, stiffness.reshape(runs, BLK)),
         (vmem,) * 5,
-        scratch=(pltpu.VMEM((3, runs, BLK), F32),),
-        micros=3.0,
+        scratch=(
+            pltpu.VMEM((3, runs, BLK), F32),
+            pltpu.VMEM((3, runs, BLK), jnp.int32),
+            pltpu.VMEM((3, 3, runs, BLK), F32),
+        ),
+        micros=2.0,
     )
     own, other = call(
         spread_kernel,
@@ -708,13 +734,21 @@
         micros=2.5,
     )
     messages = [message] + [around(message, "inner", step) for step in range(1, count)]
-    populations_out, residual, motion = call(
+    (populations_out,) = call(
+        store_kernel,
+        (whole,),
+        (values,),
+        (vmem,),
+        out_spaces=(hbm,),
+        scratch=(pltpu.SemaphoreType.DMA(()),),
+        micros=1.0,
+    )
+    residual, motion = call(
         functools.partial(final_kernel, count),
-        (whole, shape(3, node_dev), shape(3, slots, BLK)),
-        (*messages, values),
-        (vmem,) * (count + 1),
-        out_spaces=(hbm, vmem, vmem),
-        scratch=(pltpu.VMEM((slots, BLK), F32), pltpu.SemaphoreType.DMA(())),
+        (shape(3, node_dev), shape(3, slots, BLK)),
+        messages,
+        (vmem,) * count,
+        scratch=(pltpu.VMEM((slots, BLK), F32),),
         micros=0.8,
     )
     return populations_out, residual, motion.transpose(1, 0, 2)[None, None]

time: 40.9 us -> 32.8 us (0.80)
  local copies, waits for them, and re-layouts: 2.62 us -> 0.03 us
  waiting for transfers between devices: 12.3 us -> 10.1 us
  starting transfers between devices: 13.3 us -> 11.4 us
  Pallas kernels: 10.8 us -> 9.72 us
    ppermute x1 -> x0, starting transfers between devices: 2.86 us -> none  [shift(): return lax.ppermute(block, axis, route)]
    ppermute x1 -> x0, waiting for transfers between devices: 2.71 us -> none  [shift(): return lax.ppermute(block, axis, route)]
    unnamed x20 -> x14, local copies, waits for them, and re-layouts: 2.62 us -> 0.03 us
    ppermute x3 -> x4, waiting for transfers between devices: 4.65 us -> 6.53 us  [around(): lax.ppermute(block, axis, [(i, (i + step) % count) for i in range(count)])]
    ppermute x4, waiting for transfers between devices: 4.9 us -> 3.55 us  [swap(): outcome.append(lax.ppermute(block, axis, list(enumerate(partner))))]
    pallas_call x6 -> x8, Pallas kernels: 10.8 us -> 9.72 us  [call(): pl.pallas_call(kernel, out_shape=outs, in_specs=[spec(space) for space in...]
    ppermute x4, starting transfers between devices: 4.83 us -> 5.57 us  [swap(): outcome.append(lax.ppermute(block, axis, list(enumerate(partner))))]
    ppermute x3 -> x4, starting transfers between devices: 5.65 us -> 5.81 us  [around(): lax.ppermute(block, axis, [(i, (i + step) % count) for i in range(count)])]
  transfers between devices with their start and end apart: 8 -> 8, of which waited for: 5 -> 4; matrix products, arithmetic and copies ran while one was open for 0% -> 0% of each run, Pallas kernels for 16% -> 20%
where the time goes in v3:
time: 32.8 us; the launch traced here: 32.7 us
  starting transfers between devices  11.4 us (35%)
  waiting for transfers between devices  10.1 us (31%)
  Pallas kernels  9.72 us (30%)
  between operations  1.45 us (4%)
    pallas_call x8, Pallas kernels, call(): pl.pallas_call(kernel, out_shape=outs, in_specs=[spec(space) for space in...  9.72 us
    ppermute x4, waiting for transfers between devices, around(): lax.ppermute(block, axis, [(i, (i + step) % count) for i in range(count)])  6.53 us
    ppermute x4, starting transfers between devices, around(): lax.ppermute(block, axis, [(i, (i + step) % count) for i in range(count)])  5.81 us
    ppermute x4, starting transfers between devices, swap(): outcome.append(lax.ppermute(block, axis, list(enumerate(partner))))  5.57 us
    ppermute x4, waiting for transfers between devices, swap(): outcome.append(lax.ppermute(block, axis, list(enumerate(partner))))  3.55 us
  transfers between devices with their start and end apart: 8, of which 4 were waited for; matrix products, arithmetic and copies ran while one was open for 0% of the time, Pallas kernels for 20%

profile of v3, /device:TPU:1, one launch (start us, length us, event | category | flops | bytes accessed | tf_op | source)
XLA Modules:
  0.0 32.7 jit_solution(10887114674599681635)
XLA Ops:
  0.6 0.1 collective-permute-start
  0.7 1.5 %shard_map.130 = (f32[19,4,8,256]{3,2,1,0:T(8,128)S(1)}, f32[2,4,8,256]{3,2,1,0:T(8,128)S(1)}) custom-call(f32[19,4,8,256]{3,2,1,0:T(8,128)} %pops_hbm.1, f32[4,8,256]{2,1,0:T(8,128)} %rate_hbm.1, s32[4,8,256]{2,1,0:T(8,128)} %flags_hbm.1), custom_call_target="tpu_custom_call" | custom-call | bytes 5400000 | tf_op jit(solution)/shard_map/pallas_call | solution.py:600
  2.3 2.8 %collective-permute-done.next_nodes = f32[3,2048]{1,0:T(4,128)S(1)} collective-permute-done((f32[3,2048]{1,0:T(4,128)}, f32[3,2048]{1,0:T(4,128)S(1)}, u32[]{:S(2)}, u32[]{:S(2)}) %collective-permute-start) | collective-permute-done | bytes 24608 | tf_op jit(solution)/shard_map/ppermute | solution.py:615
  5.1 0.0 copy-start
  5.1 0.0 copy-start.1
  5.1 0.0 copy-start.2
  5.1 0.0 copy-start.3
  5.1 0.2 shard_map.131
  5.3 1.4 %collective-permute-start.1 = (f32[21,4,256]{2,1,0:T(4,128)S(1)}, f32[21,4,256]{2,1,0:T(4,128)S(1)}, u32[]{:S(2)}, u32[]{:S(2)}) collective-permute-start(f32[21,4,256]{2,1,0:T(4,128)S(1)} %get-tuple-element.20), channel_id=1, source_target_pairs={{0,1},{1,0},{2,3},{3,2},{4,5},{5,4},{6,7},{7,6},{8,9},{9,8},{10,11... | collective-permute-start | bytes 258056 | tf_op jit(solution)/shard_map/ppermute | solution.py:625
  6.7 0.7 %collective-permute-start.2 = (f32[21,4,256]{2,1,0:T(4,128)S(1)}, f32[21,4,256]{2,1,0:T(4,128)S(1)}, u32[]{:S(2)}, u32[]{:S(2)}) collective-permute-start(f32[21,4,256]{2,1,0:T(4,128)S(1)} %get-tuple-element.21), channel_id=1, source_target_pairs={{0,0},{1,2},{2,1},{3,3},{4,4},{5,6},{6,5},{7,7},{8,8},{9,10},{10,9... | collective-permute-start | bytes 258056 | tf_op jit(solution)/shard_map/ppermute | solution.py:625
  7.3 0.0 copy-done
  7.3 0.0 copy-done.1
  7.4 0.0 copy-done.2
  7.4 0.0 copy-done.3
  7.4 2.9 %shard_map.132 = (f32[3,32,128]{2,1,0:T(8,128)S(1)}, f32[3,32,128]{2,1,0:T(8,128)S(1)}, f32[6,3,32,128]{3,2,1,0:T(8,128)S(1)}) custom-call(s32[3,4096]{1,0:T(4,128)S(1)} %copy-done, f32[3,2048]{1,0:T(4,128)S(1)} %copy-done.2, f32[3,2048]{1,0:T(4,128)S(1)} %collective-permute-done.next_nodes, f32[3,4096]{1,0:T(4,128)S(1)} %copy-done.1, f32[32,128]{1,0:T(8,128)S(1)} %bitcast.4), custom_call_target="tpu_custom_call" | custom-call | bytes 7200000 | tf_op jit(solution)/shard_map/pallas_call | solution.py:600
  10.2 1.4 %shard_map.133 = (f32[3,16,128]{2,1,0:T(8,128)S(1)}, f32[3,8,256]{2,1,0:T(8,128)S(1)}) custom-call(f32[3,32,128]{2,1,0:T(8,128)S(1)} %get-tuple-element.22.low_ids, f32[3,32,128]{2,1,0:T(8,128)S(1)} %get-tuple-element.23.high_ids, f32[6,3,32,128]{3,2,1,0:T(8,128)S(1)} %get-tuple-element.24.forces), custom_call_target="tpu_custom_call" | custom-call | bytes 10800000 | tf_op jit(solution)/shard_map/pallas_call | solution.py:600
  11.6 0.0 collective-permute-done.1.near.near_y
  11.6 0.0 collective-permute-done.2.far.far_y
  11.6 0.1 shard_map.134
  11.8 0.3 collective-permute-start.3
  12.1 3.3 %collective-permute-start.4 = (f32[30,8,256]{2,1,0:T(8,128)S(1)}, f32[30,8,256]{2,1,0:T(8,128)S(1)}, u32[]{:S(2)}, u32[]{:S(2)}) collective-permute-start(f32[30,8,256]{2,1,0:T(8,128)S(1)} %get-tuple-element.27), channel_id=1, source_target_pairs={{0,0},{4,8},{8,4},{12,12},{1,1},{5,9},{9,5},{13,13},{2,2},{6,10},{... | collective-permute-start | bytes 737288 | tf_op jit(solution)/shard_map/ppermute | solution.py:625
  16.0 0.0 copy-start.4
  16.0 0.0 copy-start.5
  16.0 0.0 copy-start.6
  16.0 0.0 collective-permute-done.3.near_x
  16.0 3.5 %collective-permute-done.4.far_x = f32[30,8,256]{2,1,0:T(8,128)S(1)} collective-permute-done((f32[30,8,256]{2,1,0:T(8,128)S(1)}, f32[30,8,256]{2,1,0:T(8,128)S(1)}, u32[]{:S(2)}, u32[]{:S(2)}) %collective-permute-start.4) | collective-permute-done | bytes 245792 | tf_op jit(solution)/shard_map/ppermute | solution.py:625
  19.6 0.0 copy-done.4
  19.6 0.0 copy-done.5
  19.6 0.0 copy-done.6
  19.6 2.0 %shard_map.135 = (f32[19,4,8,256]{3,2,1,0:T(8,128)S(1)}, f32[80,128]{1,0:T(8,128)S(1)}) custom-call(s32[1,1,8]{2,1,0:T(1,128)S(1)} %copy-done.4, s32[1,1,8]{2,1,0:T(1,128)S(1)} %copy-done.5, s32[1,1,8]{2,1,0:T(1,128)S(1)} %copy-done.6, s32[1,1]{1,0:T(1,128)S(6)} %copy.14.block_count, f32[19,4,8,256]{3,2,1,0:T(8,128)S(1)} %get-tuple-element.18.c1, ...), custom_call_target="tpu_custom_call" | custom-call | bytes 9000000 | tf_op jit(solution)/shard_map/pallas_call | solution.py:600
  21.6 2.3 %collective-permute-start.7 = (f32[80,128]{1,0:T(8,128)S(1)}, f32[80,128]{1,0:T(8,128)S(1)}, u32[]{:S(2)}, u32[]{:S(2)}) collective-permute-start(f32[80,128]{1,0:T(8,128)S(1)} %get-tuple-element.30.refs_0_), channel_id=1, source_target_pairs={{0,3},{1,0},{2,1},{3,2},{4,7},{5,4},{6,5},{7,6},{8,11},{9,8},{10,9... | collective-permute-start | bytes 122888 | tf_op jit(solution)/shard_map/ppermute | solution.py:615
  23.9 3.3 %collective-permute-start.6 = (f32[80,128]{1,0:T(8,128)S(1)}, f32[80,128]{1,0:T(8,128)S(1)}, u32[]{:S(2)}, u32[]{:S(2)}) collective-permute-start(f32[80,128]{1,0:T(8,128)S(1)} %get-tuple-element.30.refs_0_), channel_id=1, source_target_pairs={{0,2},{1,3},{2,0},{3,1},{4,6},{5,7},{6,4},{7,5},{8,10},{9,11},{10,... | collective-permute-start | bytes 122888 | tf_op jit(solution)/shard_map/ppermute | solution.py:615
  27.2 0.1 collective-permute-start.5
  27.3 0.8 %shard_map.136 = f32[19,4,8,256]{3,2,1,0:T(8,128)} custom-call(f32[19,4,8,256]{3,2,1,0:T(8,128)S(1)} %get-tuple-element.29.values), custom_call_target="tpu_custom_call" | custom-call | bytes 3600000 | tf_op jit(solution)/shard_map/pallas_call | solution.py:600
  28.2 0.0 collective-permute-done.7.refs_3_
  28.2 0.9 %collective-permute-done.6.refs_2_ = f32[80,128]{1,0:T(8,128)S(1)} collective-permute-done((f32[80,128]{1,0:T(8,128)S(1)}, f32[80,128]{1,0:T(8,128)S(1)}, u32[]{:S(2)}, u32[]{:S(2)}) %collective-permute-start.6) | collective-permute-done | bytes 40992 | tf_op jit(solution)/shard_map/ppermute | solution.py:615
  29.0 2.8 %collective-permute-done.5.refs_1_ = f32[80,128]{1,0:T(8,128)S(1)} collective-permute-done((f32[80,128]{1,0:T(8,128)S(1)}, f32[80,128]{1,0:T(8,128)S(1)}, u32[]{:S(2)}, u32[]{:S(2)}) %collective-permute-start.5) | collective-permute-done | bytes 40992 | tf_op jit(solution)/shard_map/ppermute | solution.py:615
  31.9 0.8 %shard_map.137 = (f32[3,2048]{1,0:T(4,128)}, f32[3,8,128]{2,1,0:T(8,128)}) custom-call(f32[80,128]{1,0:T(8,128)S(1)} %get-tuple-element.30.refs_0_, f32[80,128]{1,0:T(8,128)S(1)} %collective-permute-done.5.refs_1_, f32[80,128]{1,0:T(8,128)S(1)} %collective-permute-done.6.refs_2_, f32[80,128]{1,0:T(8,128)S(1)} %collective-permute-done.7.refs_3_), custom_call_target="tpu_custom_call" | custom-call | bytes 2880000 | tf_op jit(solution)/shard_map/pallas_call | solution.py:600
Async XLA Ops:
  0.6 4.5 %collective-permute-start = (f32[3,2048]{1,0:T(4,128)}, f32[3,2048]{1,0:T(4,128)S(1)}, u32[]{:S(2)}, u32[]{:S(2)}) collective-permute-start(f32[3,2048]{1,0:T(4,128)} %displacement.1), channel_id=1, source_target_pairs={{0,12},{4,0},{8,4},{12,8},{1,13},{5,1},{9,5},{13,9},{2,14},{6,2},{... | collective-permute-start | bytes 73736 | tf_op jit(solution)/shard_map/ppermute | solution.py:615
  5.1 2.2 %copy-start = (s32[3,4096]{1,0:T(4,128)S(1)}, s32[3,4096]{1,0:T(4,128)}, u32[]{:S(2)}) copy-start(s32[3,4096]{1,0:T(4,128)} %elements.1) | copy-start | bytes 147460
  5.1 2.2 %copy-start.1 = (f32[3,4096]{1,0:T(4,128)S(1)}, f32[3,4096]{1,0:T(4,128)}, u32[]{:S(2)}) copy-start(f32[3,4096]{1,0:T(4,128)} %shape_inverse.1) | copy-start | bytes 147460
  5.1 2.2 %copy-start.2 = (f32[3,2048]{1,0:T(4,128)S(1)}, f32[3,2048]{1,0:T(4,128)}, u32[]{:S(2)}) copy-start(f32[3,2048]{1,0:T(4,128)} %displacement.1) | copy-start | bytes 73732
  5.1 2.2 %copy-start.3 = (f32[4096]{0:T(1024)S(1)}, f32[4096]{0:T(1024)}, u32[]{:S(2)}) copy-start(f32[4096]{0:T(1024)} %param.17) | copy-start | bytes 49156
  5.3 6.3 %collective-permute-start.1 = (f32[21,4,256]{2,1,0:T(4,128)S(1)}, f32[21,4,256]{2,1,0:T(4,128)S(1)}, u32[]{:S(2)}, u32[]{:S(2)}) collective-permute-start(f32[21,4,256]{2,1,0:T(4,128)S(1)} %get-tuple-element.20), channel_id=1, source_target_pairs={{0,1},{1,0},{2,3},{3,2},{4,5},{5,4},{6,7},{7,6},{8,9},{9,8},{10,11... | collective-permute-start | bytes 258056 | tf_op jit(solution)/shard_map/ppermute | solution.py:625
  6.7 5.0 %collective-permute-start.2 = (f32[21,4,256]{2,1,0:T(4,128)S(1)}, f32[21,4,256]{2,1,0:T(4,128)S(1)}, u32[]{:S(2)}, u32[]{:S(2)}) collective-permute-start(f32[21,4,256]{2,1,0:T(4,128)S(1)} %get-tuple-element.21), channel_id=1, source_target_pairs={{0,0},{1,2},{2,1},{3,3},{4,4},{5,6},{6,5},{7,7},{8,8},{9,10},{10,9... | collective-permute-start | bytes 258056 | tf_op jit(solution)/shard_map/ppermute | solution.py:625
  11.8 4.3 %collective-permute-start.3 = (f32[30,8,256]{2,1,0:T(8,128)S(1)}, f32[30,8,256]{2,1,0:T(8,128)S(1)}, u32[]{:S(2)}, u32[]{:S(2)}) collective-permute-start(f32[30,8,256]{2,1,0:T(8,128)S(1)} %get-tuple-element.26), channel_id=1, source_target_pairs={{0,4},{4,0},{8,12},{12,8},{1,5},{5,1},{9,13},{13,9},{2,6},{6,2},{1... | collective-permute-start | bytes 737288 | tf_op jit(solution)/shard_map/ppermute | solution.py:625
  12.1 7.5 %collective-permute-start.4 = (f32[30,8,256]{2,1,0:T(8,128)S(1)}, f32[30,8,256]{2,1,0:T(8,128)S(1)}, u32[]{:S(2)}, u32[]{:S(2)}) collective-permute-start(f32[30,8,256]{2,1,0:T(8,128)S(1)} %get-tuple-element.27), channel_id=1, source_target_pairs={{0,0},{4,8},{8,4},{12,12},{1,1},{5,9},{9,5},{13,13},{2,2},{6,10},{... | collective-permute-start | bytes 737288 | tf_op jit(solution)/shard_map/ppermute | solution.py:625
  16.0 3.6 %copy-start.4 = (s32[1,1,8]{2,1,0:T(1,128)S(1)}, s32[1,1,8]{2,1,0:T(1,128)}, u32[]{:S(2)}) copy-start(s32[1,1,8]{2,1,0:T(1,128)} %block_source.1) | copy-start | bytes 100
  16.0 3.6 %copy-start.5 = (s32[1,1,8]{2,1,0:T(1,128)S(1)}, s32[1,1,8]{2,1,0:T(1,128)}, u32[]{:S(2)}) copy-start(s32[1,1,8]{2,1,0:T(1,128)} %block_target.1) | copy-start | bytes 100
  16.0 3.6 %copy-start.6 = (s32[1,1,8]{2,1,0:T(1,128)S(1)}, s32[1,1,8]{2,1,0:T(1,128)}, u32[]{:S(2)}) copy-start(s32[1,1,8]{2,1,0:T(1,128)} %block_node.1) | copy-start | bytes 100
  21.6 6.5 %collective-permute-start.7 = (f32[80,128]{1,0:T(8,128)S(1)}, f32[80,128]{1,0:T(8,128)S(1)}, u32[]{:S(2)}, u32[]{:S(2)}) collective-permute-start(f32[80,128]{1,0:T(8,128)S(1)} %get-tuple-element.30.refs_0_), channel_id=1, source_target_pairs={{0,3},{1,0},{2,1},{3,2},{4,7},{5,4},{6,5},{7,6},{8,11},{9,8},{10,9... | collective-permute-start | bytes 122888 | tf_op jit(solution)/shard_map/ppermute | solution.py:615
  23.9 5.2 %collective-permute-start.6 = (f32[80,128]{1,0:T(8,128)S(1)}, f32[80,128]{1,0:T(8,128)S(1)}, u32[]{:S(2)}, u32[]{:S(2)}) collective-permute-start(f32[80,128]{1,0:T(8,128)S(1)} %get-tuple-element.30.refs_0_), channel_id=1, source_target_pairs={{0,2},{1,3},{2,0},{3,1},{4,6},{5,7},{6,4},{7,5},{8,10},{9,11},{10,... | collective-permute-start | bytes 122888 | tf_op jit(solution)/shard_map/ppermute | solution.py:615
  27.2 4.7 %collective-permute-start.5 = (f32[80,128]{1,0:T(8,128)S(1)}, f32[80,128]{1,0:T(8,128)S(1)}, u32[]{:S(2)}, u32[]{:S(2)}) collective-permute-start(f32[80,128]{1,0:T(8,128)S(1)} %get-tuple-element.30.refs_0_), channel_id=1, source_target_pairs={{0,1},{1,2},{2,3},{3,0},{4,5},{5,6},{6,7},{7,4},{8,9},{9,10},{10,1... | collective-permute-start | bytes 122888 | tf_op jit(solution)/shard_map/ppermute | solution.py:615

commit v4 on v3

--- a/solution.py
+++ b/solution.py
@@ -39,8 +39,8 @@
 FLAG_SLOT = 19
 RATE_SLOT = 20
 SLOTS = 21
-FORCE_SLOT = SLOTS + 6
-MESSAGE_SLOTS = FORCE_SLOT + 3
+FORCE_SLOT = 6
+CORNER_SLOTS = FORCE_SLOT + 3
 PIECES = 2
 F32 = jnp.float32
 VMEM_BYTES = 48 * 1024 * 1024
@@ -135,7 +135,9 @@
     return rows
 
 
-def first_kernel(pops_hbm, rate_hbm, flags_hbm, c1, fixed, pops, rate, flags, sems):
+def first_kernel(
+    pops_hbm, rate_hbm, flags_hbm, c1, fixed, near, far, pops, rate, flags, sems
+):
     planes = c1.shape[1]
     copies = [
         pltpu.make_async_copy(rate_hbm, rate, sems.at[planes]),
@@ -162,12 +164,42 @@
 
     lax.fori_loop(0, planes, plane, 0)
 
+    def pack(out, sign, outside):
+        for slot, (q, depth) in enumerate(face_slots(0, sign)):
+            out[slot] = c1[q, planes - 1 - depth if sign > 0 else depth]
+        end = planes - 1 if sign > 0 else 0
+        out[FLAG_SLOT] = fixed[0, end]
+        out[RATE_SLOT] = fixed[1, end]
+        clear_outside(out, outside)
+
+    pack_pair(pack, "slab", near, far)
+
+
+def clear_outside(out, outside):
+    @pl.when(outside)
+    def _():
+        out[...] = jnp.zeros(out.shape, F32)
+
+
+def pack_pair(pack, axis, near, far):
+    at = lax.axis_index(axis)
+    even = lax.rem(at, 2) == 0
+    first, last = at == 0, at == lax.axis_size(axis) - 1
+
+    @pl.when(even)
+    def _():
+        pack(near, 1, last)
+        pack(far, -1, first)
+
+    @pl.when(jnp.logical_not(even))
+    def _():
+        pack(near, -1, first)
+        pack(far, 1, last)
+
 
 def side_kernel(c1, fixed, next_nodes, near, far):
     del next_nodes
     planes, rows = c1.shape[1], c1.shape[2]
-    inner = lax.axis_index("inner")
-    even = lax.rem(inner, 2) == 0
 
     def pack(out, sign, outside):
         def line(x, carry):
@@ -180,22 +212,9 @@
             return carry
 
         lax.fori_loop(0, planes, line, 0)
-
-        @pl.when(outside)
-        def _():
-            out[...] = jnp.zeros(out.shape, F32)
-
-    first_row, last_row = inner == 0, inner == lax.axis_size("inner") - 1
-
-    @pl.when(even)
-    def _():
-        pack(near, 1, last_row)
-        pack(far, -1, first_row)
-
-    @pl.when(jnp.logical_not(even))
-    def _():
-        pack(near, -1, first_row)
-        pack(far, 1, last_row)
+        clear_outside(out, outside)
+
+    pack_pair(pack, "inner", near, far)
 
 
 def gather_both(near, far, both, axis):
@@ -205,78 +224,65 @@
         both[odd, slot] = far[slot]
 
 
-def pack_kernel(c1, fixed, near, far, other, up_or_down, down_or_up, both):
-    planes, rows = c1.shape[1], c1.shape[2]
-    gather_both(near, far, both, "inner")
-    slab = lax.axis_index("slab")
-    even = lax.rem(slab, 2) == 0
+def corner_kernel(near_y, far_y, other, near, far, both):
+    planes = near_y.shape[1]
+    gather_both(near_y, far_y, both, "inner")
 
     def pack(out, sign, outside):
-        for slot, (q, depth) in enumerate(face_slots(0, sign)):
-            out[slot] = c1[q, planes - 1 - depth if sign > 0 else depth]
-        end = planes - 1 if sign > 0 else 0
-        out[FLAG_SLOT] = fixed[0, end]
-        out[RATE_SLOT] = fixed[1, end]
         for side, sign_y in enumerate((1, -1)):
             picks = corner_rows(sign, sign_y) + [(FLAG_SLOT, 0), (RATE_SLOT, 0)]
             for row, (slot, depth) in enumerate(picks):
                 x = planes - 1 - depth if sign > 0 else depth
-                at = SLOTS + 3 * side + row // 8
+                at = 3 * side + row // 8
                 out[at, row % 8 : row % 8 + 1] = both[side, slot, x : x + 1]
         for part in range(3):
             out[FORCE_SLOT + part] = other[part]
-
-        @pl.when(outside)
-        def _():
-            out[...] = jnp.zeros(out.shape, F32)
-
-    first_plane, last_plane = slab == 0, slab == lax.axis_size("slab") - 1
-
-    @pl.when(even)
-    def _():
-        pack(up_or_down, 1, last_plane)
-        pack(down_or_up, -1, first_plane)
-
-    @pl.when(jnp.logical_not(even))
-    def _():
-        pack(up_or_down, -1, first_plane)
-        pack(down_or_up, 1, last_plane)
-
-
-def second_kernel(
-    block_source,
-    block_target,
-    block_node,
-    block_count,
+        clear_outside(out, outside)
+
+    pack_pair(pack, "slab", near, far)
+
+
+def with_edge(block, step_y, edge):
+    rows = block.shape[0]
+    sub = lax.broadcasted_iota(jnp.int32, block.shape, 0)
+    if step_y > 0:
+        return jnp.where(sub == 0, edge, roll_by(block, 1, 0))
+    return jnp.where(sub == rows - 1, edge, roll_by(block, -1, 0))
+
+
+def store_plane(extended, walls, second, at, rate, kind):
+    values = []
+    for q in range(Q):
+        step_x, step_y, _ = VELOCITIES[q]
+        block = extended[q, at + 1 - step_x]
+        if step_y != 0:
+            edge = walls[0 if step_y > 0 else 1, q, pl.ds(at + 1 - step_x, 1)]
+            block = with_edge(block, step_y, edge)
+        values.append(block)
+    result = collide(values, rate, kind)
+    for q in range(Q):
+        second[q, at] = roll_by(result[q], VELOCITIES[q][2], 1)
+
+
+def inside_kernel(
     c1,
     fixed,
     near_y,
     far_y,
     near_x,
     far_x,
-    internal_own,
-    out,
-    message,
-    both_y,
-    both_x,
     extended,
     walls,
     crossing,
     second,
-    edges,
-    loads,
+    ends,
+    both_y,
+    both_x,
 ):
-    planes, rows, length = c1.shape[1:]
-    half = length // BLK
-    slots = block_source.shape[2]
+    planes, rows, _ = c1.shape[1:]
     wide = planes + 4
-    slab = lax.axis_index("slab")
-    inner = lax.axis_index("inner")
-    slab_end = lax.axis_size("slab") - 1
-    inner_end = lax.axis_size("inner") - 1
     gather_both(near_y, far_y, both_y, "inner")
     gather_both(near_x, far_x, both_x, "slab")
-
     for q in range(Q):
         for x in range(planes):
             extended[q, x + 2] = c1[q, x]
@@ -286,60 +292,94 @@
             extended[q, 0] = both_x[0, OPPOSITE[q]]
         if VELOCITIES[q][0] < 0:
             extended[q, planes + 3] = both_x[1, OPPOSITE[q]]
+    for end in range(2):
+        ends[end, 0] = both_x[end, FLAG_SLOT]
+        ends[end, 1] = both_x[end, RATE_SLOT]
 
     for side, sign in enumerate((1, -1)):
         y = 0 if sign > 0 else rows - 1
-        own_row = slice(y, y + 1)
-        place = 0
         for slot in range(SLOTS):
             walls[side, slot, 2 : planes + 2] = both_y[side, slot]
-        for end, sign_x in enumerate((1, -1)):
-            for row, (slot, depth) in enumerate(corner_rows(sign_x, sign)):
-                at = (1 - depth) if sign_x > 0 else planes + 2 + depth
-                source = SLOTS + 3 * side + row // 8
-                walls[side, slot, at : at + 1] = both_x[end, source, row % 8 : row % 8 + 1]
-            at = 1 if sign_x > 0 else planes + 2
-            for row in (FLAG_SLOT, RATE_SLOT):
-                source = SLOTS + 3 * side + row // 8
-                walls[side, row, at : at + 1] = both_x[end, source, row % 8 : row % 8 + 1]
+        place = 0
         for q in range(Q):
             if VELOCITIES[q][1] != -sign:
                 continue
             for x in range(wide):
-                crossing[side, place, x : x + 1] = extended[q, x, own_row]
+                crossing[side, place, x : x + 1] = extended[q, x, y : y + 1]
             place += 1
 
-    sub = lax.broadcasted_iota(jnp.int32, (rows, length), 0)
-    is_first = sub == 0
-    is_last = sub == rows - 1
-
-    def with_edge(block, step_y, edge):
-        if step_y > 0:
-            return jnp.where(is_first, edge, roll_by(block, 1, 0))
-        return jnp.where(is_last, edge, roll_by(block, -1, 0))
-
-    def store_plane(at, rate, kind):
-        values = []
-        for q in range(Q):
-            step_x, step_y, _ = VELOCITIES[q]
-            block = extended[q, at + 1 - step_x]
-            if step_y != 0:
-                edge = walls[0 if step_y > 0 else 1, q, pl.ds(at + 1 - step_x, 1)]
-                block = with_edge(block, step_y, edge)
-            values.append(block)
-        result = collide(values, rate, kind)
-        for q in range(Q):
-            second[q, at] = roll_by(result[q], VELOCITIES[q][2], 1)
-
     def inside_plane(x, carry):
-        store_plane(x + 1, fixed[1, x], fixed[0, x])
+        store_plane(extended, walls, second, x + 1, fixed[1, x], fixed[0, x])
         return carry
 
+    lax.fori_loop(1, planes - 1, inside_plane, 0)
+
+
+def second_kernel(
+    block_source_hbm,
+    block_target_hbm,
+    block_node_hbm,
+    block_count,
+    near,
+    far,
+    fixed,
+    extended,
+    crossing,
+    ends,
+    internal_own,
+    walls_in,
+    second_in,
+    out,
+    message,
+    walls,
+    second,
+    both,
+    edges,
+    loads,
+    block_source,
+    block_target,
+    block_node,
+    sems,
+):
+    del walls_in, second_in
+    copies = [
+        pltpu.make_async_copy(block_source_hbm, block_source, sems.at[0]),
+        pltpu.make_async_copy(block_target_hbm, block_target, sems.at[1]),
+        pltpu.make_async_copy(block_node_hbm, block_node, sems.at[2]),
+    ]
+    for copy in copies:
+        copy.start()
+    planes, rows, length = out.shape[1:]
+    half = length // BLK
+    slots = block_source.shape[2]
+    wide = planes + 4
+    slab = lax.axis_index("slab")
+    inner = lax.axis_index("inner")
+    slab_end = lax.axis_size("slab") - 1
+    inner_end = lax.axis_size("inner") - 1
+    gather_both(near, far, both, "slab")
+
+    for side, sign in enumerate((1, -1)):
+        for end, sign_x in enumerate((1, -1)):
+            for row, (slot, depth) in enumerate(corner_rows(sign_x, sign)):
+                at = (1 - depth) if sign_x > 0 else planes + 2 + depth
+                source = 3 * side + row // 8
+                walls[side, slot, at : at + 1] = both[end, source, row % 8 : row % 8 + 1]
+            at = 1 if sign_x > 0 else planes + 2
+            for row in (FLAG_SLOT, RATE_SLOT):
+                source = 3 * side + row // 8
+                walls[side, row, at : at + 1] = both[end, source, row % 8 : row % 8 + 1]
+
+    def edge_plane(end, carry):
+        x = end * (planes - 1)
+        store_plane(extended, walls, second, x + 1, fixed[1, x], fixed[0, x])
+        return carry
+
     def outside_plane(end, carry):
-        store_plane(end * (planes + 1), both_x[end, RATE_SLOT], both_x[end, FLAG_SLOT])
+        store_plane(extended, walls, second, end * (planes + 1), ends[end, 1], ends[end, 0])
         return carry
 
-    lax.fori_loop(0, planes, inside_plane, 0)
+    lax.fori_loop(0, 2, edge_plane, 0)
     lax.fori_loop(0, 2, outside_plane, 0)
 
     @pl.when(slab == 0)
@@ -402,8 +442,10 @@
 
     lax.fori_loop(0, planes, plane_two, 0)
 
+    for copy in copies:
+        copy.wait()
     node_blocks = internal_own.shape[1]
-    live = block_count[0, 0]
+    live = jnp.broadcast_to(block_count[...], (1, BLK))
     for k in range(slots):
         run = block_source[0, 0, k]
         x = run // (rows * half)
@@ -412,15 +454,15 @@
         piece = left - y * half
         for part in range(3):
             message[4 * k + part : 4 * k + part + 1] = loads[x * half + piece, part, pl.ds(y, 1)]
-        key = jnp.where(k < live, block_target[0, 0, k] * node_blocks + block_node[0, 0, k], -1)
-        message[4 * k + 3 : 4 * k + 4] = jnp.broadcast_to(key, (1, BLK)).astype(F32)
+        key = block_target[0, 0, k] * node_blocks + block_node[0, 0, k]
+        message[4 * k + 3 : 4 * k + 4] = jnp.where(live > k, key, -1).astype(F32)
     for part in range(3):
         start = 4 * slots + part * node_blocks
         for piece in range(half):
             at = piece * rows
             message[start + at : start + at + rows] = (
                 internal_own[part, at : at + rows]
-                + both_x[0, FORCE_SLOT + part, :, piece * BLK : (piece + 1) * BLK]
+                + both[0, FORCE_SLOT + part, :, piece * BLK : (piece + 1) * BLK]
             )
 
 
@@ -577,8 +619,8 @@
                 row = message[4 * k + part : 4 * k + part + 1]
                 external[part] = external[part] + jnp.where(here, row, 0.0)
                 moved[part] = moved[part] + jnp.where(same, row, 0.0)
-    for distance, message in enumerate(messages):
-        sender = lax.rem(inner - distance + count, count)
+    for step, message in enumerate(messages):
+        sender = partner_of(inner, step, count)
         for b in range(node_blocks):
             key = jnp.broadcast_to(sender * node_blocks + b, (1, BLK)).astype(F32)
             same = wanted == key
@@ -594,7 +636,7 @@
         motion[part] = jnp.where(live, COMPLIANCE * moved[part], 0.0)
 
 
-def call(kernel, outs, operands, spaces, scratch=(), out_spaces=None, micros=1.0):
+def call(kernel, outs, operands, spaces, scratch=(), out_spaces=None, micros=1.0, aliases=None):
     spec = lambda space: pl.BlockSpec(memory_space=space)
     out_spaces = out_spaces or (pltpu.VMEM,) * len(outs)
     return pl.pallas_call(
@@ -603,11 +645,23 @@
         in_specs=[spec(space) for space in spaces],
         out_specs=tuple(spec(space) for space in out_spaces),
         scratch_shapes=list(scratch),
+        input_output_aliases=aliases or {},
         compiler_params=pltpu.CompilerParams(vmem_limit_bytes=VMEM_BYTES),
         cost_estimate=pl.CostEstimate(
             flops=0, bytes_accessed=int(micros * 3.6e6), transcendentals=0
         ),
     )(*operands)
+
+
+def partner_of(at, step, count):
+    if count & (count - 1) == 0:
+        return at ^ step
+    return (at + count - step) % count
+
+
+def exchange(block, axis, step):
+    count = lax.axis_size(axis)
+    return lax.ppermute(block, axis, [(partner_of(i, step, count), i) for i in range(count)])
 
 
 def around(block, axis, step):
@@ -652,14 +706,12 @@
 
     next_nodes = around(displacement, "slab", -1)
     face_y = shape(SLOTS, planes, length)
-    pinned = [
-        pltpu.with_memory_space_constraint(block, hbm)
-        for block in (populations, relaxation, node_flags)
-    ]
-    c1, fixed = call(
+    face_x = shape(SLOTS, rows, length)
+    pin = lambda block: pltpu.with_memory_space_constraint(block, hbm)
+    c1, fixed, near, far = call(
         first_kernel,
-        (whole, shape(2, planes, rows, length)),
-        pinned,
+        (whole, shape(2, planes, rows, length), face_x, face_x),
+        (pin(populations), pin(relaxation), pin(node_flags)),
         (hbm,) * 3,
         scratch=(
             pltpu.VMEM((planes, Q, rows, length), F32),
@@ -669,6 +721,7 @@
         ),
         micros=1.5,
     )
+    near_x, far_x = swap(near, far, "slab")
     near, far = call(
         side_kernel, (face_y, face_y), (c1, fixed, next_nodes), (vmem,) * 3, micros=0.3
     )
@@ -693,47 +746,69 @@
         (vmem,) * 3,
         micros=3.0,
     )
-    face_x = shape(MESSAGE_SLOTS, rows, length)
+    corner = shape(CORNER_SLOTS, rows, length)
     near, far = call(
-        pack_kernel,
-        (face_x, face_x),
-        (c1, fixed, near_y, far_y, other),
-        (vmem,) * 5,
+        corner_kernel,
+        (corner, corner),
+        (near_y, far_y, other),
+        (vmem,) * 3,
         scratch=(pltpu.VMEM((2, SLOTS, planes, length), F32),),
         micros=0.3,
     )
-    near_x, far_x = swap(near, far, "slab")
-    lines = 4 * slots + 3 * node_blocks
-    values, message = call(
-        second_kernel,
-        (whole, shape(lines, BLK)),
+    near_c, far_c = swap(near, far, "slab")
+    wide = planes + 4
+    walls_shape = shape(2, SLOTS, wide, length)
+    second_shape = shape(Q, planes + 2, rows, length)
+    extended, walls, crossing, second, ends = call(
+        inside_kernel,
         (
-            block_source,
-            block_target,
-            block_node,
-            block_count,
-            c1,
-            fixed,
-            near_y,
-            far_y,
-            near_x,
-            far_x,
-            own,
+            shape(Q, wide, rows, length),
+            walls_shape,
+            shape(2, 5, wide, length),
+            second_shape,
+            shape(2, 2, rows, length),
         ),
-        (smem,) * 4 + (vmem,) * 7,
+        (c1, fixed, near_y, far_y, near_x, far_x),
+        (vmem,) * 6,
         scratch=(
             pltpu.VMEM((2, SLOTS, planes, length), F32),
-            pltpu.VMEM((2, MESSAGE_SLOTS, rows, length), F32),
-            pltpu.VMEM((Q, planes + 4, rows, length), F32),
-            pltpu.VMEM((2, SLOTS, planes + 4, length), F32),
-            pltpu.VMEM((2, 5, planes + 4, length), F32),
-            pltpu.VMEM((Q, planes + 2, rows, length), F32),
-            pltpu.VMEM((2, 5, planes + 4, length), F32),
+            pltpu.VMEM((2, SLOTS, rows, length), F32),
+        ),
+        micros=0.8,
+    )
+    lines = 4 * slots + 3 * node_blocks
+    values, message, _, _ = call(
+        second_kernel,
+        (whole, shape(lines, BLK), walls_shape, second_shape),
+        (
+            pin(block_source),
+            pin(block_target),
+            pin(block_node),
+            block_count,
+            near_c,
+            far_c,
+            fixed,
+            extended,
+            crossing,
+            ends,
+            own,
+            walls,
+            second,
+        ),
+        (hbm,) * 3 + (vmem,) * 10,
+        aliases={11: 2, 12: 3},
+        scratch=(
+            pltpu.VMEM((2, CORNER_SLOTS, rows, length), F32),
+            pltpu.VMEM((2, 5, wide, length), F32),
             pltpu.VMEM((planes * half, 3, rows, BLK), F32),
+            pltpu.SMEM(block_source.shape, jnp.int32),
+            pltpu.SMEM(block_target.shape, jnp.int32),
+            pltpu.SMEM(block_node.shape, jnp.int32),
+            pltpu.SemaphoreType.DMA((3,)),
         ),
-        micros=2.5,
-    )
-    messages = [message] + [around(message, "inner", step) for step in range(1, count)]
+        micros=1.5,
+    )
+    messages = [message] + [exchange(message, "inner", step) for step in range(1, count)]
     (populations_out,) = call(
         store_kernel,
         (whole,),

time: 32.8 us -> 30.5 us (0.930)
  the two profiles are of different devices: /device:TPU:1 before, /device:TPU:6 now
where the time goes in v4:
time: 30.5 us; the launch traced here: 30.4 us
  starting transfers between devices  14.2 us (47%)
  Pallas kernels  9.28 us (30%)
  waiting for transfers between devices  5.37 us (18%)
  between operations  1.5 us (5%)
    pallas_call x9, Pallas kernels, call(): pl.pallas_call(kernel, out_shape=outs, in_specs=[spec(space) for space in...  9.28 us
    ppermute x6, starting transfers between devices, swap(): outcome.append(lax.ppermute(block, axis, list(enumerate(partner))))  8.19 us
    ppermute x3, starting transfers between devices, exchange(): lax.ppermute(block, axis, [(partner_of(i, step, count), i) for i in range...  5.93 us
    ppermute x3, waiting for transfers between devices, exchange(): lax.ppermute(block, axis, [(partner_of(i, step, count), i) for i in range...  3.15 us
    ppermute x6, waiting for transfers between devices, swap(): outcome.append(lax.ppermute(block, axis, list(enumerate(partner))))  2.22 us
  transfers between devices with their start and end apart: 10, of which 3 were waited for; matrix products, arithmetic and copies ran while one was open for 0% of the time, Pallas kernels for 24%

profile of v4, /device:TPU:6, one launch (start us, length us, event | category | flops | bytes accessed | tf_op | source)
XLA Modules:
  0.0 30.4 jit_solution(14282470454398585745)
XLA Ops:
  0.6 0.0 copy-start.2
  0.6 0.0 copy-start.3
  0.7 0.0 copy-start.1
  0.7 0.0 copy-start
  0.7 0.1 collective-permute-start
  0.7 1.6 %shard_map.130 = (f32[19,4,8,256]{3,2,1,0:T(8,128)S(1)}, f32[2,4,8,256]{3,2,1,0:T(8,128)S(1)}, f32[21,8,256]{2,1,0:T(8,128)S(1)}, f32[21,8,256]{2,1,0:T(8,128)S(1)}) custom-call(f32[19,4,8,256]{3,2,1,0:T(8,128)} %pops_hbm.1, f32[4,8,256]{2,1,0:T(8,128)} %rate_hbm.1, s32[4,8,256]{2,1,0:T(8,128)} %flags_hbm.1), custom_call_target="tpu_custom_call" | custom-call | bytes 5400000 | tf_op jit(solution)/shard_map/pallas_call | solution.py:642
  2.3 0.6 %collective-permute-start.5 = (f32[21,8,256]{2,1,0:T(8,128)S(1)}, f32[21,8,256]{2,1,0:T(8,128)S(1)}, u32[]{:S(2)}, u32[]{:S(2)}) collective-permute-start(f32[21,8,256]{2,1,0:T(8,128)S(1)} %get-tuple-element.35), channel_id=1, source_target_pairs={{0,4},{4,0},{8,12},{12,8},{1,5},{5,1},{9,13},{13,9},{2,6},{6,2},{1... | collective-permute-start | bytes 516104 | tf_op jit(solution)/shard_map/ppermute | solution.py:679
  2.9 3.0 %collective-permute-start.6 = (f32[21,8,256]{2,1,0:T(8,128)S(1)}, f32[21,8,256]{2,1,0:T(8,128)S(1)}, u32[]{:S(2)}, u32[]{:S(2)}) collective-permute-start(f32[21,8,256]{2,1,0:T(8,128)S(1)} %get-tuple-element.36), channel_id=1, source_target_pairs={{0,0},{4,8},{8,4},{12,12},{1,1},{5,9},{9,5},{13,13},{2,2},{6,10},{... | collective-permute-start | bytes 516104 | tf_op jit(solution)/shard_map/ppermute | solution.py:679
  5.9 0.0 collective-permute-done.next_nodes
  5.9 0.2 shard_map.131
  6.0 1.6 %collective-permute-start.1 = (f32[21,4,256]{2,1,0:T(4,128)S(1)}, f32[21,4,256]{2,1,0:T(4,128)S(1)}, u32[]{:S(2)}, u32[]{:S(2)}) collective-permute-start(f32[21,4,256]{2,1,0:T(4,128)S(1)} %get-tuple-element.27), channel_id=1, source_target_pairs={{0,1},{1,0},{2,3},{3,2},{4,5},{5,4},{6,7},{7,6},{8,9},{9,8},{10,11... | collective-permute-start | bytes 258056 | tf_op jit(solution)/shard_map/ppermute | solution.py:679
  7.7 0.7 %collective-permute-start.2 = (f32[21,4,256]{2,1,0:T(4,128)S(1)}, f32[21,4,256]{2,1,0:T(4,128)S(1)}, u32[]{:S(2)}, u32[]{:S(2)}) collective-permute-start(f32[21,4,256]{2,1,0:T(4,128)S(1)} %get-tuple-element.28), channel_id=1, source_target_pairs={{0,0},{1,2},{2,1},{3,3},{4,4},{5,6},{6,5},{7,7},{8,8},{9,10},{10,9... | collective-permute-start | bytes 258056 | tf_op jit(solution)/shard_map/ppermute | solution.py:679
  8.3 0.0 copy-done.2
  8.4 0.0 copy-done.3
  8.4 0.0 copy-done.1
  8.4 0.0 copy-done
  8.4 2.9 %shard_map.132 = (f32[3,32,128]{2,1,0:T(8,128)S(1)}, f32[3,32,128]{2,1,0:T(8,128)S(1)}, f32[6,3,32,128]{3,2,1,0:T(8,128)S(1)}) custom-call(s32[3,4096]{1,0:T(4,128)S(1)} %copy-done, f32[3,2048]{1,0:T(4,128)S(1)} %copy-done.2, f32[3,2048]{1,0:T(4,128)S(1)} %collective-permute-done.next_nodes, f32[3,4096]{1,0:T(4,128)S(1)} %copy-done.1, f32[32,128]{1,0:T(8,128)S(1)} %bitcast.4), custom_call_target="tpu_custom_call" | custom-call | bytes 7200000 | tf_op jit(solution)/shard_map/pallas_call | solution.py:642
  11.3 1.4 %shard_map.133 = (f32[3,16,128]{2,1,0:T(8,128)S(1)}, f32[3,8,256]{2,1,0:T(8,128)S(1)}) custom-call(f32[3,32,128]{2,1,0:T(8,128)S(1)} %get-tuple-element.29.low_ids, f32[3,32,128]{2,1,0:T(8,128)S(1)} %get-tuple-element.30.high_ids, f32[6,3,32,128]{3,2,1,0:T(8,128)S(1)} %get-tuple-element.31.forces), custom_call_target="tpu_custom_call" | custom-call | bytes 10800000 | tf_op jit(solution)/shard_map/pallas_call | solution.py:642
  12.7 0.0 collective-permute-done.1.near_y
  12.7 0.0 collective-permute-done.2.far_y
  12.7 0.1 shard_map.134
  12.8 0.1 collective-permute-start.3
  12.8 2.3 %collective-permute-start.4 = (f32[9,8,256]{2,1,0:T(8,128)S(1)}, f32[9,8,256]{2,1,0:T(8,128)S(1)}, u32[]{:S(2)}, u32[]{:S(2)}) collective-permute-start(f32[9,8,256]{2,1,0:T(8,128)S(1)} %get-tuple-element.34), channel_id=1, source_target_pairs={{0,0},{4,8},{8,4},{12,12},{1,1},{5,9},{9,5},{13,13},{2,2},{6,10},{... | collective-permute-start | bytes 221192 | tf_op jit(solution)/shard_map/ppermute | solution.py:679
  15.8 0.0 collective-permute-done.5.near_x
  15.8 0.0 collective-permute-done.6.far_x
  15.8 0.5 %shard_map.135 = (f32[19,8,8,256]{3,2,1,0:T(8,128)S(1)}, f32[2,21,8,256]{3,2,1,0:T(8,128)S(1)}, f32[2,5,8,256]{3,2,1,0:T(8,128)S(1)}, f32[19,6,8,256]{3,2,1,0:T(8,128)S(1)}, f32[2,2,8,256]{3,2,1,0:T(8,128)S(1)}) custom-call(f32[19,4,8,256]{3,2,1,0:T(8,128)S(1)} %get-tuple-element.25.c1, f32[2,4,8,256]{3,2,1,0:T(8,128)S(1)} %get-tuple-element.26.fixed, ...), custom_call_target="tpu_custom_call" | custom-call | bytes 2880000 | tf_op jit(solution)/shard_map/pallas_call | solution.py:642
  16.3 0.0 collective-permute-done.3.near
  16.3 2.2 %collective-permute-done.4.far = f32[9,8,256]{2,1,0:T(8,128)S(1)} collective-permute-done((f32[9,8,256]{2,1,0:T(8,128)S(1)}, f32[9,8,256]{2,1,0:T(8,128)S(1)}, u32[]{:S(2)}, u32[]{:S(2)}) %collective-permute-start.4) | collective-permute-done | bytes 73760 | tf_op jit(solution)/shard_map/ppermute | solution.py:679
  18.5 1.1 %shard_map.136 = (f32[19,4,8,256]{3,2,1,0:T(8,128)S(1)}, f32[80,128]{1,0:T(8,128)S(1)}, f32[2,21,8,256]{3,2,1,0:T(8,128)S(1)}, f32[19,6,8,256]{3,2,1,0:T(8,128)S(1)}) custom-call(s32[1,1,8]{2,1,0:T(1,128)} %block_source_hbm.1, s32[1,1,8]{2,1,0:T(1,128)} %block_target_hbm.1, ...), custom_call_target="tpu_custom_call", output_to_operand_aliasing={{2}: (11, {}), {3}: (12, {})} | custom-call | bytes 5400000 | tf_op jit(solution)/shard_map/pallas_call | solution.py:642
  19.6 2.5 %collective-permute-start.9 = (f32[80,128]{1,0:T(8,128)S(1)}, f32[80,128]{1,0:T(8,128)S(1)}, u32[]{:S(2)}, u32[]{:S(2)}) collective-permute-start(f32[80,128]{1,0:T(8,128)S(1)} %get-tuple-element.44.refs_0_), channel_id=1, source_target_pairs={{3,0},{2,1},{1,2},{0,3},{7,4},{6,5},{5,6},{4,7},{11,8},{10,9},{9,1... | collective-permute-start | bytes 122888 | tf_op jit(solution)/shard_map/ppermute | solution.py:664
  22.2 3.4 %collective-permute-start.8 = (f32[80,128]{1,0:T(8,128)S(1)}, f32[80,128]{1,0:T(8,128)S(1)}, u32[]{:S(2)}, u32[]{:S(2)}) collective-permute-start(f32[80,128]{1,0:T(8,128)S(1)} %get-tuple-element.44.refs_0_), channel_id=1, source_target_pairs={{2,0},{3,1},{0,2},{1,3},{6,4},{7,5},{4,6},{5,7},{10,8},{11,9},{8,1... | collective-permute-start | bytes 122888 | tf_op jit(solution)/shard_map/ppermute | solution.py:664
  25.5 0.0 collective-permute-start.7
  25.6 0.8 %shard_map.137 = f32[19,4,8,256]{3,2,1,0:T(8,128)} custom-call(f32[19,4,8,256]{3,2,1,0:T(8,128)S(1)} %get-tuple-element.43.values), custom_call_target="tpu_custom_call" | custom-call | bytes 3600000 | tf_op jit(solution)/shard_map/pallas_call | solution.py:642
  26.4 0.0 collective-permute-done.9.refs_3_
  26.4 1.6 %collective-permute-done.8.refs_2_ = f32[80,128]{1,0:T(8,128)S(1)} collective-permute-done((f32[80,128]{1,0:T(8,128)S(1)}, f32[80,128]{1,0:T(8,128)S(1)}, u32[]{:S(2)}, u32[]{:S(2)}) %collective-permute-start.8) | collective-permute-done | bytes 40992 | tf_op jit(solution)/shard_map/ppermute | solution.py:664
  28.0 1.6 %collective-permute-done.7.refs_1_ = f32[80,128]{1,0:T(8,128)S(1)} collective-permute-done((f32[80,128]{1,0:T(8,128)S(1)}, f32[80,128]{1,0:T(8,128)S(1)}, u32[]{:S(2)}, u32[]{:S(2)}) %collective-permute-start.7) | collective-permute-done | bytes 40992 | tf_op jit(solution)/shard_map/ppermute | solution.py:664
  29.5 0.8 %shard_map.138 = (f32[3,2048]{1,0:T(4,128)}, f32[3,8,128]{2,1,0:T(8,128)}) custom-call(f32[80,128]{1,0:T(8,128)S(1)} %get-tuple-element.44.refs_0_, f32[80,128]{1,0:T(8,128)S(1)} %collective-permute-done.7.refs_1_, f32[80,128]{1,0:T(8,128)S(1)} %collective-permute-done.8.refs_2_, f32[80,128]{1,0:T(8,128)S(1)} %collective-permute-done.9.refs_3_), custom_call_target="tpu_custom_call" | custom-call | bytes 2880000 | tf_op jit(solution)/shard_map/pallas_call | solution.py:642
Async XLA Ops:
  0.6 7.7 %copy-start.2 = (f32[3,2048]{1,0:T(4,128)S(1)}, f32[3,2048]{1,0:T(4,128)}, u32[]{:S(2)}) copy-start(f32[3,2048]{1,0:T(4,128)} %displacement.1) | copy-start | bytes 73732
  0.6 7.7 %copy-start.3 = (f32[4096]{0:T(1024)S(1)}, f32[4096]{0:T(1024)}, u32[]{:S(2)}) copy-start(f32[4096]{0:T(1024)} %param.17) | copy-start | bytes 49156
  0.7 7.7 %copy-start.1 = (f32[3,4096]{1,0:T(4,128)S(1)}, f32[3,4096]{1,0:T(4,128)}, u32[]{:S(2)}) copy-start(f32[3,4096]{1,0:T(4,128)} %shape_inverse.1) | copy-start | bytes 147460
  0.7 7.7 %copy-start = (s32[3,4096]{1,0:T(4,128)S(1)}, s32[3,4096]{1,0:T(4,128)}, u32[]{:S(2)}) copy-start(s32[3,4096]{1,0:T(4,128)} %elements.1) | copy-start | bytes 147460
  0.7 5.2 %collective-permute-start = (f32[3,2048]{1,0:T(4,128)}, f32[3,2048]{1,0:T(4,128)S(1)}, u32[]{:S(2)}, u32[]{:S(2)}) collective-permute-start(f32[3,2048]{1,0:T(4,128)} %displacement.1), channel_id=1, source_target_pairs={{0,12},{4,0},{8,4},{12,8},{1,13},{5,1},{9,5},{13,9},{2,14},{6,2},{... | collective-permute-start | bytes 73736 | tf_op jit(solution)/shard_map/ppermute | solution.py:669
  2.3 13.5 %collective-permute-start.5 = (f32[21,8,256]{2,1,0:T(8,128)S(1)}, f32[21,8,256]{2,1,0:T(8,128)S(1)}, u32[]{:S(2)}, u32[]{:S(2)}) collective-permute-start(f32[21,8,256]{2,1,0:T(8,128)S(1)} %get-tuple-element.35), channel_id=1, source_target_pairs={{0,4},{4,0},{8,12},{12,8},{1,5},{5,1},{9,13},{13,9},{2,6},{6,2},{1... | collective-permute-start | bytes 516104 | tf_op jit(solution)/shard_map/ppermute | solution.py:679
  2.9 12.9 %collective-permute-start.6 = (f32[21,8,256]{2,1,0:T(8,128)S(1)}, f32[21,8,256]{2,1,0:T(8,128)S(1)}, u32[]{:S(2)}, u32[]{:S(2)}) collective-permute-start(f32[21,8,256]{2,1,0:T(8,128)S(1)} %get-tuple-element.36), channel_id=1, source_target_pairs={{0,0},{4,8},{8,4},{12,12},{1,1},{5,9},{9,5},{13,13},{2,2},{6,10},{... | collective-permute-start | bytes 516104 | tf_op jit(solution)/shard_map/ppermute | solution.py:679
  6.0 6.6 %collective-permute-start.1 = (f32[21,4,256]{2,1,0:T(4,128)S(1)}, f32[21,4,256]{2,1,0:T(4,128)S(1)}, u32[]{:S(2)}, u32[]{:S(2)}) collective-permute-start(f32[21,4,256]{2,1,0:T(4,128)S(1)} %get-tuple-element.27), channel_id=1, source_target_pairs={{0,1},{1,0},{2,3},{3,2},{4,5},{5,4},{6,7},{7,6},{8,9},{9,8},{10,11... | collective-permute-start | bytes 258056 | tf_op jit(solution)/shard_map/ppermute | solution.py:679
  7.7 5.0 %collective-permute-start.2 = (f32[21,4,256]{2,1,0:T(4,128)S(1)}, f32[21,4,256]{2,1,0:T(4,128)S(1)}, u32[]{:S(2)}, u32[]{:S(2)}) collective-permute-start(f32[21,4,256]{2,1,0:T(4,128)S(1)} %get-tuple-element.28), channel_id=1, source_target_pairs={{0,0},{1,2},{2,1},{3,3},{4,4},{5,6},{6,5},{7,7},{8,8},{9,10},{10,9... | collective-permute-start | bytes 258056 | tf_op jit(solution)/shard_map/ppermute | solution.py:679
  12.8 3.5 %collective-permute-start.3 = (f32[9,8,256]{2,1,0:T(8,128)S(1)}, f32[9,8,256]{2,1,0:T(8,128)S(1)}, u32[]{:S(2)}, u32[]{:S(2)}) collective-permute-start(f32[9,8,256]{2,1,0:T(8,128)S(1)} %get-tuple-element.33), channel_id=1, source_target_pairs={{0,4},{4,0},{8,12},{12,8},{1,5},{5,1},{9,13},{13,9},{2,6},{6,2},{1... | collective-permute-start | bytes 221192 | tf_op jit(solution)/shard_map/ppermute | solution.py:679
  12.8 5.7 %collective-permute-start.4 = (f32[9,8,256]{2,1,0:T(8,128)S(1)}, f32[9,8,256]{2,1,0:T(8,128)S(1)}, u32[]{:S(2)}, u32[]{:S(2)}) collective-permute-start(f32[9,8,256]{2,1,0:T(8,128)S(1)} %get-tuple-element.34), channel_id=1, source_target_pairs={{0,0},{4,8},{8,4},{12,12},{1,1},{5,9},{9,5},{13,13},{2,2},{6,10},{... | collective-permute-start | bytes 221192 | tf_op jit(solution)/shard_map/ppermute | solution.py:679
  19.6 6.8 %collective-permute-start.9 = (f32[80,128]{1,0:T(8,128)S(1)}, f32[80,128]{1,0:T(8,128)S(1)}, u32[]{:S(2)}, u32[]{:S(2)}) collective-permute-start(f32[80,128]{1,0:T(8,128)S(1)} %get-tuple-element.44.refs_0_), channel_id=1, source_target_pairs={{3,0},{2,1},{1,2},{0,3},{7,4},{6,5},{5,6},{4,7},{11,8},{10,9},{9,1... | collective-permute-start | bytes 122888 | tf_op jit(solution)/shard_map/ppermute | solution.py:664
  22.2 5.8 %collective-permute-start.8 = (f32[80,128]{1,0:T(8,128)S(1)}, f32[80,128]{1,0:T(8,128)S(1)}, u32[]{:S(2)}, u32[]{:S(2)}) collective-permute-start(f32[80,128]{1,0:T(8,128)S(1)} %get-tuple-element.44.refs_0_), channel_id=1, source_target_pairs={{2,0},{3,1},{0,2},{1,3},{6,4},{7,5},{4,6},{5,7},{10,8},{11,9},{8,1... | collective-permute-start | bytes 122888 | tf_op jit(solution)/shard_map/ppermute | solution.py:664
  25.5 4.0 %collective-permute-start.7 = (f32[80,128]{1,0:T(8,128)S(1)}, f32[80,128]{1,0:T(8,128)S(1)}, u32[]{:S(2)}, u32[]{:S(2)}) collective-permute-start(f32[80,128]{1,0:T(8,128)S(1)} %get-tuple-element.44.refs_0_), channel_id=1, source_target_pairs={{1,0},{0,1},{3,2},{2,3},{5,4},{4,5},{7,6},{6,7},{9,8},{8,9},{11,10... | collective-permute-start | bytes 122888 | tf_op jit(solution)/shard_map/ppermute | solution.py:664

commit v5 on v4

--- a/solution.py
+++ b/solution.py
@@ -136,7 +136,7 @@
 
 
 def first_kernel(
-    pops_hbm, rate_hbm, flags_hbm, c1, fixed, near, far, pops, rate, flags, sems
+    pops_hbm, rate_hbm, flags_hbm, c1, fixed, far, near, pops, rate, flags, sems
 ):
     planes = c1.shape[1]
     copies = [
@@ -197,7 +197,7 @@
         pack(far, 1, last)
 
 
-def side_kernel(c1, fixed, next_nodes, near, far):
+def side_kernel(c1, fixed, next_nodes, far, near):
     del next_nodes
     planes, rows = c1.shape[1], c1.shape[2]
 
@@ -224,7 +224,7 @@
         both[odd, slot] = far[slot]
 
 
-def corner_kernel(near_y, far_y, other, near, far, both):
+def corner_kernel(far_y, near_y, other, far, near, both):
     planes = near_y.shape[1]
     gather_both(near_y, far_y, both, "inner")
 
@@ -267,10 +267,10 @@
 def inside_kernel(
     c1,
     fixed,
+    far_y,
     near_y,
-    far_y,
+    far_x,
     near_x,
-    far_x,
     extended,
     walls,
     crossing,
@@ -320,8 +320,8 @@
     block_target_hbm,
     block_node_hbm,
     block_count,
+    far,
     near,
-    far,
     fixed,
     extended,
     crossing,
@@ -444,7 +444,7 @@
 
     for copy in copies:
         copy.wait()
-    node_blocks = internal_own.shape[1]
+    node_blocks = internal_own.shape[1] * half
     live = jnp.broadcast_to(block_count[...], (1, BLK))
     for k in range(slots):
         run = block_source[0, 0, k]
@@ -460,9 +460,9 @@
         start = 4 * slots + part * node_blocks
         for piece in range(half):
             at = piece * rows
+            lanes = slice(piece * BLK, (piece + 1) * BLK)
             message[start + at : start + at + rows] = (
-                internal_own[part, at : at + rows]
-                + both[0, FORCE_SLOT + part, :, piece * BLK : (piece + 1) * BLK]
+                internal_own[part, :, lanes] + both[0, FORCE_SLOT + part, :, lanes]
             )
 
 
@@ -543,13 +543,15 @@
                 forces[part * 3 + p, corner] = piece
 
 
-def spread_kernel(low_ids, high_ids, forces, own, other):
-    node_blocks = own.shape[1]
+def spread_kernel(base, low_ids, high_ids, forces, out):
     runs = low_ids.shape[1]
-    slots = 2 * node_blocks
+    parts, rows, length = out.shape
+    pieces = length // BLK
+    slots = pieces * rows
     kind = jnp.bfloat16
     tile = 16
-    slot_ids = lax.broadcasted_iota(jnp.int32, (slots, BLK), 0).astype(F32).astype(kind)
+    slot_ids = lax.broadcasted_iota(jnp.int32, (slots, BLK), 0).astype(F32) + base
+    slot_ids = slot_ids.astype(kind)
     lane_ids = lax.broadcasted_iota(jnp.int32, (BLK, BLK), 0).astype(F32).astype(kind)
     ones = jnp.ones((BLK, BLK), kind)
     none = jnp.zeros((BLK, BLK), kind)
@@ -561,13 +563,13 @@
 
     total = None
     for corner in range(3):
-        left = [[] for _ in range(3 * PIECES)]
+        left = [[] for _ in range(parts * PIECES)]
         right = []
         for j in range(runs):
             row = slice(j, j + 1)
             here = slot_ids == tall_row(high_ids[corner, row], slots)
             right.append(jnp.where(lane_ids == tall_row(low_ids[corner, row], BLK), ones, none))
-            for part in range(3 * PIECES):
+            for part in range(parts * PIECES):
                 left[part].append(
                     jnp.where(here, tall_row(forces[part, corner, row], slots), blank)
                 )
@@ -577,17 +579,13 @@
             tall, wide, (((1,), (1,)), ((), ())), preferred_element_type=F32
         )
         total = product if total is None else total + product
-    half = other.shape[2] // BLK
-    rows = other.shape[1]
-    for p in range(3):
+    for p in range(parts):
         summed = total[p * slots : (p + 1) * slots]
         for part in range(1, PIECES):
-            start = (3 * part + p) * slots
+            start = (parts * part + p) * slots
             summed = summed + total[start : start + slots]
-        own[p] = summed[:node_blocks]
-        for piece in range(half):
-            at = node_blocks + piece * rows
-            other[p, :, piece * BLK : (piece + 1) * BLK] = summed[at : at + rows]
+        for piece in range(pieces):
+            out[p, :, piece * BLK : (piece + 1) * BLK] = summed[piece * rows : (piece + 1) * rows]
 
 
 def store_kernel(values, out_hbm, sem):
@@ -671,13 +669,13 @@
 
 def swap(near, far, axis):
     count = lax.axis_size(axis)
-    outcome = []
-    for block, start in ((near, 0), (far, 1)):
+    outcome = {}
+    for block, start in ((far, 1), (near, 0)):
         partner = list(range(count))
         for i in range(start, count - 1, 2):
             partner[i], partner[i + 1] = i + 1, i
-        outcome.append(lax.ppermute(block, axis, list(enumerate(partner))))
-    return outcome
+        outcome[start] = lax.ppermute(block, axis, list(enumerate(partner)))
+    return outcome[0], outcome[1]
 
 
 def shards(
@@ -708,7 +706,7 @@
     face_y = shape(SLOTS, planes, length)
     face_x = shape(SLOTS, rows, length)
     pin = lambda block: pltpu.with_memory_space_constraint(block, hbm)
-    c1, fixed, near, far = call(
+    c1, fixed, far, near = call(
         first_kernel,
         (whole, shape(2, planes, rows, length), face_x, face_x),
         (pin(populations), pin(relaxation), pin(node_flags)),
@@ -722,7 +720,7 @@
         micros=1.5,
     )
     near_x, far_x = swap(near, far, "slab")
-    near, far = call(
+    far, near = call(
         side_kernel, (face_y, face_y), (c1, fixed, next_nodes), (vmem,) * 3, micros=0.3
     )
     near_y, far_y = swap(near, far, "inner")
@@ -739,23 +737,31 @@
         ),
         micros=2.0,
     )
-    own, other = call(
-        spread_kernel,
-        (shape(3, node_blocks, BLK), shape(3, node_blocks // half, length)),
+    nodal = shape(3, node_blocks // half, length)
+    (other,) = call(
+        functools.partial(spread_kernel, node_blocks),
+        (nodal,),
         (low_ids, high_ids, forces),
         (vmem,) * 3,
-        micros=3.0,
+        micros=0.8,
     )
     corner = shape(CORNER_SLOTS, rows, length)
-    near, far = call(
+    far, near = call(
         corner_kernel,
         (corner, corner),
-        (near_y, far_y, other),
+        (far_y, near_y, other),
         (vmem,) * 3,
         scratch=(pltpu.VMEM((2, SLOTS, planes, length), F32),),
         micros=0.3,
     )
     near_c, far_c = swap(near, far, "slab")
+    (own,) = call(
+        functools.partial(spread_kernel, 0),
+        (nodal,),
+        (low_ids, high_ids, forces),
+        (vmem,) * 3,
+        micros=0.8,
+    )
     wide = planes + 4
     walls_shape = shape(2, SLOTS, wide, length)
     second_shape = shape(Q, planes + 2, rows, length)
@@ -768,7 +774,7 @@
             second_shape,
             shape(2, 2, rows, length),
         ),
-        (c1, fixed, near_y, far_y, near_x, far_x),
+        (c1, fixed, far_y, near_y, far_x, near_x),
         (vmem,) * 6,
         scratch=(
             pltpu.VMEM((2, SLOTS, planes, length), F32),
@@ -785,8 +791,8 @@
             pin(block_target),
             pin(block_node),
             block_count,
+            far_c,
             near_c,
-            far_c,
             fixed,
             extended,
             crossing,

time: 30.5 us -> 31.1 us (1.020)
  the two profiles are of different devices: /device:TPU:6 before, /device:TPU:0 now
where the time goes in v5:
time: 31.1 us; the launch traced here: 30.9 us
  starting transfers between devices  17.3 us (56%)
  Pallas kernels  10.1 us (32%)
  waiting for transfers between devices  2.06 us (7%)
  between operations  1.45 us (5%)
    ppermute x6, starting transfers between devices, swap(): outcome[start] = lax.ppermute(block, axis, list(enumerate(partner)))  10.4 us
    pallas_call x10, Pallas kernels, call(): pl.pallas_call(kernel, out_shape=outs, in_specs=[spec(space) for space in...  10.1 us
    ppermute x3, starting transfers between devices, exchange(): lax.ppermute(block, axis, [(partner_of(i, step, count), i) for i in range...  4.45 us
    ppermute x1, starting transfers between devices, around(): lax.ppermute(block, axis, [(i, (i + step) % count) for i in range(count)])  2.46 us
    ppermute x3, waiting for transfers between devices, exchange(): lax.ppermute(block, axis, [(partner_of(i, step, count), i) for i in range...  2 us
  transfers between devices with their start and end apart: 10, of which 2 were waited for; matrix products, arithmetic and copies ran while one was open for 0% of the time, Pallas kernels for 27%

profile of v5, /device:TPU:0, one launch (start us, length us, event | category | flops | bytes accessed | tf_op | source)
XLA Modules:
  0.0 30.9 jit_solution(276021652436003395)
XLA Ops:
  0.6 0.0 copy-start.2
  0.6 0.0 copy-start.3
  0.7 0.0 copy-start.1
  0.7 0.0 copy-start
  0.7 2.5 %collective-permute-start = (f32[3,2048]{1,0:T(4,128)}, f32[3,2048]{1,0:T(4,128)S(1)}, u32[]{:S(2)}, u32[]{:S(2)}) collective-permute-start(f32[3,2048]{1,0:T(4,128)} %displacement.1), channel_id=1, source_target_pairs={{0,12},{4,0},{8,4},{12,8},{1,13},{5,1},{9,5},{13,9},{2,14},{6,2},{... | collective-permute-start | bytes 73736 | tf_op jit(solution)/shard_map/ppermute | solution.py:667
  3.1 1.6 %shard_map.130 = (f32[19,4,8,256]{3,2,1,0:T(8,128)S(1)}, f32[2,4,8,256]{3,2,1,0:T(8,128)S(1)}, f32[21,8,256]{2,1,0:T(8,128)S(1)}, f32[21,8,256]{2,1,0:T(8,128)S(1)}) custom-call(f32[19,4,8,256]{3,2,1,0:T(8,128)} %pops_hbm.1, f32[4,8,256]{2,1,0:T(8,128)} %rate_hbm.1, s32[4,8,256]{2,1,0:T(8,128)} %flags_hbm.1), custom_call_target="tpu_custom_call" | custom-call | bytes 5400000 | tf_op jit(solution)/shard_map/pallas_call | solution.py:640
  4.7 0.7 %collective-permute-start.5 = (f32[21,8,256]{2,1,0:T(8,128)S(1)}, f32[21,8,256]{2,1,0:T(8,128)S(1)}, u32[]{:S(2)}, u32[]{:S(2)}) collective-permute-start(f32[21,8,256]{2,1,0:T(8,128)S(1)} %get-tuple-element.32), channel_id=1, source_target_pairs={{0,0},{4,8},{8,4},{12,12},{1,1},{5,9},{9,5},{13,13},{2,2},{6,10},{... | collective-permute-start | bytes 516104 | tf_op jit(solution)/shard_map/ppermute | solution.py:677
  5.4 2.0 %collective-permute-start.6 = (f32[21,8,256]{2,1,0:T(8,128)S(1)}, f32[21,8,256]{2,1,0:T(8,128)S(1)}, u32[]{:S(2)}, u32[]{:S(2)}) collective-permute-start(f32[21,8,256]{2,1,0:T(8,128)S(1)} %get-tuple-element.33), channel_id=1, source_target_pairs={{0,4},{4,0},{8,12},{12,8},{1,5},{5,1},{9,13},{13,9},{2,6},{6,2},{1... | collective-permute-start | bytes 516104 | tf_op jit(solution)/shard_map/ppermute | solution.py:677
  7.4 0.0 collective-permute-done.next_nodes
  7.4 0.2 shard_map.131
  7.5 0.7 %collective-permute-start.1 = (f32[21,4,256]{2,1,0:T(4,128)S(1)}, f32[21,4,256]{2,1,0:T(4,128)S(1)}, u32[]{:S(2)}, u32[]{:S(2)}) collective-permute-start(f32[21,4,256]{2,1,0:T(4,128)S(1)} %get-tuple-element.25), channel_id=1, source_target_pairs={{0,0},{1,2},{2,1},{3,3},{4,4},{5,6},{6,5},{7,7},{8,8},{9,10},{10,9... | collective-permute-start | bytes 258056 | tf_op jit(solution)/shard_map/ppermute | solution.py:677
  8.2 4.5 %collective-permute-start.2 = (f32[21,4,256]{2,1,0:T(4,128)S(1)}, f32[21,4,256]{2,1,0:T(4,128)S(1)}, u32[]{:S(2)}, u32[]{:S(2)}) collective-permute-start(f32[21,4,256]{2,1,0:T(4,128)S(1)} %get-tuple-element.26), channel_id=1, source_target_pairs={{0,1},{1,0},{2,3},{3,2},{4,5},{5,4},{6,7},{7,6},{8,9},{9,8},{10,11... | collective-permute-start | bytes 258056 | tf_op jit(solution)/shard_map/ppermute | solution.py:677
  12.7 0.0 copy-done.2
  12.7 0.0 copy-done.3
  12.7 0.0 copy-done.1
  12.7 0.0 copy-done
  12.7 2.9 %shard_map.132 = (f32[3,32,128]{2,1,0:T(8,128)S(1)}, f32[3,32,128]{2,1,0:T(8,128)S(1)}, f32[6,3,32,128]{3,2,1,0:T(8,128)S(1)}) custom-call(s32[3,4096]{1,0:T(4,128)S(1)} %copy-done, f32[3,2048]{1,0:T(4,128)S(1)} %copy-done.2, f32[3,2048]{1,0:T(4,128)S(1)} %collective-permute-done.next_nodes, f32[3,4096]{1,0:T(4,128)S(1)} %copy-done.1, f32[32,128]{1,0:T(8,128)S(1)} %bitcast.4), custom_call_target="tpu_custom_call" | custom-call | bytes 7200000 | tf_op jit(solution)/shard_map/pallas_call | solution.py:640
  15.6 1.1 %shard_map.133.other = f32[3,8,256]{2,1,0:T(8,128)S(1)} custom-call(f32[3,32,128]{2,1,0:T(8,128)S(1)} %get-tuple-element.27.low_ids, f32[3,32,128]{2,1,0:T(8,128)S(1)} %get-tuple-element.28.high_ids, f32[6,3,32,128]{3,2,1,0:T(8,128)S(1)} %get-tuple-element.29.forces), custom_call_target="tpu_custom_call" | custom-call | bytes 2880000 | tf_op jit(solution)/shard_map/pallas_call | solution.py:640
  16.7 0.0 collective-permute-done.1.far_y
  16.7 0.0 collective-permute-done.2.near_y
  16.7 0.1 shard_map.134
  16.8 0.7 %collective-permute-start.3 = (f32[9,8,256]{2,1,0:T(8,128)S(1)}, f32[9,8,256]{2,1,0:T(8,128)S(1)}, u32[]{:S(2)}, u32[]{:S(2)}) collective-permute-start(f32[9,8,256]{2,1,0:T(8,128)S(1)} %get-tuple-element.30), channel_id=1, source_target_pairs={{0,0},{4,8},{8,4},{12,12},{1,1},{5,9},{9,5},{13,13},{2,2},{6,10},{... | collective-permute-start | bytes 221192 | tf_op jit(solution)/shard_map/ppermute | solution.py:677
  17.5 2.0 %collective-permute-start.4 = (f32[9,8,256]{2,1,0:T(8,128)S(1)}, f32[9,8,256]{2,1,0:T(8,128)S(1)}, u32[]{:S(2)}, u32[]{:S(2)}) collective-permute-start(f32[9,8,256]{2,1,0:T(8,128)S(1)} %get-tuple-element.31), channel_id=1, source_target_pairs={{0,4},{4,0},{8,12},{12,8},{1,5},{5,1},{9,13},{13,9},{2,6},{6,2},{1... | collective-permute-start | bytes 221192 | tf_op jit(solution)/shard_map/ppermute | solution.py:677
  20.1 1.1 %shard_map.136.internal_own = f32[3,8,256]{2,1,0:T(8,128)S(1)} custom-call(f32[3,32,128]{2,1,0:T(8,128)S(1)} %get-tuple-element.27.low_ids, f32[3,32,128]{2,1,0:T(8,128)S(1)} %get-tuple-element.28.high_ids, f32[6,3,32,128]{3,2,1,0:T(8,128)S(1)} %get-tuple-element.29.forces), custom_call_target="tpu_custom_call" | custom-call | bytes 2880000 | tf_op jit(solution)/shard_map/pallas_call | solution.py:640
  21.2 0.0 collective-permute-done.5.far_x
  21.2 0.0 collective-permute-done.6.near_x
  21.2 0.5 %shard_map.135 = (f32[19,8,8,256]{3,2,1,0:T(8,128)S(1)}, f32[2,21,8,256]{3,2,1,0:T(8,128)S(1)}, f32[2,5,8,256]{3,2,1,0:T(8,128)S(1)}, f32[19,6,8,256]{3,2,1,0:T(8,128)S(1)}, f32[2,2,8,256]{3,2,1,0:T(8,128)S(1)}) custom-call(f32[19,4,8,256]{3,2,1,0:T(8,128)S(1)} %get-tuple-element.23.c1, f32[2,4,8,256]{3,2,1,0:T(8,128)S(1)} %get-tuple-element.24.fixed, ...), custom_call_target="tpu_custom_call" | custom-call | bytes 2880000 | tf_op jit(solution)/shard_map/pallas_call | solution.py:640
  21.7 0.0 collective-permute-done.3.far
  21.7 0.0 collective-permute-done.4.near
  21.7 1.1 %shard_map.137 = (f32[19,4,8,256]{3,2,1,0:T(8,128)S(1)}, f32[80,128]{1,0:T(8,128)S(1)}, f32[2,21,8,256]{3,2,1,0:T(8,128)S(1)}, f32[19,6,8,256]{3,2,1,0:T(8,128)S(1)}) custom-call(s32[1,1,8]{2,1,0:T(1,128)} %block_source_hbm.1, s32[1,1,8]{2,1,0:T(1,128)} %block_target_hbm.1, ...), custom_call_target="tpu_custom_call", output_to_operand_aliasing={{2}: (11, {}), {3}: (12, {})} | custom-call | bytes 5400000 | tf_op jit(solution)/shard_map/pallas_call | solution.py:640
  22.8 1.4 %collective-permute-start.9 = (f32[80,128]{1,0:T(8,128)S(1)}, f32[80,128]{1,0:T(8,128)S(1)}, u32[]{:S(2)}, u32[]{:S(2)}) collective-permute-start(f32[80,128]{1,0:T(8,128)S(1)} %get-tuple-element.40.refs_0_), channel_id=1, source_target_pairs={{3,0},{2,1},{1,2},{0,3},{7,4},{6,5},{5,6},{4,7},{11,8},{10,9},{9,1... | collective-permute-start | bytes 122888 | tf_op jit(solution)/shard_map/ppermute | solution.py:662
  24.3 0.7 %collective-permute-start.8 = (f32[80,128]{1,0:T(8,128)S(1)}, f32[80,128]{1,0:T(8,128)S(1)}, u32[]{:S(2)}, u32[]{:S(2)}) collective-permute-start(f32[80,128]{1,0:T(8,128)S(1)} %get-tuple-element.40.refs_0_), channel_id=1, source_target_pairs={{2,0},{3,1},{0,2},{1,3},{6,4},{7,5},{4,6},{5,7},{10,8},{11,9},{8,1... | collective-permute-start | bytes 122888 | tf_op jit(solution)/shard_map/ppermute | solution.py:662
  25.0 2.3 %collective-permute-start.7 = (f32[80,128]{1,0:T(8,128)S(1)}, f32[80,128]{1,0:T(8,128)S(1)}, u32[]{:S(2)}, u32[]{:S(2)}) collective-permute-start(f32[80,128]{1,0:T(8,128)S(1)} %get-tuple-element.40.refs_0_), channel_id=1, source_target_pairs={{1,0},{0,1},{3,2},{2,3},{5,4},{4,5},{7,6},{6,7},{9,8},{8,9},{11,10... | collective-permute-start | bytes 122888 | tf_op jit(solution)/shard_map/ppermute | solution.py:662
  27.3 0.8 %shard_map.138 = f32[19,4,8,256]{3,2,1,0:T(8,128)} custom-call(f32[19,4,8,256]{3,2,1,0:T(8,128)S(1)} %get-tuple-element.39.values), custom_call_target="tpu_custom_call" | custom-call | bytes 3600000 | tf_op jit(solution)/shard_map/pallas_call | solution.py:640
  28.1 0.8 %collective-permute-done.9.refs_3_ = f32[80,128]{1,0:T(8,128)S(1)} collective-permute-done((f32[80,128]{1,0:T(8,128)S(1)}, f32[80,128]{1,0:T(8,128)S(1)}, u32[]{:S(2)}, u32[]{:S(2)}) %collective-permute-start.9) | collective-permute-done | bytes 40992 | tf_op jit(solution)/shard_map/ppermute | solution.py:662
  28.9 1.2 %collective-permute-done.8.refs_2_ = f32[80,128]{1,0:T(8,128)S(1)} collective-permute-done((f32[80,128]{1,0:T(8,128)S(1)}, f32[80,128]{1,0:T(8,128)S(1)}, u32[]{:S(2)}, u32[]{:S(2)}) %collective-permute-start.8) | collective-permute-done | bytes 40992 | tf_op jit(solution)/shard_map/ppermute | solution.py:662
  30.1 0.0 collective-permute-done.7.refs_1_
  30.1 0.8 %shard_map.139 = (f32[3,2048]{1,0:T(4,128)}, f32[3,8,128]{2,1,0:T(8,128)}) custom-call(f32[80,128]{1,0:T(8,128)S(1)} %get-tuple-element.40.refs_0_, f32[80,128]{1,0:T(8,128)S(1)} %collective-permute-done.7.refs_1_, f32[80,128]{1,0:T(8,128)S(1)} %collective-permute-done.8.refs_2_, f32[80,128]{1,0:T(8,128)S(1)} %collective-permute-done.9.refs_3_), custom_call_target="tpu_custom_call" | custom-call | bytes 2880000 | tf_op jit(solution)/shard_map/pallas_call | solution.py:640
Async XLA Ops:
  0.6 12.0 %copy-start.2 = (f32[3,2048]{1,0:T(4,128)S(1)}, f32[3,2048]{1,0:T(4,128)}, u32[]{:S(2)}) copy-start(f32[3,2048]{1,0:T(4,128)} %displacement.1) | copy-start | bytes 73732
  0.6 12.0 %copy-start.3 = (f32[4096]{0:T(1024)S(1)}, f32[4096]{0:T(1024)}, u32[]{:S(2)}) copy-start(f32[4096]{0:T(1024)} %param.17) | copy-start | bytes 49156
  0.7 12.0 %copy-start.1 = (f32[3,4096]{1,0:T(4,128)S(1)}, f32[3,4096]{1,0:T(4,128)}, u32[]{:S(2)}) copy-start(f32[3,4096]{1,0:T(4,128)} %shape_inverse.1) | copy-start | bytes 147460
  0.7 12.0 %copy-start = (s32[3,4096]{1,0:T(4,128)S(1)}, s32[3,4096]{1,0:T(4,128)}, u32[]{:S(2)}) copy-start(s32[3,4096]{1,0:T(4,128)} %elements.1) | copy-start | bytes 147460
  0.7 6.7 %collective-permute-start = (f32[3,2048]{1,0:T(4,128)}, f32[3,2048]{1,0:T(4,128)S(1)}, u32[]{:S(2)}, u32[]{:S(2)}) collective-permute-start(f32[3,2048]{1,0:T(4,128)} %displacement.1), channel_id=1, source_target_pairs={{0,12},{4,0},{8,4},{12,8},{1,13},{5,1},{9,5},{13,9},{2,14},{6,2},{... | collective-permute-start | bytes 73736 | tf_op jit(solution)/shard_map/ppermute | solution.py:667
  4.7 16.5 %collective-permute-start.5 = (f32[21,8,256]{2,1,0:T(8,128)S(1)}, f32[21,8,256]{2,1,0:T(8,128)S(1)}, u32[]{:S(2)}, u32[]{:S(2)}) collective-permute-start(f32[21,8,256]{2,1,0:T(8,128)S(1)} %get-tuple-element.32), channel_id=1, source_target_pairs={{0,0},{4,8},{8,4},{12,12},{1,1},{5,9},{9,5},{13,13},{2,2},{6,10},{... | collective-permute-start | bytes 516104 | tf_op jit(solution)/shard_map/ppermute | solution.py:677
  5.4 15.8 %collective-permute-start.6 = (f32[21,8,256]{2,1,0:T(8,128)S(1)}, f32[21,8,256]{2,1,0:T(8,128)S(1)}, u32[]{:S(2)}, u32[]{:S(2)}) collective-permute-start(f32[21,8,256]{2,1,0:T(8,128)S(1)} %get-tuple-element.33), channel_id=1, source_target_pairs={{0,4},{4,0},{8,12},{12,8},{1,5},{5,1},{9,13},{13,9},{2,6},{6,2},{1... | collective-permute-start | bytes 516104 | tf_op jit(solution)/shard_map/ppermute | solution.py:677
  7.5 9.1 %collective-permute-start.1 = (f32[21,4,256]{2,1,0:T(4,128)S(1)}, f32[21,4,256]{2,1,0:T(4,128)S(1)}, u32[]{:S(2)}, u32[]{:S(2)}) collective-permute-start(f32[21,4,256]{2,1,0:T(4,128)S(1)} %get-tuple-element.25), channel_id=1, source_target_pairs={{0,0},{1,2},{2,1},{3,3},{4,4},{5,6},{6,5},{7,7},{8,8},{9,10},{10,9... | collective-permute-start | bytes 258056 | tf_op jit(solution)/shard_map/ppermute | solution.py:677
  8.2 8.5 %collective-permute-start.2 = (f32[21,4,256]{2,1,0:T(4,128)S(1)}, f32[21,4,256]{2,1,0:T(4,128)S(1)}, u32[]{:S(2)}, u32[]{:S(2)}) collective-permute-start(f32[21,4,256]{2,1,0:T(4,128)S(1)} %get-tuple-element.26), channel_id=1, source_target_pairs={{0,1},{1,0},{2,3},{3,2},{4,5},{5,4},{6,7},{7,6},{8,9},{9,8},{10,11... | collective-permute-start | bytes 258056 | tf_op jit(solution)/shard_map/ppermute | solution.py:677
  16.8 4.9 %collective-permute-start.3 = (f32[9,8,256]{2,1,0:T(8,128)S(1)}, f32[9,8,256]{2,1,0:T(8,128)S(1)}, u32[]{:S(2)}, u32[]{:S(2)}) collective-permute-start(f32[9,8,256]{2,1,0:T(8,128)S(1)} %get-tuple-element.30), channel_id=1, source_target_pairs={{0,0},{4,8},{8,4},{12,12},{1,1},{5,9},{9,5},{13,13},{2,2},{6,10},{... | collective-permute-start | bytes 221192 | tf_op jit(solution)/shard_map/ppermute | solution.py:677
  17.5 4.2 %collective-permute-start.4 = (f32[9,8,256]{2,1,0:T(8,128)S(1)}, f32[9,8,256]{2,1,0:T(8,128)S(1)}, u32[]{:S(2)}, u32[]{:S(2)}) collective-permute-start(f32[9,8,256]{2,1,0:T(8,128)S(1)} %get-tuple-element.31), channel_id=1, source_target_pairs={{0,4},{4,0},{8,12},{12,8},{1,5},{5,1},{9,13},{13,9},{2,6},{6,2},{1... | collective-permute-start | bytes 221192 | tf_op jit(solution)/shard_map/ppermute | solution.py:677
  22.8 6.1 %collective-permute-start.9 = (f32[80,128]{1,0:T(8,128)S(1)}, f32[80,128]{1,0:T(8,128)S(1)}, u32[]{:S(2)}, u32[]{:S(2)}) collective-permute-start(f32[80,128]{1,0:T(8,128)S(1)} %get-tuple-element.40.refs_0_), channel_id=1, source_target_pairs={{3,0},{2,1},{1,2},{0,3},{7,4},{6,5},{5,6},{4,7},{11,8},{10,9},{9,1... | collective-permute-start | bytes 122888 | tf_op jit(solution)/shard_map/ppermute | solution.py:662
  24.3 5.9 %collective-permute-start.8 = (f32[80,128]{1,0:T(8,128)S(1)}, f32[80,128]{1,0:T(8,128)S(1)}, u32[]{:S(2)}, u32[]{:S(2)}) collective-permute-start(f32[80,128]{1,0:T(8,128)S(1)} %get-tuple-element.40.refs_0_), channel_id=1, source_target_pairs={{2,0},{3,1},{0,2},{1,3},{6,4},{7,5},{4,6},{5,7},{10,8},{11,9},{8,1... | collective-permute-start | bytes 122888 | tf_op jit(solution)/shard_map/ppermute | solution.py:662
  25.0 5.2 %collective-permute-start.7 = (f32[80,128]{1,0:T(8,128)S(1)}, f32[80,128]{1,0:T(8,128)S(1)}, u32[]{:S(2)}, u32[]{:S(2)}) collective-permute-start(f32[80,128]{1,0:T(8,128)S(1)} %get-tuple-element.40.refs_0_), channel_id=1, source_target_pairs={{1,0},{0,1},{3,2},{2,3},{5,4},{4,5},{7,6},{6,7},{9,8},{8,9},{11,10... | collective-permute-start | bytes 122888 | tf_op jit(solution)/shard_map/ppermute | solution.py:662

commit v6 on v5

--- a/solution.py
+++ b/solution.py
@@ -672,8 +672,9 @@
     outcome = {}
     for block, start in ((far, 1), (near, 0)):
         partner = list(range(count))
-        for i in range(start, count - 1, 2):
-            partner[i], partner[i + 1] = i + 1, i
+        for i in range(start, start + count - count % 2, 2):
+            one, two = i % count, (i + 1) % count
+            partner[one], partner[two] = two, one
         outcome[start] = lax.ppermute(block, axis, list(enumerate(partner)))
     return outcome[0], outcome[1]
 

time: 31.1 us -> 29 us (0.932)
  starting transfers between devices: 17.3 us -> 12.7 us
  waiting for transfers between devices: 2.06 us -> 4.68 us
    ppermute x6, starting transfers between devices: 10.4 us -> 5.78 us  [swap(): outcome[start] = lax.ppermute(block, axis, list(enumerate(partner)))]
    ppermute x6, waiting for transfers between devices: 0.06 us -> 2.13 us  [swap(): outcome[start] = lax.ppermute(block, axis, list(enumerate(partner)))]
    ppermute x3, waiting for transfers between devices: 2 us -> 2.54 us  [exchange(): lax.ppermute(block, axis, [(partner_of(i, step, count), i) for i in range...]
  transfers between devices with their start and end apart: 10 -> 10, of which waited for: 2 -> 5; matrix products, arithmetic and copies ran while one was open for 0% -> 0% of each run, Pallas kernels for 27% -> 28%
where the time goes in v6:
time: 29 us; the launch traced here: 28.9 us
  starting transfers between devices  12.7 us (44%)
  Pallas kernels  10.1 us (35%)
  waiting for transfers between devices  4.68 us (16%)
  between operations  1.42 us (5%)
    pallas_call x10, Pallas kernels, call(): pl.pallas_call(kernel, out_shape=outs, in_specs=[spec(space) for space in...  10.1 us
    ppermute x6, starting transfers between devices, swap(): outcome[start] = lax.ppermute(block, axis, list(enumerate(partner)))  5.78 us
    ppermute x3, starting transfers between devices, exchange(): lax.ppermute(block, axis, [(partner_of(i, step, count), i) for i in range...  4.45 us
    ppermute x3, waiting for transfers between devices, exchange(): lax.ppermute(block, axis, [(partner_of(i, step, count), i) for i in range...  2.54 us
    ppermute x1, starting transfers between devices, around(): lax.ppermute(block, axis, [(i, (i + step) % count) for i in range(count)])  2.46 us
    ppermute x6, waiting for transfers between devices, swap(): outcome[start] = lax.ppermute(block, axis, list(enumerate(partner)))  2.13 us
  transfers between devices with their start and end apart: 10, of which 5 were waited for; matrix products, arithmetic and copies ran while one was open for 0% of the time, Pallas kernels for 28%

profile of v6, /device:TPU:0, one launch (start us, length us, event | category | flops | bytes accessed | tf_op | source)
XLA Modules:
  0.0 28.9 jit_solution(7125900045950223568)
XLA Ops:
  0.6 0.0 copy-start.2
  0.6 0.0 copy-start.3
  0.7 0.0 copy-start.1
  0.7 0.0 copy-start
  0.7 2.5 %collective-permute-start = (f32[3,2048]{1,0:T(4,128)}, f32[3,2048]{1,0:T(4,128)S(1)}, u32[]{:S(2)}, u32[]{:S(2)}) collective-permute-start(f32[3,2048]{1,0:T(4,128)} %displacement.1), channel_id=1, source_target_pairs={{0,12},{4,0},{8,4},{12,8},{1,13},{5,1},{9,5},{13,9},{2,14},{6,2},{... | collective-permute-start | bytes 73736 | tf_op jit(solution)/shard_map/ppermute | solution.py:667
  3.1 1.6 %shard_map.130 = (f32[19,4,8,256]{3,2,1,0:T(8,128)S(1)}, f32[2,4,8,256]{3,2,1,0:T(8,128)S(1)}, f32[21,8,256]{2,1,0:T(8,128)S(1)}, f32[21,8,256]{2,1,0:T(8,128)S(1)}) custom-call(f32[19,4,8,256]{3,2,1,0:T(8,128)} %pops_hbm.1, f32[4,8,256]{2,1,0:T(8,128)} %rate_hbm.1, s32[4,8,256]{2,1,0:T(8,128)} %flags_hbm.1), custom_call_target="tpu_custom_call" | custom-call | bytes 5400000 | tf_op jit(solution)/shard_map/pallas_call | solution.py:640
  4.7 0.7 %collective-permute-start.5 = (f32[21,8,256]{2,1,0:T(8,128)S(1)}, f32[21,8,256]{2,1,0:T(8,128)S(1)}, u32[]{:S(2)}, u32[]{:S(2)}) collective-permute-start(f32[21,8,256]{2,1,0:T(8,128)S(1)} %get-tuple-element.32), channel_id=1, source_target_pairs={{0,12},{4,8},{8,4},{12,0},{1,13},{5,9},{9,5},{13,1},{2,14},{6,10},... | collective-permute-start | bytes 516104 | tf_op jit(solution)/shard_map/ppermute | solution.py:678
  5.5 0.0 collective-permute-start.6
  5.5 0.0 collective-permute-done.next_nodes
  5.5 0.2 shard_map.131
  5.6 3.7 %collective-permute-start.1 = (f32[21,4,256]{2,1,0:T(4,128)S(1)}, f32[21,4,256]{2,1,0:T(4,128)S(1)}, u32[]{:S(2)}, u32[]{:S(2)}) collective-permute-start(f32[21,4,256]{2,1,0:T(4,128)S(1)} %get-tuple-element.25), channel_id=1, source_target_pairs={{0,3},{1,2},{2,1},{3,0},{4,7},{5,6},{6,5},{7,4},{8,11},{9,10},{10,... | collective-permute-start | bytes 258056 | tf_op jit(solution)/shard_map/ppermute | solution.py:678
  9.3 0.0 collective-permute-start.2
  9.3 0.0 copy-done.2
  9.3 0.0 copy-done.3
  9.3 0.0 copy-done.1
  9.3 0.0 copy-done
  9.3 2.9 %shard_map.132 = (f32[3,32,128]{2,1,0:T(8,128)S(1)}, f32[3,32,128]{2,1,0:T(8,128)S(1)}, f32[6,3,32,128]{3,2,1,0:T(8,128)S(1)}) custom-call(s32[3,4096]{1,0:T(4,128)S(1)} %copy-done, f32[3,2048]{1,0:T(4,128)S(1)} %copy-done.2, f32[3,2048]{1,0:T(4,128)S(1)} %collective-permute-done.next_nodes, f32[3,4096]{1,0:T(4,128)S(1)} %copy-done.1, f32[32,128]{1,0:T(8,128)S(1)} %bitcast.4), custom_call_target="tpu_custom_call" | custom-call | bytes 7200000 | tf_op jit(solution)/shard_map/pallas_call | solution.py:640
  12.2 1.1 %shard_map.133.other = f32[3,8,256]{2,1,0:T(8,128)S(1)} custom-call(f32[3,32,128]{2,1,0:T(8,128)S(1)} %get-tuple-element.27.low_ids, f32[3,32,128]{2,1,0:T(8,128)S(1)} %get-tuple-element.28.high_ids, f32[6,3,32,128]{3,2,1,0:T(8,128)S(1)} %get-tuple-element.29.forces), custom_call_target="tpu_custom_call" | custom-call | bytes 2880000 | tf_op jit(solution)/shard_map/pallas_call | solution.py:640
  13.3 0.0 collective-permute-done.1.far_y
  13.3 1.1 %collective-permute-done.2.near_y = f32[21,4,256]{2,1,0:T(4,128)S(1)} collective-permute-done((f32[21,4,256]{2,1,0:T(4,128)S(1)}, f32[21,4,256]{2,1,0:T(4,128)S(1)}, u32[]{:S(2)}, u32[]{:S(2)}) %collective-permute-start.2) | collective-permute-done | bytes 86048 | tf_op jit(solution)/shard_map/ppermute | solution.py:678
  14.4 0.1 shard_map.134
  14.5 0.4 %collective-permute-start.3 = (f32[9,8,256]{2,1,0:T(8,128)S(1)}, f32[9,8,256]{2,1,0:T(8,128)S(1)}, u32[]{:S(2)}, u32[]{:S(2)}) collective-permute-start(f32[9,8,256]{2,1,0:T(8,128)S(1)} %get-tuple-element.30), channel_id=1, source_target_pairs={{0,12},{4,8},{8,4},{12,0},{1,13},{5,9},{9,5},{13,1},{2,14},{6,10},... | collective-permute-start | bytes 221192 | tf_op jit(solution)/shard_map/ppermute | solution.py:678
  14.9 1.0 %collective-permute-start.4 = (f32[9,8,256]{2,1,0:T(8,128)S(1)}, f32[9,8,256]{2,1,0:T(8,128)S(1)}, u32[]{:S(2)}, u32[]{:S(2)}) collective-permute-start(f32[9,8,256]{2,1,0:T(8,128)S(1)} %get-tuple-element.31), channel_id=1, source_target_pairs={{0,4},{4,0},{8,12},{12,8},{1,5},{5,1},{9,13},{13,9},{2,6},{6,2},{1... | collective-permute-start | bytes 221192 | tf_op jit(solution)/shard_map/ppermute | solution.py:678
  16.6 1.1 %shard_map.136.internal_own = f32[3,8,256]{2,1,0:T(8,128)S(1)} custom-call(f32[3,32,128]{2,1,0:T(8,128)S(1)} %get-tuple-element.27.low_ids, f32[3,32,128]{2,1,0:T(8,128)S(1)} %get-tuple-element.28.high_ids, f32[6,3,32,128]{3,2,1,0:T(8,128)S(1)} %get-tuple-element.29.forces), custom_call_target="tpu_custom_call" | custom-call | bytes 2880000 | tf_op jit(solution)/shard_map/pallas_call | solution.py:640
  17.6 0.0 collective-permute-done.5.far_x
  17.7 0.0 collective-permute-done.6.near_x
  17.7 0.5 %shard_map.135 = (f32[19,8,8,256]{3,2,1,0:T(8,128)S(1)}, f32[2,21,8,256]{3,2,1,0:T(8,128)S(1)}, f32[2,5,8,256]{3,2,1,0:T(8,128)S(1)}, f32[19,6,8,256]{3,2,1,0:T(8,128)S(1)}, f32[2,2,8,256]{3,2,1,0:T(8,128)S(1)}) custom-call(f32[19,4,8,256]{3,2,1,0:T(8,128)S(1)} %get-tuple-element.23.c1, f32[2,4,8,256]{3,2,1,0:T(8,128)S(1)} %get-tuple-element.24.fixed, ...), custom_call_target="tpu_custom_call" | custom-call | bytes 2880000 | tf_op jit(solution)/shard_map/pallas_call | solution.py:640
  18.2 1.0 %collective-permute-done.3.far = f32[9,8,256]{2,1,0:T(8,128)S(1)} collective-permute-done((f32[9,8,256]{2,1,0:T(8,128)S(1)}, f32[9,8,256]{2,1,0:T(8,128)S(1)}, u32[]{:S(2)}, u32[]{:S(2)}) %collective-permute-start.3) | collective-permute-done | bytes 73760 | tf_op jit(solution)/shard_map/ppermute | solution.py:678
  19.1 0.0 collective-permute-done.4.near
  19.1 1.1 %shard_map.137 = (f32[19,4,8,256]{3,2,1,0:T(8,128)S(1)}, f32[80,128]{1,0:T(8,128)S(1)}, f32[2,21,8,256]{3,2,1,0:T(8,128)S(1)}, f32[19,6,8,256]{3,2,1,0:T(8,128)S(1)}) custom-call(s32[1,1,8]{2,1,0:T(1,128)} %block_source_hbm.1, s32[1,1,8]{2,1,0:T(1,128)} %block_target_hbm.1, ...), custom_call_target="tpu_custom_call", output_to_operand_aliasing={{2}: (11, {}), {3}: (12, {})} | custom-call | bytes 5400000 | tf_op jit(solution)/shard_map/pallas_call | solution.py:640
  20.2 2.0 %collective-permute-start.9 = (f32[80,128]{1,0:T(8,128)S(1)}, f32[80,128]{1,0:T(8,128)S(1)}, u32[]{:S(2)}, u32[]{:S(2)}) collective-permute-start(f32[80,128]{1,0:T(8,128)S(1)} %get-tuple-element.40.refs_0_), channel_id=1, source_target_pairs={{3,0},{2,1},{1,2},{0,3},{7,4},{6,5},{5,6},{4,7},{11,8},{10,9},{9,1... | collective-permute-start | bytes 122888 | tf_op jit(solution)/shard_map/ppermute | solution.py:662
  22.2 1.1 %collective-permute-start.8 = (f32[80,128]{1,0:T(8,128)S(1)}, f32[80,128]{1,0:T(8,128)S(1)}, u32[]{:S(2)}, u32[]{:S(2)}) collective-permute-start(f32[80,128]{1,0:T(8,128)S(1)} %get-tuple-element.40.refs_0_), channel_id=1, source_target_pairs={{2,0},{3,1},{0,2},{1,3},{6,4},{7,5},{4,6},{5,7},{10,8},{11,9},{8,1... | collective-permute-start | bytes 122888 | tf_op jit(solution)/shard_map/ppermute | solution.py:662
  23.3 1.4 %collective-permute-start.7 = (f32[80,128]{1,0:T(8,128)S(1)}, f32[80,128]{1,0:T(8,128)S(1)}, u32[]{:S(2)}, u32[]{:S(2)}) collective-permute-start(f32[80,128]{1,0:T(8,128)S(1)} %get-tuple-element.40.refs_0_), channel_id=1, source_target_pairs={{1,0},{0,1},{3,2},{2,3},{5,4},{4,5},{7,6},{6,7},{9,8},{8,9},{11,10... | collective-permute-start | bytes 122888 | tf_op jit(solution)/shard_map/ppermute | solution.py:662
  24.7 0.8 %shard_map.138 = f32[19,4,8,256]{3,2,1,0:T(8,128)} custom-call(f32[19,4,8,256]{3,2,1,0:T(8,128)S(1)} %get-tuple-element.39.values), custom_call_target="tpu_custom_call" | custom-call | bytes 3600000 | tf_op jit(solution)/shard_map/pallas_call | solution.py:640
  25.5 0.7 %collective-permute-done.9.refs_3_ = f32[80,128]{1,0:T(8,128)S(1)} collective-permute-done((f32[80,128]{1,0:T(8,128)S(1)}, f32[80,128]{1,0:T(8,128)S(1)}, u32[]{:S(2)}, u32[]{:S(2)}) %collective-permute-start.9) | collective-permute-done | bytes 40992 | tf_op jit(solution)/shard_map/ppermute | solution.py:662
  26.3 1.7 %collective-permute-done.8.refs_2_ = f32[80,128]{1,0:T(8,128)S(1)} collective-permute-done((f32[80,128]{1,0:T(8,128)S(1)}, f32[80,128]{1,0:T(8,128)S(1)}, u32[]{:S(2)}, u32[]{:S(2)}) %collective-permute-start.8) | collective-permute-done | bytes 40992 | tf_op jit(solution)/shard_map/ppermute | solution.py:662
  27.9 0.1 collective-permute-done.7.refs_1_
  28.1 0.8 %shard_map.139 = (f32[3,2048]{1,0:T(4,128)}, f32[3,8,128]{2,1,0:T(8,128)}) custom-call(f32[80,128]{1,0:T(8,128)S(1)} %get-tuple-element.40.refs_0_, f32[80,128]{1,0:T(8,128)S(1)} %collective-permute-done.7.refs_1_, f32[80,128]{1,0:T(8,128)S(1)} %collective-permute-done.8.refs_2_, f32[80,128]{1,0:T(8,128)S(1)} %collective-permute-done.9.refs_3_), custom_call_target="tpu_custom_call" | custom-call | bytes 2880000 | tf_op jit(solution)/shard_map/pallas_call | solution.py:640
Async XLA Ops:
  0.6 8.7 %copy-start.2 = (f32[3,2048]{1,0:T(4,128)S(1)}, f32[3,2048]{1,0:T(4,128)}, u32[]{:S(2)}) copy-start(f32[3,2048]{1,0:T(4,128)} %displacement.1) | copy-start | bytes 73732
  0.6 8.7 %copy-start.3 = (f32[4096]{0:T(1024)S(1)}, f32[4096]{0:T(1024)}, u32[]{:S(2)}) copy-start(f32[4096]{0:T(1024)} %param.17) | copy-start | bytes 49156
  0.7 8.6 %copy-start.1 = (f32[3,4096]{1,0:T(4,128)S(1)}, f32[3,4096]{1,0:T(4,128)}, u32[]{:S(2)}) copy-start(f32[3,4096]{1,0:T(4,128)} %shape_inverse.1) | copy-start | bytes 147460
  0.7 8.6 %copy-start = (s32[3,4096]{1,0:T(4,128)S(1)}, s32[3,4096]{1,0:T(4,128)}, u32[]{:S(2)}) copy-start(s32[3,4096]{1,0:T(4,128)} %elements.1) | copy-start | bytes 147460
  0.7 4.8 %collective-permute-start = (f32[3,2048]{1,0:T(4,128)}, f32[3,2048]{1,0:T(4,128)S(1)}, u32[]{:S(2)}, u32[]{:S(2)}) collective-permute-start(f32[3,2048]{1,0:T(4,128)} %displacement.1), channel_id=1, source_target_pairs={{0,12},{4,0},{8,4},{12,8},{1,13},{5,1},{9,5},{13,9},{2,14},{6,2},{... | collective-permute-start | bytes 73736 | tf_op jit(solution)/shard_map/ppermute | solution.py:667
  4.7 13.0 %collective-permute-start.5 = (f32[21,8,256]{2,1,0:T(8,128)S(1)}, f32[21,8,256]{2,1,0:T(8,128)S(1)}, u32[]{:S(2)}, u32[]{:S(2)}) collective-permute-start(f32[21,8,256]{2,1,0:T(8,128)S(1)} %get-tuple-element.32), channel_id=1, source_target_pairs={{0,12},{4,8},{8,4},{12,0},{1,13},{5,9},{9,5},{13,1},{2,14},{6,10},... | collective-permute-start | bytes 516104 | tf_op jit(solution)/shard_map/ppermute | solution.py:678
  5.5 12.2 %collective-permute-start.6 = (f32[21,8,256]{2,1,0:T(8,128)S(1)}, f32[21,8,256]{2,1,0:T(8,128)S(1)}, u32[]{:S(2)}, u32[]{:S(2)}) collective-permute-start(f32[21,8,256]{2,1,0:T(8,128)S(1)} %get-tuple-element.33), channel_id=1, source_target_pairs={{0,4},{4,0},{8,12},{12,8},{1,5},{5,1},{9,13},{13,9},{2,6},{6,2},{1... | collective-permute-start | bytes 516104 | tf_op jit(solution)/shard_map/ppermute | solution.py:678
  5.6 7.7 %collective-permute-start.1 = (f32[21,4,256]{2,1,0:T(4,128)S(1)}, f32[21,4,256]{2,1,0:T(4,128)S(1)}, u32[]{:S(2)}, u32[]{:S(2)}) collective-permute-start(f32[21,4,256]{2,1,0:T(4,128)S(1)} %get-tuple-element.25), channel_id=1, source_target_pairs={{0,3},{1,2},{2,1},{3,0},{4,7},{5,6},{6,5},{7,4},{8,11},{9,10},{10,... | collective-permute-start | bytes 258056 | tf_op jit(solution)/shard_map/ppermute | solution.py:678
  9.3 5.1 %collective-permute-start.2 = (f32[21,4,256]{2,1,0:T(4,128)S(1)}, f32[21,4,256]{2,1,0:T(4,128)S(1)}, u32[]{:S(2)}, u32[]{:S(2)}) collective-permute-start(f32[21,4,256]{2,1,0:T(4,128)S(1)} %get-tuple-element.26), channel_id=1, source_target_pairs={{0,1},{1,0},{2,3},{3,2},{4,5},{5,4},{6,7},{7,6},{8,9},{9,8},{10,11... | collective-permute-start | bytes 258056 | tf_op jit(solution)/shard_map/ppermute | solution.py:678
  14.5 4.6 %collective-permute-start.3 = (f32[9,8,256]{2,1,0:T(8,128)S(1)}, f32[9,8,256]{2,1,0:T(8,128)S(1)}, u32[]{:S(2)}, u32[]{:S(2)}) collective-permute-start(f32[9,8,256]{2,1,0:T(8,128)S(1)} %get-tuple-element.30), channel_id=1, source_target_pairs={{0,12},{4,8},{8,4},{12,0},{1,13},{5,9},{9,5},{13,1},{2,14},{6,10},... | collective-permute-start | bytes 221192 | tf_op jit(solution)/shard_map/ppermute | solution.py:678
  14.9 4.2 %collective-permute-start.4 = (f32[9,8,256]{2,1,0:T(8,128)S(1)}, f32[9,8,256]{2,1,0:T(8,128)S(1)}, u32[]{:S(2)}, u32[]{:S(2)}) collective-permute-start(f32[9,8,256]{2,1,0:T(8,128)S(1)} %get-tuple-element.31), channel_id=1, source_target_pairs={{0,4},{4,0},{8,12},{12,8},{1,5},{5,1},{9,13},{13,9},{2,6},{6,2},{1... | collective-permute-start | bytes 221192 | tf_op jit(solution)/shard_map/ppermute | solution.py:678
  20.2 6.0 %collective-permute-start.9 = (f32[80,128]{1,0:T(8,128)S(1)}, f32[80,128]{1,0:T(8,128)S(1)}, u32[]{:S(2)}, u32[]{:S(2)}) collective-permute-start(f32[80,128]{1,0:T(8,128)S(1)} %get-tuple-element.40.refs_0_), channel_id=1, source_target_pairs={{3,0},{2,1},{1,2},{0,3},{7,4},{6,5},{5,6},{4,7},{11,8},{10,9},{9,1... | collective-permute-start | bytes 122888 | tf_op jit(solution)/shard_map/ppermute | solution.py:662
  22.2 5.7 %collective-permute-start.8 = (f32[80,128]{1,0:T(8,128)S(1)}, f32[80,128]{1,0:T(8,128)S(1)}, u32[]{:S(2)}, u32[]{:S(2)}) collective-permute-start(f32[80,128]{1,0:T(8,128)S(1)} %get-tuple-element.40.refs_0_), channel_id=1, source_target_pairs={{2,0},{3,1},{0,2},{1,3},{6,4},{7,5},{4,6},{5,7},{10,8},{11,9},{8,1... | collective-permute-start | bytes 122888 | tf_op jit(solution)/shard_map/ppermute | solution.py:662
  23.3 4.7 %collective-permute-start.7 = (f32[80,128]{1,0:T(8,128)S(1)}, f32[80,128]{1,0:T(8,128)S(1)}, u32[]{:S(2)}, u32[]{:S(2)}) collective-permute-start(f32[80,128]{1,0:T(8,128)S(1)} %get-tuple-element.40.refs_0_), channel_id=1, source_target_pairs={{1,0},{0,1},{3,2},{2,3},{5,4},{4,5},{7,6},{6,7},{9,8},{8,9},{11,10... | collective-permute-start | bytes 122888 | tf_op jit(solution)/shard_map/ppermute | solution.py:662

commit v7 on v5

--- a/solution.py
+++ b/solution.py
@@ -486,24 +486,23 @@
         rows = pl.ds(pl.multiple_of(group * 8, 8), 8)
         low = [numbers[corner, rows] & (BLK - 1) for corner in range(3)]
         high = [numbers[corner, rows] >> 7 for corner in range(3)]
-        nodes = [[jnp.zeros((8, BLK), F32)] * 3 for _ in range(3)]
-        for block in range(2 * node_blocks):
-            source = displacement if block < node_blocks else next_nodes
-            start = (block % node_blocks) * BLK
-            table = [
-                jnp.broadcast_to(source[part : part + 1, start : start + BLK], (8, BLK))
-                for part in range(3)
-            ]
-            for corner in range(3):
+        for corner in range(3):
+            nodes = [jnp.zeros((8, BLK), F32)] * 3
+            for block in range(2 * node_blocks):
+                source = displacement if block < node_blocks else next_nodes
+                start = (block % node_blocks) * BLK
                 here = high[corner] == block
                 for part in range(3):
+                    row = source[part : part + 1, start : start + BLK]
                     picked = jnp.take_along_axis(
-                        table[part], low[corner], axis=1, mode="promise_in_bounds"
+                        jnp.broadcast_to(row, (8, BLK)),
+                        low[corner],
+                        axis=1,
+                        mode="promise_in_bounds",
                     )
-                    nodes[corner][part] = jnp.where(here, picked, nodes[corner][part])
-        for corner in range(3):
+                    nodes[part] = jnp.where(here, picked, nodes[part])
             for part in range(3):
-                corners[corner, part, rows] = nodes[corner][part]
+                corners[corner, part, rows] = nodes[part]
         return carry
 
     lax.fori_loop(0, runs // 8, gather, 0)
@@ -667,15 +666,22 @@
     return lax.ppermute(block, axis, [(i, (i + step) % count) for i in range(count)])
 
 
-def swap(near, far, axis):
-    count = lax.axis_size(axis)
-    outcome = {}
-    for block, start in ((far, 1), (near, 0)):
-        partner = list(range(count))
-        for i in range(start, count - 1, 2):
-            partner[i], partner[i + 1] = i + 1, i
-        outcome[start] = lax.ppermute(block, axis, list(enumerate(partner)))
-    return outcome[0], outcome[1]
+def swap(near, far, axis, beside):
+    count, others = lax.axis_size(axis), lax.axis_size(beside)
+    routes = []
+    for start in (0, 1):
+        route = []
+        for other in range(others):
+            for i in range(count):
+                j = i + 1 if i % 2 == start else i - 1
+                to = other
+                if not 0 <= j < count:
+                    j = i
+                    to = other ^ 1 if others % 2 == 0 else other
+                route.append((other * count + i, to * count + j))
+        routes.append(route)
+    axes = (beside, axis)
+    return lax.ppermute(near, axes, routes[0]), lax.ppermute(far, axes, routes[1])
 
 
 def shards(
@@ -719,11 +725,11 @@
         ),
         micros=1.5,
     )
-    near_x, far_x = swap(near, far, "slab")
+    near_x, far_x = swap(near, far, "slab", "group")
     far, near = call(
         side_kernel, (face_y, face_y), (c1, fixed, next_nodes), (vmem,) * 3, micros=0.3
     )
-    near_y, far_y = swap(near, far, "inner")
+    near_y, far_y = swap(near, far, "inner", "slab")
     numbers = shape(3, runs, BLK)
     low_ids, high_ids, forces = call(
         element_kernel,
@@ -754,7 +760,7 @@
         scratch=(pltpu.VMEM((2, SLOTS, planes, length), F32),),
         micros=0.3,
     )
-    near_c, far_c = swap(near, far, "slab")
+    near_c, far_c = swap(near, far, "slab", "group")
     (own,) = call(
         functools.partial(spread_kernel, 0),
         (nodal,),

time: 31.1 us -> 26.9 us (0.86)
  starting transfers between devices: 17.3 us -> 12.6 us
  waiting for transfers between devices: 2.06 us -> 3.77 us
  Pallas kernels: 10.1 us -> 8.92 us
    ppermute x6, starting transfers between devices: 10.4 us -> 5.68 us  [the longest x3 2.86 us: swap(): lax.ppermute(near, axes, routes[0])]
    ppermute x6, waiting for transfers between devices: 0.06 us -> 1.35 us  [the longest x3 1.28 us: swap(): lax.ppermute(far, axes, routes[1])]
    pallas_call x10, Pallas kernels: 10.1 us -> 8.92 us  [call(): pl.pallas_call(kernel, out_shape=outs, in_specs=[spec(space) for space in...]
    ppermute x3, waiting for transfers between devices: 2 us -> 2.42 us  [exchange(): lax.ppermute(block, axis, [(partner_of(i, step, count), i) for i in range...]
  transfers between devices with their start and end apart: 10 -> 10, of which waited for: 2 -> 5; matrix products, arithmetic and copies ran while one was open for 0% -> 0% of each run, Pallas kernels for 27% -> 26%
where the time goes in v7:
time: 26.9 us; the launch traced here: 26.7 us
  starting transfers between devices  12.6 us (47%)
  Pallas kernels  8.92 us (33%)
  waiting for transfers between devices  3.77 us (14%)
  between operations  1.41 us (5%)
    pallas_call x10, Pallas kernels, call(): pl.pallas_call(kernel, out_shape=outs, in_specs=[spec(space) for space in...  8.92 us
    ppermute x3, starting transfers between devices, exchange(): lax.ppermute(block, axis, [(partner_of(i, step, count), i) for i in range...  4.45 us
    ppermute x3, starting transfers between devices, swap(): lax.ppermute(near, axes, routes[0])  2.86 us
    ppermute x3, starting transfers between devices, swap(): lax.ppermute(far, axes, routes[1])  2.82 us
    ppermute x1, starting transfers between devices, around(): lax.ppermute(block, axis, [(i, (i + step) % count) for i in range(count)])  2.46 us
    ppermute x3, waiting for transfers between devices, exchange(): lax.ppermute(block, axis, [(partner_of(i, step, count), i) for i in range...  2.42 us
    ppermute x3, waiting for transfers between devices, swap(): lax.ppermute(far, axes, routes[1])  1.28 us
  transfers between devices with their start and end apart: 10, of which 5 were waited for; matrix products, arithmetic and copies ran while one was open for 0% of the time, Pallas kernels for 26%

profile of v7, /device:TPU:0, one launch (start us, length us, event | category | flops | bytes accessed | tf_op | source)
XLA Modules:
  0.0 26.7 jit_solution(6741937022482577141)
XLA Ops:
  0.6 0.0 copy-start.2
  0.6 0.0 copy-start.3
  0.7 0.0 copy-start.1
  0.7 0.0 copy-start
  0.7 2.5 %collective-permute-start = (f32[3,2048]{1,0:T(4,128)}, f32[3,2048]{1,0:T(4,128)S(1)}, u32[]{:S(2)}, u32[]{:S(2)}) collective-permute-start(f32[3,2048]{1,0:T(4,128)} %displacement.1), channel_id=1, source_target_pairs={{0,12},{4,0},{8,4},{12,8},{1,13},{5,1},{9,5},{13,9},{2,14},{6,2},{... | collective-permute-start | bytes 73736 | tf_op jit(solution)/shard_map/ppermute | solution.py:666
  3.1 1.6 %shard_map.130 = (f32[19,4,8,256]{3,2,1,0:T(8,128)S(1)}, f32[2,4,8,256]{3,2,1,0:T(8,128)S(1)}, f32[21,8,256]{2,1,0:T(8,128)S(1)}, f32[21,8,256]{2,1,0:T(8,128)S(1)}) custom-call(f32[19,4,8,256]{3,2,1,0:T(8,128)} %pops_hbm.1, f32[4,8,256]{2,1,0:T(8,128)} %rate_hbm.1, s32[4,8,256]{2,1,0:T(8,128)} %flags_hbm.1), custom_call_target="tpu_custom_call" | custom-call | bytes 5400000 | tf_op jit(solution)/shard_map/pallas_call | solution.py:639
  4.7 1.6 %collective-permute-start.5 = (f32[21,8,256]{2,1,0:T(8,128)S(1)}, f32[21,8,256]{2,1,0:T(8,128)S(1)}, u32[]{:S(2)}, u32[]{:S(2)}) collective-permute-start(f32[21,8,256]{2,1,0:T(8,128)S(1)} %get-tuple-element.32), channel_id=1, source_target_pairs={{0,16},{4,8},{8,4},{12,28},{16,0},{20,24},{24,20},{28,12},{1,17},{... | collective-permute-start | bytes 516104 | tf_op jit(solution)/shard_map/ppermute | solution.py:684
  6.3 0.0 collective-permute-start.6
  6.3 0.0 collective-permute-done.next_nodes
  6.3 0.2 shard_map.131
  6.4 0.6 %collective-permute-start.1 = (f32[21,4,256]{2,1,0:T(4,128)S(1)}, f32[21,4,256]{2,1,0:T(4,128)S(1)}, u32[]{:S(2)}, u32[]{:S(2)}) collective-permute-start(f32[21,4,256]{2,1,0:T(4,128)S(1)} %get-tuple-element.25), channel_id=1, source_target_pairs={{0,4},{1,2},{2,1},{3,7},{4,0},{5,6},{6,5},{7,3},{8,12},{9,10},{10,... | collective-permute-start | bytes 258056 | tf_op jit(solution)/shard_map/ppermute | solution.py:684
  7.0 2.6 %collective-permute-start.2 = (f32[21,4,256]{2,1,0:T(4,128)S(1)}, f32[21,4,256]{2,1,0:T(4,128)S(1)}, u32[]{:S(2)}, u32[]{:S(2)}) collective-permute-start(f32[21,4,256]{2,1,0:T(4,128)S(1)} %get-tuple-element.26), channel_id=1, source_target_pairs={{0,1},{1,0},{2,3},{3,2},{4,5},{5,4},{6,7},{7,6},{8,9},{9,8},{10,11... | collective-permute-start | bytes 258056 | tf_op jit(solution)/shard_map/ppermute | solution.py:684
  9.7 0.0 copy-done.2
  9.7 0.0 copy-done.3
  9.7 0.0 copy-done.1
  9.7 0.0 copy-done
  9.7 1.7 %shard_map.132 = (f32[3,32,128]{2,1,0:T(8,128)S(1)}, f32[3,32,128]{2,1,0:T(8,128)S(1)}, f32[6,3,32,128]{3,2,1,0:T(8,128)S(1)}) custom-call(s32[3,4096]{1,0:T(4,128)S(1)} %copy-done, f32[3,2048]{1,0:T(4,128)S(1)} %copy-done.2, f32[3,2048]{1,0:T(4,128)S(1)} %collective-permute-done.next_nodes, f32[3,4096]{1,0:T(4,128)S(1)} %copy-done.1, f32[32,128]{1,0:T(8,128)S(1)} %bitcast.4), custom_call_target="tpu_custom_call" | custom-call | bytes 7200000 | tf_op jit(solution)/shard_map/pallas_call | solution.py:639
  11.4 1.1 %shard_map.133.other = f32[3,8,256]{2,1,0:T(8,128)S(1)} custom-call(f32[3,32,128]{2,1,0:T(8,128)S(1)} %get-tuple-element.27.low_ids, f32[3,32,128]{2,1,0:T(8,128)S(1)} %get-tuple-element.28.high_ids, f32[6,3,32,128]{3,2,1,0:T(8,128)S(1)} %get-tuple-element.29.forces), custom_call_target="tpu_custom_call" | custom-call | bytes 2880000 | tf_op jit(solution)/shard_map/pallas_call | solution.py:639
  12.5 0.0 collective-permute-done.1.far_y
  12.5 0.1 collective-permute-done.2.near_y
  12.6 0.1 shard_map.134
  12.7 0.7 %collective-permute-start.3 = (f32[9,8,256]{2,1,0:T(8,128)S(1)}, f32[9,8,256]{2,1,0:T(8,128)S(1)}, u32[]{:S(2)}, u32[]{:S(2)}) collective-permute-start(f32[9,8,256]{2,1,0:T(8,128)S(1)} %get-tuple-element.30), channel_id=1, source_target_pairs={{0,16},{4,8},{8,4},{12,28},{16,0},{20,24},{24,20},{28,12},{1,17},{... | collective-permute-start | bytes 221192 | tf_op jit(solution)/shard_map/ppermute | solution.py:684
  13.4 0.2 collective-permute-start.4
  14.2 1.1 %shard_map.136.internal_own = f32[3,8,256]{2,1,0:T(8,128)S(1)} custom-call(f32[3,32,128]{2,1,0:T(8,128)S(1)} %get-tuple-element.27.low_ids, f32[3,32,128]{2,1,0:T(8,128)S(1)} %get-tuple-element.28.high_ids, f32[6,3,32,128]{3,2,1,0:T(8,128)S(1)} %get-tuple-element.29.forces), custom_call_target="tpu_custom_call" | custom-call | bytes 2880000 | tf_op jit(solution)/shard_map/pallas_call | solution.py:639
  15.3 0.0 collective-permute-done.5.far_x
  15.4 0.0 collective-permute-done.6.near_x
  15.4 0.5 %shard_map.135 = (f32[19,8,8,256]{3,2,1,0:T(8,128)S(1)}, f32[2,21,8,256]{3,2,1,0:T(8,128)S(1)}, f32[2,5,8,256]{3,2,1,0:T(8,128)S(1)}, f32[19,6,8,256]{3,2,1,0:T(8,128)S(1)}, f32[2,2,8,256]{3,2,1,0:T(8,128)S(1)}) custom-call(f32[19,4,8,256]{3,2,1,0:T(8,128)S(1)} %get-tuple-element.23.c1, f32[2,4,8,256]{3,2,1,0:T(8,128)S(1)} %get-tuple-element.24.fixed, ...), custom_call_target="tpu_custom_call" | custom-call | bytes 2880000 | tf_op jit(solution)/shard_map/pallas_call | solution.py:639
  15.9 1.2 %collective-permute-done.3.far = f32[9,8,256]{2,1,0:T(8,128)S(1)} collective-permute-done((f32[9,8,256]{2,1,0:T(8,128)S(1)}, f32[9,8,256]{2,1,0:T(8,128)S(1)}, u32[]{:S(2)}, u32[]{:S(2)}) %collective-permute-start.3) | collective-permute-done | bytes 73760 | tf_op jit(solution)/shard_map/ppermute | solution.py:684
  17.1 0.0 collective-permute-done.4.near
  17.1 1.1 %shard_map.137 = (f32[19,4,8,256]{3,2,1,0:T(8,128)S(1)}, f32[80,128]{1,0:T(8,128)S(1)}, f32[2,21,8,256]{3,2,1,0:T(8,128)S(1)}, f32[19,6,8,256]{3,2,1,0:T(8,128)S(1)}) custom-call(s32[1,1,8]{2,1,0:T(1,128)} %block_source_hbm.1, s32[1,1,8]{2,1,0:T(1,128)} %block_target_hbm.1, ...), custom_call_target="tpu_custom_call", output_to_operand_aliasing={{2}: (11, {}), {3}: (12, {})} | custom-call | bytes 5400000 | tf_op jit(solution)/shard_map/pallas_call | solution.py:639
  18.2 2.6 %collective-permute-start.9 = (f32[80,128]{1,0:T(8,128)S(1)}, f32[80,128]{1,0:T(8,128)S(1)}, u32[]{:S(2)}, u32[]{:S(2)}) collective-permute-start(f32[80,128]{1,0:T(8,128)S(1)} %get-tuple-element.40.refs_0_), channel_id=1, source_target_pairs={{3,0},{2,1},{1,2},{0,3},{7,4},{6,5},{5,6},{4,7},{11,8},{10,9},{9,1... | collective-permute-start | bytes 122888 | tf_op jit(solution)/shard_map/ppermute | solution.py:661
  20.8 0.7 %collective-permute-start.8 = (f32[80,128]{1,0:T(8,128)S(1)}, f32[80,128]{1,0:T(8,128)S(1)}, u32[]{:S(2)}, u32[]{:S(2)}) collective-permute-start(f32[80,128]{1,0:T(8,128)S(1)} %get-tuple-element.40.refs_0_), channel_id=1, source_target_pairs={{2,0},{3,1},{0,2},{1,3},{6,4},{7,5},{4,6},{5,7},{10,8},{11,9},{8,1... | collective-permute-start | bytes 122888 | tf_op jit(solution)/shard_map/ppermute | solution.py:661
  21.5 1.2 %collective-permute-start.7 = (f32[80,128]{1,0:T(8,128)S(1)}, f32[80,128]{1,0:T(8,128)S(1)}, u32[]{:S(2)}, u32[]{:S(2)}) collective-permute-start(f32[80,128]{1,0:T(8,128)S(1)} %get-tuple-element.40.refs_0_), channel_id=1, source_target_pairs={{1,0},{0,1},{3,2},{2,3},{5,4},{4,5},{7,6},{6,7},{9,8},{8,9},{11,10... | collective-permute-start | bytes 122888 | tf_op jit(solution)/shard_map/ppermute | solution.py:661
  22.6 0.8 %shard_map.138 = f32[19,4,8,256]{3,2,1,0:T(8,128)} custom-call(f32[19,4,8,256]{3,2,1,0:T(8,128)S(1)} %get-tuple-element.39.values), custom_call_target="tpu_custom_call" | custom-call | bytes 3600000 | tf_op jit(solution)/shard_map/pallas_call | solution.py:639
  23.5 0.7 %collective-permute-done.9.refs_3_ = f32[80,128]{1,0:T(8,128)S(1)} collective-permute-done((f32[80,128]{1,0:T(8,128)S(1)}, f32[80,128]{1,0:T(8,128)S(1)}, u32[]{:S(2)}, u32[]{:S(2)}) %collective-permute-start.9) | collective-permute-done | bytes 40992 | tf_op jit(solution)/shard_map/ppermute | solution.py:661
  24.2 1.7 %collective-permute-done.8.refs_2_ = f32[80,128]{1,0:T(8,128)S(1)} collective-permute-done((f32[80,128]{1,0:T(8,128)S(1)}, f32[80,128]{1,0:T(8,128)S(1)}, u32[]{:S(2)}, u32[]{:S(2)}) %collective-permute-start.8) | collective-permute-done | bytes 40992 | tf_op jit(solution)/shard_map/ppermute | solution.py:661
  25.8 0.1 collective-permute-done.7.refs_1_
  25.9 0.8 %shard_map.139 = (f32[3,2048]{1,0:T(4,128)}, f32[3,8,128]{2,1,0:T(8,128)}) custom-call(f32[80,128]{1,0:T(8,128)S(1)} %get-tuple-element.40.refs_0_, f32[80,128]{1,0:T(8,128)S(1)} %collective-permute-done.7.refs_1_, f32[80,128]{1,0:T(8,128)S(1)} %collective-permute-done.8.refs_2_, f32[80,128]{1,0:T(8,128)S(1)} %collective-permute-done.9.refs_3_), custom_call_target="tpu_custom_call" | custom-call | bytes 2880000 | tf_op jit(solution)/shard_map/pallas_call | solution.py:639
Async XLA Ops:
  0.6 9.0 %copy-start.2 = (f32[3,2048]{1,0:T(4,128)S(1)}, f32[3,2048]{1,0:T(4,128)}, u32[]{:S(2)}) copy-start(f32[3,2048]{1,0:T(4,128)} %displacement.1) | copy-start | bytes 73732
  0.6 9.0 %copy-start.3 = (f32[4096]{0:T(1024)S(1)}, f32[4096]{0:T(1024)}, u32[]{:S(2)}) copy-start(f32[4096]{0:T(1024)} %param.17) | copy-start | bytes 49156
  0.7 9.0 %copy-start.1 = (f32[3,4096]{1,0:T(4,128)S(1)}, f32[3,4096]{1,0:T(4,128)}, u32[]{:S(2)}) copy-start(f32[3,4096]{1,0:T(4,128)} %shape_inverse.1) | copy-start | bytes 147460
  0.7 9.0 %copy-start = (s32[3,4096]{1,0:T(4,128)S(1)}, s32[3,4096]{1,0:T(4,128)}, u32[]{:S(2)}) copy-start(s32[3,4096]{1,0:T(4,128)} %elements.1) | copy-start | bytes 147460
  0.7 5.6 %collective-permute-start = (f32[3,2048]{1,0:T(4,128)}, f32[3,2048]{1,0:T(4,128)S(1)}, u32[]{:S(2)}, u32[]{:S(2)}) collective-permute-start(f32[3,2048]{1,0:T(4,128)} %displacement.1), channel_id=1, source_target_pairs={{0,12},{4,0},{8,4},{12,8},{1,13},{5,1},{9,5},{13,9},{2,14},{6,2},{... | collective-permute-start | bytes 73736 | tf_op jit(solution)/shard_map/ppermute | solution.py:666
  4.7 10.6 %collective-permute-start.5 = (f32[21,8,256]{2,1,0:T(8,128)S(1)}, f32[21,8,256]{2,1,0:T(8,128)S(1)}, u32[]{:S(2)}, u32[]{:S(2)}) collective-permute-start(f32[21,8,256]{2,1,0:T(8,128)S(1)} %get-tuple-element.32), channel_id=1, source_target_pairs={{0,16},{4,8},{8,4},{12,28},{16,0},{20,24},{24,20},{28,12},{1,17},{... | collective-permute-start | bytes 516104 | tf_op jit(solution)/shard_map/ppermute | solution.py:684
  6.3 9.1 %collective-permute-start.6 = (f32[21,8,256]{2,1,0:T(8,128)S(1)}, f32[21,8,256]{2,1,0:T(8,128)S(1)}, u32[]{:S(2)}, u32[]{:S(2)}) collective-permute-start(f32[21,8,256]{2,1,0:T(8,128)S(1)} %get-tuple-element.33), channel_id=1, source_target_pairs={{0,4},{4,0},{8,12},{12,8},{16,20},{20,16},{24,28},{28,24},{1,5},{5... | collective-permute-start | bytes 516104 | tf_op jit(solution)/shard_map/ppermute | solution.py:684
  6.4 6.1 %collective-permute-start.1 = (f32[21,4,256]{2,1,0:T(4,128)S(1)}, f32[21,4,256]{2,1,0:T(4,128)S(1)}, u32[]{:S(2)}, u32[]{:S(2)}) collective-permute-start(f32[21,4,256]{2,1,0:T(4,128)S(1)} %get-tuple-element.25), channel_id=1, source_target_pairs={{0,4},{1,2},{2,1},{3,7},{4,0},{5,6},{6,5},{7,3},{8,12},{9,10},{10,... | collective-permute-start | bytes 258056 | tf_op jit(solution)/shard_map/ppermute | solution.py:684
  7.0 5.6 %collective-permute-start.2 = (f32[21,4,256]{2,1,0:T(4,128)S(1)}, f32[21,4,256]{2,1,0:T(4,128)S(1)}, u32[]{:S(2)}, u32[]{:S(2)}) collective-permute-start(f32[21,4,256]{2,1,0:T(4,128)S(1)} %get-tuple-element.26), channel_id=1, source_target_pairs={{0,1},{1,0},{2,3},{3,2},{4,5},{5,4},{6,7},{7,6},{8,9},{9,8},{10,11... | collective-permute-start | bytes 258056 | tf_op jit(solution)/shard_map/ppermute | solution.py:684
  12.7 4.4 %collective-permute-start.3 = (f32[9,8,256]{2,1,0:T(8,128)S(1)}, f32[9,8,256]{2,1,0:T(8,128)S(1)}, u32[]{:S(2)}, u32[]{:S(2)}) collective-permute-start(f32[9,8,256]{2,1,0:T(8,128)S(1)} %get-tuple-element.30), channel_id=1, source_target_pairs={{0,16},{4,8},{8,4},{12,28},{16,0},{20,24},{24,20},{28,12},{1,17},{... | collective-permute-start | bytes 221192 | tf_op jit(solution)/shard_map/ppermute | solution.py:684
  13.4 3.7 %collective-permute-start.4 = (f32[9,8,256]{2,1,0:T(8,128)S(1)}, f32[9,8,256]{2,1,0:T(8,128)S(1)}, u32[]{:S(2)}, u32[]{:S(2)}) collective-permute-start(f32[9,8,256]{2,1,0:T(8,128)S(1)} %get-tuple-element.31), channel_id=1, source_target_pairs={{0,4},{4,0},{8,12},{12,8},{16,20},{20,16},{24,28},{28,24},{1,5},{5... | collective-permute-start | bytes 221192 | tf_op jit(solution)/shard_map/ppermute | solution.py:684
  18.2 6.0 %collective-permute-start.9 = (f32[80,128]{1,0:T(8,128)S(1)}, f32[80,128]{1,0:T(8,128)S(1)}, u32[]{:S(2)}, u32[]{:S(2)}) collective-permute-start(f32[80,128]{1,0:T(8,128)S(1)} %get-tuple-element.40.refs_0_), channel_id=1, source_target_pairs={{3,0},{2,1},{1,2},{0,3},{7,4},{6,5},{5,6},{4,7},{11,8},{10,9},{9,1... | collective-permute-start | bytes 122888 | tf_op jit(solution)/shard_map/ppermute | solution.py:661
  20.8 5.0 %collective-permute-start.8 = (f32[80,128]{1,0:T(8,128)S(1)}, f32[80,128]{1,0:T(8,128)S(1)}, u32[]{:S(2)}, u32[]{:S(2)}) collective-permute-start(f32[80,128]{1,0:T(8,128)S(1)} %get-tuple-element.40.refs_0_), channel_id=1, source_target_pairs={{2,0},{3,1},{0,2},{1,3},{6,4},{7,5},{4,6},{5,7},{10,8},{11,9},{8,1... | collective-permute-start | bytes 122888 | tf_op jit(solution)/shard_map/ppermute | solution.py:661
  21.5 4.4 %collective-permute-start.7 = (f32[80,128]{1,0:T(8,128)S(1)}, f32[80,128]{1,0:T(8,128)S(1)}, u32[]{:S(2)}, u32[]{:S(2)}) collective-permute-start(f32[80,128]{1,0:T(8,128)S(1)} %get-tuple-element.40.refs_0_), channel_id=1, source_target_pairs={{1,0},{0,1},{3,2},{2,3},{5,4},{4,5},{7,6},{6,7},{9,8},{8,9},{11,10... | collective-permute-start | bytes 122888 | tf_op jit(solution)/shard_map/ppermute | solution.py:661

commit v8 on v7

--- a/solution.py
+++ b/solution.py
@@ -42,6 +42,7 @@
 FORCE_SLOT = 6
 CORNER_SLOTS = FORCE_SLOT + 3
 PIECES = 2
+CAP = 3
 F32 = jnp.float32
 VMEM_BYTES = 48 * 1024 * 1024
 
@@ -315,40 +316,27 @@
     lax.fori_loop(1, planes - 1, inside_plane, 0)
 
 
-def second_kernel(
-    block_source_hbm,
-    block_target_hbm,
-    block_node_hbm,
-    block_count,
-    far,
-    near,
-    fixed,
-    extended,
-    crossing,
-    ends,
-    internal_own,
-    walls_in,
-    second_in,
-    out,
-    message,
-    walls,
-    second,
-    both,
-    edges,
-    loads,
-    block_source,
-    block_target,
-    block_node,
-    sems,
-):
-    del walls_in, second_in
-    copies = [
-        pltpu.make_async_copy(block_source_hbm, block_source, sems.at[0]),
-        pltpu.make_async_copy(block_target_hbm, block_target, sems.at[1]),
-        pltpu.make_async_copy(block_node_hbm, block_node, sems.at[2]),
-    ]
-    for copy in copies:
-        copy.start()
+def targets_of(keys, dest, node_blocks):
+    found = []
+    before = jnp.zeros((1, BLK), F32)
+    low = (dest * node_blocks).astype(F32)
+    for k in range(keys.shape[0]):
+        key = keys[k : k + 1]
+        named = (key >= low) & (key < low + node_blocks)
+        found.append((key, named, before))
+        before = before + jnp.where(named, 1.0, 0.0)
+    return found
+
+
+def second_kernel(count, *refs):
+    block_source_hbm, keys = refs[0], refs[1 : 1 + count]
+    far, near, fixed, extended, crossing, ends, internal_own = refs[1 + count : 8 + count]
+    out = refs[10 + count]
+    messages = refs[11 + count : 11 + 2 * count]
+    walls, second = refs[11 + 2 * count : 13 + 2 * count]
+    both, edges, loads, internal, block_source, sem = refs[13 + 2 * count :]
+    copy = pltpu.make_async_copy(block_source_hbm, block_source, sem)
+    copy.start()
     planes, rows, length = out.shape[1:]
     half = length // BLK
     slots = block_source.shape[2]
@@ -442,33 +430,62 @@
 
     lax.fori_loop(0, planes, plane_two, 0)
 
-    for copy in copies:
-        copy.wait()
     node_blocks = internal_own.shape[1] * half
-    live = jnp.broadcast_to(block_count[...], (1, BLK))
+    for part in range(3):
+        for piece in range(half):
+            at = piece * rows
+            lanes = slice(piece * BLK, (piece + 1) * BLK)
+            internal[part, at : at + rows] = (
+                internal_own[part, :, lanes] + both[0, FORCE_SLOT + part, :, lanes]
+            )
+    copy.wait()
+    blocks = []
     for k in range(slots):
         run = block_source[0, 0, k]
         x = run // (rows * half)
         left = run - x * (rows * half)
         y = left // half
         piece = left - y * half
+        blocks.append([loads[x * half + piece, part, pl.ds(y, 1)] for part in range(3)])
+    slot_ids = lax.broadcasted_iota(jnp.int32, (8, BLK), 0).astype(F32)
+    for step in range(count):
+        message = messages[-step]
+        dest = partner_of(inner, step, count)
+        wanted = keys[step][...]
+        moved = [jnp.zeros((slots, BLK), F32)] * 3
+        chosen = [jnp.zeros((8, BLK), F32)] * 3
+        for k, (key, named, before) in enumerate(targets_of(keys[0], dest, node_blocks)):
+            same = (wanted == key) & (key >= 0.0)
+            here = named & (slot_ids == before)
+            for part in range(3):
+                moved[part] = moved[part] + jnp.where(same, blocks[k][part], 0.0)
+                chosen[part] = chosen[part] + jnp.where(here, blocks[k][part], 0.0)
+        for b in range(node_blocks):
+            same = wanted == (inner * node_blocks + b).astype(F32)
+            for part in range(3):
+                moved[part] = moved[part] - jnp.where(same, internal[part, b : b + 1], 0.0)
         for part in range(3):
-            message[4 * k + part : 4 * k + part + 1] = loads[x * half + piece, part, pl.ds(y, 1)]
-        key = block_target[0, 0, k] * node_blocks + block_node[0, 0, k]
-        message[4 * k + 3 : 4 * k + 4] = jnp.where(live > k, key, -1).astype(F32)
-    for part in range(3):
-        start = 4 * slots + part * node_blocks
-        for piece in range(half):
-            at = piece * rows
-            lanes = slice(piece * BLK, (piece + 1) * BLK)
-            message[start + at : start + at + rows] = (
-                internal_own[part, :, lanes] + both[0, FORCE_SLOT + part, :, lanes]
-            )
+            message[part * slots : (part + 1) * slots] = moved[part]
+            at = 3 * slots + part * CAP
+            message[at : at + CAP] = chosen[part][:CAP]
+        if step == 0:
+            for part in range(3):
+                at = 3 * slots + 3 * CAP + part * node_blocks
+                message[at : at + node_blocks] = internal[part]
 
 
 def element_kernel(
-    elements, displacement, next_nodes, shape_inverse, stiffness, low_ids, high_ids, forces, shapes,
-    numbers, corners,
+    elements,
+    displacement,
+    next_nodes,
+    shape_inverse,
+    stiffness,
+    low_ids,
+    high_ids,
+    forces,
+    shapes,
+    numbers,
+    corners,
 ):
     node_dev = displacement.shape[1]
     node_blocks = node_dev // BLK
@@ -542,6 +559,14 @@
                 forces[part * 3 + p, corner] = piece
 
 
+def key_kernel(node_blocks, block_target, block_node, block_count, face, keys):
+    del face
+    live = block_count[0, 0]
+    for k in range(keys.shape[0]):
+        key = jnp.where(k < live, block_target[0, 0, k] * node_blocks + block_node[0, 0, k], -1)
+        keys[k : k + 1] = jnp.broadcast_to(key, (1, BLK)).astype(F32)
+
+
 def spread_kernel(base, low_ids, high_ids, forces, out):
     runs = low_ids.shape[1]
     parts, rows, length = out.shape
@@ -594,43 +619,32 @@
 
 
 def final_kernel(count, *refs):
-    messages = refs[:count]
-    residual, motion, keys = refs[count:]
-    slots = keys.shape[0]
+    messages, keys = refs[:count], refs[count : 2 * count]
+    residual, motion = refs[2 * count :]
+    slots = keys[0].shape[0]
     node_blocks = residual.shape[1] // BLK
     inner = lax.axis_index("inner")
-    mine = messages[0]
-    for k in range(slots):
-        keys[k : k + 1] = mine[4 * k + 3 : 4 * k + 4]
-    wanted = keys[...]
     node_ids = lax.broadcasted_iota(jnp.int32, (node_blocks, BLK), 0)
     own_ids = (node_ids + inner * node_blocks).astype(F32)
-    external = [jnp.zeros((node_blocks, BLK), F32)] * 3
+    slot_ids = lax.broadcasted_iota(jnp.int32, (8, BLK), 0).astype(F32)
+    start = 3 * slots + 3 * CAP
+    total = [-messages[0][start + p * node_blocks : start + (p + 1) * node_blocks] for p in range(3)]
     moved = [jnp.zeros((slots, BLK), F32)] * 3
-    for message in messages:
-        for k in range(slots):
-            key = message[4 * k + 3 : 4 * k + 4]
-            here = own_ids == key
-            same = wanted == key
+    for message, sender in zip(messages, keys):
+        nodes = jnp.full((8, BLK), -1.0, F32)
+        for key, named, before in targets_of(sender, inner, node_blocks):
+            nodes = jnp.where(named & (slot_ids == before), key, nodes)
+        for place in range(CAP):
+            here = own_ids == nodes[place : place + 1]
             for part in range(3):
-                row = message[4 * k + part : 4 * k + part + 1]
-                external[part] = external[part] + jnp.where(here, row, 0.0)
-                moved[part] = moved[part] + jnp.where(same, row, 0.0)
-    for step, message in enumerate(messages):
-        sender = partner_of(inner, step, count)
+                at = 3 * slots + part * CAP + place
+                total[part] = total[part] + jnp.where(here, message[at : at + 1], 0.0)
+        for part in range(3):
+            moved[part] = moved[part] + message[part * slots : (part + 1) * slots]
+    for part in range(3):
         for b in range(node_blocks):
-            key = jnp.broadcast_to(sender * node_blocks + b, (1, BLK)).astype(F32)
-            same = wanted == key
-            for part in range(3):
-                at = 4 * slots + part * node_blocks + b
-                moved[part] = moved[part] - jnp.where(same, message[at : at + 1], 0.0)
-    live = wanted >= 0.0
-    for part in range(3):
-        start = 4 * slots + part * node_blocks
-        left = external[part] - mine[start : start + node_blocks]
-        for b in range(node_blocks):
-            residual[part : part + 1, b * BLK : (b + 1) * BLK] = left[b : b + 1]
-        motion[part] = jnp.where(live, COMPLIANCE * moved[part], 0.0)
+            residual[part : part + 1, b * BLK : (b + 1) * BLK] = total[part][b : b + 1]
+        motion[part] = COMPLIANCE * moved[part]
 
 
 def call(kernel, outs, operands, spaces, scratch=(), out_spaces=None, micros=1.0, aliases=None):
@@ -653,12 +667,16 @@
 def partner_of(at, step, count):
     if count & (count - 1) == 0:
         return at ^ step
-    return (at + count - step) % count
+    return (at + step) % count
+
+
+def reply(step, count):
+    return step if count & (count - 1) == 0 else count - step
 
 
 def exchange(block, axis, step):
     count = lax.axis_size(axis)
-    return lax.ppermute(block, axis, [(partner_of(i, step, count), i) for i in range(count)])
+    return lax.ppermute(block, axis, [(i, partner_of(i, step, count)) for i in range(count)])
 
 
 def around(block, axis, step):
@@ -788,15 +806,28 @@
         ),
         micros=0.8,
     )
-    lines = 4 * slots + 3 * node_blocks
-    values, message, _, _ = call(
-        second_kernel,
-        (whole, shape(lines, BLK), walls_shape, second_shape),
+    (own_keys,) = call(
+        functools.partial(key_kernel, node_blocks),
+        (shape(slots, BLK),),
+        (block_target, block_node, block_count, near),
+        (smem,) * 3 + (vmem,),
+        micros=0.1,
+    )
+    keys = [own_keys] + [exchange(own_keys, "inner", step) for step in range(1, count)]
+    towards = [keys[0]] + [keys[reply(step, count)] for step in range(1, count)]
+    lines = -(-(3 * slots + 3 * CAP) // 8) * 8
+    outs = call(
+        functools.partial(second_kernel, count),
+        (
+            whole,
+            shape(lines + 3 * node_blocks, BLK),
+            *([shape(lines, BLK)] * (count - 1)),
+            walls_shape,
+            second_shape,
+        ),
         (
             pin(block_source),
-            pin(block_target),
-            pin(block_node),
-            block_count,
+            *towards,
             far_c,
             near_c,
             fixed,
@@ -807,20 +838,21 @@
             walls,
             second,
         ),
-        (hbm,) * 3 + (vmem,) * 10,
-        aliases={11: 2, 12: 3},
+        (hbm,) + (vmem,) * (9 + count),
+        aliases={8 + count: 1 + count, 9 + count: 2 + count},
         scratch=(
             pltpu.VMEM((2, CORNER_SLOTS, rows, length), F32),
             pltpu.VMEM((2, 5, wide, length), F32),
             pltpu.VMEM((planes * half, 3, rows, BLK), F32),
+            pltpu.VMEM((3, node_blocks, BLK), F32),
             pltpu.SMEM(block_source.shape, jnp.int32),
-            pltpu.SMEM(block_target.shape, jnp.int32),
-            pltpu.SMEM(block_node.shape, jnp.int32),
-            pltpu.SemaphoreType.DMA((3,)),
+            pltpu.SemaphoreType.DMA(()),
         ),
         micros=1.5,
     )
-    messages = [message] + [exchange(message, "inner", step) for step in range(1, count)]
+    values = outs[0]
+    messages = [outs[1]]
+    messages += [exchange(outs[1 + count - step], "inner", step) for step in range(1, count)]
     (populations_out,) = call(
         store_kernel,
         (whole,),
@@ -833,9 +865,8 @@
     residual, motion = call(
         functools.partial(final_kernel, count),
         (shape(3, node_dev), shape(3, slots, BLK)),
-        messages,
-        (vmem,) * count,
-        scratch=(pltpu.VMEM((slots, BLK), F32),),
+        (*messages, *keys),
+        (vmem,) * (2 * count),
         micros=0.8,
     )
     return populations_out, residual, motion.transpose(1, 0, 2)[None, None]

time: 26.9 us -> 31.8 us (1.18)
  starting transfers between devices: 12.6 us -> 17 us
  Pallas kernels: 8.92 us -> 9.54 us
    ppermute x3 -> x6, starting transfers between devices: 4.45 us -> 8.91 us  [exchange(): lax.ppermute(block, axis, [(i, partner_of(i, step, count)) for i in range...]
    ppermute x3, waiting for transfers between devices: 1.28 us -> 0.03 us  [swap(): lax.ppermute(far, axes, routes[1])]
    ppermute x3 -> x6, waiting for transfers between devices: 2.42 us -> 3.49 us  [exchange(): lax.ppermute(block, axis, [(i, partner_of(i, step, count)) for i in range...]
    pallas_call x10 -> x11, Pallas kernels: 8.92 us -> 9.54 us  [call(): pl.pallas_call(kernel, out_shape=outs, in_specs=[spec(space) for space in...]
  transfers between devices with their start and end apart: 10 -> 13, of which waited for: 5 -> 4; matrix products, arithmetic and copies ran while one was open for 0% -> 0% of each run, Pallas kernels for 26% -> 24%
where the time goes in v8:
time: 31.8 us; the launch traced here: 31.7 us
  starting transfers between devices  17 us (53%)
  Pallas kernels  9.54 us (30%)
  waiting for transfers between devices  3.6 us (11%)
  between operations  1.46 us (5%)
    pallas_call x11, Pallas kernels, call(): pl.pallas_call(kernel, out_shape=outs, in_specs=[spec(space) for space in...  9.54 us
    ppermute x6, starting transfers between devices, exchange(): lax.ppermute(block, axis, [(i, partner_of(i, step, count)) for i in range...  8.91 us
    ppermute x6, waiting for transfers between devices, exchange(): lax.ppermute(block, axis, [(i, partner_of(i, step, count)) for i in range...  3.49 us
    ppermute x3, starting transfers between devices, swap(): lax.ppermute(near, axes, routes[0])  2.84 us
    ppermute x3, starting transfers between devices, swap(): lax.ppermute(far, axes, routes[1])  2.83 us
    ppermute x1, starting transfers between devices, around(): lax.ppermute(block, axis, [(i, (i + step) % count) for i in range(count)])  2.46 us
  transfers between devices with their start and end apart: 13, of which 4 were waited for; matrix products, arithmetic and copies ran while one was open for 0% of the time, Pallas kernels for 24%

profile of v8, /device:TPU:0, one launch (start us, length us, event | category | flops | bytes accessed | tf_op | source)
XLA Modules:
  0.0 31.7 jit_solution(6630751019828055902)
XLA Ops:
  0.6 0.0 copy-start.2
  0.6 0.0 copy-start.3
  0.7 0.0 copy-start.1
  0.7 0.0 copy-start
  0.7 0.0 copy-start.5
  0.7 0.0 copy-start.4
  0.7 2.5 %collective-permute-start = (f32[3,2048]{1,0:T(4,128)}, f32[3,2048]{1,0:T(4,128)S(1)}, u32[]{:S(2)}, u32[]{:S(2)}) collective-permute-start(f32[3,2048]{1,0:T(4,128)} %displacement.1), channel_id=1, source_target_pairs={{0,12},{4,0},{8,4},{12,8},{1,13},{5,1},{9,5},{13,9},{2,14},{6,2},{... | collective-permute-start | bytes 73736 | tf_op jit(solution)/shard_map/ppermute | solution.py:684
  3.2 1.6 %shard_map.130 = (f32[19,4,8,256]{3,2,1,0:T(8,128)S(1)}, f32[2,4,8,256]{3,2,1,0:T(8,128)S(1)}, f32[21,8,256]{2,1,0:T(8,128)S(1)}, f32[21,8,256]{2,1,0:T(8,128)S(1)}) custom-call(f32[19,4,8,256]{3,2,1,0:T(8,128)} %pops_hbm.1, f32[4,8,256]{2,1,0:T(8,128)} %rate_hbm.1, s32[4,8,256]{2,1,0:T(8,128)} %flags_hbm.1), custom_call_target="tpu_custom_call" | custom-call | bytes 5400000 | tf_op jit(solution)/shard_map/pallas_call | solution.py:653
  4.7 1.6 %collective-permute-start.8 = (f32[21,8,256]{2,1,0:T(8,128)S(1)}, f32[21,8,256]{2,1,0:T(8,128)S(1)}, u32[]{:S(2)}, u32[]{:S(2)}) collective-permute-start(f32[21,8,256]{2,1,0:T(8,128)S(1)} %get-tuple-element.35), channel_id=1, source_target_pairs={{0,16},{4,8},{8,4},{12,28},{16,0},{20,24},{24,20},{28,12},{1,17},{... | collective-permute-start | bytes 516104 | tf_op jit(solution)/shard_map/ppermute | solution.py:702
  6.3 0.0 collective-permute-start.9
  6.3 0.0 collective-permute-done.next_nodes
  6.3 0.2 shard_map.131
  6.5 0.6 %collective-permute-start.1 = (f32[21,4,256]{2,1,0:T(4,128)S(1)}, f32[21,4,256]{2,1,0:T(4,128)S(1)}, u32[]{:S(2)}, u32[]{:S(2)}) collective-permute-start(f32[21,4,256]{2,1,0:T(4,128)S(1)} %get-tuple-element.28), channel_id=1, source_target_pairs={{0,4},{1,2},{2,1},{3,7},{4,0},{5,6},{6,5},{7,3},{8,12},{9,10},{10,... | collective-permute-start | bytes 258056 | tf_op jit(solution)/shard_map/ppermute | solution.py:702
  7.0 2.6 %collective-permute-start.2 = (f32[21,4,256]{2,1,0:T(4,128)S(1)}, f32[21,4,256]{2,1,0:T(4,128)S(1)}, u32[]{:S(2)}, u32[]{:S(2)}) collective-permute-start(f32[21,4,256]{2,1,0:T(4,128)S(1)} %get-tuple-element.29), channel_id=1, source_target_pairs={{0,1},{1,0},{2,3},{3,2},{4,5},{5,4},{6,7},{7,6},{8,9},{9,8},{10,11... | collective-permute-start | bytes 258056 | tf_op jit(solution)/shard_map/ppermute | solution.py:702
  9.7 0.0 copy-done.2
  9.7 0.0 copy-done.3
  9.7 0.0 copy-done.1
  9.7 0.0 copy-done
  9.7 1.7 %shard_map.132 = (f32[3,32,128]{2,1,0:T(8,128)S(1)}, f32[3,32,128]{2,1,0:T(8,128)S(1)}, f32[6,3,32,128]{3,2,1,0:T(8,128)S(1)}) custom-call(s32[3,4096]{1,0:T(4,128)S(1)} %copy-done, f32[3,2048]{1,0:T(4,128)S(1)} %copy-done.2, f32[3,2048]{1,0:T(4,128)S(1)} %collective-permute-done.next_nodes, f32[3,4096]{1,0:T(4,128)S(1)} %copy-done.1, f32[32,128]{1,0:T(8,128)S(1)} %bitcast.4), custom_call_target="tpu_custom_call" | custom-call | bytes 7200000 | tf_op jit(solution)/shard_map/pallas_call | solution.py:653
  11.4 1.1 %shard_map.133.other = f32[3,8,256]{2,1,0:T(8,128)S(1)} custom-call(f32[3,32,128]{2,1,0:T(8,128)S(1)} %get-tuple-element.30.low_ids, f32[3,32,128]{2,1,0:T(8,128)S(1)} %get-tuple-element.31.high_ids, f32[6,3,32,128]{3,2,1,0:T(8,128)S(1)} %get-tuple-element.32.forces), custom_call_target="tpu_custom_call" | custom-call | bytes 2880000 | tf_op jit(solution)/shard_map/pallas_call | solution.py:653
  12.5 0.0 collective-permute-done.1.far_y
  12.5 0.1 collective-permute-done.2.near_y
  12.6 0.1 shard_map.134
  12.7 0.7 %collective-permute-start.6 = (f32[9,8,256]{2,1,0:T(8,128)S(1)}, f32[9,8,256]{2,1,0:T(8,128)S(1)}, u32[]{:S(2)}, u32[]{:S(2)}) collective-permute-start(f32[9,8,256]{2,1,0:T(8,128)S(1)} %get-tuple-element.34), channel_id=1, source_target_pairs={{0,16},{4,8},{8,4},{12,28},{16,0},{20,24},{24,20},{28,12},{1,17},{... | collective-permute-start | bytes 221192 | tf_op jit(solution)/shard_map/ppermute | solution.py:702
  13.4 0.2 collective-permute-start.7
  14.2 0.0 copy-done.5
  14.3 0.0 copy-done.4
  14.3 0.6 %shard_map.135.refs_1_.refs_4_ = f32[8,128]{1,0:T(8,128)S(1)} custom-call(s32[1,1,8]{2,1,0:T(1,128)S(1)} %copy-done.4, s32[1,1,8]{2,1,0:T(1,128)S(1)} %copy-done.5, s32[1,1]{1,0:T(1,128)S(6)} %copy.18.block_count, f32[9,8,256]{2,1,0:T(8,128)S(1)} %get-tuple-element.33.face), custom_call_target="tpu_custom_call" | custom-call | bytes 360000 | tf_op jit(solution)/shard_map/pallas_call | solution.py:653
  14.8 2.6 %collective-permute-start.5 = (f32[8,128]{1,0:T(8,128)S(1)}, f32[8,128]{1,0:T(8,128)S(1)}, u32[]{:S(2)}, u32[]{:S(2)}) collective-permute-start(f32[8,128]{1,0:T(8,128)S(1)} %shard_map.135.refs_1_.refs_4_), channel_id=1, source_target_pairs={{0,3},{1,2},{2,1},{3,0},{4,7},{5,6},{6,5},{7,4},{8,11},{9,10},{10,... | collective-permute-start | bytes 12296 | tf_op jit(solution)/shard_map/ppermute | solution.py:679
  17.4 0.0 collective-permute-done.8.far_x
  17.4 0.5 %collective-permute-start.4 = (f32[8,128]{1,0:T(8,128)S(1)}, f32[8,128]{1,0:T(8,128)S(1)}, u32[]{:S(2)}, u32[]{:S(2)}) collective-permute-start(f32[8,128]{1,0:T(8,128)S(1)} %shard_map.135.refs_1_.refs_4_), channel_id=1, source_target_pairs={{0,2},{1,3},{2,0},{3,1},{4,6},{5,7},{6,4},{7,5},{8,10},{9,11},{10,... | collective-permute-start | bytes 12296 | tf_op jit(solution)/shard_map/ppermute | solution.py:679
  18.0 0.0 collective-permute-done.9.near_x
  18.0 1.3 %collective-permute-start.3 = (f32[8,128]{1,0:T(8,128)S(1)}, f32[8,128]{1,0:T(8,128)S(1)}, u32[]{:S(2)}, u32[]{:S(2)}) collective-permute-start(f32[8,128]{1,0:T(8,128)S(1)} %shard_map.135.refs_1_.refs_4_), channel_id=1, source_target_pairs={{0,1},{1,0},{2,3},{3,2},{4,5},{5,4},{6,7},{7,6},{8,9},{9,8},{10,11... | collective-permute-start | bytes 12296 | tf_op jit(solution)/shard_map/ppermute | solution.py:679
  19.3 1.1 %shard_map.137.refs_11_ = f32[3,8,256]{2,1,0:T(8,128)S(1)} custom-call(f32[3,32,128]{2,1,0:T(8,128)S(1)} %get-tuple-element.30.low_ids, f32[3,32,128]{2,1,0:T(8,128)S(1)} %get-tuple-element.31.high_ids, f32[6,3,32,128]{3,2,1,0:T(8,128)S(1)} %get-tuple-element.32.forces), custom_call_target="tpu_custom_call" | custom-call | bytes 2880000 | tf_op jit(solution)/shard_map/pallas_call | solution.py:653
  20.4 0.5 %shard_map.136 = (f32[19,8,8,256]{3,2,1,0:T(8,128)S(1)}, f32[2,21,8,256]{3,2,1,0:T(8,128)S(1)}, f32[2,5,8,256]{3,2,1,0:T(8,128)S(1)}, f32[19,6,8,256]{3,2,1,0:T(8,128)S(1)}, f32[2,2,8,256]{3,2,1,0:T(8,128)S(1)}) custom-call(f32[19,4,8,256]{3,2,1,0:T(8,128)S(1)} %get-tuple-element.26.c1, f32[2,4,8,256]{3,2,1,0:T(8,128)S(1)} %get-tuple-element.27.fixed.refs_7_, ...), custom_call_target="tpu_custom_call" | custom-call | bytes 2880000 | tf_op jit(solution)/shard_map/pallas_call | solution.py:653
  20.9 0.0 collective-permute-done.5.refs_4_.refs_7_
  20.9 1.0 %collective-permute-done.4.refs_3_.refs_6_ = f32[8,128]{1,0:T(8,128)S(1)} collective-permute-done((f32[8,128]{1,0:T(8,128)S(1)}, f32[8,128]{1,0:T(8,128)S(1)}, u32[]{:S(2)}, u32[]{:S(2)}) %collective-permute-start.4) | collective-permute-done | bytes 4128 | tf_op jit(solution)/shard_map/ppermute | solution.py:679
  22.0 0.0 collective-permute-done.3.refs_2_.refs_5_
  22.0 0.0 collective-permute-done.6.refs_5_
  22.0 0.0 collective-permute-done.7.refs_6_
  22.0 1.2 %shard_map.138 = (f32[19,4,8,256]{3,2,1,0:T(8,128)S(1)}, f32[88,128]{1,0:T(8,128)S(1)}, f32[40,128]{1,0:T(8,128)S(1)}, f32[40,128]{1,0:T(8,128)S(1)}, f32[40,128...) custom-call(s32[1,1,8]{2,1,0:T(1,128)} %refs_0_.1, ...), custom_call_target="tpu_custom_call", output_to_operand_aliasing={{5}: (12, {}), {6}: (13, {})} | custom-call | bytes 5400000 | tf_op jit(solution)/shard_map/pallas_call | solution.py:653
  23.2 1.0 %collective-permute-start.10 = (f32[40,128]{1,0:T(8,128)S(1)}, f32[40,128]{1,0:T(8,128)S(1)}, u32[]{:S(2)}, u32[]{:S(2)}) collective-permute-start(f32[40,128]{1,0:T(8,128)S(1)} %get-tuple-element.44), channel_id=1, source_target_pairs={{0,1},{1,0},{2,3},{3,2},{4,5},{5,4},{6,7},{7,6},{8,9},{9,8},{10,11... | collective-permute-start | bytes 61448 | tf_op jit(solution)/shard_map/ppermute | solution.py:679
  24.2 1.2 %collective-permute-start.11 = (f32[40,128]{1,0:T(8,128)S(1)}, f32[40,128]{1,0:T(8,128)S(1)}, u32[]{:S(2)}, u32[]{:S(2)}) collective-permute-start(f32[40,128]{1,0:T(8,128)S(1)} %get-tuple-element.45), channel_id=1, source_target_pairs={{0,2},{1,3},{2,0},{3,1},{4,6},{5,7},{6,4},{7,5},{8,10},{9,11},{10,... | collective-permute-start | bytes 61448 | tf_op jit(solution)/shard_map/ppermute | solution.py:679
  25.4 2.3 %collective-permute-start.12 = (f32[40,128]{1,0:T(8,128)S(1)}, f32[40,128]{1,0:T(8,128)S(1)}, u32[]{:S(2)}, u32[]{:S(2)}) collective-permute-start(f32[40,128]{1,0:T(8,128)S(1)} %get-tuple-element.46), channel_id=1, source_target_pairs={{0,3},{1,2},{2,1},{3,0},{4,7},{5,6},{6,5},{7,4},{8,11},{9,10},{10,... | collective-permute-start | bytes 61448 | tf_op jit(solution)/shard_map/ppermute | solution.py:679
  27.7 0.8 %shard_map.139 = f32[19,4,8,256]{3,2,1,0:T(8,128)} custom-call(f32[19,4,8,256]{3,2,1,0:T(8,128)S(1)} %get-tuple-element.42.values), custom_call_target="tpu_custom_call" | custom-call | bytes 3600000 | tf_op jit(solution)/shard_map/pallas_call | solution.py:653
  28.5 0.0 collective-permute-done.10.refs_1_
  28.5 0.6 %collective-permute-done.11.refs_2_ = f32[40,128]{1,0:T(8,128)S(1)} collective-permute-done((f32[40,128]{1,0:T(8,128)S(1)}, f32[40,128]{1,0:T(8,128)S(1)}, u32[]{:S(2)}, u32[]{:S(2)}) %collective-permute-start.11) | collective-permute-done | bytes 20512 | tf_op jit(solution)/shard_map/ppermute | solution.py:679
  29.1 1.9 %collective-permute-done.12.refs_3_ = f32[40,128]{1,0:T(8,128)S(1)} collective-permute-done((f32[40,128]{1,0:T(8,128)S(1)}, f32[40,128]{1,0:T(8,128)S(1)}, u32[]{:S(2)}, u32[]{:S(2)}) %collective-permute-start.12) | collective-permute-done | bytes 20512 | tf_op jit(solution)/shard_map/ppermute | solution.py:679
  31.0 0.7 %shard_map.140 = (f32[3,2048]{1,0:T(4,128)}, f32[3,8,128]{2,1,0:T(8,128)}) custom-call(f32[88,128]{1,0:T(8,128)S(1)} %get-tuple-element.43.refs_0_, f32[40,128]{1,0:T(8,128)S(1)} %collective-permute-done.10.refs_1_, f32[40,128]{1,0:T(8,128)S(1)} %collective-permute-done.11.refs_2_, f32[40,128]{1,0:T(8,128)S(1)} %collective-permute-done.12.refs_3_, ...), custom_call_target="tpu_custom_call" | custom-call | bytes 2880000 | tf_op jit(solution)/shard_map/pallas_call | solution.py:653
Async XLA Ops:
  0.6 9.0 %copy-start.2 = (f32[3,2048]{1,0:T(4,128)S(1)}, f32[3,2048]{1,0:T(4,128)}, u32[]{:S(2)}) copy-start(f32[3,2048]{1,0:T(4,128)} %displacement.1) | copy-start | bytes 73732
  0.6 9.0 %copy-start.3 = (f32[4096]{0:T(1024)S(1)}, f32[4096]{0:T(1024)}, u32[]{:S(2)}) copy-start(f32[4096]{0:T(1024)} %param.17) | copy-start | bytes 49156
  0.7 9.0 %copy-start.1 = (f32[3,4096]{1,0:T(4,128)S(1)}, f32[3,4096]{1,0:T(4,128)}, u32[]{:S(2)}) copy-start(f32[3,4096]{1,0:T(4,128)} %shape_inverse.1) | copy-start | bytes 147460
  0.7 9.0 %copy-start = (s32[3,4096]{1,0:T(4,128)S(1)}, s32[3,4096]{1,0:T(4,128)}, u32[]{:S(2)}) copy-start(s32[3,4096]{1,0:T(4,128)} %elements.1) | copy-start | bytes 147460
  0.7 13.6 %copy-start.5 = (s32[1,1,8]{2,1,0:T(1,128)S(1)}, s32[1,1,8]{2,1,0:T(1,128)}, u32[]{:S(2)}) copy-start(s32[1,1,8]{2,1,0:T(1,128)} %block_node.1) | copy-start | bytes 100
  0.7 13.6 %copy-start.4 = (s32[1,1,8]{2,1,0:T(1,128)S(1)}, s32[1,1,8]{2,1,0:T(1,128)}, u32[]{:S(2)}) copy-start(s32[1,1,8]{2,1,0:T(1,128)} %block_target.1) | copy-start | bytes 100
  0.7 5.6 %collective-permute-start = (f32[3,2048]{1,0:T(4,128)}, f32[3,2048]{1,0:T(4,128)S(1)}, u32[]{:S(2)}, u32[]{:S(2)}) collective-permute-start(f32[3,2048]{1,0:T(4,128)} %displacement.1), channel_id=1, source_target_pairs={{0,12},{4,0},{8,4},{12,8},{1,13},{5,1},{9,5},{13,9},{2,14},{6,2},{... | collective-permute-start | bytes 73736 | tf_op jit(solution)/shard_map/ppermute | solution.py:684
  4.7 12.7 %collective-permute-start.8 = (f32[21,8,256]{2,1,0:T(8,128)S(1)}, f32[21,8,256]{2,1,0:T(8,128)S(1)}, u32[]{:S(2)}, u32[]{:S(2)}) collective-permute-start(f32[21,8,256]{2,1,0:T(8,128)S(1)} %get-tuple-element.35), channel_id=1, source_target_pairs={{0,16},{4,8},{8,4},{12,28},{16,0},{20,24},{24,20},{28,12},{1,17},{... | collective-permute-start | bytes 516104 | tf_op jit(solution)/shard_map/ppermute | solution.py:702
  6.3 11.7 %collective-permute-start.9 = (f32[21,8,256]{2,1,0:T(8,128)S(1)}, f32[21,8,256]{2,1,0:T(8,128)S(1)}, u32[]{:S(2)}, u32[]{:S(2)}) collective-permute-start(f32[21,8,256]{2,1,0:T(8,128)S(1)} %get-tuple-element.36), channel_id=1, source_target_pairs={{0,4},{4,0},{8,12},{12,8},{16,20},{20,16},{24,28},{28,24},{1,5},{5... | collective-permute-start | bytes 516104 | tf_op jit(solution)/shard_map/ppermute | solution.py:702
  6.5 6.1 %collective-permute-start.1 = (f32[21,4,256]{2,1,0:T(4,128)S(1)}, f32[21,4,256]{2,1,0:T(4,128)S(1)}, u32[]{:S(2)}, u32[]{:S(2)}) collective-permute-start(f32[21,4,256]{2,1,0:T(4,128)S(1)} %get-tuple-element.28), channel_id=1, source_target_pairs={{0,4},{1,2},{2,1},{3,7},{4,0},{5,6},{6,5},{7,3},{8,12},{9,10},{10,... | collective-permute-start | bytes 258056 | tf_op jit(solution)/shard_map/ppermute | solution.py:702
  7.0 5.6 %collective-permute-start.2 = (f32[21,4,256]{2,1,0:T(4,128)S(1)}, f32[21,4,256]{2,1,0:T(4,128)S(1)}, u32[]{:S(2)}, u32[]{:S(2)}) collective-permute-start(f32[21,4,256]{2,1,0:T(4,128)S(1)} %get-tuple-element.29), channel_id=1, source_target_pairs={{0,1},{1,0},{2,3},{3,2},{4,5},{5,4},{6,7},{7,6},{8,9},{9,8},{10,11... | collective-permute-start | bytes 258056 | tf_op jit(solution)/shard_map/ppermute | solution.py:702
  12.7 9.3 %collective-permute-start.6 = (f32[9,8,256]{2,1,0:T(8,128)S(1)}, f32[9,8,256]{2,1,0:T(8,128)S(1)}, u32[]{:S(2)}, u32[]{:S(2)}) collective-permute-start(f32[9,8,256]{2,1,0:T(8,128)S(1)} %get-tuple-element.34), channel_id=1, source_target_pairs={{0,16},{4,8},{8,4},{12,28},{16,0},{20,24},{24,20},{28,12},{1,17},{... | collective-permute-start | bytes 221192 | tf_op jit(solution)/shard_map/ppermute | solution.py:702
  13.4 8.6 %collective-permute-start.7 = (f32[9,8,256]{2,1,0:T(8,128)S(1)}, f32[9,8,256]{2,1,0:T(8,128)S(1)}, u32[]{:S(2)}, u32[]{:S(2)}) collective-permute-start(f32[9,8,256]{2,1,0:T(8,128)S(1)} %get-tuple-element.33.face), channel_id=1, source_target_pairs={{0,4},{4,0},{8,12},{12,8},{16,20},{20,16},{24,28},{28,24},{1,5},{5... | collective-permute-start | bytes 221192 | tf_op jit(solution)/shard_map/ppermute | solution.py:702
  14.8 6.1 %collective-permute-start.5 = (f32[8,128]{1,0:T(8,128)S(1)}, f32[8,128]{1,0:T(8,128)S(1)}, u32[]{:S(2)}, u32[]{:S(2)}) collective-permute-start(f32[8,128]{1,0:T(8,128)S(1)} %shard_map.135.refs_1_.refs_4_), channel_id=1, source_target_pairs={{0,3},{1,2},{2,1},{3,0},{4,7},{5,6},{6,5},{7,4},{8,11},{9,10},{10,... | collective-permute-start | bytes 12296 | tf_op jit(solution)/shard_map/ppermute | solution.py:679
  17.4 4.5 %collective-permute-start.4 = (f32[8,128]{1,0:T(8,128)S(1)}, f32[8,128]{1,0:T(8,128)S(1)}, u32[]{:S(2)}, u32[]{:S(2)}) collective-permute-start(f32[8,128]{1,0:T(8,128)S(1)} %shard_map.135.refs_1_.refs_4_), channel_id=1, source_target_pairs={{0,2},{1,3},{2,0},{3,1},{4,6},{5,7},{6,4},{7,5},{8,10},{9,11},{10,... | collective-permute-start | bytes 12296 | tf_op jit(solution)/shard_map/ppermute | solution.py:679
  18.0 4.0 %collective-permute-start.3 = (f32[8,128]{1,0:T(8,128)S(1)}, f32[8,128]{1,0:T(8,128)S(1)}, u32[]{:S(2)}, u32[]{:S(2)}) collective-permute-start(f32[8,128]{1,0:T(8,128)S(1)} %shard_map.135.refs_1_.refs_4_), channel_id=1, source_target_pairs={{0,1},{1,0},{2,3},{3,2},{4,5},{5,4},{6,7},{7,6},{8,9},{9,8},{10,11... | collective-permute-start | bytes 12296 | tf_op jit(solution)/shard_map/ppermute | solution.py:679
  23.2 5.3 %collective-permute-start.10 = (f32[40,128]{1,0:T(8,128)S(1)}, f32[40,128]{1,0:T(8,128)S(1)}, u32[]{:S(2)}, u32[]{:S(2)}) collective-permute-start(f32[40,128]{1,0:T(8,128)S(1)} %get-tuple-element.44), channel_id=1, source_target_pairs={{0,1},{1,0},{2,3},{3,2},{4,5},{5,4},{6,7},{7,6},{8,9},{9,8},{10,11... | collective-permute-start | bytes 61448 | tf_op jit(solution)/shard_map/ppermute | solution.py:679
  24.2 4.9 %collective-permute-start.11 = (f32[40,128]{1,0:T(8,128)S(1)}, f32[40,128]{1,0:T(8,128)S(1)}, u32[]{:S(2)}, u32[]{:S(2)}) collective-permute-start(f32[40,128]{1,0:T(8,128)S(1)} %get-tuple-element.45), channel_id=1, source_target_pairs={{0,2},{1,3},{2,0},{3,1},{4,6},{5,7},{6,4},{7,5},{8,10},{9,11},{10,... | collective-permute-start | bytes 61448 | tf_op jit(solution)/shard_map/ppermute | solution.py:679
  25.4 5.6 %collective-permute-start.12 = (f32[40,128]{1,0:T(8,128)S(1)}, f32[40,128]{1,0:T(8,128)S(1)}, u32[]{:S(2)}, u32[]{:S(2)}) collective-permute-start(f32[40,128]{1,0:T(8,128)S(1)} %get-tuple-element.46), channel_id=1, source_target_pairs={{0,3},{1,2},{2,1},{3,0},{4,7},{5,6},{6,5},{7,4},{8,11},{9,10},{10,... | collective-permute-start | bytes 61448 | tf_op jit(solution)/shard_map/ppermute | solution.py:679

commit v9 on v7

--- a/solution.py
+++ b/solution.py
@@ -330,7 +330,7 @@
     walls_in,
     second_in,
     out,
-    message,
+    message_all,
     walls,
     second,
     both,
@@ -342,6 +342,7 @@
     sems,
 ):
     del walls_in, second_in
+    message = message_all.at[0]
     copies = [
         pltpu.make_async_copy(block_source_hbm, block_source, sems.at[0]),
         pltpu.make_async_copy(block_target_hbm, block_target, sems.at[1]),
@@ -464,6 +465,8 @@
             message[start + at : start + at + rows] = (
                 internal_own[part, :, lanes] + both[0, FORCE_SLOT + part, :, lanes]
             )
+    for other in range(1, message_all.shape[0]):
+        message_all[other] = message[...]
 
 
 def element_kernel(
@@ -593,13 +596,12 @@
     store.wait()
 
 
-def final_kernel(count, *refs):
-    messages = refs[:count]
-    residual, motion, keys = refs[count:]
+def final_kernel(arrived, residual, motion, keys):
     slots = keys.shape[0]
     node_blocks = residual.shape[1] // BLK
     inner = lax.axis_index("inner")
-    mine = messages[0]
+    messages = [arrived.at[i] for i in range(arrived.shape[0])]
+    mine = arrived.at[inner]
     for k in range(slots):
         keys[k : k + 1] = mine[4 * k + 3 : 4 * k + 4]
     wanted = keys[...]
@@ -616,11 +618,9 @@
                 row = message[4 * k + part : 4 * k + part + 1]
                 external[part] = external[part] + jnp.where(here, row, 0.0)
                 moved[part] = moved[part] + jnp.where(same, row, 0.0)
-    for step, message in enumerate(messages):
-        sender = partner_of(inner, step, count)
+    for sender, message in enumerate(messages):
         for b in range(node_blocks):
-            key = jnp.broadcast_to(sender * node_blocks + b, (1, BLK)).astype(F32)
-            same = wanted == key
+            same = wanted == float(sender * node_blocks + b)
             for part in range(3):
                 at = 4 * slots + part * node_blocks + b
                 moved[part] = moved[part] - jnp.where(same, message[at : at + 1], 0.0)
@@ -648,17 +648,6 @@
             flops=0, bytes_accessed=int(micros * 3.6e6), transcendentals=0
         ),
     )(*operands)
-
-
-def partner_of(at, step, count):
-    if count & (count - 1) == 0:
-        return at ^ step
-    return (at + count - step) % count
-
-
-def exchange(block, axis, step):
-    count = lax.axis_size(axis)
-    return lax.ppermute(block, axis, [(partner_of(i, step, count), i) for i in range(count)])
 
 
 def around(block, axis, step):
@@ -791,7 +780,7 @@
     lines = 4 * slots + 3 * node_blocks
     values, message, _, _ = call(
         second_kernel,
-        (whole, shape(lines, BLK), walls_shape, second_shape),
+        (whole, shape(count, lines, BLK), walls_shape, second_shape),
         (
             pin(block_source),
             pin(block_target),
@@ -820,7 +809,7 @@
         ),
         micros=1.5,
     )
-    messages = [message] + [exchange(message, "inner", step) for step in range(1, count)]
+    messages = lax.all_to_all(message, "inner", split_axis=0, concat_axis=0, tiled=False)
     (populations_out,) = call(
         store_kernel,
         (whole,),
@@ -831,10 +820,10 @@
         micros=1.0,
     )
     residual, motion = call(
-        functools.partial(final_kernel, count),
+        final_kernel,
         (shape(3, node_dev), shape(3, slots, BLK)),
-        messages,
-        (vmem,) * count,
+        (messages,),
+        (vmem,),
         scratch=(pltpu.VMEM((slots, BLK), F32),),
         micros=0.8,
     )

time: 26.9 us -> 30 us (1.12)
  waiting for transfers between devices: 3.77 us -> 6.85 us
  Pallas kernels: 8.92 us -> 9.55 us
  starting transfers between devices: 12.6 us -> 12 us
    all_to_all x0 -> x1, waiting for transfers between devices: none -> 5.5 us  [shards(): lax.all_to_all(message, 'inner', split_axis=0, concat_axis=0, tiled=False)]
    ppermute x3 -> x0, starting transfers between devices: 4.45 us -> none  [exchange(): lax.ppermute(block, axis, [(partner_of(i, step, count), i) for i in range...]
    all_to_all x0 -> x1, starting transfers between devices: none -> 3.83 us  [shards(): lax.all_to_all(message, 'inner', split_axis=0, concat_axis=0, tiled=False)]
    ppermute x3 -> x0, waiting for transfers between devices: 2.42 us -> none  [exchange(): lax.ppermute(block, axis, [(partner_of(i, step, count), i) for i in range...]
    pallas_call x10, Pallas kernels: 8.92 us -> 9.55 us  [call(): pl.pallas_call(kernel, out_shape=outs, in_specs=[spec(space) for space in...]
  transfers between devices with their start and end apart: 10 -> 8, of which waited for: 5 -> 3; matrix products, arithmetic and copies ran while one was open for 0% -> 0% of each run, Pallas kernels for 26% -> 24%
where the time goes in v9:
time: 30 us; the launch traced here: 29.8 us
  starting transfers between devices  12 us (40%)
  Pallas kernels  9.55 us (32%)
  waiting for transfers between devices  6.85 us (23%)
  between operations  1.41 us (5%)
    pallas_call x10, Pallas kernels, call(): pl.pallas_call(kernel, out_shape=outs, in_specs=[spec(space) for space in...  9.55 us
    all_to_all x1, waiting for transfers between devices, shards(): lax.all_to_all(message, 'inner', split_axis=0, concat_axis=0, tiled=False)  5.5 us
    all_to_all x1, starting transfers between devices, shards(): lax.all_to_all(message, 'inner', split_axis=0, concat_axis=0, tiled=False)  3.83 us
    ppermute x3, starting transfers between devices, swap(): lax.ppermute(near, axes, routes[0])  2.86 us
    ppermute x3, starting transfers between devices, swap(): lax.ppermute(far, axes, routes[1])  2.82 us
    ppermute x1, starting transfers between devices, around(): lax.ppermute(block, axis, [(i, (i + step) % count) for i in range(count)])  2.46 us
    ppermute x3, waiting for transfers between devices, swap(): lax.ppermute(far, axes, routes[1])  1.28 us
  transfers between devices with their start and end apart: 8, of which 3 were waited for; matrix products, arithmetic and copies ran while one was open for 0% of the time, Pallas kernels for 24%

profile of v9, /device:TPU:0, one launch (start us, length us, event | category | flops | bytes accessed | tf_op | source)
XLA Modules:
  0.0 29.8 jit_solution(5441575685958961591)
XLA Ops:
  0.6 0.0 copy-start.2
  0.6 0.0 copy-start.3
  0.7 0.0 copy-start.1
  0.7 0.0 copy-start
  0.7 2.5 %collective-permute-start = (f32[3,2048]{1,0:T(4,128)}, f32[3,2048]{1,0:T(4,128)S(1)}, u32[]{:S(2)}, u32[]{:S(2)}) collective-permute-start(f32[3,2048]{1,0:T(4,128)} %displacement.1), channel_id=1, source_target_pairs={{0,12},{4,0},{8,4},{12,8},{1,13},{5,1},{9,5},{13,9},{2,14},{6,2},{... | collective-permute-start | bytes 73736 | tf_op jit(solution)/shard_map/ppermute | solution.py:655
  3.1 1.6 %shard_map.130 = (f32[19,4,8,256]{3,2,1,0:T(8,128)S(1)}, f32[2,4,8,256]{3,2,1,0:T(8,128)S(1)}, f32[21,8,256]{2,1,0:T(8,128)S(1)}, f32[21,8,256]{2,1,0:T(8,128)S(1)}) custom-call(f32[19,4,8,256]{3,2,1,0:T(8,128)} %pops_hbm.1, f32[4,8,256]{2,1,0:T(8,128)} %rate_hbm.1, s32[4,8,256]{2,1,0:T(8,128)} %flags_hbm.1), custom_call_target="tpu_custom_call" | custom-call | bytes 5400000 | tf_op jit(solution)/shard_map/pallas_call | solution.py:639
  4.7 1.6 %collective-permute-start.5 = (f32[21,8,256]{2,1,0:T(8,128)S(1)}, f32[21,8,256]{2,1,0:T(8,128)S(1)}, u32[]{:S(2)}, u32[]{:S(2)}) collective-permute-start(f32[21,8,256]{2,1,0:T(8,128)S(1)} %get-tuple-element.32), channel_id=1, source_target_pairs={{0,16},{4,8},{8,4},{12,28},{16,0},{20,24},{24,20},{28,12},{1,17},{... | collective-permute-start | bytes 516104 | tf_op jit(solution)/shard_map/ppermute | solution.py:673
  6.3 0.0 collective-permute-start.6
  6.3 0.0 collective-permute-done.next_nodes
  6.3 0.2 shard_map.131
  6.4 0.6 %collective-permute-start.1 = (f32[21,4,256]{2,1,0:T(4,128)S(1)}, f32[21,4,256]{2,1,0:T(4,128)S(1)}, u32[]{:S(2)}, u32[]{:S(2)}) collective-permute-start(f32[21,4,256]{2,1,0:T(4,128)S(1)} %get-tuple-element.25), channel_id=1, source_target_pairs={{0,4},{1,2},{2,1},{3,7},{4,0},{5,6},{6,5},{7,3},{8,12},{9,10},{10,... | collective-permute-start | bytes 258056 | tf_op jit(solution)/shard_map/ppermute | solution.py:673
  7.0 2.6 %collective-permute-start.2 = (f32[21,4,256]{2,1,0:T(4,128)S(1)}, f32[21,4,256]{2,1,0:T(4,128)S(1)}, u32[]{:S(2)}, u32[]{:S(2)}) collective-permute-start(f32[21,4,256]{2,1,0:T(4,128)S(1)} %get-tuple-element.26), channel_id=1, source_target_pairs={{0,1},{1,0},{2,3},{3,2},{4,5},{5,4},{6,7},{7,6},{8,9},{9,8},{10,11... | collective-permute-start | bytes 258056 | tf_op jit(solution)/shard_map/ppermute | solution.py:673
  9.7 0.0 copy-done.2
  9.7 0.0 copy-done.3
  9.7 0.0 copy-done.1
  9.7 0.0 copy-done
  9.7 1.7 %shard_map.132 = (f32[3,32,128]{2,1,0:T(8,128)S(1)}, f32[3,32,128]{2,1,0:T(8,128)S(1)}, f32[6,3,32,128]{3,2,1,0:T(8,128)S(1)}) custom-call(s32[3,4096]{1,0:T(4,128)S(1)} %copy-done, f32[3,2048]{1,0:T(4,128)S(1)} %copy-done.2, f32[3,2048]{1,0:T(4,128)S(1)} %collective-permute-done.next_nodes, f32[3,4096]{1,0:T(4,128)S(1)} %copy-done.1, f32[32,128]{1,0:T(8,128)S(1)} %bitcast.4), custom_call_target="tpu_custom_call" | custom-call | bytes 7200000 | tf_op jit(solution)/shard_map/pallas_call | solution.py:639
  11.4 1.1 %shard_map.133.other = f32[3,8,256]{2,1,0:T(8,128)S(1)} custom-call(f32[3,32,128]{2,1,0:T(8,128)S(1)} %get-tuple-element.27.low_ids, f32[3,32,128]{2,1,0:T(8,128)S(1)} %get-tuple-element.28.high_ids, f32[6,3,32,128]{3,2,1,0:T(8,128)S(1)} %get-tuple-element.29.forces), custom_call_target="tpu_custom_call" | custom-call | bytes 2880000 | tf_op jit(solution)/shard_map/pallas_call | solution.py:639
  12.5 0.0 collective-permute-done.1.far_y
  12.5 0.1 collective-permute-done.2.near_y
  12.6 0.1 shard_map.134
  12.7 0.7 %collective-permute-start.3 = (f32[9,8,256]{2,1,0:T(8,128)S(1)}, f32[9,8,256]{2,1,0:T(8,128)S(1)}, u32[]{:S(2)}, u32[]{:S(2)}) collective-permute-start(f32[9,8,256]{2,1,0:T(8,128)S(1)} %get-tuple-element.30), channel_id=1, source_target_pairs={{0,16},{4,8},{8,4},{12,28},{16,0},{20,24},{24,20},{28,12},{1,17},{... | collective-permute-start | bytes 221192 | tf_op jit(solution)/shard_map/ppermute | solution.py:673
  13.4 0.2 collective-permute-start.4
  14.2 1.1 %shard_map.136.internal_own = f32[3,8,256]{2,1,0:T(8,128)S(1)} custom-call(f32[3,32,128]{2,1,0:T(8,128)S(1)} %get-tuple-element.27.low_ids, f32[3,32,128]{2,1,0:T(8,128)S(1)} %get-tuple-element.28.high_ids, f32[6,3,32,128]{3,2,1,0:T(8,128)S(1)} %get-tuple-element.29.forces), custom_call_target="tpu_custom_call" | custom-call | bytes 2880000 | tf_op jit(solution)/shard_map/pallas_call | solution.py:639
  15.3 0.0 collective-permute-done.5.far_x
  15.4 0.0 collective-permute-done.6.near_x
  15.4 0.5 %shard_map.135 = (f32[19,8,8,256]{3,2,1,0:T(8,128)S(1)}, f32[2,21,8,256]{3,2,1,0:T(8,128)S(1)}, f32[2,5,8,256]{3,2,1,0:T(8,128)S(1)}, f32[19,6,8,256]{3,2,1,0:T(8,128)S(1)}, f32[2,2,8,256]{3,2,1,0:T(8,128)S(1)}) custom-call(f32[19,4,8,256]{3,2,1,0:T(8,128)S(1)} %get-tuple-element.23.c1, f32[2,4,8,256]{3,2,1,0:T(8,128)S(1)} %get-tuple-element.24.fixed, ...), custom_call_target="tpu_custom_call" | custom-call | bytes 2880000 | tf_op jit(solution)/shard_map/pallas_call | solution.py:639
  15.9 1.2 %collective-permute-done.3.far = f32[9,8,256]{2,1,0:T(8,128)S(1)} collective-permute-done((f32[9,8,256]{2,1,0:T(8,128)S(1)}, f32[9,8,256]{2,1,0:T(8,128)S(1)}, u32[]{:S(2)}, u32[]{:S(2)}) %collective-permute-start.3) | collective-permute-done | bytes 73760 | tf_op jit(solution)/shard_map/ppermute | solution.py:673
  17.1 0.0 collective-permute-done.4.near
  17.1 1.8 %shard_map.137 = (f32[19,4,8,256]{3,2,1,0:T(8,128)S(1)}, f32[4,80,128]{2,1,0:T(8,128)}, f32[2,21,8,256]{3,2,1,0:T(8,128)S(1)}, f32[19,6,8,256]{3,2,1,0:T(8,128)S(1)}) custom-call(s32[1,1,8]{2,1,0:T(1,128)} %block_source_hbm.1, s32[1,1,8]{2,1,0:T(1,128)} %block_target_hbm.1, ...), custom_call_target="tpu_custom_call", output_to_operand_aliasing={{2}: (11, {}), {3}: (12, {})} | custom-call | bytes 5400000 | tf_op jit(solution)/shard_map/pallas_call | solution.py:639
  18.8 3.8 %all-to-all-start = ((f32[4,80,128]{2,1,0:T(8,128)}), f32[4,80,128]{2,1,0:T(8,128)S(1)}, u32[]{:S(2)}, u32[]{:S(2)}) async-start(f32[4,80,128]{2,1,0:T(8,128)} %get-tuple-element.40), calls=%async_computation | async-start | bytes 327680 | tf_op jit(solution)/shard_map/all_to_all | solution.py:812
  22.7 0.8 %shard_map.138 = f32[19,4,8,256]{3,2,1,0:T(8,128)} custom-call(f32[19,4,8,256]{3,2,1,0:T(8,128)S(1)} %get-tuple-element.39.values), custom_call_target="tpu_custom_call" | custom-call | bytes 3600000 | tf_op jit(solution)/shard_map/pallas_call | solution.py:639
  23.5 5.5 %all-to-all-done.arrived = f32[4,80,128]{2,1,0:T(8,128)S(1)} async-done(((f32[4,80,128]{2,1,0:T(8,128)}), f32[4,80,128]{2,1,0:T(8,128)S(1)}, u32[]{:S(2)}, u32[]{:S(2)}) %all-to-all-start) | async-done | bytes 163872 | tf_op jit(solution)/shard_map/all_to_all | solution.py:812
  29.0 0.8 %shard_map.139 = (f32[3,2048]{1,0:T(4,128)}, f32[3,8,128]{2,1,0:T(8,128)}) custom-call(f32[4,80,128]{2,1,0:T(8,128)S(1)} %all-to-all-done.arrived), custom_call_target="tpu_custom_call" | custom-call | bytes 2880000 | tf_op jit(solution)/shard_map/pallas_call | solution.py:639
Async XLA Ops:
  0.6 9.0 %copy-start.2 = (f32[3,2048]{1,0:T(4,128)S(1)}, f32[3,2048]{1,0:T(4,128)}, u32[]{:S(2)}) copy-start(f32[3,2048]{1,0:T(4,128)} %displacement.1) | copy-start | bytes 73732
  0.6 9.0 %copy-start.3 = (f32[4096]{0:T(1024)S(1)}, f32[4096]{0:T(1024)}, u32[]{:S(2)}) copy-start(f32[4096]{0:T(1024)} %param.17) | copy-start | bytes 49156
  0.7 9.0 %copy-start.1 = (f32[3,4096]{1,0:T(4,128)S(1)}, f32[3,4096]{1,0:T(4,128)}, u32[]{:S(2)}) copy-start(f32[3,4096]{1,0:T(4,128)} %shape_inverse.1) | copy-start | bytes 147460
  0.7 9.0 %copy-start = (s32[3,4096]{1,0:T(4,128)S(1)}, s32[3,4096]{1,0:T(4,128)}, u32[]{:S(2)}) copy-start(s32[3,4096]{1,0:T(4,128)} %elements.1) | copy-start | bytes 147460
  0.7 5.6 %collective-permute-start = (f32[3,2048]{1,0:T(4,128)}, f32[3,2048]{1,0:T(4,128)S(1)}, u32[]{:S(2)}, u32[]{:S(2)}) collective-permute-start(f32[3,2048]{1,0:T(4,128)} %displacement.1), channel_id=1, source_target_pairs={{0,12},{4,0},{8,4},{12,8},{1,13},{5,1},{9,5},{13,9},{2,14},{6,2},{... | collective-permute-start | bytes 73736 | tf_op jit(solution)/shard_map/ppermute | solution.py:655
  4.7 10.6 %collective-permute-start.5 = (f32[21,8,256]{2,1,0:T(8,128)S(1)}, f32[21,8,256]{2,1,0:T(8,128)S(1)}, u32[]{:S(2)}, u32[]{:S(2)}) collective-permute-start(f32[21,8,256]{2,1,0:T(8,128)S(1)} %get-tuple-element.32), channel_id=1, source_target_pairs={{0,16},{4,8},{8,4},{12,28},{16,0},{20,24},{24,20},{28,12},{1,17},{... | collective-permute-start | bytes 516104 | tf_op jit(solution)/shard_map/ppermute | solution.py:673
  6.3 9.1 %collective-permute-start.6 = (f32[21,8,256]{2,1,0:T(8,128)S(1)}, f32[21,8,256]{2,1,0:T(8,128)S(1)}, u32[]{:S(2)}, u32[]{:S(2)}) collective-permute-start(f32[21,8,256]{2,1,0:T(8,128)S(1)} %get-tuple-element.33), channel_id=1, source_target_pairs={{0,4},{4,0},{8,12},{12,8},{16,20},{20,16},{24,28},{28,24},{1,5},{5... | collective-permute-start | bytes 516104 | tf_op jit(solution)/shard_map/ppermute | solution.py:673
  6.4 6.1 %collective-permute-start.1 = (f32[21,4,256]{2,1,0:T(4,128)S(1)}, f32[21,4,256]{2,1,0:T(4,128)S(1)}, u32[]{:S(2)}, u32[]{:S(2)}) collective-permute-start(f32[21,4,256]{2,1,0:T(4,128)S(1)} %get-tuple-element.25), channel_id=1, source_target_pairs={{0,4},{1,2},{2,1},{3,7},{4,0},{5,6},{6,5},{7,3},{8,12},{9,10},{10,... | collective-permute-start | bytes 258056 | tf_op jit(solution)/shard_map/ppermute | solution.py:673
  7.0 5.6 %collective-permute-start.2 = (f32[21,4,256]{2,1,0:T(4,128)S(1)}, f32[21,4,256]{2,1,0:T(4,128)S(1)}, u32[]{:S(2)}, u32[]{:S(2)}) collective-permute-start(f32[21,4,256]{2,1,0:T(4,128)S(1)} %get-tuple-element.26), channel_id=1, source_target_pairs={{0,1},{1,0},{2,3},{3,2},{4,5},{5,4},{6,7},{7,6},{8,9},{9,8},{10,11... | collective-permute-start | bytes 258056 | tf_op jit(solution)/shard_map/ppermute | solution.py:673
  12.7 4.4 %collective-permute-start.3 = (f32[9,8,256]{2,1,0:T(8,128)S(1)}, f32[9,8,256]{2,1,0:T(8,128)S(1)}, u32[]{:S(2)}, u32[]{:S(2)}) collective-permute-start(f32[9,8,256]{2,1,0:T(8,128)S(1)} %get-tuple-element.30), channel_id=1, source_target_pairs={{0,16},{4,8},{8,4},{12,28},{16,0},{20,24},{24,20},{28,12},{1,17},{... | collective-permute-start | bytes 221192 | tf_op jit(solution)/shard_map/ppermute | solution.py:673
  13.4 3.7 %collective-permute-start.4 = (f32[9,8,256]{2,1,0:T(8,128)S(1)}, f32[9,8,256]{2,1,0:T(8,128)S(1)}, u32[]{:S(2)}, u32[]{:S(2)}) collective-permute-start(f32[9,8,256]{2,1,0:T(8,128)S(1)} %get-tuple-element.31), channel_id=1, source_target_pairs={{0,4},{4,0},{8,12},{12,8},{16,20},{20,16},{24,28},{28,24},{1,5},{5... | collective-permute-start | bytes 221192 | tf_op jit(solution)/shard_map/ppermute | solution.py:673
  18.8 10.2 %all-to-all-start = ((f32[4,80,128]{2,1,0:T(8,128)}), f32[4,80,128]{2,1,0:T(8,128)S(1)}, u32[]{:S(2)}, u32[]{:S(2)}) async-start(f32[4,80,128]{2,1,0:T(8,128)} %get-tuple-element.40), calls=%async_computation | async-start | bytes 327680 | tf_op jit(solution)/shard_map/all_to_all | solution.py:812

commit v10 on v7

--- a/solution.py
+++ b/solution.py
@@ -39,6 +39,7 @@
 FLAG_SLOT = 19
 RATE_SLOT = 20
 SLOTS = 21
+SIDE_SLOTS = 24
 FORCE_SLOT = 6
 CORNER_SLOTS = FORCE_SLOT + 3
 PIECES = 2
@@ -138,7 +139,7 @@
 def first_kernel(
     pops_hbm, rate_hbm, flags_hbm, c1, fixed, far, near, pops, rate, flags, sems
 ):
-    planes = c1.shape[1]
+    planes, rows = c1.shape[1], c1.shape[2]
     copies = [
         pltpu.make_async_copy(rate_hbm, rate, sems.at[planes]),
         pltpu.make_async_copy(flags_hbm, flags, sems.at[planes + 1]),
@@ -165,43 +166,6 @@
     lax.fori_loop(0, planes, plane, 0)
 
     def pack(out, sign, outside):
-        for slot, (q, depth) in enumerate(face_slots(0, sign)):
-            out[slot] = c1[q, planes - 1 - depth if sign > 0 else depth]
-        end = planes - 1 if sign > 0 else 0
-        out[FLAG_SLOT] = fixed[0, end]
-        out[RATE_SLOT] = fixed[1, end]
-        clear_outside(out, outside)
-
-    pack_pair(pack, "slab", near, far)
-
-
-def clear_outside(out, outside):
-    @pl.when(outside)
-    def _():
-        out[...] = jnp.zeros(out.shape, F32)
-
-
-def pack_pair(pack, axis, near, far):
-    at = lax.axis_index(axis)
-    even = lax.rem(at, 2) == 0
-    first, last = at == 0, at == lax.axis_size(axis) - 1
-
-    @pl.when(even)
-    def _():
-        pack(near, 1, last)
-        pack(far, -1, first)
-
-    @pl.when(jnp.logical_not(even))
-    def _():
-        pack(near, -1, first)
-        pack(far, 1, last)
-
-
-def side_kernel(c1, fixed, next_nodes, far, near):
-    del next_nodes
-    planes, rows = c1.shape[1], c1.shape[2]
-
-    def pack(out, sign, outside):
         def line(x, carry):
             for slot, (q, depth) in enumerate(face_slots(1, sign)):
                 y = rows - 1 - depth if sign > 0 else depth
@@ -212,9 +176,48 @@
             return carry
 
         lax.fori_loop(0, planes, line, 0)
+        for slot in range(SLOTS, SIDE_SLOTS):
+            out[slot] = jnp.zeros(out.shape[1:], F32)
         clear_outside(out, outside)
 
     pack_pair(pack, "inner", near, far)
+
+
+def clear_outside(out, outside):
+    @pl.when(outside)
+    def _():
+        out[...] = jnp.zeros(out.shape, F32)
+
+
+def pack_pair(pack, axis, near, far):
+    at = lax.axis_index(axis)
+    even = lax.rem(at, 2) == 0
+    first, last = at == 0, at == lax.axis_size(axis) - 1
+
+    @pl.when(even)
+    def _():
+        pack(near, 1, last)
+        pack(far, -1, first)
+
+    @pl.when(jnp.logical_not(even))
+    def _():
+        pack(near, -1, first)
+        pack(far, 1, last)
+
+
+def slab_face_kernel(c1, fixed, numbers, far, near):
+    del numbers
+    planes = c1.shape[1]
+
+    def pack(out, sign, outside):
+        for slot, (q, depth) in enumerate(face_slots(0, sign)):
+            out[slot] = c1[q, planes - 1 - depth if sign > 0 else depth]
+        end = planes - 1 if sign > 0 else 0
+        out[FLAG_SLOT] = fixed[0, end]
+        out[RATE_SLOT] = fixed[1, end]
+        clear_outside(out, outside)
+
+    pack_pair(pack, "slab", near, far)
 
 
 def gather_both(near, far, both, axis):
@@ -709,12 +712,12 @@
     vmem, hbm, smem = pltpu.VMEM, pltpu.HBM, pltpu.SMEM
 
     next_nodes = around(displacement, "slab", -1)
-    face_y = shape(SLOTS, planes, length)
+    face_y = shape(SIDE_SLOTS, planes, length)
     face_x = shape(SLOTS, rows, length)
     pin = lambda block: pltpu.with_memory_space_constraint(block, hbm)
     c1, fixed, far, near = call(
         first_kernel,
-        (whole, shape(2, planes, rows, length), face_x, face_x),
+        (whole, shape(2, planes, rows, length), face_y, face_y),
         (pin(populations), pin(relaxation), pin(node_flags)),
         (hbm,) * 3,
         scratch=(
@@ -724,10 +727,6 @@
             pltpu.SemaphoreType.DMA((planes + 2,)),
         ),
         micros=1.5,
-    )
-    near_x, far_x = swap(near, far, "slab", "group")
-    far, near = call(
-        side_kernel, (face_y, face_y), (c1, fixed, next_nodes), (vmem,) * 3, micros=0.3
     )
     near_y, far_y = swap(near, far, "inner", "slab")
     numbers = shape(3, runs, BLK)
@@ -741,15 +740,19 @@
             pltpu.VMEM((3, runs, BLK), jnp.int32),
             pltpu.VMEM((3, 3, runs, BLK), F32),
         ),
-        micros=2.0,
-    )
+        micros=0.001,
+    )
+    far, near = call(
+        slab_face_kernel, (face_x, face_x), (c1, fixed, low_ids), (vmem,) * 3, micros=0.001
+    )
+    near_x, far_x = swap(near, far, "slab", "group")
     nodal = shape(3, node_blocks // half, length)
     (other,) = call(
         functools.partial(spread_kernel, node_blocks),
         (nodal,),
         (low_ids, high_ids, forces),
         (vmem,) * 3,
-        micros=0.8,
+        micros=0.001,
     )
     corner = shape(CORNER_SLOTS, rows, length)
     far, near = call(

time: 26.9 us -> 29.6 us (1.10)
  local copies, waits for them, and re-layouts: 0.02 us -> 3.15 us
  waiting for transfers between devices: 3.77 us -> 3.38 us
    unnamed x8, local copies, waits for them, and re-layouts: 0.02 us -> 3.15 us
    ppermute x3, waiting for transfers between devices: 2.42 us -> 1.92 us  [exchange(): lax.ppermute(block, axis, [(partner_of(i, step, count), i) for i in range...]
    ppermute x3, starting transfers between devices: 2.82 us -> 2.38 us  [swap(): lax.ppermute(far, axes, routes[1])]
  transfers between devices with their start and end apart: 10 -> 10, of which waited for: 5 -> 4; matrix products, arithmetic and copies ran while one was open for 0% -> 0% of each run, Pallas kernels for 26% -> 24%
where the time goes in v10:
time: 29.6 us; the launch traced here: 29.3 us
  starting transfers between devices  12.4 us (42%)
  Pallas kernels  8.92 us (30%)
  waiting for transfers between devices  3.38 us (11%)
  local copies, waits for them, and re-layouts  3.15 us (11%)
  between operations  1.38 us (5%)
    pallas_call x10, Pallas kernels, call(): pl.pallas_call(kernel, out_shape=outs, in_specs=[spec(space) for space in...  8.92 us
    ppermute x3, starting transfers between devices, exchange(): lax.ppermute(block, axis, [(partner_of(i, step, count), i) for i in range...  4.45 us
    unnamed x8, local copies, waits for them, and re-layouts  3.15 us
    ppermute x3, starting transfers between devices, swap(): lax.ppermute(near, axes, routes[0])  3.14 us
    ppermute x1, starting transfers between devices, around(): lax.ppermute(block, axis, [(i, (i + step) % count) for i in range(count)])  2.46 us
    ppermute x3, starting transfers between devices, swap(): lax.ppermute(far, axes, routes[1])  2.38 us
    ppermute x3, waiting for transfers between devices, exchange(): lax.ppermute(block, axis, [(partner_of(i, step, count), i) for i in range...  1.92 us
    ppermute x3, waiting for transfers between devices, swap(): lax.ppermute(far, axes, routes[1])  1.45 us
  transfers between devices with their start and end apart: 10, of which 4 were waited for; matrix products, arithmetic and copies ran while one was open for 0% of the time, Pallas kernels for 24%

profile of v10, /device:TPU:0, one launch (start us, length us, event | category | flops | bytes accessed | tf_op | source)
XLA Modules:
  0.0 29.3 jit_solution(7807578908065777861)
XLA Ops:
  0.6 2.5 %collective-permute-start.2 = (f32[3,2048]{1,0:T(4,128)}, f32[3,2048]{1,0:T(4,128)S(1)}, u32[]{:S(2)}, u32[]{:S(2)}) collective-permute-start(f32[3,2048]{1,0:T(4,128)} %displacement.1), channel_id=1, source_target_pairs={{0,12},{4,0},{8,4},{12,8},{1,13},{5,1},{9,5},{13,9},{2,14},{6,2},{... | collective-permute-start | bytes 73736 | tf_op jit(solution)/shard_map/ppermute | solution.py:669
  3.1 1.7 %shard_map.130 = (f32[19,4,8,256]{3,2,1,0:T(8,128)S(1)}, f32[2,4,8,256]{3,2,1,0:T(8,128)S(1)}, f32[24,4,256]{2,1,0:T(4,128)S(1)}, f32[24,4,256]{2,1,0:T(4,128)S(1)}) custom-call(f32[19,4,8,256]{3,2,1,0:T(8,128)} %pops_hbm.1, f32[4,8,256]{2,1,0:T(8,128)} %rate_hbm.1, s32[4,8,256]{2,1,0:T(8,128)} %flags_hbm.1), custom_call_target="tpu_custom_call" | custom-call | bytes 5400000 | tf_op jit(solution)/shard_map/pallas_call | solution.py:642
  4.8 0.1 collective-permute-start
  4.9 3.1 %collective-permute-start.1 = (f32[24,4,256]{2,1,0:T(4,128)S(1)}, f32[24,4,256]{2,1,0:T(4,128)S(1)}, u32[]{:S(2)}, u32[]{:S(2)}) collective-permute-start(f32[24,4,256]{2,1,0:T(4,128)S(1)} %get-tuple-element.24), channel_id=1, source_target_pairs={{0,1},{1,0},{2,3},{3,2},{4,5},{5,4},{6,7},{7,6},{8,9},{9,8},{10,11... | collective-permute-start | bytes 294920 | tf_op jit(solution)/shard_map/ppermute | solution.py:687
  8.0 0.0 collective-permute-done.2.next_nodes
  8.0 0.0 copy-start
  8.0 0.8 %copy-done = s32[3,4096]{1,0:T(4,128)S(1)} copy-done((s32[3,4096]{1,0:T(4,128)S(1)}, s32[3,4096]{1,0:T(4,128)}, u32[]{:S(2)}) %copy-start) | copy-done | bytes 49176
  8.8 0.0 copy-start.1
  8.9 0.8 %copy-done.1 = f32[3,4096]{1,0:T(4,128)S(1)} copy-done((f32[3,4096]{1,0:T(4,128)S(1)}, f32[3,4096]{1,0:T(4,128)}, u32[]{:S(2)}) %copy-start.1) | copy-done | bytes 49176
  9.7 0.0 copy-start.2
  9.7 0.8 %copy-done.2 = f32[3,2048]{1,0:T(4,128)S(1)} copy-done((f32[3,2048]{1,0:T(4,128)S(1)}, f32[3,2048]{1,0:T(4,128)}, u32[]{:S(2)}) %copy-start.2) | copy-done | bytes 24600
  10.4 0.0 copy-start.3
  10.4 0.7 %copy-done.3 = f32[4096]{0:T(1024)S(1)} copy-done((f32[4096]{0:T(1024)S(1)}, f32[4096]{0:T(1024)}, u32[]{:S(2)}) %copy-start.3) | copy-done | bytes 16408
  11.2 1.7 %shard_map.131 = (f32[3,32,128]{2,1,0:T(8,128)S(1)}, f32[3,32,128]{2,1,0:T(8,128)S(1)}, f32[6,3,32,128]{3,2,1,0:T(8,128)S(1)}) custom-call(s32[3,4096]{1,0:T(4,128)S(1)} %copy-done, f32[3,2048]{1,0:T(4,128)S(1)} %copy-done.2, f32[3,2048]{1,0:T(4,128)S(1)} %collective-permute-done.2.next_nodes, f32[3,4096]{1,0:T(4,128)S(1)} %copy-done.1, f32[32,128]{1,0:T(8,128)S(1)} %bitcast.4), custom_call_target="tpu_custom_call" | custom-call | bytes 3600 | tf_op jit(solution)/shard_map/pallas_call | solution.py:642
  12.9 0.1 shard_map.134
  12.9 1.6 %collective-permute-start.5 = (f32[21,8,256]{2,1,0:T(8,128)S(1)}, f32[21,8,256]{2,1,0:T(8,128)S(1)}, u32[]{:S(2)}, u32[]{:S(2)}) collective-permute-start(f32[21,8,256]{2,1,0:T(8,128)S(1)} %get-tuple-element.32), channel_id=1, source_target_pairs={{0,16},{4,8},{8,4},{12,28},{16,0},{20,24},{24,20},{28,12},{1,17},{... | collective-permute-start | bytes 516104 | tf_op jit(solution)/shard_map/ppermute | solution.py:687
  14.5 0.0 collective-permute-start.6
  14.5 1.1 %shard_map.132.other = f32[3,8,256]{2,1,0:T(8,128)S(1)} custom-call(f32[3,32,128]{2,1,0:T(8,128)S(1)} %get-tuple-element.25.low_ids.numbers, f32[3,32,128]{2,1,0:T(8,128)S(1)} %get-tuple-element.26.high_ids, f32[6,3,32,128]{3,2,1,0:T(8,128)S(1)} %get-tuple-element.27.forces), custom_call_target="tpu_custom_call" | custom-call | bytes 3600 | tf_op jit(solution)/shard_map/pallas_call | solution.py:642
  15.6 0.0 collective-permute-done.far_y
  15.6 0.0 collective-permute-done.1.near_y
  15.6 0.1 shard_map.133
  15.7 0.8 %collective-permute-start.3 = (f32[9,8,256]{2,1,0:T(8,128)S(1)}, f32[9,8,256]{2,1,0:T(8,128)S(1)}, u32[]{:S(2)}, u32[]{:S(2)}) collective-permute-start(f32[9,8,256]{2,1,0:T(8,128)S(1)} %get-tuple-element.28), channel_id=1, source_target_pairs={{0,16},{4,8},{8,4},{12,28},{16,0},{20,24},{24,20},{28,12},{1,17},{... | collective-permute-start | bytes 221192 | tf_op jit(solution)/shard_map/ppermute | solution.py:687
  16.5 0.0 collective-permute-start.4
  17.1 1.1 %shard_map.136.internal_own = f32[3,8,256]{2,1,0:T(8,128)S(1)} custom-call(f32[3,32,128]{2,1,0:T(8,128)S(1)} %get-tuple-element.25.low_ids.numbers, f32[3,32,128]{2,1,0:T(8,128)S(1)} %get-tuple-element.26.high_ids, f32[6,3,32,128]{3,2,1,0:T(8,128)S(1)} %get-tuple-element.27.forces), custom_call_target="tpu_custom_call" | custom-call | bytes 2880000 | tf_op jit(solution)/shard_map/pallas_call | solution.py:642
  18.2 0.2 collective-permute-done.5.far_x
  18.4 0.0 collective-permute-done.6.near_x
  18.4 0.5 %shard_map.135 = (f32[19,8,8,256]{3,2,1,0:T(8,128)S(1)}, f32[2,21,8,256]{3,2,1,0:T(8,128)S(1)}, f32[2,5,8,256]{3,2,1,0:T(8,128)S(1)}, f32[19,6,8,256]{3,2,1,0:T(8,128)S(1)}, f32[2,2,8,256]{3,2,1,0:T(8,128)S(1)}) custom-call(f32[19,4,8,256]{3,2,1,0:T(8,128)S(1)} %get-tuple-element.31.c1, f32[2,4,8,256]{3,2,1,0:T(8,128)S(1)} %get-tuple-element.30.fixed, ...), custom_call_target="tpu_custom_call" | custom-call | bytes 2880000 | tf_op jit(solution)/shard_map/pallas_call | solution.py:642
  18.9 1.2 %collective-permute-done.3.far = f32[9,8,256]{2,1,0:T(8,128)S(1)} collective-permute-done((f32[9,8,256]{2,1,0:T(8,128)S(1)}, f32[9,8,256]{2,1,0:T(8,128)S(1)}, u32[]{:S(2)}, u32[]{:S(2)}) %collective-permute-start.3) | collective-permute-done | bytes 73760 | tf_op jit(solution)/shard_map/ppermute | solution.py:687
  20.1 0.0 collective-permute-done.4.near
  20.1 1.1 %shard_map.137 = (f32[19,4,8,256]{3,2,1,0:T(8,128)S(1)}, f32[80,128]{1,0:T(8,128)S(1)}, f32[2,21,8,256]{3,2,1,0:T(8,128)S(1)}, f32[19,6,8,256]{3,2,1,0:T(8,128)S(1)}) custom-call(s32[1,1,8]{2,1,0:T(1,128)} %block_source_hbm.1, s32[1,1,8]{2,1,0:T(1,128)} %block_target_hbm.1, ...), custom_call_target="tpu_custom_call", output_to_operand_aliasing={{2}: (11, {}), {3}: (12, {})} | custom-call | bytes 5400000 | tf_op jit(solution)/shard_map/pallas_call | solution.py:642
  21.2 1.4 %collective-permute-start.9 = (f32[80,128]{1,0:T(8,128)S(1)}, f32[80,128]{1,0:T(8,128)S(1)}, u32[]{:S(2)}, u32[]{:S(2)}) collective-permute-start(f32[80,128]{1,0:T(8,128)S(1)} %get-tuple-element.40.refs_0_), channel_id=1, source_target_pairs={{3,0},{2,1},{1,2},{0,3},{7,4},{6,5},{5,6},{4,7},{11,8},{10,9},{9,1... | collective-permute-start | bytes 122888 | tf_op jit(solution)/shard_map/ppermute | solution.py:664
  22.7 0.1 collective-permute-start.8
  22.8 2.9 %collective-permute-start.7 = (f32[80,128]{1,0:T(8,128)S(1)}, f32[80,128]{1,0:T(8,128)S(1)}, u32[]{:S(2)}, u32[]{:S(2)}) collective-permute-start(f32[80,128]{1,0:T(8,128)S(1)} %get-tuple-element.40.refs_0_), channel_id=1, source_target_pairs={{1,0},{0,1},{3,2},{2,3},{5,4},{4,5},{7,6},{6,7},{9,8},{8,9},{11,10... | collective-permute-start | bytes 122888 | tf_op jit(solution)/shard_map/ppermute | solution.py:664
  25.7 0.8 %shard_map.138 = f32[19,4,8,256]{3,2,1,0:T(8,128)} custom-call(f32[19,4,8,256]{3,2,1,0:T(8,128)S(1)} %get-tuple-element.39.values), custom_call_target="tpu_custom_call" | custom-call | bytes 3600000 | tf_op jit(solution)/shard_map/pallas_call | solution.py:642
  26.5 0.7 %collective-permute-done.9.refs_3_ = f32[80,128]{1,0:T(8,128)S(1)} collective-permute-done((f32[80,128]{1,0:T(8,128)S(1)}, f32[80,128]{1,0:T(8,128)S(1)}, u32[]{:S(2)}, u32[]{:S(2)}) %collective-permute-start.9) | collective-permute-done | bytes 40992 | tf_op jit(solution)/shard_map/ppermute | solution.py:664
  27.2 1.2 %collective-permute-done.8.refs_2_ = f32[80,128]{1,0:T(8,128)S(1)} collective-permute-done((f32[80,128]{1,0:T(8,128)S(1)}, f32[80,128]{1,0:T(8,128)S(1)}, u32[]{:S(2)}, u32[]{:S(2)}) %collective-permute-start.8) | collective-permute-done | bytes 40992 | tf_op jit(solution)/shard_map/ppermute | solution.py:664
  28.5 0.0 collective-permute-done.7.refs_1_
  28.5 0.8 %shard_map.139 = (f32[3,2048]{1,0:T(4,128)}, f32[3,8,128]{2,1,0:T(8,128)}) custom-call(f32[80,128]{1,0:T(8,128)S(1)} %get-tuple-element.40.refs_0_, f32[80,128]{1,0:T(8,128)S(1)} %collective-permute-done.7.refs_1_, f32[80,128]{1,0:T(8,128)S(1)} %collective-permute-done.8.refs_2_, f32[80,128]{1,0:T(8,128)S(1)} %collective-permute-done.9.refs_3_), custom_call_target="tpu_custom_call" | custom-call | bytes 2880000 | tf_op jit(solution)/shard_map/pallas_call | solution.py:642
Async XLA Ops:
  0.6 7.4 %collective-permute-start.2 = (f32[3,2048]{1,0:T(4,128)}, f32[3,2048]{1,0:T(4,128)S(1)}, u32[]{:S(2)}, u32[]{:S(2)}) collective-permute-start(f32[3,2048]{1,0:T(4,128)} %displacement.1), channel_id=1, source_target_pairs={{0,12},{4,0},{8,4},{12,8},{1,13},{5,1},{9,5},{13,9},{2,14},{6,2},{... | collective-permute-start | bytes 73736 | tf_op jit(solution)/shard_map/ppermute | solution.py:669
  4.8 10.8 %collective-permute-start = (f32[24,4,256]{2,1,0:T(4,128)S(1)}, f32[24,4,256]{2,1,0:T(4,128)S(1)}, u32[]{:S(2)}, u32[]{:S(2)}) collective-permute-start(f32[24,4,256]{2,1,0:T(4,128)S(1)} %get-tuple-element.23), channel_id=1, source_target_pairs={{0,4},{1,2},{2,1},{3,7},{4,0},{5,6},{6,5},{7,3},{8,12},{9,10},{10,... | collective-permute-start | bytes 294920 | tf_op jit(solution)/shard_map/ppermute | solution.py:687
  4.9 10.8 %collective-permute-start.1 = (f32[24,4,256]{2,1,0:T(4,128)S(1)}, f32[24,4,256]{2,1,0:T(4,128)S(1)}, u32[]{:S(2)}, u32[]{:S(2)}) collective-permute-start(f32[24,4,256]{2,1,0:T(4,128)S(1)} %get-tuple-element.24), channel_id=1, source_target_pairs={{0,1},{1,0},{2,3},{3,2},{4,5},{5,4},{6,7},{7,6},{8,9},{9,8},{10,11... | collective-permute-start | bytes 294920 | tf_op jit(solution)/shard_map/ppermute | solution.py:687
  8.0 0.8 %copy-start = (s32[3,4096]{1,0:T(4,128)S(1)}, s32[3,4096]{1,0:T(4,128)}, u32[]{:S(2)}) copy-start(s32[3,4096]{1,0:T(4,128)} %elements.1) | copy-start | bytes 147460
  8.8 0.8 %copy-start.1 = (f32[3,4096]{1,0:T(4,128)S(1)}, f32[3,4096]{1,0:T(4,128)}, u32[]{:S(2)}) copy-start(f32[3,4096]{1,0:T(4,128)} %shape_inverse.1) | copy-start | bytes 147460
  9.7 0.8 %copy-start.2 = (f32[3,2048]{1,0:T(4,128)S(1)}, f32[3,2048]{1,0:T(4,128)}, u32[]{:S(2)}) copy-start(f32[3,2048]{1,0:T(4,128)} %displacement.1) | copy-start | bytes 73732
  10.4 0.7 %copy-start.3 = (f32[4096]{0:T(1024)S(1)}, f32[4096]{0:T(1024)}, u32[]{:S(2)}) copy-start(f32[4096]{0:T(1024)} %param.17) | copy-start | bytes 49156
  12.9 5.5 %collective-permute-start.5 = (f32[21,8,256]{2,1,0:T(8,128)S(1)}, f32[21,8,256]{2,1,0:T(8,128)S(1)}, u32[]{:S(2)}, u32[]{:S(2)}) collective-permute-start(f32[21,8,256]{2,1,0:T(8,128)S(1)} %get-tuple-element.32), channel_id=1, source_target_pairs={{0,16},{4,8},{8,4},{12,28},{16,0},{20,24},{24,20},{28,12},{1,17},{... | collective-permute-start | bytes 516104 | tf_op jit(solution)/shard_map/ppermute | solution.py:687
  14.5 3.9 %collective-permute-start.6 = (f32[21,8,256]{2,1,0:T(8,128)S(1)}, f32[21,8,256]{2,1,0:T(8,128)S(1)}, u32[]{:S(2)}, u32[]{:S(2)}) collective-permute-start(f32[21,8,256]{2,1,0:T(8,128)S(1)} %get-tuple-element.33), channel_id=1, source_target_pairs={{0,4},{4,0},{8,12},{12,8},{16,20},{20,16},{24,28},{28,24},{1,5},{5... | collective-permute-start | bytes 516104 | tf_op jit(solution)/shard_map/ppermute | solution.py:687
  15.7 4.4 %collective-permute-start.3 = (f32[9,8,256]{2,1,0:T(8,128)S(1)}, f32[9,8,256]{2,1,0:T(8,128)S(1)}, u32[]{:S(2)}, u32[]{:S(2)}) collective-permute-start(f32[9,8,256]{2,1,0:T(8,128)S(1)} %get-tuple-element.28), channel_id=1, source_target_pairs={{0,16},{4,8},{8,4},{12,28},{16,0},{20,24},{24,20},{28,12},{1,17},{... | collective-permute-start | bytes 221192 | tf_op jit(solution)/shard_map/ppermute | solution.py:687
  16.5 3.7 %collective-permute-start.4 = (f32[9,8,256]{2,1,0:T(8,128)S(1)}, f32[9,8,256]{2,1,0:T(8,128)S(1)}, u32[]{:S(2)}, u32[]{:S(2)}) collective-permute-start(f32[9,8,256]{2,1,0:T(8,128)S(1)} %get-tuple-element.29), channel_id=1, source_target_pairs={{0,4},{4,0},{8,12},{12,8},{16,20},{20,16},{24,28},{28,24},{1,5},{5... | collective-permute-start | bytes 221192 | tf_op jit(solution)/shard_map/ppermute | solution.py:687
  21.2 6.0 %collective-permute-start.9 = (f32[80,128]{1,0:T(8,128)S(1)}, f32[80,128]{1,0:T(8,128)S(1)}, u32[]{:S(2)}, u32[]{:S(2)}) collective-permute-start(f32[80,128]{1,0:T(8,128)S(1)} %get-tuple-element.40.refs_0_), channel_id=1, source_target_pairs={{3,0},{2,1},{1,2},{0,3},{7,4},{6,5},{5,6},{4,7},{11,8},{10,9},{9,1... | collective-permute-start | bytes 122888 | tf_op jit(solution)/shard_map/ppermute | solution.py:664
  22.7 5.8 %collective-permute-start.8 = (f32[80,128]{1,0:T(8,128)S(1)}, f32[80,128]{1,0:T(8,128)S(1)}, u32[]{:S(2)}, u32[]{:S(2)}) collective-permute-start(f32[80,128]{1,0:T(8,128)S(1)} %get-tuple-element.40.refs_0_), channel_id=1, source_target_pairs={{2,0},{3,1},{0,2},{1,3},{6,4},{7,5},{4,6},{5,7},{10,8},{11,9},{8,1... | collective-permute-start | bytes 122888 | tf_op jit(solution)/shard_map/ppermute | solution.py:664
  22.8 5.7 %collective-permute-start.7 = (f32[80,128]{1,0:T(8,128)S(1)}, f32[80,128]{1,0:T(8,128)S(1)}, u32[]{:S(2)}, u32[]{:S(2)}) collective-permute-start(f32[80,128]{1,0:T(8,128)S(1)} %get-tuple-element.40.refs_0_), channel_id=1, source_target_pairs={{1,0},{0,1},{3,2},{2,3},{5,4},{4,5},{7,6},{6,7},{9,8},{8,9},{11,10... | collective-permute-start | bytes 122888 | tf_op jit(solution)/shard_map/ppermute | solution.py:664

commit v11 on v10

--- a/solution.py
+++ b/solution.py
@@ -137,7 +137,25 @@
 
 
 def first_kernel(
-    pops_hbm, rate_hbm, flags_hbm, c1, fixed, far, near, pops, rate, flags, sems
+    pops_hbm,
+    rate_hbm,
+    flags_hbm,
+    displacement_hbm,
+    elements_hbm,
+    shape_hbm,
+    stiffness_hbm,
+    c1,
+    fixed,
+    far,
+    near,
+    displacement,
+    elements,
+    shape_inverse,
+    stiffness,
+    pops,
+    rate,
+    flags,
+    sems,
 ):
     planes, rows = c1.shape[1], c1.shape[2]
     copies = [
@@ -147,7 +165,18 @@
     loads = [
         pltpu.make_async_copy(pops_hbm.at[:, x], pops.at[x], sems.at[x]) for x in range(planes)
     ]
-    for copy in loads[:1] + copies + loads[1:]:
+    shell = [
+        pltpu.make_async_copy(source, target, sems.at[planes + 2 + k])
+        for k, (source, target) in enumerate(
+            (
+                (displacement_hbm, displacement),
+                (elements_hbm, elements),
+                (shape_hbm, shape_inverse),
+                (stiffness_hbm, stiffness),
+            )
+        )
+    ]
+    for copy in loads[:1] + copies + loads[1:] + shell:
         copy.start()
     for copy in copies:
         copy.wait()
@@ -181,6 +210,8 @@
         clear_outside(out, outside)
 
     pack_pair(pack, "inner", near, far)
+    for copy in shell:
+        copy.wait()
 
 
 def clear_outside(out, outside):
@@ -373,17 +404,13 @@
                 source = 3 * side + row // 8
                 walls[side, row, at : at + 1] = both[end, source, row % 8 : row % 8 + 1]
 
-    def edge_plane(end, carry):
+    def edge_planes(end, carry):
         x = end * (planes - 1)
         store_plane(extended, walls, second, x + 1, fixed[1, x], fixed[0, x])
-        return carry
-
-    def outside_plane(end, carry):
         store_plane(extended, walls, second, end * (planes + 1), ends[end, 1], ends[end, 0])
         return carry
 
-    lax.fori_loop(0, 2, edge_plane, 0)
-    lax.fori_loop(0, 2, outside_plane, 0)
+    lax.fori_loop(0, 2, edge_planes, 0)
 
     @pl.when(slab == 0)
     def _():
@@ -715,16 +742,24 @@
     face_y = shape(SIDE_SLOTS, planes, length)
     face_x = shape(SLOTS, rows, length)
     pin = lambda block: pltpu.with_memory_space_constraint(block, hbm)
-    c1, fixed, far, near = call(
+    whole_like = lambda block: jax.ShapeDtypeStruct(block.shape, block.dtype)
+    shell = (displacement, elements, shape_inverse, stiffness.reshape(runs, BLK))
+    c1, fixed, far, near, own_nodes, corners, inverses, stiff = call(
         first_kernel,
-        (whole, shape(2, planes, rows, length), face_y, face_y),
-        (pin(populations), pin(relaxation), pin(node_flags)),
-        (hbm,) * 3,
+        (
+            whole,
+            shape(2, planes, rows, length),
+            face_y,
+            face_y,
+            *(whole_like(block) for block in shell),
+        ),
+        tuple(pin(block) for block in (populations, relaxation, node_flags, *shell)),
+        (hbm,) * 7,
         scratch=(
             pltpu.VMEM((planes, Q, rows, length), F32),
             pltpu.VMEM((planes, rows, length), F32),
             pltpu.VMEM((planes, rows, length), jnp.int32),
-            pltpu.SemaphoreType.DMA((planes + 2,)),
+            pltpu.SemaphoreType.DMA((planes + 6,)),
         ),
         micros=1.5,
     )
@@ -733,7 +768,7 @@
     low_ids, high_ids, forces = call(
         element_kernel,
         (numbers, numbers, shape(3 * PIECES, 3, runs, BLK)),
-        (elements, displacement, next_nodes, shape_inverse, stiffness.reshape(runs, BLK)),
+        (corners, own_nodes, next_nodes, inverses, stiff),
         (vmem,) * 5,
         scratch=(
             pltpu.VMEM((3, runs, BLK), F32),

time: 29.6 us -> 26.1 us (0.88)
  local copies, waits for them, and re-layouts: 3.15 us -> 0 us
    unnamed x8 -> x0, local copies, waits for them, and re-layouts: 3.15 us -> none
  transfers between devices with their start and end apart: 10 -> 10, of which waited for: 4 -> 4; matrix products, arithmetic and copies ran while one was open for 0% -> 0% of each run, Pallas kernels for 24% -> 27%
where the time goes in v11:
time: 26.1 us; the launch traced here: 26 us
  starting transfers between devices  12.4 us (48%)
  Pallas kernels  8.81 us (34%)
  waiting for transfers between devices  3.38 us (13%)
  between operations  1.37 us (5%)
    pallas_call x10, Pallas kernels, call(): pl.pallas_call(kernel, out_shape=outs, in_specs=[spec(space) for space in...  8.81 us
    ppermute x3, starting transfers between devices, exchange(): lax.ppermute(block, axis, [(partner_of(i, step, count), i) for i in range...  4.45 us
    ppermute x3, starting transfers between devices, swap(): lax.ppermute(near, axes, routes[0])  3.14 us
    ppermute x1, starting transfers between devices, around(): lax.ppermute(block, axis, [(i, (i + step) % count) for i in range(count)])  2.46 us
    ppermute x3, starting transfers between devices, swap(): lax.ppermute(far, axes, routes[1])  2.37 us
    ppermute x3, waiting for transfers between devices, exchange(): lax.ppermute(block, axis, [(partner_of(i, step, count), i) for i in range...  1.92 us
    ppermute x3, waiting for transfers between devices, swap(): lax.ppermute(far, axes, routes[1])  1.45 us
  transfers between devices with their start and end apart: 10, of which 4 were waited for; matrix products, arithmetic and copies ran while one was open for 0% of the time, Pallas kernels for 27%

profile of v11, /device:TPU:0, one launch (start us, length us, event | category | flops | bytes accessed | tf_op | source)
XLA Modules:
  0.0 26.0 jit_solution(15741849464919333889)
XLA Ops:
  0.6 2.5 %collective-permute-start.2 = (f32[3,2048]{1,0:T(4,128)}, f32[3,2048]{1,0:T(4,128)S(1)}, u32[]{:S(2)}, u32[]{:S(2)}) collective-permute-start(f32[3,2048]{1,0:T(4,128)} %displacement_hbm.1), channel_id=1, source_target_pairs={{0,12},{4,0},{8,4},{12,8},{1,13},{5,1},{9,5},{13,9},{2,14},{6,2},{... | collective-permute-start | bytes 73736 | tf_op jit(solution)/shard_map/ppermute | solution.py:696
  3.1 1.7 %shard_map.130 = (f32[19,4,8,256]{3,2,1,0:T(8,128)S(1)}, f32[2,4,8,256]{3,2,1,0:T(8,128)S(1)}, f32[24,4,256]{2,1,0:T(4,128)S(1)}, f32[24,4,256]{2,1,0:T(4,128)S(...) custom-call(f32[19,4,8,256]{3,2,1,0:T(8,128)} %pops_hbm.1, ...), custom_call_target="tpu_custom_call" | custom-call | bytes 5400000 | tf_op jit(solution)/shard_map/pallas_call | solution.py:669
  4.8 0.1 collective-permute-start
  4.9 3.1 %collective-permute-start.1 = (f32[24,4,256]{2,1,0:T(4,128)S(1)}, f32[24,4,256]{2,1,0:T(4,128)S(1)}, u32[]{:S(2)}, u32[]{:S(2)}) collective-permute-start(f32[24,4,256]{2,1,0:T(4,128)S(1)} %get-tuple-element.28), channel_id=1, source_target_pairs={{0,1},{1,0},{2,3},{3,2},{4,5},{5,4},{6,7},{7,6},{8,9},{9,8},{10,11... | collective-permute-start | bytes 294920 | tf_op jit(solution)/shard_map/ppermute | solution.py:714
  8.0 0.0 collective-permute-done.2.next_nodes
  8.0 1.7 %shard_map.131 = (f32[3,32,128]{2,1,0:T(8,128)S(1)}, f32[3,32,128]{2,1,0:T(8,128)S(1)}, f32[6,3,32,128]{3,2,1,0:T(8,128)S(1)}) custom-call(s32[3,4096]{1,0:T(4,128)S(1)} %get-tuple-element.29.elements, f32[3,2048]{1,0:T(4,128)S(1)} %get-tuple-element.30.displacement, f32[3,2048]{1,0:T(4,128)S(1)} %collective-permute-done.2.next_nodes, ...), custom_call_target="tpu_custom_call" | custom-call | bytes 3600 | tf_op jit(solution)/shard_map/pallas_call | solution.py:669
  9.8 0.1 shard_map.134
  9.8 1.6 %collective-permute-start.5 = (f32[21,8,256]{2,1,0:T(8,128)S(1)}, f32[21,8,256]{2,1,0:T(8,128)S(1)}, u32[]{:S(2)}, u32[]{:S(2)}) collective-permute-start(f32[21,8,256]{2,1,0:T(8,128)S(1)} %get-tuple-element.40), channel_id=1, source_target_pairs={{0,16},{4,8},{8,4},{12,28},{16,0},{20,24},{24,20},{28,12},{1,17},{... | collective-permute-start | bytes 516104 | tf_op jit(solution)/shard_map/ppermute | solution.py:714
  11.4 0.0 collective-permute-start.6
  11.4 1.1 %shard_map.132.other = f32[3,8,256]{2,1,0:T(8,128)S(1)} custom-call(f32[3,32,128]{2,1,0:T(8,128)S(1)} %get-tuple-element.33.low_ids.numbers, f32[3,32,128]{2,1,0:T(8,128)S(1)} %get-tuple-element.34.high_ids, f32[6,3,32,128]{3,2,1,0:T(8,128)S(1)} %get-tuple-element.35.forces), custom_call_target="tpu_custom_call" | custom-call | bytes 3600 | tf_op jit(solution)/shard_map/pallas_call | solution.py:669
  12.5 0.0 collective-permute-done.far_y
  12.5 0.0 collective-permute-done.1.near_y
  12.5 0.1 shard_map.133
  12.6 0.7 %collective-permute-start.3 = (f32[9,8,256]{2,1,0:T(8,128)S(1)}, f32[9,8,256]{2,1,0:T(8,128)S(1)}, u32[]{:S(2)}, u32[]{:S(2)}) collective-permute-start(f32[9,8,256]{2,1,0:T(8,128)S(1)} %get-tuple-element.36), channel_id=1, source_target_pairs={{0,16},{4,8},{8,4},{12,28},{16,0},{20,24},{24,20},{28,12},{1,17},{... | collective-permute-start | bytes 221192 | tf_op jit(solution)/shard_map/ppermute | solution.py:714
  13.4 0.0 collective-permute-start.4
  14.0 1.1 %shard_map.136.internal_own = f32[3,8,256]{2,1,0:T(8,128)S(1)} custom-call(f32[3,32,128]{2,1,0:T(8,128)S(1)} %get-tuple-element.33.low_ids.numbers, f32[3,32,128]{2,1,0:T(8,128)S(1)} %get-tuple-element.34.high_ids, f32[6,3,32,128]{3,2,1,0:T(8,128)S(1)} %get-tuple-element.35.forces), custom_call_target="tpu_custom_call" | custom-call | bytes 2880000 | tf_op jit(solution)/shard_map/pallas_call | solution.py:669
  15.1 0.2 collective-permute-done.5.far_x
  15.3 0.0 collective-permute-done.6.near_x
  15.3 0.5 %shard_map.135 = (f32[19,8,8,256]{3,2,1,0:T(8,128)S(1)}, f32[2,21,8,256]{3,2,1,0:T(8,128)S(1)}, f32[2,5,8,256]{3,2,1,0:T(8,128)S(1)}, f32[19,6,8,256]{3,2,1,0:T(8,128)S(1)}, f32[2,2,8,256]{3,2,1,0:T(8,128)S(1)}) custom-call(f32[19,4,8,256]{3,2,1,0:T(8,128)S(1)} %get-tuple-element.39.c1, f32[2,4,8,256]{3,2,1,0:T(8,128)S(1)} %get-tuple-element.38.fixed, ...), custom_call_target="tpu_custom_call" | custom-call | bytes 2880000 | tf_op jit(solution)/shard_map/pallas_call | solution.py:669
  15.8 1.2 %collective-permute-done.3.far = f32[9,8,256]{2,1,0:T(8,128)S(1)} collective-permute-done((f32[9,8,256]{2,1,0:T(8,128)S(1)}, f32[9,8,256]{2,1,0:T(8,128)S(1)}, u32[]{:S(2)}, u32[]{:S(2)}) %collective-permute-start.3) | collective-permute-done | bytes 73760 | tf_op jit(solution)/shard_map/ppermute | solution.py:714
  17.0 0.0 collective-permute-done.4.near
  17.0 0.9 %shard_map.137 = (f32[19,4,8,256]{3,2,1,0:T(8,128)S(1)}, f32[80,128]{1,0:T(8,128)S(1)}, f32[2,21,8,256]{3,2,1,0:T(8,128)S(1)}, f32[19,6,8,256]{3,2,1,0:T(8,128)S(1)}) custom-call(s32[1,1,8]{2,1,0:T(1,128)} %block_source_hbm.1, s32[1,1,8]{2,1,0:T(1,128)} %block_target_hbm.1, ...), custom_call_target="tpu_custom_call", output_to_operand_aliasing={{2}: (11, {}), {3}: (12, {})} | custom-call | bytes 5400000 | tf_op jit(solution)/shard_map/pallas_call | solution.py:669
  18.0 1.4 %collective-permute-start.9 = (f32[80,128]{1,0:T(8,128)S(1)}, f32[80,128]{1,0:T(8,128)S(1)}, u32[]{:S(2)}, u32[]{:S(2)}) collective-permute-start(f32[80,128]{1,0:T(8,128)S(1)} %get-tuple-element.48.refs_0_), channel_id=1, source_target_pairs={{3,0},{2,1},{1,2},{0,3},{7,4},{6,5},{5,6},{4,7},{11,8},{10,9},{9,1... | collective-permute-start | bytes 122888 | tf_op jit(solution)/shard_map/ppermute | solution.py:691
  19.4 0.3 collective-permute-start.8
  19.6 2.8 %collective-permute-start.7 = (f32[80,128]{1,0:T(8,128)S(1)}, f32[80,128]{1,0:T(8,128)S(1)}, u32[]{:S(2)}, u32[]{:S(2)}) collective-permute-start(f32[80,128]{1,0:T(8,128)S(1)} %get-tuple-element.48.refs_0_), channel_id=1, source_target_pairs={{1,0},{0,1},{3,2},{2,3},{5,4},{4,5},{7,6},{6,7},{9,8},{8,9},{11,10... | collective-permute-start | bytes 122888 | tf_op jit(solution)/shard_map/ppermute | solution.py:691
  22.4 0.8 %shard_map.138 = f32[19,4,8,256]{3,2,1,0:T(8,128)} custom-call(f32[19,4,8,256]{3,2,1,0:T(8,128)S(1)} %get-tuple-element.47.values), custom_call_target="tpu_custom_call" | custom-call | bytes 3600000 | tf_op jit(solution)/shard_map/pallas_call | solution.py:669
  23.3 0.7 %collective-permute-done.9.refs_3_ = f32[80,128]{1,0:T(8,128)S(1)} collective-permute-done((f32[80,128]{1,0:T(8,128)S(1)}, f32[80,128]{1,0:T(8,128)S(1)}, u32[]{:S(2)}, u32[]{:S(2)}) %collective-permute-start.9) | collective-permute-done | bytes 40992 | tf_op jit(solution)/shard_map/ppermute | solution.py:691
  24.0 1.2 %collective-permute-done.8.refs_2_ = f32[80,128]{1,0:T(8,128)S(1)} collective-permute-done((f32[80,128]{1,0:T(8,128)S(1)}, f32[80,128]{1,0:T(8,128)S(1)}, u32[]{:S(2)}, u32[]{:S(2)}) %collective-permute-start.8) | collective-permute-done | bytes 40992 | tf_op jit(solution)/shard_map/ppermute | solution.py:691
  25.2 0.0 collective-permute-done.7.refs_1_
  25.2 0.8 %shard_map.139 = (f32[3,2048]{1,0:T(4,128)}, f32[3,8,128]{2,1,0:T(8,128)}) custom-call(f32[80,128]{1,0:T(8,128)S(1)} %get-tuple-element.48.refs_0_, f32[80,128]{1,0:T(8,128)S(1)} %collective-permute-done.7.refs_1_, f32[80,128]{1,0:T(8,128)S(1)} %collective-permute-done.8.refs_2_, f32[80,128]{1,0:T(8,128)S(1)} %collective-permute-done.9.refs_3_), custom_call_target="tpu_custom_call" | custom-call | bytes 2880000 | tf_op jit(solution)/shard_map/pallas_call | solution.py:669
Async XLA Ops:
  0.6 7.4 %collective-permute-start.2 = (f32[3,2048]{1,0:T(4,128)}, f32[3,2048]{1,0:T(4,128)S(1)}, u32[]{:S(2)}, u32[]{:S(2)}) collective-permute-start(f32[3,2048]{1,0:T(4,128)} %displacement_hbm.1), channel_id=1, source_target_pairs={{0,12},{4,0},{8,4},{12,8},{1,13},{5,1},{9,5},{13,9},{2,14},{6,2},{... | collective-permute-start | bytes 73736 | tf_op jit(solution)/shard_map/ppermute | solution.py:696
  4.8 7.7 %collective-permute-start = (f32[24,4,256]{2,1,0:T(4,128)S(1)}, f32[24,4,256]{2,1,0:T(4,128)S(1)}, u32[]{:S(2)}, u32[]{:S(2)}) collective-permute-start(f32[24,4,256]{2,1,0:T(4,128)S(1)} %get-tuple-element.27), channel_id=1, source_target_pairs={{0,4},{1,2},{2,1},{3,7},{4,0},{5,6},{6,5},{7,3},{8,12},{9,10},{10,... | collective-permute-start | bytes 294920 | tf_op jit(solution)/shard_map/ppermute | solution.py:714
  4.9 7.6 %collective-permute-start.1 = (f32[24,4,256]{2,1,0:T(4,128)S(1)}, f32[24,4,256]{2,1,0:T(4,128)S(1)}, u32[]{:S(2)}, u32[]{:S(2)}) collective-permute-start(f32[24,4,256]{2,1,0:T(4,128)S(1)} %get-tuple-element.28), channel_id=1, source_target_pairs={{0,1},{1,0},{2,3},{3,2},{4,5},{5,4},{6,7},{7,6},{8,9},{9,8},{10,11... | collective-permute-start | bytes 294920 | tf_op jit(solution)/shard_map/ppermute | solution.py:714
  9.8 5.5 %collective-permute-start.5 = (f32[21,8,256]{2,1,0:T(8,128)S(1)}, f32[21,8,256]{2,1,0:T(8,128)S(1)}, u32[]{:S(2)}, u32[]{:S(2)}) collective-permute-start(f32[21,8,256]{2,1,0:T(8,128)S(1)} %get-tuple-element.40), channel_id=1, source_target_pairs={{0,16},{4,8},{8,4},{12,28},{16,0},{20,24},{24,20},{28,12},{1,17},{... | collective-permute-start | bytes 516104 | tf_op jit(solution)/shard_map/ppermute | solution.py:714
  11.4 3.9 %collective-permute-start.6 = (f32[21,8,256]{2,1,0:T(8,128)S(1)}, f32[21,8,256]{2,1,0:T(8,128)S(1)}, u32[]{:S(2)}, u32[]{:S(2)}) collective-permute-start(f32[21,8,256]{2,1,0:T(8,128)S(1)} %get-tuple-element.41), channel_id=1, source_target_pairs={{0,4},{4,0},{8,12},{12,8},{16,20},{20,16},{24,28},{28,24},{1,5},{5... | collective-permute-start | bytes 516104 | tf_op jit(solution)/shard_map/ppermute | solution.py:714
  12.6 4.4 %collective-permute-start.3 = (f32[9,8,256]{2,1,0:T(8,128)S(1)}, f32[9,8,256]{2,1,0:T(8,128)S(1)}, u32[]{:S(2)}, u32[]{:S(2)}) collective-permute-start(f32[9,8,256]{2,1,0:T(8,128)S(1)} %get-tuple-element.36), channel_id=1, source_target_pairs={{0,16},{4,8},{8,4},{12,28},{16,0},{20,24},{24,20},{28,12},{1,17},{... | collective-permute-start | bytes 221192 | tf_op jit(solution)/shard_map/ppermute | solution.py:714
  13.4 3.7 %collective-permute-start.4 = (f32[9,8,256]{2,1,0:T(8,128)S(1)}, f32[9,8,256]{2,1,0:T(8,128)S(1)}, u32[]{:S(2)}, u32[]{:S(2)}) collective-permute-start(f32[9,8,256]{2,1,0:T(8,128)S(1)} %get-tuple-element.37), channel_id=1, source_target_pairs={{0,4},{4,0},{8,12},{12,8},{16,20},{20,16},{24,28},{28,24},{1,5},{5... | collective-permute-start | bytes 221192 | tf_op jit(solution)/shard_map/ppermute | solution.py:714
  18.0 6.0 %collective-permute-start.9 = (f32[80,128]{1,0:T(8,128)S(1)}, f32[80,128]{1,0:T(8,128)S(1)}, u32[]{:S(2)}, u32[]{:S(2)}) collective-permute-start(f32[80,128]{1,0:T(8,128)S(1)} %get-tuple-element.48.refs_0_), channel_id=1, source_target_pairs={{3,0},{2,1},{1,2},{0,3},{7,4},{6,5},{5,6},{4,7},{11,8},{10,9},{9,1... | collective-permute-start | bytes 122888 | tf_op jit(solution)/shard_map/ppermute | solution.py:691
  19.4 5.8 %collective-permute-start.8 = (f32[80,128]{1,0:T(8,128)S(1)}, f32[80,128]{1,0:T(8,128)S(1)}, u32[]{:S(2)}, u32[]{:S(2)}) collective-permute-start(f32[80,128]{1,0:T(8,128)S(1)} %get-tuple-element.48.refs_0_), channel_id=1, source_target_pairs={{2,0},{3,1},{0,2},{1,3},{6,4},{7,5},{4,6},{5,7},{10,8},{11,9},{8,1... | collective-permute-start | bytes 122888 | tf_op jit(solution)/shard_map/ppermute | solution.py:691
  19.6 5.5 %collective-permute-start.7 = (f32[80,128]{1,0:T(8,128)S(1)}, f32[80,128]{1,0:T(8,128)S(1)}, u32[]{:S(2)}, u32[]{:S(2)}) collective-permute-start(f32[80,128]{1,0:T(8,128)S(1)} %get-tuple-element.48.refs_0_), channel_id=1, source_target_pairs={{1,0},{0,1},{3,2},{2,3},{5,4},{4,5},{7,6},{6,7},{9,8},{8,9},{11,10... | collective-permute-start | bytes 122888 | tf_op jit(solution)/shard_map/ppermute | solution.py:691

commit v12 on v11

--- a/solution.py
+++ b/solution.py
@@ -43,6 +43,7 @@
 FORCE_SLOT = 6
 CORNER_SLOTS = FORCE_SLOT + 3
 PIECES = 2
+STEP = 4
 F32 = jnp.float32
 VMEM_BYTES = 48 * 1024 * 1024
 
@@ -476,6 +477,8 @@
         copy.wait()
     node_blocks = internal_own.shape[1] * half
     live = jnp.broadcast_to(block_count[...], (1, BLK))
+    lanes_of = lax.broadcasted_iota(jnp.int32, (1, BLK), 1) // (BLK // slots)
+    all_keys = jnp.full((1, BLK), -1, jnp.int32)
     for k in range(slots):
         run = block_source[0, 0, k]
         x = run // (rows * half)
@@ -483,15 +486,16 @@
         y = left // half
         piece = left - y * half
         for part in range(3):
-            message[4 * k + part : 4 * k + part + 1] = loads[x * half + piece, part, pl.ds(y, 1)]
+            message[3 * k + part] = loads[x * half + piece, part, pl.ds(y, 1)]
         key = block_target[0, 0, k] * node_blocks + block_node[0, 0, k]
-        message[4 * k + 3 : 4 * k + 4] = jnp.where(live > k, key, -1).astype(F32)
+        all_keys = jnp.where((lanes_of == k) & (live > k), key, all_keys)
+    message[3 * slots] = all_keys.astype(F32)
     for part in range(3):
-        start = 4 * slots + part * node_blocks
+        start = 3 * slots + 1 + part * node_blocks
         for piece in range(half):
             at = piece * rows
             lanes = slice(piece * BLK, (piece + 1) * BLK)
-            message[start + at : start + at + rows] = (
+            message[start + at : start + at + rows, 0] = (
                 internal_own[part, :, lanes] + both[0, FORCE_SLOT + part, :, lanes]
             )
 
@@ -592,22 +596,24 @@
 
     total = None
     for corner in range(3):
-        left = [[] for _ in range(parts * PIECES)]
-        right = []
-        for j in range(runs):
-            row = slice(j, j + 1)
-            here = slot_ids == tall_row(high_ids[corner, row], slots)
-            right.append(jnp.where(lane_ids == tall_row(low_ids[corner, row], BLK), ones, none))
-            for part in range(parts * PIECES):
-                left[part].append(
-                    jnp.where(here, tall_row(forces[part, corner, row], slots), blank)
-                )
-        tall = jnp.concatenate([jnp.concatenate(part, axis=1) for part in left], axis=0)
-        wide = jnp.concatenate(right, axis=1)
-        product = lax.dot_general(
-            tall, wide, (((1,), (1,)), ((), ())), preferred_element_type=F32
-        )
-        total = product if total is None else total + product
+        for first in range(0, runs, STEP):
+            left = [[] for _ in range(parts * PIECES)]
+            right = []
+            for j in range(first, min(first + STEP, runs)):
+                row = slice(j, j + 1)
+                here = slot_ids == tall_row(high_ids[corner, row], slots)
+                there = lane_ids == tall_row(low_ids[corner, row], BLK)
+                right.append(jnp.where(there, ones, none))
+                for part in range(parts * PIECES):
+                    left[part].append(
+                        jnp.where(here, tall_row(forces[part, corner, row], slots), blank)
+                    )
+            tall = jnp.concatenate([jnp.concatenate(part, axis=1) for part in left], axis=0)
+            wide = jnp.concatenate(right, axis=1)
+            product = lax.dot_general(
+                tall, wide, (((1,), (1,)), ((), ())), preferred_element_type=F32
+            )
+            total = product if total is None else total + product
     for p in range(parts):
         summed = total[p * slots : (p + 1) * slots]
         for part in range(1, PIECES):
@@ -629,9 +635,14 @@
     slots = keys.shape[0]
     node_blocks = residual.shape[1] // BLK
     inner = lax.axis_index("inner")
+    width = BLK // slots
+
+    def key_of(message, k):
+        return jnp.broadcast_to(message[3 * slots][:, k * width : k * width + 1], (1, BLK))
+
     mine = messages[0]
     for k in range(slots):
-        keys[k : k + 1] = mine[4 * k + 3 : 4 * k + 4]
+        keys[k : k + 1] = key_of(mine, k)
     wanted = keys[...]
     node_ids = lax.broadcasted_iota(jnp.int32, (node_blocks, BLK), 0)
     own_ids = (node_ids + inner * node_blocks).astype(F32)
@@ -639,11 +650,11 @@
     moved = [jnp.zeros((slots, BLK), F32)] * 3
     for message in messages:
         for k in range(slots):
-            key = message[4 * k + 3 : 4 * k + 4]
+            key = key_of(message, k)
             here = own_ids == key
             same = wanted == key
             for part in range(3):
-                row = message[4 * k + part : 4 * k + part + 1]
+                row = message[3 * k + part]
                 external[part] = external[part] + jnp.where(here, row, 0.0)
                 moved[part] = moved[part] + jnp.where(same, row, 0.0)
     for step, message in enumerate(messages):
@@ -652,12 +663,12 @@
             key = jnp.broadcast_to(sender * node_blocks + b, (1, BLK)).astype(F32)
             same = wanted == key
             for part in range(3):
-                at = 4 * slots + part * node_blocks + b
-                moved[part] = moved[part] - jnp.where(same, message[at : at + 1], 0.0)
+                at = 3 * slots + 1 + part * node_blocks + b
+                moved[part] = moved[part] - jnp.where(same, message[at], 0.0)
     live = wanted >= 0.0
     for part in range(3):
-        start = 4 * slots + part * node_blocks
-        left = external[part] - mine[start : start + node_blocks]
+        start = 3 * slots + 1 + part * node_blocks
+        left = external[part] - mine[start : start + node_blocks, 0]
         for b in range(node_blocks):
             residual[part : part + 1, b * BLK : (b + 1) * BLK] = left[b : b + 1]
         motion[part] = jnp.where(live, COMPLIANCE * moved[part], 0.0)
@@ -826,10 +837,10 @@
         ),
         micros=0.8,
     )
-    lines = 4 * slots + 3 * node_blocks
+    lines = 3 * slots + 1 + 3 * node_blocks
     values, message, _, _ = call(
         second_kernel,
-        (whole, shape(lines, BLK), walls_shape, second_shape),
+        (whole, shape(lines, 1, BLK), walls_shape, second_shape),
         (
             pin(block_source),
             pin(block_target),

time: 26.1 us -> 26.1 us (level)
  transfers between devices with their start and end apart: 10 -> 10, of which waited for: 4 -> 5; matrix products, arithmetic and copies ran while one was open for 0% -> 0% of each run, Pallas kernels for 27% -> 27%
where the time goes in v12:
time: 26.1 us; the launch traced here: 25.9 us
  starting transfers between devices  12.4 us (48%)
  Pallas kernels  8.88 us (34%)
  waiting for transfers between devices  3.24 us (12%)
  between operations  1.37 us (5%)
    pallas_call x10, Pallas kernels, call(): pl.pallas_call(kernel, out_shape=outs, in_specs=[spec(space) for space in...  8.88 us
    ppermute x3, starting transfers between devices, exchange(): lax.ppermute(block, axis, [(partner_of(i, step, count), i) for i in range...  4.45 us
    ppermute x3, starting transfers between devices, swap(): lax.ppermute(near, axes, routes[0])  3.14 us
    ppermute x1, starting transfers between devices, around(): lax.ppermute(block, axis, [(i, (i + step) % count) for i in range(count)])  2.46 us
    ppermute x3, starting transfers between devices, swap(): lax.ppermute(far, axes, routes[1])  2.37 us
    ppermute x3, waiting for transfers between devices, exchange(): lax.ppermute(block, axis, [(partner_of(i, step, count), i) for i in range...  1.78 us
    ppermute x3, waiting for transfers between devices, swap(): lax.ppermute(far, axes, routes[1])  1.45 us
  transfers between devices with their start and end apart: 10, of which 5 were waited for; matrix products, arithmetic and copies ran while one was open for 0% of the time, Pallas kernels for 27%

profile of v12, /device:TPU:0, one launch (start us, length us, event | category | flops | bytes accessed | tf_op | source)
XLA Modules:
  0.0 25.9 jit_solution(17766558958435425082)
XLA Ops:
  0.6 2.5 %collective-permute-start.2 = (f32[3,2048]{1,0:T(4,128)}, f32[3,2048]{1,0:T(4,128)S(1)}, u32[]{:S(2)}, u32[]{:S(2)}) collective-permute-start(f32[3,2048]{1,0:T(4,128)} %displacement_hbm.1), channel_id=1, source_target_pairs={{0,12},{4,0},{8,4},{12,8},{1,13},{5,1},{9,5},{13,9},{2,14},{6,2},{... | collective-permute-start | bytes 73736 | tf_op jit(solution)/shard_map/ppermute | solution.py:707
  3.1 1.7 %shard_map.130 = (f32[19,4,8,256]{3,2,1,0:T(8,128)S(1)}, f32[2,4,8,256]{3,2,1,0:T(8,128)S(1)}, f32[24,4,256]{2,1,0:T(4,128)S(1)}, f32[24,4,256]{2,1,0:T(4,128)S(...) custom-call(f32[19,4,8,256]{3,2,1,0:T(8,128)} %pops_hbm.1, ...), custom_call_target="tpu_custom_call" | custom-call | bytes 5400000 | tf_op jit(solution)/shard_map/pallas_call | solution.py:680
  4.8 0.1 collective-permute-start
  4.9 3.1 %collective-permute-start.1 = (f32[24,4,256]{2,1,0:T(4,128)S(1)}, f32[24,4,256]{2,1,0:T(4,128)S(1)}, u32[]{:S(2)}, u32[]{:S(2)}) collective-permute-start(f32[24,4,256]{2,1,0:T(4,128)S(1)} %get-tuple-element.28), channel_id=1, source_target_pairs={{0,1},{1,0},{2,3},{3,2},{4,5},{5,4},{6,7},{7,6},{8,9},{9,8},{10,11... | collective-permute-start | bytes 294920 | tf_op jit(solution)/shard_map/ppermute | solution.py:725
  8.0 0.0 collective-permute-done.2.next_nodes
  8.0 1.7 %shard_map.131 = (f32[3,32,128]{2,1,0:T(8,128)S(1)}, f32[3,32,128]{2,1,0:T(8,128)S(1)}, f32[6,3,32,128]{3,2,1,0:T(8,128)S(1)}) custom-call(s32[3,4096]{1,0:T(4,128)S(1)} %get-tuple-element.29.elements, f32[3,2048]{1,0:T(4,128)S(1)} %get-tuple-element.30.displacement, f32[3,2048]{1,0:T(4,128)S(1)} %collective-permute-done.2.next_nodes, ...), custom_call_target="tpu_custom_call" | custom-call | bytes 3600 | tf_op jit(solution)/shard_map/pallas_call | solution.py:680
  9.8 0.1 shard_map.134
  9.8 1.6 %collective-permute-start.5 = (f32[21,8,256]{2,1,0:T(8,128)S(1)}, f32[21,8,256]{2,1,0:T(8,128)S(1)}, u32[]{:S(2)}, u32[]{:S(2)}) collective-permute-start(f32[21,8,256]{2,1,0:T(8,128)S(1)} %get-tuple-element.40), channel_id=1, source_target_pairs={{0,16},{4,8},{8,4},{12,28},{16,0},{20,24},{24,20},{28,12},{1,17},{... | collective-permute-start | bytes 516104 | tf_op jit(solution)/shard_map/ppermute | solution.py:725
  11.4 0.0 collective-permute-start.6
  11.4 1.1 %shard_map.132.other = f32[3,8,256]{2,1,0:T(8,128)S(1)} custom-call(f32[3,32,128]{2,1,0:T(8,128)S(1)} %get-tuple-element.33.low_ids.numbers, f32[3,32,128]{2,1,0:T(8,128)S(1)} %get-tuple-element.34.high_ids, f32[6,3,32,128]{3,2,1,0:T(8,128)S(1)} %get-tuple-element.35.forces), custom_call_target="tpu_custom_call" | custom-call | bytes 3600 | tf_op jit(solution)/shard_map/pallas_call | solution.py:680
  12.5 0.0 collective-permute-done.far_y
  12.5 0.0 collective-permute-done.1.near_y
  12.5 0.1 shard_map.133
  12.6 0.7 %collective-permute-start.3 = (f32[9,8,256]{2,1,0:T(8,128)S(1)}, f32[9,8,256]{2,1,0:T(8,128)S(1)}, u32[]{:S(2)}, u32[]{:S(2)}) collective-permute-start(f32[9,8,256]{2,1,0:T(8,128)S(1)} %get-tuple-element.36), channel_id=1, source_target_pairs={{0,16},{4,8},{8,4},{12,28},{16,0},{20,24},{24,20},{28,12},{1,17},{... | collective-permute-start | bytes 221192 | tf_op jit(solution)/shard_map/ppermute | solution.py:725
  13.4 0.0 collective-permute-start.4
  14.0 1.1 %shard_map.136.internal_own = f32[3,8,256]{2,1,0:T(8,128)S(1)} custom-call(f32[3,32,128]{2,1,0:T(8,128)S(1)} %get-tuple-element.33.low_ids.numbers, f32[3,32,128]{2,1,0:T(8,128)S(1)} %get-tuple-element.34.high_ids, f32[6,3,32,128]{3,2,1,0:T(8,128)S(1)} %get-tuple-element.35.forces), custom_call_target="tpu_custom_call" | custom-call | bytes 2880000 | tf_op jit(solution)/shard_map/pallas_call | solution.py:680
  15.1 0.2 collective-permute-done.5.far_x
  15.3 0.0 collective-permute-done.6.near_x
  15.3 0.5 %shard_map.135 = (f32[19,8,8,256]{3,2,1,0:T(8,128)S(1)}, f32[2,21,8,256]{3,2,1,0:T(8,128)S(1)}, f32[2,5,8,256]{3,2,1,0:T(8,128)S(1)}, f32[19,6,8,256]{3,2,1,0:T(8,128)S(1)}, f32[2,2,8,256]{3,2,1,0:T(8,128)S(1)}) custom-call(f32[19,4,8,256]{3,2,1,0:T(8,128)S(1)} %get-tuple-element.39.c1, f32[2,4,8,256]{3,2,1,0:T(8,128)S(1)} %get-tuple-element.38.fixed, ...), custom_call_target="tpu_custom_call" | custom-call | bytes 2880000 | tf_op jit(solution)/shard_map/pallas_call | solution.py:680
  15.8 1.2 %collective-permute-done.3.far = f32[9,8,256]{2,1,0:T(8,128)S(1)} collective-permute-done((f32[9,8,256]{2,1,0:T(8,128)S(1)}, f32[9,8,256]{2,1,0:T(8,128)S(1)}, u32[]{:S(2)}, u32[]{:S(2)}) %collective-permute-start.3) | collective-permute-done | bytes 73760 | tf_op jit(solution)/shard_map/ppermute | solution.py:725
  17.0 0.0 collective-permute-done.4.near
  17.0 0.9 %shard_map.137 = (f32[19,4,8,256]{3,2,1,0:T(8,128)S(1)}, f32[73,1,128]{2,1,0:T(1,128)S(1)}, f32[2,21,8,256]{3,2,1,0:T(8,128)S(1)}, f32[19,6,8,256]{3,2,1,0:T(8,128)S(1)}) custom-call(s32[1,1,8]{2,1,0:T(1,128)} %block_source_hbm.1, s32[1,1,8]{2,1,0:T(1,128)} %block_target_hbm.1, ...), custom_call_target="tpu_custom_call", output_to_operand_aliasing={{2}: (11, {}), {3}: (12, {})} | custom-call | bytes 5400000 | tf_op jit(solution)/shard_map/pallas_call | solution.py:680
  18.0 1.4 %collective-permute-start.9 = (f32[73,1,128]{2,1,0:T(1,128)S(1)}, f32[73,1,128]{2,1,0:T(1,128)S(1)}, u32[]{:S(2)}, u32[]{:S(2)}) collective-permute-start(f32[73,1,128]{2,1,0:T(1,128)S(1)} %get-tuple-element.48.refs_0_), channel_id=1, source_target_pairs={{3,0},{2,1},{1,2},{0,3},{7,4},{6,5},{5,6},{4,7},{11,8},{10,9},{9,1... | collective-permute-start | bytes 112136 | tf_op jit(solution)/shard_map/ppermute | solution.py:702
  19.4 0.3 collective-permute-start.8
  19.6 2.8 %collective-permute-start.7 = (f32[73,1,128]{2,1,0:T(1,128)S(1)}, f32[73,1,128]{2,1,0:T(1,128)S(1)}, u32[]{:S(2)}, u32[]{:S(2)}) collective-permute-start(f32[73,1,128]{2,1,0:T(1,128)S(1)} %get-tuple-element.48.refs_0_), channel_id=1, source_target_pairs={{1,0},{0,1},{3,2},{2,3},{5,4},{4,5},{7,6},{6,7},{9,8},{8,9},{11,10... | collective-permute-start | bytes 112136 | tf_op jit(solution)/shard_map/ppermute | solution.py:702
  22.4 0.8 %shard_map.138 = f32[19,4,8,256]{3,2,1,0:T(8,128)} custom-call(f32[19,4,8,256]{3,2,1,0:T(8,128)S(1)} %get-tuple-element.47.values), custom_call_target="tpu_custom_call" | custom-call | bytes 3600000 | tf_op jit(solution)/shard_map/pallas_call | solution.py:680
  23.3 0.6 %collective-permute-done.9.refs_3_ = f32[73,1,128]{2,1,0:T(1,128)S(1)} collective-permute-done((f32[73,1,128]{2,1,0:T(1,128)S(1)}, f32[73,1,128]{2,1,0:T(1,128)S(1)}, u32[]{:S(2)}, u32[]{:S(2)}) %collective-permute-start.9) | collective-permute-done | bytes 37408 | tf_op jit(solution)/shard_map/ppermute | solution.py:702
  23.8 1.1 %collective-permute-done.8.refs_2_ = f32[73,1,128]{2,1,0:T(1,128)S(1)} collective-permute-done((f32[73,1,128]{2,1,0:T(1,128)S(1)}, f32[73,1,128]{2,1,0:T(1,128)S(1)}, u32[]{:S(2)}, u32[]{:S(2)}) %collective-permute-start.8) | collective-permute-done | bytes 37408 | tf_op jit(solution)/shard_map/ppermute | solution.py:702
  25.0 0.1 collective-permute-done.7.refs_1_
  25.0 0.9 %shard_map.139 = (f32[3,2048]{1,0:T(4,128)}, f32[3,8,128]{2,1,0:T(8,128)}) custom-call(f32[73,1,128]{2,1,0:T(1,128)S(1)} %get-tuple-element.48.refs_0_, f32[73,1,128]{2,1,0:T(1,128)S(1)} %collective-permute-done.7.refs_1_, f32[73,1,128]{2,1,0:T(1,128)S(1)} %collective-permute-done.8.refs_2_, f32[73,1,128]{2,1,0:T(1,128)S(1)} %collective-permute-done.9.refs_3_), custom_call_target="tpu_custom_call" | custom-call | bytes 2880000 | tf_op jit(solution)/shard_map/pallas_call | solution.py:680
Async XLA Ops:
  0.6 7.4 %collective-permute-start.2 = (f32[3,2048]{1,0:T(4,128)}, f32[3,2048]{1,0:T(4,128)S(1)}, u32[]{:S(2)}, u32[]{:S(2)}) collective-permute-start(f32[3,2048]{1,0:T(4,128)} %displacement_hbm.1), channel_id=1, source_target_pairs={{0,12},{4,0},{8,4},{12,8},{1,13},{5,1},{9,5},{13,9},{2,14},{6,2},{... | collective-permute-start | bytes 73736 | tf_op jit(solution)/shard_map/ppermute | solution.py:707
  4.8 7.7 %collective-permute-start = (f32[24,4,256]{2,1,0:T(4,128)S(1)}, f32[24,4,256]{2,1,0:T(4,128)S(1)}, u32[]{:S(2)}, u32[]{:S(2)}) collective-permute-start(f32[24,4,256]{2,1,0:T(4,128)S(1)} %get-tuple-element.27), channel_id=1, source_target_pairs={{0,4},{1,2},{2,1},{3,7},{4,0},{5,6},{6,5},{7,3},{8,12},{9,10},{10,... | collective-permute-start | bytes 294920 | tf_op jit(solution)/shard_map/ppermute | solution.py:725
  4.9 7.6 %collective-permute-start.1 = (f32[24,4,256]{2,1,0:T(4,128)S(1)}, f32[24,4,256]{2,1,0:T(4,128)S(1)}, u32[]{:S(2)}, u32[]{:S(2)}) collective-permute-start(f32[24,4,256]{2,1,0:T(4,128)S(1)} %get-tuple-element.28), channel_id=1, source_target_pairs={{0,1},{1,0},{2,3},{3,2},{4,5},{5,4},{6,7},{7,6},{8,9},{9,8},{10,11... | collective-permute-start | bytes 294920 | tf_op jit(solution)/shard_map/ppermute | solution.py:725
  9.8 5.5 %collective-permute-start.5 = (f32[21,8,256]{2,1,0:T(8,128)S(1)}, f32[21,8,256]{2,1,0:T(8,128)S(1)}, u32[]{:S(2)}, u32[]{:S(2)}) collective-permute-start(f32[21,8,256]{2,1,0:T(8,128)S(1)} %get-tuple-element.40), channel_id=1, source_target_pairs={{0,16},{4,8},{8,4},{12,28},{16,0},{20,24},{24,20},{28,12},{1,17},{... | collective-permute-start | bytes 516104 | tf_op jit(solution)/shard_map/ppermute | solution.py:725
  11.4 3.9 %collective-permute-start.6 = (f32[21,8,256]{2,1,0:T(8,128)S(1)}, f32[21,8,256]{2,1,0:T(8,128)S(1)}, u32[]{:S(2)}, u32[]{:S(2)}) collective-permute-start(f32[21,8,256]{2,1,0:T(8,128)S(1)} %get-tuple-element.41), channel_id=1, source_target_pairs={{0,4},{4,0},{8,12},{12,8},{16,20},{20,16},{24,28},{28,24},{1,5},{5... | collective-permute-start | bytes 516104 | tf_op jit(solution)/shard_map/ppermute | solution.py:725
  12.6 4.4 %collective-permute-start.3 = (f32[9,8,256]{2,1,0:T(8,128)S(1)}, f32[9,8,256]{2,1,0:T(8,128)S(1)}, u32[]{:S(2)}, u32[]{:S(2)}) collective-permute-start(f32[9,8,256]{2,1,0:T(8,128)S(1)} %get-tuple-element.36), channel_id=1, source_target_pairs={{0,16},{4,8},{8,4},{12,28},{16,0},{20,24},{24,20},{28,12},{1,17},{... | collective-permute-start | bytes 221192 | tf_op jit(solution)/shard_map/ppermute | solution.py:725
  13.4 3.7 %collective-permute-start.4 = (f32[9,8,256]{2,1,0:T(8,128)S(1)}, f32[9,8,256]{2,1,0:T(8,128)S(1)}, u32[]{:S(2)}, u32[]{:S(2)}) collective-permute-start(f32[9,8,256]{2,1,0:T(8,128)S(1)} %get-tuple-element.37), channel_id=1, source_target_pairs={{0,4},{4,0},{8,12},{12,8},{16,20},{20,16},{24,28},{28,24},{1,5},{5... | collective-permute-start | bytes 221192 | tf_op jit(solution)/shard_map/ppermute | solution.py:725
  18.0 5.9 %collective-permute-start.9 = (f32[73,1,128]{2,1,0:T(1,128)S(1)}, f32[73,1,128]{2,1,0:T(1,128)S(1)}, u32[]{:S(2)}, u32[]{:S(2)}) collective-permute-start(f32[73,1,128]{2,1,0:T(1,128)S(1)} %get-tuple-element.48.refs_0_), channel_id=1, source_target_pairs={{3,0},{2,1},{1,2},{0,3},{7,4},{6,5},{5,6},{4,7},{11,8},{10,9},{9,1... | collective-permute-start | bytes 112136 | tf_op jit(solution)/shard_map/ppermute | solution.py:702
  19.4 5.6 %collective-permute-start.8 = (f32[73,1,128]{2,1,0:T(1,128)S(1)}, f32[73,1,128]{2,1,0:T(1,128)S(1)}, u32[]{:S(2)}, u32[]{:S(2)}) collective-permute-start(f32[73,1,128]{2,1,0:T(1,128)S(1)} %get-tuple-element.48.refs_0_), channel_id=1, source_target_pairs={{2,0},{3,1},{0,2},{1,3},{6,4},{7,5},{4,6},{5,7},{10,8},{11,9},{8,1... | collective-permute-start | bytes 112136 | tf_op jit(solution)/shard_map/ppermute | solution.py:702
  19.6 5.4 %collective-permute-start.7 = (f32[73,1,128]{2,1,0:T(1,128)S(1)}, f32[73,1,128]{2,1,0:T(1,128)S(1)}, u32[]{:S(2)}, u32[]{:S(2)}) collective-permute-start(f32[73,1,128]{2,1,0:T(1,128)S(1)} %get-tuple-element.48.refs_0_), channel_id=1, source_target_pairs={{1,0},{0,1},{3,2},{2,3},{5,4},{4,5},{7,6},{6,7},{9,8},{8,9},{11,10... | collective-permute-start | bytes 112136 | tf_op jit(solution)/shard_map/ppermute | solution.py:702

commit v13 on v12

--- a/solution.py
+++ b/solution.py
@@ -147,8 +147,8 @@
     stiffness_hbm,
     c1,
     fixed,
+    near,
     far,
-    near,
     displacement,
     elements,
     shape_inverse,
@@ -237,7 +237,7 @@
         pack(far, 1, last)
 
 
-def slab_face_kernel(c1, fixed, numbers, far, near):
+def slab_face_kernel(c1, fixed, numbers, near, far):
     del numbers
     planes = c1.shape[1]
 
@@ -259,7 +259,7 @@
         both[odd, slot] = far[slot]
 
 
-def corner_kernel(far_y, near_y, other, far, near, both):
+def corner_kernel(near_y, far_y, other, near, far, both):
     planes = near_y.shape[1]
     gather_both(near_y, far_y, both, "inner")
 
@@ -302,10 +302,10 @@
 def inside_kernel(
     c1,
     fixed,
+    near_y,
     far_y,
-    near_y,
+    near_x,
     far_x,
-    near_x,
     extended,
     walls,
     crossing,
@@ -355,8 +355,8 @@
     block_target_hbm,
     block_node_hbm,
     block_count,
+    near,
     far,
-    near,
     fixed,
     extended,
     crossing,
@@ -631,47 +631,56 @@
 
 def final_kernel(count, *refs):
     messages = refs[:count]
-    residual, motion, keys = refs[count:]
+    residual_hbm, motion_hbm, residual, motion, keys, sems = refs[count:]
     slots = keys.shape[0]
     node_blocks = residual.shape[1] // BLK
     inner = lax.axis_index("inner")
     width = BLK // slots
-
-    def key_of(message, k):
-        return jnp.broadcast_to(message[3 * slots][:, k * width : k * width + 1], (1, BLK))
-
-    mine = messages[0]
-    for k in range(slots):
-        keys[k : k + 1] = key_of(mine, k)
-    wanted = keys[...]
+    found = [
+        [
+            jnp.broadcast_to(message[3 * slots][:, k * width : k * width + 1], (1, BLK))
+            for k in range(slots)
+        ]
+        for message in messages
+    ]
     node_ids = lax.broadcasted_iota(jnp.int32, (node_blocks, BLK), 0)
     own_ids = (node_ids + inner * node_blocks).astype(F32)
-    external = [jnp.zeros((node_blocks, BLK), F32)] * 3
+    start = 3 * slots + 1
+    left = [-messages[0][start + p * node_blocks : start + (p + 1) * node_blocks, 0] for p in range(3)]
+    for message, all_keys in zip(messages, found):
+        for k, key in enumerate(all_keys):
+            here = own_ids == key
+            for part in range(3):
+                left[part] = left[part] + jnp.where(here, message[3 * k + part], 0.0)
+    for part in range(3):
+        for b in range(node_blocks):
+            residual[part : part + 1, b * BLK : (b + 1) * BLK] = left[part][b : b + 1]
+    store_residual = pltpu.make_async_copy(residual, residual_hbm, sems.at[0])
+    store_residual.start()
+
+    for k in range(slots):
+        keys[k : k + 1] = found[0][k]
+    wanted = keys[...]
     moved = [jnp.zeros((slots, BLK), F32)] * 3
-    for message in messages:
-        for k in range(slots):
-            key = key_of(message, k)
-            here = own_ids == key
+    for message, all_keys in zip(messages, found):
+        for k, key in enumerate(all_keys):
             same = wanted == key
             for part in range(3):
-                row = message[3 * k + part]
-                external[part] = external[part] + jnp.where(here, row, 0.0)
-                moved[part] = moved[part] + jnp.where(same, row, 0.0)
+                moved[part] = moved[part] + jnp.where(same, message[3 * k + part], 0.0)
     for step, message in enumerate(messages):
         sender = partner_of(inner, step, count)
         for b in range(node_blocks):
-            key = jnp.broadcast_to(sender * node_blocks + b, (1, BLK)).astype(F32)
-            same = wanted == key
+            same = wanted == (sender * node_blocks + b).astype(F32)
             for part in range(3):
-                at = 3 * slots + 1 + part * node_blocks + b
-                moved[part] = moved[part] - jnp.where(same, message[at], 0.0)
+                row = message[start + part * node_blocks + b]
+                moved[part] = moved[part] - jnp.where(same, row, 0.0)
     live = wanted >= 0.0
     for part in range(3):
-        start = 3 * slots + 1 + part * node_blocks
-        left = external[part] - mine[start : start + node_blocks, 0]
-        for b in range(node_blocks):
-            residual[part : part + 1, b * BLK : (b + 1) * BLK] = left[b : b + 1]
         motion[part] = jnp.where(live, COMPLIANCE * moved[part], 0.0)
+    store_motion = pltpu.make_async_copy(motion, motion_hbm, sems.at[1])
+    store_motion.start()
+    store_residual.wait()
+    store_motion.wait()
 
 
 def call(kernel, outs, operands, spaces, scratch=(), out_spaces=None, micros=1.0, aliases=None):
@@ -755,7 +764,7 @@
     pin = lambda block: pltpu.with_memory_space_constraint(block, hbm)
     whole_like = lambda block: jax.ShapeDtypeStruct(block.shape, block.dtype)
     shell = (displacement, elements, shape_inverse, stiffness.reshape(runs, BLK))
-    c1, fixed, far, near, own_nodes, corners, inverses, stiff = call(
+    c1, fixed, near, far, own_nodes, corners, inverses, stiff = call(
         first_kernel,
         (
             whole,
@@ -788,7 +797,7 @@
         ),
         micros=0.001,
     )
-    far, near = call(
+    near, far = call(
         slab_face_kernel, (face_x, face_x), (c1, fixed, low_ids), (vmem,) * 3, micros=0.001
     )
     near_x, far_x = swap(near, far, "slab", "group")
@@ -801,10 +810,10 @@
         micros=0.001,
     )
     corner = shape(CORNER_SLOTS, rows, length)
-    far, near = call(
+    near, far = call(
         corner_kernel,
         (corner, corner),
-        (far_y, near_y, other),
+        (near_y, far_y, other),
         (vmem,) * 3,
         scratch=(pltpu.VMEM((2, SLOTS, planes, length), F32),),
         micros=0.3,
@@ -829,7 +838,7 @@
             second_shape,
             shape(2, 2, rows, length),
         ),
-        (c1, fixed, far_y, near_y, far_x, near_x),
+        (c1, fixed, near_y, far_y, near_x, far_x),
         (vmem,) * 6,
         scratch=(
             pltpu.VMEM((2, SLOTS, planes, length), F32),
@@ -846,8 +855,8 @@
             pin(block_target),
             pin(block_node),
             block_count,
+            near_c,
             far_c,
-            near_c,
             fixed,
             extended,
             crossing,
@@ -884,7 +893,13 @@
         (shape(3, node_dev), shape(3, slots, BLK)),
         messages,
         (vmem,) * count,
-        scratch=(pltpu.VMEM((slots, BLK), F32),),
+        out_spaces=(hbm, hbm),
+        scratch=(
+            pltpu.VMEM((3, node_dev), F32),
+            pltpu.VMEM((3, slots, BLK), F32),
+            pltpu.VMEM((slots, BLK), F32),
+            pltpu.SemaphoreType.DMA((2,)),
+        ),
         micros=0.8,
     )
     return populations_out, residual, motion.transpose(1, 0, 2)[None, None]

time: 26.1 us -> 26.2 us (level)
  waiting for transfers between devices: 3.24 us -> 4.46 us
  starting transfers between devices: 12.4 us -> 11.3 us
    ppermute x3, waiting for transfers between devices: 1.78 us -> 2.94 us  [exchange(): lax.ppermute(block, axis, [(partner_of(i, step, count), i) for i in range...]
    ppermute x3, starting transfers between devices: 3.14 us -> 2.27 us  [swap(): lax.ppermute(near, axes, routes[0])]
where the time goes in v13:
time: 26.2 us; the launch traced here: 26.1 us
  starting transfers between devices  11.3 us (43%)
  Pallas kernels  8.88 us (34%)
  waiting for transfers between devices  4.46 us (17%)
  between operations  1.39 us (5%)
    pallas_call x10, Pallas kernels, call(): pl.pallas_call(kernel, out_shape=outs, in_specs=[spec(space) for space in...  8.88 us
    ppermute x3, starting transfers between devices, exchange(): lax.ppermute(block, axis, [(partner_of(i, step, count), i) for i in range...  4.45 us
    ppermute x3, waiting for transfers between devices, exchange(): lax.ppermute(block, axis, [(partner_of(i, step, count), i) for i in range...  2.94 us
    ppermute x1, starting transfers between devices, around(): lax.ppermute(block, axis, [(i, (i + step) % count) for i in range(count)])  2.46 us
    ppermute x3, starting transfers between devices, swap(): lax.ppermute(near, axes, routes[0])  2.27 us
    ppermute x3, starting transfers between devices, swap(): lax.ppermute(far, axes, routes[1])  2.17 us
    ppermute x3, waiting for transfers between devices, swap(): lax.ppermute(far, axes, routes[1])  1.47 us
  transfers between devices with their start and end apart: 10, of which 5 were waited for; matrix products, arithmetic and copies ran while one was open for 0% of the time, Pallas kernels for 27%

profile of v13, /device:TPU:0, one launch (start us, length us, event | category | flops | bytes accessed | tf_op | source)
XLA Modules:
  0.0 26.1 jit_solution(7772181237019253339)
XLA Ops:
  0.6 2.5 %collective-permute-start.2 = (f32[3,2048]{1,0:T(4,128)}, f32[3,2048]{1,0:T(4,128)S(1)}, u32[]{:S(2)}, u32[]{:S(2)}) collective-permute-start(f32[3,2048]{1,0:T(4,128)} %displacement_hbm.1), channel_id=1, source_target_pairs={{0,12},{4,0},{8,4},{12,8},{1,13},{5,1},{9,5},{13,9},{2,14},{6,2},{... | collective-permute-start | bytes 73736 | tf_op jit(solution)/shard_map/ppermute | solution.py:716
  3.1 1.7 %shard_map.130 = (f32[19,4,8,256]{3,2,1,0:T(8,128)S(1)}, f32[2,4,8,256]{3,2,1,0:T(8,128)S(1)}, f32[24,4,256]{2,1,0:T(4,128)S(1)}, f32[24,4,256]{2,1,0:T(4,128)S(...) custom-call(f32[19,4,8,256]{3,2,1,0:T(8,128)} %pops_hbm.1, ...), custom_call_target="tpu_custom_call" | custom-call | bytes 5400000 | tf_op jit(solution)/shard_map/pallas_call | solution.py:689
  4.8 1.6 %collective-permute-start = (f32[24,4,256]{2,1,0:T(4,128)S(1)}, f32[24,4,256]{2,1,0:T(4,128)S(1)}, u32[]{:S(2)}, u32[]{:S(2)}) collective-permute-start(f32[24,4,256]{2,1,0:T(4,128)S(1)} %get-tuple-element.27), channel_id=1, source_target_pairs={{0,1},{1,0},{2,3},{3,2},{4,5},{5,4},{6,7},{7,6},{8,9},{9,8},{10,11... | collective-permute-start | bytes 294920 | tf_op jit(solution)/shard_map/ppermute | solution.py:734
  6.5 0.0 collective-permute-start.1
  6.5 0.0 collective-permute-done.2.next_nodes
  6.5 1.7 %shard_map.131 = (f32[3,32,128]{2,1,0:T(8,128)S(1)}, f32[3,32,128]{2,1,0:T(8,128)S(1)}, f32[6,3,32,128]{3,2,1,0:T(8,128)S(1)}) custom-call(s32[3,4096]{1,0:T(4,128)S(1)} %get-tuple-element.29.elements, f32[3,2048]{1,0:T(4,128)S(1)} %get-tuple-element.30.displacement, f32[3,2048]{1,0:T(4,128)S(1)} %collective-permute-done.2.next_nodes, ...), custom_call_target="tpu_custom_call" | custom-call | bytes 3600 | tf_op jit(solution)/shard_map/pallas_call | solution.py:689
  8.2 0.1 shard_map.134
  8.2 0.6 %collective-permute-start.5 = (f32[21,8,256]{2,1,0:T(8,128)S(1)}, f32[21,8,256]{2,1,0:T(8,128)S(1)}, u32[]{:S(2)}, u32[]{:S(2)}) collective-permute-start(f32[21,8,256]{2,1,0:T(8,128)S(1)} %get-tuple-element.40), channel_id=1, source_target_pairs={{0,4},{4,0},{8,12},{12,8},{16,20},{20,16},{24,28},{28,24},{1,5},{5... | collective-permute-start | bytes 516104 | tf_op jit(solution)/shard_map/ppermute | solution.py:734
  8.8 1.5 %collective-permute-start.6 = (f32[21,8,256]{2,1,0:T(8,128)S(1)}, f32[21,8,256]{2,1,0:T(8,128)S(1)}, u32[]{:S(2)}, u32[]{:S(2)}) collective-permute-start(f32[21,8,256]{2,1,0:T(8,128)S(1)} %get-tuple-element.41), channel_id=1, source_target_pairs={{0,16},{4,8},{8,4},{12,28},{16,0},{20,24},{24,20},{28,12},{1,17},{... | collective-permute-start | bytes 516104 | tf_op jit(solution)/shard_map/ppermute | solution.py:734
  10.3 1.1 %shard_map.132.other = f32[3,8,256]{2,1,0:T(8,128)S(1)} custom-call(f32[3,32,128]{2,1,0:T(8,128)S(1)} %get-tuple-element.33.low_ids.numbers, f32[3,32,128]{2,1,0:T(8,128)S(1)} %get-tuple-element.34.high_ids, f32[6,3,32,128]{3,2,1,0:T(8,128)S(1)} %get-tuple-element.35.forces), custom_call_target="tpu_custom_call" | custom-call | bytes 3600 | tf_op jit(solution)/shard_map/pallas_call | solution.py:689
  11.4 0.0 collective-permute-done.near_y
  11.4 0.0 collective-permute-done.1.far_y
  11.4 0.1 shard_map.133
  11.5 0.1 collective-permute-start.3
  11.6 0.7 %collective-permute-start.4 = (f32[9,8,256]{2,1,0:T(8,128)S(1)}, f32[9,8,256]{2,1,0:T(8,128)S(1)}, u32[]{:S(2)}, u32[]{:S(2)}) collective-permute-start(f32[9,8,256]{2,1,0:T(8,128)S(1)} %get-tuple-element.37), channel_id=1, source_target_pairs={{0,16},{4,8},{8,4},{12,28},{16,0},{20,24},{24,20},{28,12},{1,17},{... | collective-permute-start | bytes 221192 | tf_op jit(solution)/shard_map/ppermute | solution.py:734
  12.9 1.1 %shard_map.136.internal_own = f32[3,8,256]{2,1,0:T(8,128)S(1)} custom-call(f32[3,32,128]{2,1,0:T(8,128)S(1)} %get-tuple-element.33.low_ids.numbers, f32[3,32,128]{2,1,0:T(8,128)S(1)} %get-tuple-element.34.high_ids, f32[6,3,32,128]{3,2,1,0:T(8,128)S(1)} %get-tuple-element.35.forces), custom_call_target="tpu_custom_call" | custom-call | bytes 2880000 | tf_op jit(solution)/shard_map/pallas_call | solution.py:689
  14.0 0.0 collective-permute-done.5.near_x
  14.1 0.1 collective-permute-done.6.far_x
  14.2 0.5 %shard_map.135 = (f32[19,8,8,256]{3,2,1,0:T(8,128)S(1)}, f32[2,21,8,256]{3,2,1,0:T(8,128)S(1)}, f32[2,5,8,256]{3,2,1,0:T(8,128)S(1)}, f32[19,6,8,256]{3,2,1,0:T(8,128)S(1)}, f32[2,2,8,256]{3,2,1,0:T(8,128)S(1)}) custom-call(f32[19,4,8,256]{3,2,1,0:T(8,128)S(1)} %get-tuple-element.39.c1, f32[2,4,8,256]{3,2,1,0:T(8,128)S(1)} %get-tuple-element.38.fixed, ...), custom_call_target="tpu_custom_call" | custom-call | bytes 2880000 | tf_op jit(solution)/shard_map/pallas_call | solution.py:689
  14.7 0.0 collective-permute-done.3.near
  14.7 1.3 %collective-permute-done.4.far = f32[9,8,256]{2,1,0:T(8,128)S(1)} collective-permute-done((f32[9,8,256]{2,1,0:T(8,128)S(1)}, f32[9,8,256]{2,1,0:T(8,128)S(1)}, u32[]{:S(2)}, u32[]{:S(2)}) %collective-permute-start.4) | collective-permute-done | bytes 73760 | tf_op jit(solution)/shard_map/ppermute | solution.py:734
  16.0 0.9 %shard_map.137 = (f32[19,4,8,256]{3,2,1,0:T(8,128)S(1)}, f32[73,1,128]{2,1,0:T(1,128)S(1)}, f32[2,21,8,256]{3,2,1,0:T(8,128)S(1)}, f32[19,6,8,256]{3,2,1,0:T(8,128)S(1)}) custom-call(s32[1,1,8]{2,1,0:T(1,128)} %block_source_hbm.1, s32[1,1,8]{2,1,0:T(1,128)} %block_target_hbm.1, ...), custom_call_target="tpu_custom_call", output_to_operand_aliasing={{2}: (11, {}), {3}: (12, {})} | custom-call | bytes 5400000 | tf_op jit(solution)/shard_map/pallas_call | solution.py:689
  17.0 2.5 %collective-permute-start.9 = (f32[73,1,128]{2,1,0:T(1,128)S(1)}, f32[73,1,128]{2,1,0:T(1,128)S(1)}, u32[]{:S(2)}, u32[]{:S(2)}) collective-permute-start(f32[73,1,128]{2,1,0:T(1,128)S(1)} %get-tuple-element.48.refs_0_), channel_id=1, source_target_pairs={{3,0},{2,1},{1,2},{0,3},{7,4},{6,5},{5,6},{4,7},{11,8},{10,9},{9,1... | collective-permute-start | bytes 112136 | tf_op jit(solution)/shard_map/ppermute | solution.py:711
  19.5 1.7 %collective-permute-start.8 = (f32[73,1,128]{2,1,0:T(1,128)S(1)}, f32[73,1,128]{2,1,0:T(1,128)S(1)}, u32[]{:S(2)}, u32[]{:S(2)}) collective-permute-start(f32[73,1,128]{2,1,0:T(1,128)S(1)} %get-tuple-element.48.refs_0_), channel_id=1, source_target_pairs={{2,0},{3,1},{0,2},{1,3},{6,4},{7,5},{4,6},{5,7},{10,8},{11,9},{8,1... | collective-permute-start | bytes 112136 | tf_op jit(solution)/shard_map/ppermute | solution.py:711
  21.2 0.2 collective-permute-start.7
  21.4 0.8 %shard_map.138 = f32[19,4,8,256]{3,2,1,0:T(8,128)} custom-call(f32[19,4,8,256]{3,2,1,0:T(8,128)S(1)} %get-tuple-element.47.values), custom_call_target="tpu_custom_call" | custom-call | bytes 3600000 | tf_op jit(solution)/shard_map/pallas_call | solution.py:689
  22.3 0.5 %collective-permute-done.9.refs_3_ = f32[73,1,128]{2,1,0:T(1,128)S(1)} collective-permute-done((f32[73,1,128]{2,1,0:T(1,128)S(1)}, f32[73,1,128]{2,1,0:T(1,128)S(1)}, u32[]{:S(2)}, u32[]{:S(2)}) %collective-permute-start.9) | collective-permute-done | bytes 37408 | tf_op jit(solution)/shard_map/ppermute | solution.py:711
  22.8 2.0 %collective-permute-done.8.refs_2_ = f32[73,1,128]{2,1,0:T(1,128)S(1)} collective-permute-done((f32[73,1,128]{2,1,0:T(1,128)S(1)}, f32[73,1,128]{2,1,0:T(1,128)S(1)}, u32[]{:S(2)}, u32[]{:S(2)}) %collective-permute-start.8) | collective-permute-done | bytes 37408 | tf_op jit(solution)/shard_map/ppermute | solution.py:711
  24.8 0.4 %collective-permute-done.7.refs_1_ = f32[73,1,128]{2,1,0:T(1,128)S(1)} collective-permute-done((f32[73,1,128]{2,1,0:T(1,128)S(1)}, f32[73,1,128]{2,1,0:T(1,128)S(1)}, u32[]{:S(2)}, u32[]{:S(2)}) %collective-permute-start.7) | collective-permute-done | bytes 37408 | tf_op jit(solution)/shard_map/ppermute | solution.py:711
  25.2 0.9 %shard_map.139 = (f32[3,2048]{1,0:T(4,128)}, f32[3,8,128]{2,1,0:T(8,128)}) custom-call(f32[73,1,128]{2,1,0:T(1,128)S(1)} %get-tuple-element.48.refs_0_, f32[73,1,128]{2,1,0:T(1,128)S(1)} %collective-permute-done.7.refs_1_, f32[73,1,128]{2,1,0:T(1,128)S(1)} %collective-permute-done.8.refs_2_, f32[73,1,128]{2,1,0:T(1,128)S(1)} %collective-permute-done.9.refs_3_), custom_call_target="tpu_custom_call" | custom-call | bytes 2880000 | tf_op jit(solution)/shard_map/pallas_call | solution.py:689
Async XLA Ops:
  0.6 5.8 %collective-permute-start.2 = (f32[3,2048]{1,0:T(4,128)}, f32[3,2048]{1,0:T(4,128)S(1)}, u32[]{:S(2)}, u32[]{:S(2)}) collective-permute-start(f32[3,2048]{1,0:T(4,128)} %displacement_hbm.1), channel_id=1, source_target_pairs={{0,12},{4,0},{8,4},{12,8},{1,13},{5,1},{9,5},{13,9},{2,14},{6,2},{... | collective-permute-start | bytes 73736 | tf_op jit(solution)/shard_map/ppermute | solution.py:716
  4.8 6.6 %collective-permute-start = (f32[24,4,256]{2,1,0:T(4,128)S(1)}, f32[24,4,256]{2,1,0:T(4,128)S(1)}, u32[]{:S(2)}, u32[]{:S(2)}) collective-permute-start(f32[24,4,256]{2,1,0:T(4,128)S(1)} %get-tuple-element.27), channel_id=1, source_target_pairs={{0,1},{1,0},{2,3},{3,2},{4,5},{5,4},{6,7},{7,6},{8,9},{9,8},{10,11... | collective-permute-start | bytes 294920 | tf_op jit(solution)/shard_map/ppermute | solution.py:734
  6.5 5.0 %collective-permute-start.1 = (f32[24,4,256]{2,1,0:T(4,128)S(1)}, f32[24,4,256]{2,1,0:T(4,128)S(1)}, u32[]{:S(2)}, u32[]{:S(2)}) collective-permute-start(f32[24,4,256]{2,1,0:T(4,128)S(1)} %get-tuple-element.28), channel_id=1, source_target_pairs={{0,4},{1,2},{2,1},{3,7},{4,0},{5,6},{6,5},{7,3},{8,12},{9,10},{10,... | collective-permute-start | bytes 294920 | tf_op jit(solution)/shard_map/ppermute | solution.py:734
  8.2 5.8 %collective-permute-start.5 = (f32[21,8,256]{2,1,0:T(8,128)S(1)}, f32[21,8,256]{2,1,0:T(8,128)S(1)}, u32[]{:S(2)}, u32[]{:S(2)}) collective-permute-start(f32[21,8,256]{2,1,0:T(8,128)S(1)} %get-tuple-element.40), channel_id=1, source_target_pairs={{0,4},{4,0},{8,12},{12,8},{16,20},{20,16},{24,28},{28,24},{1,5},{5... | collective-permute-start | bytes 516104 | tf_op jit(solution)/shard_map/ppermute | solution.py:734
  8.8 5.4 %collective-permute-start.6 = (f32[21,8,256]{2,1,0:T(8,128)S(1)}, f32[21,8,256]{2,1,0:T(8,128)S(1)}, u32[]{:S(2)}, u32[]{:S(2)}) collective-permute-start(f32[21,8,256]{2,1,0:T(8,128)S(1)} %get-tuple-element.41), channel_id=1, source_target_pairs={{0,16},{4,8},{8,4},{12,28},{16,0},{20,24},{24,20},{28,12},{1,17},{... | collective-permute-start | bytes 516104 | tf_op jit(solution)/shard_map/ppermute | solution.py:734
  11.5 3.2 %collective-permute-start.3 = (f32[9,8,256]{2,1,0:T(8,128)S(1)}, f32[9,8,256]{2,1,0:T(8,128)S(1)}, u32[]{:S(2)}, u32[]{:S(2)}) collective-permute-start(f32[9,8,256]{2,1,0:T(8,128)S(1)} %get-tuple-element.36), channel_id=1, source_target_pairs={{0,4},{4,0},{8,12},{12,8},{16,20},{20,16},{24,28},{28,24},{1,5},{5... | collective-permute-start | bytes 221192 | tf_op jit(solution)/shard_map/ppermute | solution.py:734
  11.6 4.4 %collective-permute-start.4 = (f32[9,8,256]{2,1,0:T(8,128)S(1)}, f32[9,8,256]{2,1,0:T(8,128)S(1)}, u32[]{:S(2)}, u32[]{:S(2)}) collective-permute-start(f32[9,8,256]{2,1,0:T(8,128)S(1)} %get-tuple-element.37), channel_id=1, source_target_pairs={{0,16},{4,8},{8,4},{12,28},{16,0},{20,24},{24,20},{28,12},{1,17},{... | collective-permute-start | bytes 221192 | tf_op jit(solution)/shard_map/ppermute | solution.py:734
  17.0 5.8 %collective-permute-start.9 = (f32[73,1,128]{2,1,0:T(1,128)S(1)}, f32[73,1,128]{2,1,0:T(1,128)S(1)}, u32[]{:S(2)}, u32[]{:S(2)}) collective-permute-start(f32[73,1,128]{2,1,0:T(1,128)S(1)} %get-tuple-element.48.refs_0_), channel_id=1, source_target_pairs={{3,0},{2,1},{1,2},{0,3},{7,4},{6,5},{5,6},{4,7},{11,8},{10,9},{9,1... | collective-permute-start | bytes 112136 | tf_op jit(solution)/shard_map/ppermute | solution.py:711
  19.5 5.3 %collective-permute-start.8 = (f32[73,1,128]{2,1,0:T(1,128)S(1)}, f32[73,1,128]{2,1,0:T(1,128)S(1)}, u32[]{:S(2)}, u32[]{:S(2)}) collective-permute-start(f32[73,1,128]{2,1,0:T(1,128)S(1)} %get-tuple-element.48.refs_0_), channel_id=1, source_target_pairs={{2,0},{3,1},{0,2},{1,3},{6,4},{7,5},{4,6},{5,7},{10,8},{11,9},{8,1... | collective-permute-start | bytes 112136 | tf_op jit(solution)/shard_map/ppermute | solution.py:711
  21.2 4.0 %collective-permute-start.7 = (f32[73,1,128]{2,1,0:T(1,128)S(1)}, f32[73,1,128]{2,1,0:T(1,128)S(1)}, u32[]{:S(2)}, u32[]{:S(2)}) collective-permute-start(f32[73,1,128]{2,1,0:T(1,128)S(1)} %get-tuple-element.48.refs_0_), channel_id=1, source_target_pairs={{1,0},{0,1},{3,2},{2,3},{5,4},{4,5},{7,6},{6,7},{9,8},{8,9},{11,10... | collective-permute-start | bytes 112136 | tf_op jit(solution)/shard_map/ppermute | solution.py:711

commit v14 on v12

--- a/solution.py
+++ b/solution.py
@@ -39,10 +39,11 @@
 FLAG_SLOT = 19
 RATE_SLOT = 20
 SLOTS = 21
-SIDE_SLOTS = 24
+PADDED_SLOTS = 24
 FORCE_SLOT = 6
 CORNER_SLOTS = FORCE_SLOT + 3
 PIECES = 2
+CAP = 3
 STEP = 4
 F32 = jnp.float32
 VMEM_BYTES = 48 * 1024 * 1024
@@ -145,6 +146,8 @@
     elements_hbm,
     shape_hbm,
     stiffness_hbm,
+    block_target_hbm,
+    block_node_hbm,
     c1,
     fixed,
     far,
@@ -153,9 +156,12 @@
     elements,
     shape_inverse,
     stiffness,
+    keys,
     pops,
     rate,
     flags,
+    block_target,
+    block_node,
     sems,
 ):
     planes, rows = c1.shape[1], c1.shape[2]
@@ -174,6 +180,8 @@
                 (elements_hbm, elements),
                 (shape_hbm, shape_inverse),
                 (stiffness_hbm, stiffness),
+                (block_target_hbm, block_target),
+                (block_node_hbm, block_node),
             )
         )
     ]
@@ -206,13 +214,27 @@
             return carry
 
         lax.fori_loop(0, planes, line, 0)
-        for slot in range(SLOTS, SIDE_SLOTS):
+        for slot in range(SLOTS, out.shape[0]):
             out[slot] = jnp.zeros(out.shape[1:], F32)
         clear_outside(out, outside)
 
     pack_pair(pack, "inner", near, far)
     for copy in shell:
         copy.wait()
+    node_blocks = displacement.shape[1] // BLK
+    for k in range(keys.shape[0]):
+        key = block_target[0, 0, k] * node_blocks + block_node[0, 0, k]
+        line = jnp.broadcast_to(key, (1, BLK)).astype(F32)
+        keys[k : k + 1] = line
+        slot, row, lanes = key_place(near, k)
+        near[slot, row, lanes] = line
+
+
+def key_place(face, k):
+    planes, pieces = face.shape[1], face.shape[2] // BLK
+    row, piece = divmod(k, pieces)
+    slot, row = divmod(row, planes)
+    return SLOTS + slot, slice(row, row + 1), slice(piece * BLK, (piece + 1) * BLK)
 
 
 def clear_outside(out, outside):
@@ -259,7 +281,7 @@
         both[odd, slot] = far[slot]
 
 
-def corner_kernel(far_y, near_y, other, far, near, both):
+def corner_kernel(far_y, near_y, other, keys, far, near, known, both):
     planes = near_y.shape[1]
     gather_both(near_y, far_y, both, "inner")
 
@@ -275,6 +297,11 @@
         clear_outside(out, outside)
 
     pack_pair(pack, "slab", near, far)
+    slots = keys.shape[0]
+    known[:slots] = keys[...]
+    for k in range(slots):
+        slot, row, lanes = key_place(near_y, k)
+        known[slots + k : slots + k + 1] = near_y[slot, row, lanes]
 
 
 def with_edge(block, step_y, edge):
@@ -350,40 +377,17 @@
     lax.fori_loop(1, planes - 1, inside_plane, 0)
 
 
-def second_kernel(
-    block_source_hbm,
-    block_target_hbm,
-    block_node_hbm,
-    block_count,
-    far,
-    near,
-    fixed,
-    extended,
-    crossing,
-    ends,
-    internal_own,
-    walls_in,
-    second_in,
-    out,
-    message,
-    walls,
-    second,
-    both,
-    edges,
-    loads,
-    block_source,
-    block_target,
-    block_node,
-    sems,
-):
-    del walls_in, second_in
-    copies = [
-        pltpu.make_async_copy(block_source_hbm, block_source, sems.at[0]),
-        pltpu.make_async_copy(block_target_hbm, block_target, sems.at[1]),
-        pltpu.make_async_copy(block_node_hbm, block_node, sems.at[2]),
-    ]
-    for copy in copies:
-        copy.start()
+def second_kernel(count, tables, *refs):
+    block_source_hbm, block_count = refs[:2]
+    known = refs[2 : 2 + tables]
+    far, near, fixed, extended, crossing, ends, internal_own = refs[2 + tables : 9 + tables]
+    rest = refs[11 + tables :]
+    out, mine = rest[:2]
+    messages = rest[2 : 1 + count]
+    walls, second = rest[1 + count : 3 + count]
+    both, edges, loads, internal, block_source, sem = rest[3 + count :]
+    copy = pltpu.make_async_copy(block_source_hbm, block_source, sem)
+    copy.start()
     planes, rows, length = out.shape[1:]
     half = length // BLK
     slots = block_source.shape[2]
@@ -473,31 +477,76 @@
 
     lax.fori_loop(0, planes, plane_two, 0)
 
-    for copy in copies:
-        copy.wait()
     node_blocks = internal_own.shape[1] * half
+    for part in range(3):
+        for piece in range(half):
+            at = piece * rows
+            lanes = slice(piece * BLK, (piece + 1) * BLK)
+            internal[part, at : at + rows] = (
+                internal_own[part, :, lanes] + both[0, FORCE_SLOT + part, :, lanes]
+            )
+    copy.wait()
     live = jnp.broadcast_to(block_count[...], (1, BLK))
-    lanes_of = lax.broadcasted_iota(jnp.int32, (1, BLK), 1) // (BLK // slots)
-    all_keys = jnp.full((1, BLK), -1, jnp.int32)
+    blocks, keys = [], []
     for k in range(slots):
         run = block_source[0, 0, k]
         x = run // (rows * half)
         left = run - x * (rows * half)
         y = left // half
         piece = left - y * half
+        blocks.append([loads[x * half + piece, part, pl.ds(y, 1)] for part in range(3)])
+        keys.append(jnp.where(live > k, known[0][k : k + 1], -1.0))
+
+    def summed(wanted):
+        moved = [jnp.zeros((slots, BLK), F32)] * 3
+        for k in range(slots):
+            same = wanted == keys[k]
+            for part in range(3):
+                moved[part] = moved[part] + jnp.where(same, blocks[k][part], 0.0)
+        for b in range(node_blocks):
+            same = wanted == (inner * node_blocks + b).astype(F32)
+            for part in range(3):
+                moved[part] = moved[part] - jnp.where(same, internal[part, b : b + 1], 0.0)
+        return moved
+
+    node_ids = lax.broadcasted_iota(jnp.int32, (node_blocks, BLK), 0)
+    own_ids = (node_ids + inner * node_blocks).astype(F32)
+    moved = summed(known[0][:slots])
+    for part in range(3):
+        total = -internal[part]
+        for k in range(slots):
+            total = total + jnp.where(own_ids == keys[k], blocks[k][part], 0.0)
+        mine[part * node_blocks : (part + 1) * node_blocks] = total
+        start = 3 * node_blocks + part * slots
+        mine[start : start + slots] = moved[part]
+    for k in range(slots):
+        start = 3 * (node_blocks + slots) + k
+        mine[start : start + 1] = keys[k]
+
+    table = []
+    for ref in known:
+        table += [ref[k * slots : (k + 1) * slots] for k in range(ref.shape[0] // slots)]
+    place_ids = lax.broadcasted_iota(jnp.int32, (8, BLK), 0).astype(F32)
+    for step, message in enumerate(messages, 1):
+        dest = partner_of(inner, step, count)
+        moved = summed(table[step])
+        low = (dest * node_blocks).astype(F32)
+        before = jnp.zeros((1, BLK), F32)
+        chosen = [jnp.zeros((8, BLK), F32)] * 3
+        nodes = jnp.full((8, BLK), -1.0, F32)
+        for k in range(slots):
+            named = (keys[k] >= low) & (keys[k] < low + node_blocks)
+            here = named & (place_ids == before)
+            for part in range(3):
+                chosen[part] = jnp.where(here, blocks[k][part], chosen[part])
+            nodes = jnp.where(here, keys[k], nodes)
+            before = before + jnp.where(named, 1.0, 0.0)
         for part in range(3):
-            message[3 * k + part] = loads[x * half + piece, part, pl.ds(y, 1)]
-        key = block_target[0, 0, k] * node_blocks + block_node[0, 0, k]
-        all_keys = jnp.where((lanes_of == k) & (live > k), key, all_keys)
-    message[3 * slots] = all_keys.astype(F32)
-    for part in range(3):
-        start = 3 * slots + 1 + part * node_blocks
-        for piece in range(half):
-            at = piece * rows
-            lanes = slice(piece * BLK, (piece + 1) * BLK)
-            message[start + at : start + at + rows, 0] = (
-                internal_own[part, :, lanes] + both[0, FORCE_SLOT + part, :, lanes]
-            )
+            message[part * slots : (part + 1) * slots, 0] = moved[part]
+            at = 3 * slots + part * CAP
+            message[at : at + CAP, 0] = chosen[part][:CAP]
+        at = 3 * slots + 3 * CAP
+        message[at : at + CAP, 0] = nodes[:CAP]
 
 
 def element_kernel(
@@ -629,48 +678,28 @@
     store.wait()
 
 
-def final_kernel(count, *refs):
-    messages = refs[:count]
-    residual, motion, keys = refs[count:]
-    slots = keys.shape[0]
+def final_kernel(mine, *refs):
+    messages, (residual, motion) = refs[:-2], refs[-2:]
+    slots = motion.shape[1]
     node_blocks = residual.shape[1] // BLK
     inner = lax.axis_index("inner")
-    width = BLK // slots
-
-    def key_of(message, k):
-        return jnp.broadcast_to(message[3 * slots][:, k * width : k * width + 1], (1, BLK))
-
-    mine = messages[0]
-    for k in range(slots):
-        keys[k : k + 1] = key_of(mine, k)
-    wanted = keys[...]
     node_ids = lax.broadcasted_iota(jnp.int32, (node_blocks, BLK), 0)
     own_ids = (node_ids + inner * node_blocks).astype(F32)
-    external = [jnp.zeros((node_blocks, BLK), F32)] * 3
-    moved = [jnp.zeros((slots, BLK), F32)] * 3
+    total = [mine[p * node_blocks : (p + 1) * node_blocks] for p in range(3)]
+    start = 3 * node_blocks
+    moved = [mine[start + p * slots : start + (p + 1) * slots] for p in range(3)]
+    live = mine[start + 3 * slots : start + 4 * slots] >= 0.0
     for message in messages:
-        for k in range(slots):
-            key = key_of(message, k)
-            here = own_ids == key
-            same = wanted == key
+        for place in range(CAP):
+            here = own_ids == message[3 * slots + 3 * CAP + place]
             for part in range(3):
-                row = message[3 * k + part]
-                external[part] = external[part] + jnp.where(here, row, 0.0)
-                moved[part] = moved[part] + jnp.where(same, row, 0.0)
-    for step, message in enumerate(messages):
-        sender = partner_of(inner, step, count)
+                row = message[3 * slots + part * CAP + place]
+                total[part] = total[part] + jnp.where(here, row, 0.0)
+        for part in range(3):
+            moved[part] = moved[part] + message[part * slots : (part + 1) * slots, 0]
+    for part in range(3):
         for b in range(node_blocks):
-            key = jnp.broadcast_to(sender * node_blocks + b, (1, BLK)).astype(F32)
-            same = wanted == key
-            for part in range(3):
-                at = 3 * slots + 1 + part * node_blocks + b
-                moved[part] = moved[part] - jnp.where(same, message[at], 0.0)
-    live = wanted >= 0.0
-    for part in range(3):
-        start = 3 * slots + 1 + part * node_blocks
-        left = external[part] - mine[start : start + node_blocks, 0]
-        for b in range(node_blocks):
-            residual[part : part + 1, b * BLK : (b + 1) * BLK] = left[b : b + 1]
+            residual[part : part + 1, b * BLK : (b + 1) * BLK] = total[part][b : b + 1]
         motion[part] = jnp.where(live, COMPLIANCE * moved[part], 0.0)
 
 
@@ -691,15 +720,30 @@
     )(*operands)
 
 
+def in_pairs(count):
+    return count > 1 and count & (count - 1) == 0
+
+
 def partner_of(at, step, count):
-    if count & (count - 1) == 0:
-        return at ^ step
-    return (at + count - step) % count
+    return at ^ step if in_pairs(count) else (at + step) % count
 
 
 def exchange(block, axis, step):
     count = lax.axis_size(axis)
-    return lax.ppermute(block, axis, [(partner_of(i, step, count), i) for i in range(count)])
+    return lax.ppermute(block, axis, [(i, partner_of(i, step, count)) for i in range(count)])
+
+
+def all_keys(own, known, axis):
+    count = lax.axis_size(axis)
+    if not in_pairs(count):
+        return [own] + [exchange(own, axis, count - step) for step in range(1, count)]
+    tables = [known]
+    reach = 2
+    while reach < count:
+        joined = tables[0] if len(tables) == 1 else jnp.concatenate(tables, axis=0)
+        tables.append(exchange(joined, axis, reach))
+        reach *= 2
+    return tables
 
 
 def around(block, axis, step):
@@ -750,12 +794,13 @@
     vmem, hbm, smem = pltpu.VMEM, pltpu.HBM, pltpu.SMEM
 
     next_nodes = around(displacement, "slab", -1)
-    face_y = shape(SIDE_SLOTS, planes, length)
+    room = -(-slots // (planes * half))
+    face_y = shape(max(SLOTS + room, PADDED_SLOTS), planes, length)
     face_x = shape(SLOTS, rows, length)
     pin = lambda block: pltpu.with_memory_space_constraint(block, hbm)
     whole_like = lambda block: jax.ShapeDtypeStruct(block.shape, block.dtype)
     shell = (displacement, elements, shape_inverse, stiffness.reshape(runs, BLK))
-    c1, fixed, far, near, own_nodes, corners, inverses, stiff = call(
+    c1, fixed, far, near, own_nodes, corners, inverses, stiff, own_keys = call(
         first_kernel,
         (
             whole,
@@ -763,14 +808,20 @@
             face_y,
             face_y,
             *(whole_like(block) for block in shell),
-        ),
-        tuple(pin(block) for block in (populations, relaxation, node_flags, *shell)),
-        (hbm,) * 7,
+            shape(slots, BLK),
+        ),
+        tuple(
+            pin(block)
+            for block in (populations, relaxation, node_flags, *shell, block_target, block_node)
+        ),
+        (hbm,) * 9,
         scratch=(
             pltpu.VMEM((planes, Q, rows, length), F32),
             pltpu.VMEM((planes, rows, length), F32),
             pltpu.VMEM((planes, rows, length), jnp.int32),
-            pltpu.SemaphoreType.DMA((planes + 6,)),
+            pltpu.SMEM(block_target.shape, jnp.int32),
+            pltpu.SMEM(block_node.shape, jnp.int32),
+            pltpu.SemaphoreType.DMA((planes + 8,)),
         ),
         micros=1.5,
     )
@@ -801,11 +852,11 @@
         micros=0.001,
     )
     corner = shape(CORNER_SLOTS, rows, length)
-    far, near = call(
+    far, near, known = call(
         corner_kernel,
-        (corner, corner),
-        (far_y, near_y, other),
-        (vmem,) * 3,
+        (corner, corner, shape(2 * slots, BLK)),
+        (far_y, near_y, other, own_keys),
+        (vmem,) * 4,
         scratch=(pltpu.VMEM((2, SLOTS, planes, length), F32),),
         micros=0.3,
     )
@@ -837,15 +888,22 @@
         ),
         micros=0.8,
     )
-    lines = 3 * slots + 1 + 3 * node_blocks
-    values, message, _, _ = call(
-        second_kernel,
-        (whole, shape(lines, 1, BLK), walls_shape, second_shape),
+    tables = all_keys(own_keys, known, "inner")
+    first = 2 + len(tables)
+    line = shape(3 * slots + 4 * CAP, 1, BLK)
+    outs = call(
+        functools.partial(second_kernel, count, len(tables)),
+        (
+            whole,
+            shape(3 * node_blocks + 4 * slots, BLK),
+            *([line] * (count - 1)),
+            walls_shape,
+            second_shape,
+        ),
         (
             pin(block_source),
-            pin(block_target),
-            pin(block_node),
             block_count,
+            *tables,
             far_c,
             near_c,
             fixed,
@@ -856,20 +914,20 @@
             walls,
             second,
         ),
-        (hbm,) * 3 + (vmem,) * 10,
-        aliases={11: 2, 12: 3},
+        (hbm,) + (vmem,) * (first + 8),
+        aliases={first + 7: 1 + count, first + 8: 2 + count},
         scratch=(
             pltpu.VMEM((2, CORNER_SLOTS, rows, length), F32),
             pltpu.VMEM((2, 5, wide, length), F32),
             pltpu.VMEM((planes * half, 3, rows, BLK), F32),
+            pltpu.VMEM((3, node_blocks, BLK), F32),
             pltpu.SMEM(block_source.shape, jnp.int32),
-            pltpu.SMEM(block_target.shape, jnp.int32),
-            pltpu.SMEM(block_node.shape, jnp.int32),
-            pltpu.SemaphoreType.DMA((3,)),
+            pltpu.SemaphoreType.DMA(()),
         ),
         micros=1.5,
     )
-    messages = [message] + [exchange(message, "inner", step) for step in range(1, count)]
+    values, mine = outs[:2]
+    arrived = [exchange(outs[1 + step], "inner", step) for step in range(count - 1, 0, -1)]
     (populations_out,) = call(
         store_kernel,
         (whole,),
@@ -880,11 +938,10 @@
         micros=1.0,
     )
     residual, motion = call(
-        functools.partial(final_kernel, count),
+        final_kernel,
         (shape(3, node_dev), shape(3, slots, BLK)),
-        messages,
+        (mine, *arrived),
         (vmem,) * count,
-        scratch=(pltpu.VMEM((slots, BLK), F32),),
         micros=0.8,
     )
     return populations_out, residual, motion.transpose(1, 0, 2)[None, None]

time: 26.1 us -> 26.7 us (1.023)
  starting transfers between devices: 12.4 us -> 13.9 us
  waiting for transfers between devices: 3.24 us -> 2.29 us
    ppermute x3 -> x4, starting transfers between devices: 4.45 us -> 5.96 us  [exchange(): lax.ppermute(block, axis, [(i, partner_of(i, step, count)) for i in range...]
    ppermute x3, waiting for transfers between devices: 1.45 us -> 0.05 us  [swap(): lax.ppermute(far, axes, routes[1])]
    ppermute x3 -> x4, waiting for transfers between devices: 1.78 us -> 2.23 us  [exchange(): lax.ppermute(block, axis, [(i, partner_of(i, step, count)) for i in range...]
  transfers between devices with their start and end apart: 10 -> 11, of which waited for: 5 -> 3; matrix products, arithmetic and copies ran while one was open for 0% -> 0% of each run, Pallas kernels for 27% -> 27%
where the time goes in v14:
time: 26.7 us; the launch traced here: 26.5 us
  starting transfers between devices  13.9 us (52%)
  Pallas kernels  8.87 us (33%)
  waiting for transfers between devices  2.29 us (9%)
  between operations  1.39 us (5%)
    pallas_call x10, Pallas kernels, call(): pl.pallas_call(kernel, out_shape=outs, in_specs=[spec(space) for space in...  8.87 us
    ppermute x4, starting transfers between devices, exchange(): lax.ppermute(block, axis, [(i, partner_of(i, step, count)) for i in range...  5.96 us
    ppermute x3, starting transfers between devices, swap(): lax.ppermute(near, axes, routes[0])  3.14 us
    ppermute x1, starting transfers between devices, around(): lax.ppermute(block, axis, [(i, (i + step) % count) for i in range(count)])  2.46 us
    ppermute x3, starting transfers between devices, swap(): lax.ppermute(far, axes, routes[1])  2.38 us
    ppermute x4, waiting for transfers between devices, exchange(): lax.ppermute(block, axis, [(i, partner_of(i, step, count)) for i in range...  2.23 us
  transfers between devices with their start and end apart: 11, of which 3 were waited for; matrix products, arithmetic and copies ran while one was open for 0% of the time, Pallas kernels for 27%

profile of v14, /device:TPU:0, one launch (start us, length us, event | category | flops | bytes accessed | tf_op | source)
XLA Modules:
  0.0 26.5 jit_solution(12303157323587667445)
XLA Ops:
  0.6 2.5 %collective-permute-start.2 = (f32[3,2048]{1,0:T(4,128)}, f32[3,2048]{1,0:T(4,128)S(1)}, u32[]{:S(2)}, u32[]{:S(2)}) collective-permute-start(f32[3,2048]{1,0:T(4,128)} %displacement_hbm.1), channel_id=1, source_target_pairs={{0,12},{4,0},{8,4},{12,8},{1,13},{5,1},{9,5},{13,9},{2,14},{6,2},{... | collective-permute-start | bytes 73736 | tf_op jit(solution)/shard_map/ppermute | solution.py:751
  3.1 1.8 %shard_map.130 = (f32[19,4,8,256]{3,2,1,0:T(8,128)S(1)}, f32[2,4,8,256]{3,2,1,0:T(8,128)S(1)}, f32[24,4,256]{2,1,0:T(4,128)S(1)}, f32[24,4,256]{2,1,0:T(4,128)S(...) custom-call(f32[19,4,8,256]{3,2,1,0:T(8,128)} %pops_hbm.1, ...), custom_call_target="tpu_custom_call" | custom-call | bytes 5400000 | tf_op jit(solution)/shard_map/pallas_call | solution.py:709
  4.9 0.1 collective-permute-start
  5.0 3.1 %collective-permute-start.1 = (f32[24,4,256]{2,1,0:T(4,128)S(1)}, f32[24,4,256]{2,1,0:T(4,128)S(1)}, u32[]{:S(2)}, u32[]{:S(2)}) collective-permute-start(f32[24,4,256]{2,1,0:T(4,128)S(1)} %get-tuple-element.33), channel_id=1, source_target_pairs={{0,1},{1,0},{2,3},{3,2},{4,5},{5,4},{6,7},{7,6},{8,9},{9,8},{10,11... | collective-permute-start | bytes 294920 | tf_op jit(solution)/shard_map/ppermute | solution.py:769
  8.1 0.0 collective-permute-done.2.next_nodes
  8.1 1.7 %shard_map.131 = (f32[3,32,128]{2,1,0:T(8,128)S(1)}, f32[3,32,128]{2,1,0:T(8,128)S(1)}, f32[6,3,32,128]{3,2,1,0:T(8,128)S(1)}) custom-call(s32[3,4096]{1,0:T(4,128)S(1)} %get-tuple-element.34.elements, f32[3,2048]{1,0:T(4,128)S(1)} %get-tuple-element.35.displacement, f32[3,2048]{1,0:T(4,128)S(1)} %collective-permute-done.2.next_nodes, ...), custom_call_target="tpu_custom_call" | custom-call | bytes 3600 | tf_op jit(solution)/shard_map/pallas_call | solution.py:709
  9.8 0.1 shard_map.134
  9.9 1.6 %collective-permute-start.6 = (f32[21,8,256]{2,1,0:T(8,128)S(1)}, f32[21,8,256]{2,1,0:T(8,128)S(1)}, u32[]{:S(2)}, u32[]{:S(2)}) collective-permute-start(f32[21,8,256]{2,1,0:T(8,128)S(1)} %get-tuple-element.47), channel_id=1, source_target_pairs={{0,16},{4,8},{8,4},{12,28},{16,0},{20,24},{24,20},{28,12},{1,17},{... | collective-permute-start | bytes 516104 | tf_op jit(solution)/shard_map/ppermute | solution.py:769
  11.4 0.0 collective-permute-start.7
  11.4 1.1 %shard_map.132.other = f32[3,8,256]{2,1,0:T(8,128)S(1)} custom-call(f32[3,32,128]{2,1,0:T(8,128)S(1)} %get-tuple-element.38.low_ids.numbers, f32[3,32,128]{2,1,0:T(8,128)S(1)} %get-tuple-element.39.high_ids, f32[6,3,32,128]{3,2,1,0:T(8,128)S(1)} %get-tuple-element.40.forces), custom_call_target="tpu_custom_call" | custom-call | bytes 3600 | tf_op jit(solution)/shard_map/pallas_call | solution.py:709
  12.5 0.0 collective-permute-done.far_y
  12.6 0.0 collective-permute-done.1.near_y
  12.6 0.1 shard_map.133
  12.7 0.8 %collective-permute-start.4 = (f32[9,8,256]{2,1,0:T(8,128)S(1)}, f32[9,8,256]{2,1,0:T(8,128)S(1)}, u32[]{:S(2)}, u32[]{:S(2)}) collective-permute-start(f32[9,8,256]{2,1,0:T(8,128)S(1)} %get-tuple-element.43), channel_id=1, source_target_pairs={{0,16},{4,8},{8,4},{12,28},{16,0},{20,24},{24,20},{28,12},{1,17},{... | collective-permute-start | bytes 221192 | tf_op jit(solution)/shard_map/ppermute | solution.py:769
  13.4 0.0 collective-permute-start.5
  13.4 1.5 %collective-permute-start.3 = (f32[16,128]{1,0:T(8,128)S(1)}, f32[16,128]{1,0:T(8,128)S(1)}, u32[]{:S(2)}, u32[]{:S(2)}) collective-permute-start(f32[16,128]{1,0:T(8,128)S(1)} %get-tuple-element.42.refs_2_), channel_id=1, source_target_pairs={{0,2},{1,3},{2,0},{3,1},{4,6},{5,7},{6,4},{7,5},{8,10},{9,11},{10,... | collective-permute-start | bytes 24584 | tf_op jit(solution)/shard_map/ppermute | solution.py:733
  15.6 1.1 %shard_map.136.refs_10_ = f32[3,8,256]{2,1,0:T(8,128)S(1)} custom-call(f32[3,32,128]{2,1,0:T(8,128)S(1)} %get-tuple-element.38.low_ids.numbers, f32[3,32,128]{2,1,0:T(8,128)S(1)} %get-tuple-element.39.high_ids, f32[6,3,32,128]{3,2,1,0:T(8,128)S(1)} %get-tuple-element.40.forces), custom_call_target="tpu_custom_call" | custom-call | bytes 2880000 | tf_op jit(solution)/shard_map/pallas_call | solution.py:709
  16.7 0.0 collective-permute-done.6.far_x
  16.7 0.0 collective-permute-done.7.near_x
  16.7 0.5 %shard_map.135 = (f32[19,8,8,256]{3,2,1,0:T(8,128)S(1)}, f32[2,21,8,256]{3,2,1,0:T(8,128)S(1)}, f32[2,5,8,256]{3,2,1,0:T(8,128)S(1)}, f32[19,6,8,256]{3,2,1,0:T(8,128)S(1)}, f32[2,2,8,256]{3,2,1,0:T(8,128)S(1)}) custom-call(f32[19,4,8,256]{3,2,1,0:T(8,128)S(1)} %get-tuple-element.46.c1, f32[2,4,8,256]{3,2,1,0:T(8,128)S(1)} %get-tuple-element.45.fixed.refs_6_, ...), custom_call_target="tpu_custom_call" | custom-call | bytes 2880000 | tf_op jit(solution)/shard_map/pallas_call | solution.py:709
  17.2 0.8 %collective-permute-done.3.refs_3_ = f32[16,128]{1,0:T(8,128)S(1)} collective-permute-done((f32[16,128]{1,0:T(8,128)S(1)}, f32[16,128]{1,0:T(8,128)S(1)}, u32[]{:S(2)}, u32[]{:S(2)}) %collective-permute-start.3) | collective-permute-done | bytes 8224 | tf_op jit(solution)/shard_map/ppermute | solution.py:733
  18.0 0.0 collective-permute-done.4.refs_4_
  18.0 0.0 collective-permute-done.5.refs_5_
  18.0 1.1 %shard_map.137 = (f32[19,4,8,256]{3,2,1,0:T(8,128)S(1)}, f32[80,128]{1,0:T(8,128)S(1)}, f32[36,1,128]{2,1,0:T(1,128)S(1)}, f32[36,1,128]{2,1,0:T(1,128)S(1)}, f3...) custom-call(s32[1,1,8]{2,1,0:T(1,128)} %refs_0_.1, ...), custom_call_target="tpu_custom_call", output_to_operand_aliasing={{5}: (11, {}), {6}: (12, {})} | custom-call | bytes 5400000 | tf_op jit(solution)/shard_map/pallas_call | solution.py:709
  19.1 2.1 %collective-permute-start.8 = (f32[36,1,128]{2,1,0:T(1,128)S(1)}, f32[36,1,128]{2,1,0:T(1,128)S(1)}, u32[]{:S(2)}, u32[]{:S(2)}) collective-permute-start(f32[36,1,128]{2,1,0:T(1,128)S(1)} %get-tuple-element.56), channel_id=1, source_target_pairs={{0,3},{1,2},{2,1},{3,0},{4,7},{5,6},{6,5},{7,4},{8,11},{9,10},{10,... | collective-permute-start | bytes 55304 | tf_op jit(solution)/shard_map/ppermute | solution.py:733
  21.1 0.4 %collective-permute-start.9 = (f32[36,1,128]{2,1,0:T(1,128)S(1)}, f32[36,1,128]{2,1,0:T(1,128)S(1)}, u32[]{:S(2)}, u32[]{:S(2)}) collective-permute-start(f32[36,1,128]{2,1,0:T(1,128)S(1)} %get-tuple-element.57), channel_id=1, source_target_pairs={{0,2},{1,3},{2,0},{3,1},{4,6},{5,7},{6,4},{7,5},{8,10},{9,11},{10,... | collective-permute-start | bytes 55304 | tf_op jit(solution)/shard_map/ppermute | solution.py:733
  21.5 2.0 %collective-permute-start.10 = (f32[36,1,128]{2,1,0:T(1,128)S(1)}, f32[36,1,128]{2,1,0:T(1,128)S(1)}, u32[]{:S(2)}, u32[]{:S(2)}) collective-permute-start(f32[36,1,128]{2,1,0:T(1,128)S(1)} %get-tuple-element.58), channel_id=1, source_target_pairs={{0,1},{1,0},{2,3},{3,2},{4,5},{5,4},{6,7},{7,6},{8,9},{9,8},{10,11... | collective-permute-start | bytes 55304 | tf_op jit(solution)/shard_map/ppermute | solution.py:733
  23.5 0.8 %shard_map.138 = f32[19,4,8,256]{3,2,1,0:T(8,128)} custom-call(f32[19,4,8,256]{3,2,1,0:T(8,128)S(1)} %get-tuple-element.54.values), custom_call_target="tpu_custom_call" | custom-call | bytes 3600000 | tf_op jit(solution)/shard_map/pallas_call | solution.py:709
  24.4 0.3 %collective-permute-done.8.refs_0_ = f32[36,1,128]{2,1,0:T(1,128)S(1)} collective-permute-done((f32[36,1,128]{2,1,0:T(1,128)S(1)}, f32[36,1,128]{2,1,0:T(1,128)S(1)}, u32[]{:S(2)}, u32[]{:S(2)}) %collective-permute-start.8) | collective-permute-done | bytes 18464 | tf_op jit(solution)/shard_map/ppermute | solution.py:733
  24.7 1.1 %collective-permute-done.9.refs_1_ = f32[36,1,128]{2,1,0:T(1,128)S(1)} collective-permute-done((f32[36,1,128]{2,1,0:T(1,128)S(1)}, f32[36,1,128]{2,1,0:T(1,128)S(1)}, u32[]{:S(2)}, u32[]{:S(2)}) %collective-permute-start.9) | collective-permute-done | bytes 18464 | tf_op jit(solution)/shard_map/ppermute | solution.py:733
  25.8 0.0 collective-permute-done.10.refs_2_
  25.8 0.7 %shard_map.139 = (f32[3,2048]{1,0:T(4,128)}, f32[3,8,128]{2,1,0:T(8,128)}) custom-call(f32[80,128]{1,0:T(8,128)S(1)} %get-tuple-element.55.mine, f32[36,1,128]{2,1,0:T(1,128)S(1)} %collective-permute-done.8.refs_0_, f32[36,1,128]{2,1,0:T(1,128)S(1)} %collective-permute-done.9.refs_1_, f32[36,1,128]{2,1,0:T(1,128)S(1)} %collective-permute-done.10.refs_2_), custom_call_target="tpu_custom_call" | custom-call | bytes 2880000 | tf_op jit(solution)/shard_map/pallas_call | solution.py:709
Async XLA Ops:
  0.6 7.5 %collective-permute-start.2 = (f32[3,2048]{1,0:T(4,128)}, f32[3,2048]{1,0:T(4,128)S(1)}, u32[]{:S(2)}, u32[]{:S(2)}) collective-permute-start(f32[3,2048]{1,0:T(4,128)} %displacement_hbm.1), channel_id=1, source_target_pairs={{0,12},{4,0},{8,4},{12,8},{1,13},{5,1},{9,5},{13,9},{2,14},{6,2},{... | collective-permute-start | bytes 73736 | tf_op jit(solution)/shard_map/ppermute | solution.py:751
  4.9 7.7 %collective-permute-start = (f32[24,4,256]{2,1,0:T(4,128)S(1)}, f32[24,4,256]{2,1,0:T(4,128)S(1)}, u32[]{:S(2)}, u32[]{:S(2)}) collective-permute-start(f32[24,4,256]{2,1,0:T(4,128)S(1)} %get-tuple-element.32), channel_id=1, source_target_pairs={{0,4},{1,2},{2,1},{3,7},{4,0},{5,6},{6,5},{7,3},{8,12},{9,10},{10,... | collective-permute-start | bytes 294920 | tf_op jit(solution)/shard_map/ppermute | solution.py:769
  5.0 7.6 %collective-permute-start.1 = (f32[24,4,256]{2,1,0:T(4,128)S(1)}, f32[24,4,256]{2,1,0:T(4,128)S(1)}, u32[]{:S(2)}, u32[]{:S(2)}) collective-permute-start(f32[24,4,256]{2,1,0:T(4,128)S(1)} %get-tuple-element.33), channel_id=1, source_target_pairs={{0,1},{1,0},{2,3},{3,2},{4,5},{5,4},{6,7},{7,6},{8,9},{9,8},{10,11... | collective-permute-start | bytes 294920 | tf_op jit(solution)/shard_map/ppermute | solution.py:769
  9.9 6.8 %collective-permute-start.6 = (f32[21,8,256]{2,1,0:T(8,128)S(1)}, f32[21,8,256]{2,1,0:T(8,128)S(1)}, u32[]{:S(2)}, u32[]{:S(2)}) collective-permute-start(f32[21,8,256]{2,1,0:T(8,128)S(1)} %get-tuple-element.47), channel_id=1, source_target_pairs={{0,16},{4,8},{8,4},{12,28},{16,0},{20,24},{24,20},{28,12},{1,17},{... | collective-permute-start | bytes 516104 | tf_op jit(solution)/shard_map/ppermute | solution.py:769
  11.4 5.3 %collective-permute-start.7 = (f32[21,8,256]{2,1,0:T(8,128)S(1)}, f32[21,8,256]{2,1,0:T(8,128)S(1)}, u32[]{:S(2)}, u32[]{:S(2)}) collective-permute-start(f32[21,8,256]{2,1,0:T(8,128)S(1)} %get-tuple-element.48), channel_id=1, source_target_pairs={{0,4},{4,0},{8,12},{12,8},{16,20},{20,16},{24,28},{28,24},{1,5},{5... | collective-permute-start | bytes 516104 | tf_op jit(solution)/shard_map/ppermute | solution.py:769
  12.7 5.3 %collective-permute-start.4 = (f32[9,8,256]{2,1,0:T(8,128)S(1)}, f32[9,8,256]{2,1,0:T(8,128)S(1)}, u32[]{:S(2)}, u32[]{:S(2)}) collective-permute-start(f32[9,8,256]{2,1,0:T(8,128)S(1)} %get-tuple-element.43), channel_id=1, source_target_pairs={{0,16},{4,8},{8,4},{12,28},{16,0},{20,24},{24,20},{28,12},{1,17},{... | collective-permute-start | bytes 221192 | tf_op jit(solution)/shard_map/ppermute | solution.py:769
  13.4 4.6 %collective-permute-start.5 = (f32[9,8,256]{2,1,0:T(8,128)S(1)}, f32[9,8,256]{2,1,0:T(8,128)S(1)}, u32[]{:S(2)}, u32[]{:S(2)}) collective-permute-start(f32[9,8,256]{2,1,0:T(8,128)S(1)} %get-tuple-element.44), channel_id=1, source_target_pairs={{0,4},{4,0},{8,12},{12,8},{16,20},{20,16},{24,28},{28,24},{1,5},{5... | collective-permute-start | bytes 221192 | tf_op jit(solution)/shard_map/ppermute | solution.py:769
  13.4 4.6 %collective-permute-start.3 = (f32[16,128]{1,0:T(8,128)S(1)}, f32[16,128]{1,0:T(8,128)S(1)}, u32[]{:S(2)}, u32[]{:S(2)}) collective-permute-start(f32[16,128]{1,0:T(8,128)S(1)} %get-tuple-element.42.refs_2_), channel_id=1, source_target_pairs={{0,2},{1,3},{2,0},{3,1},{4,6},{5,7},{6,4},{7,5},{8,10},{9,11},{10,... | collective-permute-start | bytes 24584 | tf_op jit(solution)/shard_map/ppermute | solution.py:733
  19.1 5.6 %collective-permute-start.8 = (f32[36,1,128]{2,1,0:T(1,128)S(1)}, f32[36,1,128]{2,1,0:T(1,128)S(1)}, u32[]{:S(2)}, u32[]{:S(2)}) collective-permute-start(f32[36,1,128]{2,1,0:T(1,128)S(1)} %get-tuple-element.56), channel_id=1, source_target_pairs={{0,3},{1,2},{2,1},{3,0},{4,7},{5,6},{6,5},{7,4},{8,11},{9,10},{10,... | collective-permute-start | bytes 55304 | tf_op jit(solution)/shard_map/ppermute | solution.py:733
  21.1 4.7 %collective-permute-start.9 = (f32[36,1,128]{2,1,0:T(1,128)S(1)}, f32[36,1,128]{2,1,0:T(1,128)S(1)}, u32[]{:S(2)}, u32[]{:S(2)}) collective-permute-start(f32[36,1,128]{2,1,0:T(1,128)S(1)} %get-tuple-element.57), channel_id=1, source_target_pairs={{0,2},{1,3},{2,0},{3,1},{4,6},{5,7},{6,4},{7,5},{8,10},{9,11},{10,... | collective-permute-start | bytes 55304 | tf_op jit(solution)/shard_map/ppermute | solution.py:733
  21.5 4.3 %collective-permute-start.10 = (f32[36,1,128]{2,1,0:T(1,128)S(1)}, f32[36,1,128]{2,1,0:T(1,128)S(1)}, u32[]{:S(2)}, u32[]{:S(2)}) collective-permute-start(f32[36,1,128]{2,1,0:T(1,128)S(1)} %get-tuple-element.58), channel_id=1, source_target_pairs={{0,1},{1,0},{2,3},{3,2},{4,5},{5,4},{6,7},{7,6},{8,9},{9,8},{10,11... | collective-permute-start | bytes 55304 | tf_op jit(solution)/shard_map/ppermute | solution.py:733

commit v15 on v14

--- a/solution.py
+++ b/solution.py
@@ -625,15 +625,15 @@
                 forces[part * 3 + p, corner] = piece
 
 
-def spread_kernel(base, low_ids, high_ids, forces, out):
+def spread_kernel(low_ids, high_ids, forces, own, other):
     runs = low_ids.shape[1]
-    parts, rows, length = out.shape
+    parts, rows, length = own.shape
     pieces = length // BLK
-    slots = pieces * rows
+    node_blocks = pieces * rows
+    slots = 2 * node_blocks
     kind = jnp.bfloat16
     tile = 16
-    slot_ids = lax.broadcasted_iota(jnp.int32, (slots, BLK), 0).astype(F32) + base
-    slot_ids = slot_ids.astype(kind)
+    slot_ids = lax.broadcasted_iota(jnp.int32, (slots, BLK), 0).astype(F32).astype(kind)
     lane_ids = lax.broadcasted_iota(jnp.int32, (BLK, BLK), 0).astype(F32).astype(kind)
     ones = jnp.ones((BLK, BLK), kind)
     none = jnp.zeros((BLK, BLK), kind)
@@ -668,8 +668,10 @@
         for part in range(1, PIECES):
             start = (parts * part + p) * slots
             summed = summed + total[start : start + slots]
-        for piece in range(pieces):
-            out[p, :, piece * BLK : (piece + 1) * BLK] = summed[piece * rows : (piece + 1) * rows]
+        for out, first in ((own, 0), (other, node_blocks)):
+            for piece in range(pieces):
+                at = first + piece * rows
+                out[p, :, piece * BLK : (piece + 1) * BLK] = summed[at : at + rows]
 
 
 def store_kernel(values, out_hbm, sem):
@@ -844,9 +846,9 @@
     )
     near_x, far_x = swap(near, far, "slab", "group")
     nodal = shape(3, node_blocks // half, length)
-    (other,) = call(
-        functools.partial(spread_kernel, node_blocks),
-        (nodal,),
+    own, other = call(
+        spread_kernel,
+        (nodal, nodal),
         (low_ids, high_ids, forces),
         (vmem,) * 3,
         micros=0.001,
@@ -861,13 +863,6 @@
         micros=0.3,
     )
     near_c, far_c = swap(near, far, "slab", "group")
-    (own,) = call(
-        functools.partial(spread_kernel, 0),
-        (nodal,),
-        (low_ids, high_ids, forces),
-        (vmem,) * 3,
-        micros=0.8,
-    )
     wide = planes + 4
     walls_shape = shape(2, SLOTS, wide, length)
     second_shape = shape(Q, planes + 2, rows, length)

time: 26.7 us -> 26.6 us (level)
  Pallas kernels: 8.87 us -> 8.06 us
  waiting for transfers between devices: 2.29 us -> 3.09 us
    ppermute x4, waiting for transfers between devices: 2.23 us -> 3.07 us  [exchange(): lax.ppermute(block, axis, [(i, partner_of(i, step, count)) for i in range...]
    pallas_call x10 -> x9, Pallas kernels: 8.87 us -> 8.06 us  [call(): pl.pallas_call(kernel, out_shape=outs, in_specs=[spec(space) for space in...]
  transfers between devices with their start and end apart: 11 -> 11, of which waited for: 3 -> 3; matrix products, arithmetic and copies ran while one was open for 0% -> 0% of each run, Pallas kernels for 27% -> 24%
where the time goes in v15:
time: 26.6 us; the launch traced here: 26.5 us
  starting transfers between devices  13.9 us (52%)
  Pallas kernels  8.06 us (30%)
  waiting for transfers between devices  3.09 us (12%)
  between operations  1.39 us (5%)
    pallas_call x9, Pallas kernels, call(): pl.pallas_call(kernel, out_shape=outs, in_specs=[spec(space) for space in...  8.06 us
    ppermute x4, starting transfers between devices, exchange(): lax.ppermute(block, axis, [(i, partner_of(i, step, count)) for i in range...  5.94 us
    ppermute x3, starting transfers between devices, swap(): lax.ppermute(near, axes, routes[0])  3.14 us
    ppermute x4, waiting for transfers between devices, exchange(): lax.ppermute(block, axis, [(i, partner_of(i, step, count)) for i in range...  3.07 us
    ppermute x1, starting transfers between devices, around(): lax.ppermute(block, axis, [(i, (i + step) % count) for i in range(count)])  2.46 us
    ppermute x3, starting transfers between devices, swap(): lax.ppermute(far, axes, routes[1])  2.38 us
  transfers between devices with their start and end apart: 11, of which 3 were waited for; matrix products, arithmetic and copies ran while one was open for 0% of the time, Pallas kernels for 24%

profile of v15, /device:TPU:0, one launch (start us, length us, event | category | flops | bytes accessed | tf_op | source)
XLA Modules:
  0.0 26.5 jit_solution(7569706091249440379)
XLA Ops:
  0.6 2.5 %collective-permute-start.2 = (f32[3,2048]{1,0:T(4,128)}, f32[3,2048]{1,0:T(4,128)S(1)}, u32[]{:S(2)}, u32[]{:S(2)}) collective-permute-start(f32[3,2048]{1,0:T(4,128)} %displacement_hbm.1), channel_id=1, source_target_pairs={{0,12},{4,0},{8,4},{12,8},{1,13},{5,1},{9,5},{13,9},{2,14},{6,2},{... | collective-permute-start | bytes 73736 | tf_op jit(solution)/shard_map/ppermute | solution.py:753
  3.1 1.8 %shard_map.130 = (f32[19,4,8,256]{3,2,1,0:T(8,128)S(1)}, f32[2,4,8,256]{3,2,1,0:T(8,128)S(1)}, f32[24,4,256]{2,1,0:T(4,128)S(1)}, f32[24,4,256]{2,1,0:T(4,128)S(...) custom-call(f32[19,4,8,256]{3,2,1,0:T(8,128)} %pops_hbm.1, ...), custom_call_target="tpu_custom_call" | custom-call | bytes 5400000 | tf_op jit(solution)/shard_map/pallas_call | solution.py:711
  4.9 0.1 collective-permute-start
  5.0 3.1 %collective-permute-start.1 = (f32[24,4,256]{2,1,0:T(4,128)S(1)}, f32[24,4,256]{2,1,0:T(4,128)S(1)}, u32[]{:S(2)}, u32[]{:S(2)}) collective-permute-start(f32[24,4,256]{2,1,0:T(4,128)S(1)} %get-tuple-element.35), channel_id=1, source_target_pairs={{0,1},{1,0},{2,3},{3,2},{4,5},{5,4},{6,7},{7,6},{8,9},{9,8},{10,11... | collective-permute-start | bytes 294920 | tf_op jit(solution)/shard_map/ppermute | solution.py:771
  8.1 0.0 collective-permute-done.2.next_nodes
  8.1 1.7 %shard_map.131 = (f32[3,32,128]{2,1,0:T(8,128)S(1)}, f32[3,32,128]{2,1,0:T(8,128)S(1)}, f32[6,3,32,128]{3,2,1,0:T(8,128)S(1)}) custom-call(s32[3,4096]{1,0:T(4,128)S(1)} %get-tuple-element.36.elements, f32[3,2048]{1,0:T(4,128)S(1)} %get-tuple-element.37.displacement, f32[3,2048]{1,0:T(4,128)S(1)} %collective-permute-done.2.next_nodes, ...), custom_call_target="tpu_custom_call" | custom-call | bytes 3600 | tf_op jit(solution)/shard_map/pallas_call | solution.py:711
  9.8 0.1 shard_map.134
  9.9 1.6 %collective-permute-start.6 = (f32[21,8,256]{2,1,0:T(8,128)S(1)}, f32[21,8,256]{2,1,0:T(8,128)S(1)}, u32[]{:S(2)}, u32[]{:S(2)}) collective-permute-start(f32[21,8,256]{2,1,0:T(8,128)S(1)} %get-tuple-element.50), channel_id=1, source_target_pairs={{0,16},{4,8},{8,4},{12,28},{16,0},{20,24},{24,20},{28,12},{1,17},{... | collective-permute-start | bytes 516104 | tf_op jit(solution)/shard_map/ppermute | solution.py:771
  11.4 0.0 collective-permute-start.7
  11.4 1.4 %shard_map.132 = (f32[3,8,256]{2,1,0:T(8,128)S(1)}, f32[3,8,256]{2,1,0:T(8,128)S(1)}) custom-call(f32[3,32,128]{2,1,0:T(8,128)S(1)} %get-tuple-element.40.low_ids.numbers, f32[3,32,128]{2,1,0:T(8,128)S(1)} %get-tuple-element.41.high_ids, f32[6,3,32,128]{3,2,1,0:T(8,128)S(1)} %get-tuple-element.42.forces), custom_call_target="tpu_custom_call" | custom-call | bytes 3600 | tf_op jit(solution)/shard_map/pallas_call | solution.py:711
  12.8 0.0 collective-permute-done.far_y
  12.8 0.0 collective-permute-done.1.near_y
  12.8 0.1 shard_map.133
  12.9 0.8 %collective-permute-start.4 = (f32[9,8,256]{2,1,0:T(8,128)S(1)}, f32[9,8,256]{2,1,0:T(8,128)S(1)}, u32[]{:S(2)}, u32[]{:S(2)}) collective-permute-start(f32[9,8,256]{2,1,0:T(8,128)S(1)} %get-tuple-element.46), channel_id=1, source_target_pairs={{0,16},{4,8},{8,4},{12,28},{16,0},{20,24},{24,20},{28,12},{1,17},{... | collective-permute-start | bytes 221192 | tf_op jit(solution)/shard_map/ppermute | solution.py:771
  13.7 0.0 collective-permute-start.5
  13.7 1.5 %collective-permute-start.3 = (f32[16,128]{1,0:T(8,128)S(1)}, f32[16,128]{1,0:T(8,128)S(1)}, u32[]{:S(2)}, u32[]{:S(2)}) collective-permute-start(f32[16,128]{1,0:T(8,128)S(1)} %get-tuple-element.45.refs_2_), channel_id=1, source_target_pairs={{0,2},{1,3},{2,0},{3,1},{4,6},{5,7},{6,4},{7,5},{8,10},{9,11},{10,... | collective-permute-start | bytes 24584 | tf_op jit(solution)/shard_map/ppermute | solution.py:735
  15.8 0.0 collective-permute-done.6.far_x
  15.9 0.0 collective-permute-done.7.near_x
  15.9 0.5 %shard_map.135 = (f32[19,8,8,256]{3,2,1,0:T(8,128)S(1)}, f32[2,21,8,256]{3,2,1,0:T(8,128)S(1)}, f32[2,5,8,256]{3,2,1,0:T(8,128)S(1)}, f32[19,6,8,256]{3,2,1,0:T(8,128)S(1)}, f32[2,2,8,256]{3,2,1,0:T(8,128)S(1)}) custom-call(f32[19,4,8,256]{3,2,1,0:T(8,128)S(1)} %get-tuple-element.49.c1, f32[2,4,8,256]{3,2,1,0:T(8,128)S(1)} %get-tuple-element.48.fixed.refs_6_, ...), custom_call_target="tpu_custom_call" | custom-call | bytes 2880000 | tf_op jit(solution)/shard_map/pallas_call | solution.py:711
  16.4 1.9 %collective-permute-done.3.refs_3_ = f32[16,128]{1,0:T(8,128)S(1)} collective-permute-done((f32[16,128]{1,0:T(8,128)S(1)}, f32[16,128]{1,0:T(8,128)S(1)}, u32[]{:S(2)}, u32[]{:S(2)}) %collective-permute-start.3) | collective-permute-done | bytes 8224 | tf_op jit(solution)/shard_map/ppermute | solution.py:735
  18.3 0.0 collective-permute-done.4.refs_4_
  18.3 0.0 collective-permute-done.5.refs_5_
  18.3 1.1 %shard_map.136 = (f32[19,4,8,256]{3,2,1,0:T(8,128)S(1)}, f32[80,128]{1,0:T(8,128)S(1)}, f32[36,1,128]{2,1,0:T(1,128)S(1)}, f32[36,1,128]{2,1,0:T(1,128)S(1)}, f3...) custom-call(s32[1,1,8]{2,1,0:T(1,128)} %refs_0_.1, ...), custom_call_target="tpu_custom_call", output_to_operand_aliasing={{5}: (11, {}), {6}: (12, {})} | custom-call | bytes 5400000 | tf_op jit(solution)/shard_map/pallas_call | solution.py:711
  19.3 1.8 %collective-permute-start.8 = (f32[36,1,128]{2,1,0:T(1,128)S(1)}, f32[36,1,128]{2,1,0:T(1,128)S(1)}, u32[]{:S(2)}, u32[]{:S(2)}) collective-permute-start(f32[36,1,128]{2,1,0:T(1,128)S(1)} %get-tuple-element.60), channel_id=1, source_target_pairs={{0,3},{1,2},{2,1},{3,0},{4,7},{5,6},{6,5},{7,4},{8,11},{9,10},{10,... | collective-permute-start | bytes 55304 | tf_op jit(solution)/shard_map/ppermute | solution.py:735
  21.1 0.4 %collective-permute-start.9 = (f32[36,1,128]{2,1,0:T(1,128)S(1)}, f32[36,1,128]{2,1,0:T(1,128)S(1)}, u32[]{:S(2)}, u32[]{:S(2)}) collective-permute-start(f32[36,1,128]{2,1,0:T(1,128)S(1)} %get-tuple-element.61), channel_id=1, source_target_pairs={{0,2},{1,3},{2,0},{3,1},{4,6},{5,7},{6,4},{7,5},{8,10},{9,11},{10,... | collective-permute-start | bytes 55304 | tf_op jit(solution)/shard_map/ppermute | solution.py:735
  21.5 2.2 %collective-permute-start.10 = (f32[36,1,128]{2,1,0:T(1,128)S(1)}, f32[36,1,128]{2,1,0:T(1,128)S(1)}, u32[]{:S(2)}, u32[]{:S(2)}) collective-permute-start(f32[36,1,128]{2,1,0:T(1,128)S(1)} %get-tuple-element.62), channel_id=1, source_target_pairs={{0,1},{1,0},{2,3},{3,2},{4,5},{5,4},{6,7},{7,6},{8,9},{9,8},{10,11... | collective-permute-start | bytes 55304 | tf_op jit(solution)/shard_map/ppermute | solution.py:735
  23.8 0.8 %shard_map.137 = f32[19,4,8,256]{3,2,1,0:T(8,128)} custom-call(f32[19,4,8,256]{3,2,1,0:T(8,128)S(1)} %get-tuple-element.58.values), custom_call_target="tpu_custom_call" | custom-call | bytes 3600000 | tf_op jit(solution)/shard_map/pallas_call | solution.py:711
  24.6 0.4 %collective-permute-done.8.refs_0_ = f32[36,1,128]{2,1,0:T(1,128)S(1)} collective-permute-done((f32[36,1,128]{2,1,0:T(1,128)S(1)}, f32[36,1,128]{2,1,0:T(1,128)S(1)}, u32[]{:S(2)}, u32[]{:S(2)}) %collective-permute-start.8) | collective-permute-done | bytes 18464 | tf_op jit(solution)/shard_map/ppermute | solution.py:735
  25.0 0.8 %collective-permute-done.9.refs_1_ = f32[36,1,128]{2,1,0:T(1,128)S(1)} collective-permute-done((f32[36,1,128]{2,1,0:T(1,128)S(1)}, f32[36,1,128]{2,1,0:T(1,128)S(1)}, u32[]{:S(2)}, u32[]{:S(2)}) %collective-permute-start.9) | collective-permute-done | bytes 18464 | tf_op jit(solution)/shard_map/ppermute | solution.py:735
  25.8 0.0 collective-permute-done.10.refs_2_
  25.8 0.7 %shard_map.138 = (f32[3,2048]{1,0:T(4,128)}, f32[3,8,128]{2,1,0:T(8,128)}) custom-call(f32[80,128]{1,0:T(8,128)S(1)} %get-tuple-element.59.mine, f32[36,1,128]{2,1,0:T(1,128)S(1)} %collective-permute-done.8.refs_0_, f32[36,1,128]{2,1,0:T(1,128)S(1)} %collective-permute-done.9.refs_1_, f32[36,1,128]{2,1,0:T(1,128)S(1)} %collective-permute-done.10.refs_2_), custom_call_target="tpu_custom_call" | custom-call | bytes 2880000 | tf_op jit(solution)/shard_map/pallas_call | solution.py:711
Async XLA Ops:
  0.6 7.5 %collective-permute-start.2 = (f32[3,2048]{1,0:T(4,128)}, f32[3,2048]{1,0:T(4,128)S(1)}, u32[]{:S(2)}, u32[]{:S(2)}) collective-permute-start(f32[3,2048]{1,0:T(4,128)} %displacement_hbm.1), channel_id=1, source_target_pairs={{0,12},{4,0},{8,4},{12,8},{1,13},{5,1},{9,5},{13,9},{2,14},{6,2},{... | collective-permute-start | bytes 73736 | tf_op jit(solution)/shard_map/ppermute | solution.py:753
  4.9 7.9 %collective-permute-start = (f32[24,4,256]{2,1,0:T(4,128)S(1)}, f32[24,4,256]{2,1,0:T(4,128)S(1)}, u32[]{:S(2)}, u32[]{:S(2)}) collective-permute-start(f32[24,4,256]{2,1,0:T(4,128)S(1)} %get-tuple-element.34), channel_id=1, source_target_pairs={{0,4},{1,2},{2,1},{3,7},{4,0},{5,6},{6,5},{7,3},{8,12},{9,10},{10,... | collective-permute-start | bytes 294920 | tf_op jit(solution)/shard_map/ppermute | solution.py:771
  5.0 7.9 %collective-permute-start.1 = (f32[24,4,256]{2,1,0:T(4,128)S(1)}, f32[24,4,256]{2,1,0:T(4,128)S(1)}, u32[]{:S(2)}, u32[]{:S(2)}) collective-permute-start(f32[24,4,256]{2,1,0:T(4,128)S(1)} %get-tuple-element.35), channel_id=1, source_target_pairs={{0,1},{1,0},{2,3},{3,2},{4,5},{5,4},{6,7},{7,6},{8,9},{9,8},{10,11... | collective-permute-start | bytes 294920 | tf_op jit(solution)/shard_map/ppermute | solution.py:771
  9.9 6.0 %collective-permute-start.6 = (f32[21,8,256]{2,1,0:T(8,128)S(1)}, f32[21,8,256]{2,1,0:T(8,128)S(1)}, u32[]{:S(2)}, u32[]{:S(2)}) collective-permute-start(f32[21,8,256]{2,1,0:T(8,128)S(1)} %get-tuple-element.50), channel_id=1, source_target_pairs={{0,16},{4,8},{8,4},{12,28},{16,0},{20,24},{24,20},{28,12},{1,17},{... | collective-permute-start | bytes 516104 | tf_op jit(solution)/shard_map/ppermute | solution.py:771
  11.4 4.4 %collective-permute-start.7 = (f32[21,8,256]{2,1,0:T(8,128)S(1)}, f32[21,8,256]{2,1,0:T(8,128)S(1)}, u32[]{:S(2)}, u32[]{:S(2)}) collective-permute-start(f32[21,8,256]{2,1,0:T(8,128)S(1)} %get-tuple-element.51), channel_id=1, source_target_pairs={{0,4},{4,0},{8,12},{12,8},{16,20},{20,16},{24,28},{28,24},{1,5},{5... | collective-permute-start | bytes 516104 | tf_op jit(solution)/shard_map/ppermute | solution.py:771
  12.9 5.3 %collective-permute-start.4 = (f32[9,8,256]{2,1,0:T(8,128)S(1)}, f32[9,8,256]{2,1,0:T(8,128)S(1)}, u32[]{:S(2)}, u32[]{:S(2)}) collective-permute-start(f32[9,8,256]{2,1,0:T(8,128)S(1)} %get-tuple-element.46), channel_id=1, source_target_pairs={{0,16},{4,8},{8,4},{12,28},{16,0},{20,24},{24,20},{28,12},{1,17},{... | collective-permute-start | bytes 221192 | tf_op jit(solution)/shard_map/ppermute | solution.py:771
  13.7 4.6 %collective-permute-start.5 = (f32[9,8,256]{2,1,0:T(8,128)S(1)}, f32[9,8,256]{2,1,0:T(8,128)S(1)}, u32[]{:S(2)}, u32[]{:S(2)}) collective-permute-start(f32[9,8,256]{2,1,0:T(8,128)S(1)} %get-tuple-element.47), channel_id=1, source_target_pairs={{0,4},{4,0},{8,12},{12,8},{16,20},{20,16},{24,28},{28,24},{1,5},{5... | collective-permute-start | bytes 221192 | tf_op jit(solution)/shard_map/ppermute | solution.py:771
  13.7 4.5 %collective-permute-start.3 = (f32[16,128]{1,0:T(8,128)S(1)}, f32[16,128]{1,0:T(8,128)S(1)}, u32[]{:S(2)}, u32[]{:S(2)}) collective-permute-start(f32[16,128]{1,0:T(8,128)S(1)} %get-tuple-element.45.refs_2_), channel_id=1, source_target_pairs={{0,2},{1,3},{2,0},{3,1},{4,6},{5,7},{6,4},{7,5},{8,10},{9,11},{10,... | collective-permute-start | bytes 24584 | tf_op jit(solution)/shard_map/ppermute | solution.py:735
  19.3 5.7 %collective-permute-start.8 = (f32[36,1,128]{2,1,0:T(1,128)S(1)}, f32[36,1,128]{2,1,0:T(1,128)S(1)}, u32[]{:S(2)}, u32[]{:S(2)}) collective-permute-start(f32[36,1,128]{2,1,0:T(1,128)S(1)} %get-tuple-element.60), channel_id=1, source_target_pairs={{0,3},{1,2},{2,1},{3,0},{4,7},{5,6},{6,5},{7,4},{8,11},{9,10},{10,... | collective-permute-start | bytes 55304 | tf_op jit(solution)/shard_map/ppermute | solution.py:735
  21.1 4.7 %collective-permute-start.9 = (f32[36,1,128]{2,1,0:T(1,128)S(1)}, f32[36,1,128]{2,1,0:T(1,128)S(1)}, u32[]{:S(2)}, u32[]{:S(2)}) collective-permute-start(f32[36,1,128]{2,1,0:T(1,128)S(1)} %get-tuple-element.61), channel_id=1, source_target_pairs={{0,2},{1,3},{2,0},{3,1},{4,6},{5,7},{6,4},{7,5},{8,10},{9,11},{10,... | collective-permute-start | bytes 55304 | tf_op jit(solution)/shard_map/ppermute | solution.py:735
  21.5 4.3 %collective-permute-start.10 = (f32[36,1,128]{2,1,0:T(1,128)S(1)}, f32[36,1,128]{2,1,0:T(1,128)S(1)}, u32[]{:S(2)}, u32[]{:S(2)}) collective-permute-start(f32[36,1,128]{2,1,0:T(1,128)S(1)} %get-tuple-element.62), channel_id=1, source_target_pairs={{0,1},{1,0},{2,3},{3,2},{4,5},{5,4},{6,7},{7,6},{8,9},{9,8},{10,11... | collective-permute-start | bytes 55304 | tf_op jit(solution)/shard_map/ppermute | solution.py:735

commit v16 on v15

--- a/solution.py
+++ b/solution.py
@@ -377,15 +377,29 @@
     lax.fori_loop(1, planes - 1, inside_plane, 0)
 
 
-def second_kernel(count, tables, *refs):
-    block_source_hbm, block_count = refs[:2]
-    known = refs[2 : 2 + tables]
-    far, near, fixed, extended, crossing, ends, internal_own = refs[2 + tables : 9 + tables]
-    rest = refs[11 + tables :]
-    out, mine = rest[:2]
-    messages = rest[2 : 1 + count]
-    walls, second = rest[1 + count : 3 + count]
-    both, edges, loads, internal, block_source, sem = rest[3 + count :]
+def second_kernel(
+    block_source_hbm,
+    far,
+    near,
+    fixed,
+    extended,
+    crossing,
+    ends,
+    internal_own,
+    walls_in,
+    second_in,
+    out,
+    blocks,
+    internal,
+    walls,
+    second,
+    both,
+    edges,
+    loads,
+    block_source,
+    sem,
+):
+    del walls_in, second_in
     copy = pltpu.make_async_copy(block_source_hbm, block_source, sem)
     copy.start()
     planes, rows, length = out.shape[1:]
@@ -486,15 +500,28 @@
                 internal_own[part, :, lanes] + both[0, FORCE_SLOT + part, :, lanes]
             )
     copy.wait()
-    live = jnp.broadcast_to(block_count[...], (1, BLK))
-    blocks, keys = [], []
     for k in range(slots):
         run = block_source[0, 0, k]
         x = run // (rows * half)
         left = run - x * (rows * half)
         y = left // half
         piece = left - y * half
-        blocks.append([loads[x * half + piece, part, pl.ds(y, 1)] for part in range(3)])
+        for part in range(3):
+            row = 3 * k + part
+            blocks[row : row + 1] = loads[x * half + piece, part, pl.ds(y, 1)]
+
+
+def message_kernel(count, tables, block_count, *refs):
+    known = refs[:tables]
+    block_rows, internal, mine = refs[tables : tables + 3]
+    messages = refs[tables + 3 :]
+    slots = block_rows.shape[0] // 3
+    node_blocks = internal.shape[1]
+    inner = lax.axis_index("inner")
+    live = jnp.broadcast_to(block_count[...], (1, BLK))
+    blocks, keys = [], []
+    for k in range(slots):
+        blocks.append([block_rows[3 * k + part : 3 * k + part + 1] for part in range(3)])
         keys.append(jnp.where(live > k, known[0][k : k + 1], -1.0))
 
     def summed(wanted):
@@ -884,21 +911,11 @@
         micros=0.8,
     )
     tables = all_keys(own_keys, known, "inner")
-    first = 2 + len(tables)
-    line = shape(3 * slots + 4 * CAP, 1, BLK)
-    outs = call(
-        functools.partial(second_kernel, count, len(tables)),
-        (
-            whole,
-            shape(3 * node_blocks + 4 * slots, BLK),
-            *([line] * (count - 1)),
-            walls_shape,
-            second_shape,
-        ),
+    values, blocks, internal, _, _ = call(
+        second_kernel,
+        (whole, shape(3 * slots, BLK), shape(3, node_blocks, BLK), walls_shape, second_shape),
         (
             pin(block_source),
-            block_count,
-            *tables,
             far_c,
             near_c,
             fixed,
@@ -909,20 +926,26 @@
             walls,
             second,
         ),
-        (hbm,) + (vmem,) * (first + 8),
-        aliases={first + 7: 1 + count, first + 8: 2 + count},
+        (hbm,) + (vmem,) * 9,
+        aliases={8: 3, 9: 4},
         scratch=(
             pltpu.VMEM((2, CORNER_SLOTS, rows, length), F32),
             pltpu.VMEM((2, 5, wide, length), F32),
             pltpu.VMEM((planes * half, 3, rows, BLK), F32),
-            pltpu.VMEM((3, node_blocks, BLK), F32),
             pltpu.SMEM(block_source.shape, jnp.int32),
             pltpu.SemaphoreType.DMA(()),
         ),
         micros=1.5,
     )
-    values, mine = outs[:2]
-    arrived = [exchange(outs[1 + step], "inner", step) for step in range(count - 1, 0, -1)]
+    line = shape(3 * slots + 4 * CAP, 1, BLK)
+    mine, *outgoing = call(
+        functools.partial(message_kernel, count, len(tables)),
+        (shape(3 * node_blocks + 4 * slots, BLK), *([line] * (count - 1))),
+        (block_count, *tables, blocks, internal),
+        (vmem,) * (len(tables) + 3),
+        micros=0.3,
+    )
+    arrived = [exchange(outgoing[step - 1], "inner", step) for step in range(count - 1, 0, -1)]
     (populations_out,) = call(
         store_kernel,
         (whole,),

time: 26.6 us -> 27 us (1.015)
  waiting for transfers between devices: 3.09 us -> 4.28 us
  starting transfers between devices: 13.9 us -> 13 us
    ppermute x3, waiting for transfers between devices: 0.01 us -> 1.02 us  [swap(): lax.ppermute(far, axes, routes[1])]
    ppermute x4, starting transfers between devices: 5.94 us -> 5.05 us  [exchange(): lax.ppermute(block, axis, [(i, partner_of(i, step, count)) for i in range...]
    pallas_call x9 -> x10, Pallas kernels: 8.06 us -> 8.14 us  [call(): pl.pallas_call(kernel, out_shape=outs, in_specs=[spec(space) for space in...]
  transfers between devices with their start and end apart: 11 -> 11, of which waited for: 3 -> 3; matrix products, arithmetic and copies ran while one was open for 0% -> 0% of each run, Pallas kernels for 24% -> 27%
where the time goes in v16:
time: 27 us; the launch traced here: 26.9 us
  starting transfers between devices  13 us (48%)
  Pallas kernels  8.14 us (30%)
  waiting for transfers between devices  4.28 us (16%)
  between operations  1.41 us (5%)
    pallas_call x10, Pallas kernels, call(): pl.pallas_call(kernel, out_shape=outs, in_specs=[spec(space) for space in...  8.14 us
    ppermute x4, starting transfers between devices, exchange(): lax.ppermute(block, axis, [(i, partner_of(i, step, count)) for i in range...  5.05 us
    ppermute x4, waiting for transfers between devices, exchange(): lax.ppermute(block, axis, [(i, partner_of(i, step, count)) for i in range...  3.26 us
    ppermute x3, starting transfers between devices, swap(): lax.ppermute(near, axes, routes[0])  3.14 us
    ppermute x1, starting transfers between devices, around(): lax.ppermute(block, axis, [(i, (i + step) % count) for i in range(count)])  2.46 us
    ppermute x3, starting transfers between devices, swap(): lax.ppermute(far, axes, routes[1])  2.38 us
    ppermute x3, waiting for transfers between devices, swap(): lax.ppermute(far, axes, routes[1])  1.02 us
  transfers between devices with their start and end apart: 11, of which 3 were waited for; matrix products, arithmetic and copies ran while one was open for 0% of the time, Pallas kernels for 27%

profile of v16, /device:TPU:0, one launch (start us, length us, event | category | flops | bytes accessed | tf_op | source)
XLA Modules:
  0.0 26.9 jit_solution(10026869039032468680)
XLA Ops:
  0.6 2.5 %collective-permute-start.2 = (f32[3,2048]{1,0:T(4,128)}, f32[3,2048]{1,0:T(4,128)S(1)}, u32[]{:S(2)}, u32[]{:S(2)}) collective-permute-start(f32[3,2048]{1,0:T(4,128)} %displacement_hbm.1), channel_id=1, source_target_pairs={{0,12},{4,0},{8,4},{12,8},{1,13},{5,1},{9,5},{13,9},{2,14},{6,2},{... | collective-permute-start | bytes 73736 | tf_op jit(solution)/shard_map/ppermute | solution.py:780
  3.1 1.8 %shard_map.130 = (f32[19,4,8,256]{3,2,1,0:T(8,128)S(1)}, f32[2,4,8,256]{3,2,1,0:T(8,128)S(1)}, f32[24,4,256]{2,1,0:T(4,128)S(1)}, f32[24,4,256]{2,1,0:T(4,128)S(...) custom-call(f32[19,4,8,256]{3,2,1,0:T(8,128)} %pops_hbm.1, ...), custom_call_target="tpu_custom_call" | custom-call | bytes 5400000 | tf_op jit(solution)/shard_map/pallas_call | solution.py:738
  4.9 0.1 collective-permute-start
  5.0 3.1 %collective-permute-start.1 = (f32[24,4,256]{2,1,0:T(4,128)S(1)}, f32[24,4,256]{2,1,0:T(4,128)S(1)}, u32[]{:S(2)}, u32[]{:S(2)}) collective-permute-start(f32[24,4,256]{2,1,0:T(4,128)S(1)} %get-tuple-element.37), channel_id=1, source_target_pairs={{0,1},{1,0},{2,3},{3,2},{4,5},{5,4},{6,7},{7,6},{8,9},{9,8},{10,11... | collective-permute-start | bytes 294920 | tf_op jit(solution)/shard_map/ppermute | solution.py:798
  8.1 0.0 collective-permute-done.2.next_nodes
  8.1 1.7 %shard_map.131 = (f32[3,32,128]{2,1,0:T(8,128)S(1)}, f32[3,32,128]{2,1,0:T(8,128)S(1)}, f32[6,3,32,128]{3,2,1,0:T(8,128)S(1)}) custom-call(s32[3,4096]{1,0:T(4,128)S(1)} %get-tuple-element.38.elements, f32[3,2048]{1,0:T(4,128)S(1)} %get-tuple-element.39.displacement, f32[3,2048]{1,0:T(4,128)S(1)} %collective-permute-done.2.next_nodes, ...), custom_call_target="tpu_custom_call" | custom-call | bytes 3600 | tf_op jit(solution)/shard_map/pallas_call | solution.py:738
  9.8 0.1 shard_map.134
  9.9 1.6 %collective-permute-start.5 = (f32[21,8,256]{2,1,0:T(8,128)S(1)}, f32[21,8,256]{2,1,0:T(8,128)S(1)}, u32[]{:S(2)}, u32[]{:S(2)}) collective-permute-start(f32[21,8,256]{2,1,0:T(8,128)S(1)} %get-tuple-element.51), channel_id=1, source_target_pairs={{0,16},{4,8},{8,4},{12,28},{16,0},{20,24},{24,20},{28,12},{1,17},{... | collective-permute-start | bytes 516104 | tf_op jit(solution)/shard_map/ppermute | solution.py:798
  11.4 0.0 collective-permute-start.6
  11.4 1.4 %shard_map.132 = (f32[3,8,256]{2,1,0:T(8,128)S(1)}, f32[3,8,256]{2,1,0:T(8,128)S(1)}) custom-call(f32[3,32,128]{2,1,0:T(8,128)S(1)} %get-tuple-element.42.low_ids.numbers, f32[3,32,128]{2,1,0:T(8,128)S(1)} %get-tuple-element.43.high_ids, f32[6,3,32,128]{3,2,1,0:T(8,128)S(1)} %get-tuple-element.44.forces), custom_call_target="tpu_custom_call" | custom-call | bytes 3600 | tf_op jit(solution)/shard_map/pallas_call | solution.py:738
  12.8 0.0 collective-permute-done.far_y
  12.8 0.0 collective-permute-done.1.near_y
  12.8 0.1 shard_map.133
  12.9 0.8 %collective-permute-start.3 = (f32[9,8,256]{2,1,0:T(8,128)S(1)}, f32[9,8,256]{2,1,0:T(8,128)S(1)}, u32[]{:S(2)}, u32[]{:S(2)}) collective-permute-start(f32[9,8,256]{2,1,0:T(8,128)S(1)} %get-tuple-element.47), channel_id=1, source_target_pairs={{0,16},{4,8},{8,4},{12,28},{16,0},{20,24},{24,20},{28,12},{1,17},{... | collective-permute-start | bytes 221192 | tf_op jit(solution)/shard_map/ppermute | solution.py:798
  13.7 0.0 collective-permute-start.4
  13.7 1.5 %collective-permute-start.7 = (f32[16,128]{1,0:T(8,128)S(1)}, f32[16,128]{1,0:T(8,128)S(1)}, u32[]{:S(2)}, u32[]{:S(2)}) collective-permute-start(f32[16,128]{1,0:T(8,128)S(1)} %get-tuple-element.60.refs_0_), channel_id=1, source_target_pairs={{0,2},{1,3},{2,0},{3,1},{4,6},{5,7},{6,4},{7,5},{8,10},{9,11},{10,... | collective-permute-start | bytes 24584 | tf_op jit(solution)/shard_map/ppermute | solution.py:762
  15.8 0.0 collective-permute-done.5.far_x
  15.9 0.0 collective-permute-done.6.near_x
  15.9 0.5 %shard_map.135 = (f32[19,8,8,256]{3,2,1,0:T(8,128)S(1)}, f32[2,21,8,256]{3,2,1,0:T(8,128)S(1)}, f32[2,5,8,256]{3,2,1,0:T(8,128)S(1)}, f32[19,6,8,256]{3,2,1,0:T(8,128)S(1)}, f32[2,2,8,256]{3,2,1,0:T(8,128)S(1)}) custom-call(f32[19,4,8,256]{3,2,1,0:T(8,128)S(1)} %get-tuple-element.50.c1, f32[2,4,8,256]{3,2,1,0:T(8,128)S(1)} %get-tuple-element.49.fixed, ...), custom_call_target="tpu_custom_call" | custom-call | bytes 2880000 | tf_op jit(solution)/shard_map/pallas_call | solution.py:738
  16.4 1.0 %collective-permute-done.3.far = f32[9,8,256]{2,1,0:T(8,128)S(1)} collective-permute-done((f32[9,8,256]{2,1,0:T(8,128)S(1)}, f32[9,8,256]{2,1,0:T(8,128)S(1)}, u32[]{:S(2)}, u32[]{:S(2)}) %collective-permute-start.3) | collective-permute-done | bytes 73760 | tf_op jit(solution)/shard_map/ppermute | solution.py:798
  17.4 0.0 collective-permute-done.4.near
  17.4 0.9 %shard_map.136 = (f32[19,4,8,256]{3,2,1,0:T(8,128)S(1)}, f32[24,128]{1,0:T(8,128)S(1)}, f32[3,16,128]{2,1,0:T(8,128)S(1)}, f32[2,21,8,256]{3,2,1,0:T(8,128)S(1)}, f32[19,6,8,256]{3,2,1,0:T(8,128)S(1)}) custom-call(s32[1,1,8]{2,1,0:T(1,128)} %block_source_hbm.1, ...), custom_call_target="tpu_custom_call", output_to_operand_aliasing={{3}: (8, {}), {4}: (9, {})} | custom-call | bytes 5400000 | tf_op jit(solution)/shard_map/pallas_call | solution.py:738
  18.3 0.0 collective-permute-done.7.refs_1_
  18.3 0.2 shard_map.138
  18.5 0.7 %collective-permute-start.10 = (f32[36,1,128]{2,1,0:T(1,128)S(1)}, f32[36,1,128]{2,1,0:T(1,128)S(1)}, u32[]{:S(2)}, u32[]{:S(2)}) collective-permute-start(f32[36,1,128]{2,1,0:T(1,128)S(1)} %get-tuple-element.66), channel_id=1, source_target_pairs={{0,1},{1,0},{2,3},{3,2},{4,5},{5,4},{6,7},{7,6},{8,9},{9,8},{10,11... | collective-permute-start | bytes 55304 | tf_op jit(solution)/shard_map/ppermute | solution.py:762
  19.2 2.3 %collective-permute-start.8 = (f32[36,1,128]{2,1,0:T(1,128)S(1)}, f32[36,1,128]{2,1,0:T(1,128)S(1)}, u32[]{:S(2)}, u32[]{:S(2)}) collective-permute-start(f32[36,1,128]{2,1,0:T(1,128)S(1)} %get-tuple-element.64), channel_id=1, source_target_pairs={{0,3},{1,2},{2,1},{3,0},{4,7},{5,6},{6,5},{7,4},{8,11},{9,10},{10,... | collective-permute-start | bytes 55304 | tf_op jit(solution)/shard_map/ppermute | solution.py:762
  21.5 0.6 %collective-permute-start.9 = (f32[36,1,128]{2,1,0:T(1,128)S(1)}, f32[36,1,128]{2,1,0:T(1,128)S(1)}, u32[]{:S(2)}, u32[]{:S(2)}) collective-permute-start(f32[36,1,128]{2,1,0:T(1,128)S(1)} %get-tuple-element.65), channel_id=1, source_target_pairs={{0,2},{1,3},{2,0},{3,1},{4,6},{5,7},{6,4},{7,5},{8,10},{9,11},{10,... | collective-permute-start | bytes 55304 | tf_op jit(solution)/shard_map/ppermute | solution.py:762
  22.1 0.8 %shard_map.137 = f32[19,4,8,256]{3,2,1,0:T(8,128)} custom-call(f32[19,4,8,256]{3,2,1,0:T(8,128)S(1)} %get-tuple-element.59.values), custom_call_target="tpu_custom_call" | custom-call | bytes 3600000 | tf_op jit(solution)/shard_map/pallas_call | solution.py:738
  22.9 0.0 collective-permute-done.10.refs_2_
  22.9 1.9 %collective-permute-done.8.refs_0_ = f32[36,1,128]{2,1,0:T(1,128)S(1)} collective-permute-done((f32[36,1,128]{2,1,0:T(1,128)S(1)}, f32[36,1,128]{2,1,0:T(1,128)S(1)}, u32[]{:S(2)}, u32[]{:S(2)}) %collective-permute-start.8) | collective-permute-done | bytes 18464 | tf_op jit(solution)/shard_map/ppermute | solution.py:762
  24.8 1.4 %collective-permute-done.9.refs_1_ = f32[36,1,128]{2,1,0:T(1,128)S(1)} collective-permute-done((f32[36,1,128]{2,1,0:T(1,128)S(1)}, f32[36,1,128]{2,1,0:T(1,128)S(1)}, u32[]{:S(2)}, u32[]{:S(2)}) %collective-permute-start.9) | collective-permute-done | bytes 18464 | tf_op jit(solution)/shard_map/ppermute | solution.py:762
  26.2 0.7 %shard_map.139 = (f32[3,2048]{1,0:T(4,128)}, f32[3,8,128]{2,1,0:T(8,128)}) custom-call(f32[80,128]{1,0:T(8,128)S(1)} %get-tuple-element.63.mine, f32[36,1,128]{2,1,0:T(1,128)S(1)} %collective-permute-done.8.refs_0_, f32[36,1,128]{2,1,0:T(1,128)S(1)} %collective-permute-done.9.refs_1_, f32[36,1,128]{2,1,0:T(1,128)S(1)} %collective-permute-done.10.refs_2_), custom_call_target="tpu_custom_call" | custom-call | bytes 2880000 | tf_op jit(solution)/shard_map/pallas_call | solution.py:738
Async XLA Ops:
  0.6 7.5 %collective-permute-start.2 = (f32[3,2048]{1,0:T(4,128)}, f32[3,2048]{1,0:T(4,128)S(1)}, u32[]{:S(2)}, u32[]{:S(2)}) collective-permute-start(f32[3,2048]{1,0:T(4,128)} %displacement_hbm.1), channel_id=1, source_target_pairs={{0,12},{4,0},{8,4},{12,8},{1,13},{5,1},{9,5},{13,9},{2,14},{6,2},{... | collective-permute-start | bytes 73736 | tf_op jit(solution)/shard_map/ppermute | solution.py:780
  4.9 7.9 %collective-permute-start = (f32[24,4,256]{2,1,0:T(4,128)S(1)}, f32[24,4,256]{2,1,0:T(4,128)S(1)}, u32[]{:S(2)}, u32[]{:S(2)}) collective-permute-start(f32[24,4,256]{2,1,0:T(4,128)S(1)} %get-tuple-element.36), channel_id=1, source_target_pairs={{0,4},{1,2},{2,1},{3,7},{4,0},{5,6},{6,5},{7,3},{8,12},{9,10},{10,... | collective-permute-start | bytes 294920 | tf_op jit(solution)/shard_map/ppermute | solution.py:798
  5.0 7.9 %collective-permute-start.1 = (f32[24,4,256]{2,1,0:T(4,128)S(1)}, f32[24,4,256]{2,1,0:T(4,128)S(1)}, u32[]{:S(2)}, u32[]{:S(2)}) collective-permute-start(f32[24,4,256]{2,1,0:T(4,128)S(1)} %get-tuple-element.37), channel_id=1, source_target_pairs={{0,1},{1,0},{2,3},{3,2},{4,5},{5,4},{6,7},{7,6},{8,9},{9,8},{10,11... | collective-permute-start | bytes 294920 | tf_op jit(solution)/shard_map/ppermute | solution.py:798
  9.9 6.0 %collective-permute-start.5 = (f32[21,8,256]{2,1,0:T(8,128)S(1)}, f32[21,8,256]{2,1,0:T(8,128)S(1)}, u32[]{:S(2)}, u32[]{:S(2)}) collective-permute-start(f32[21,8,256]{2,1,0:T(8,128)S(1)} %get-tuple-element.51), channel_id=1, source_target_pairs={{0,16},{4,8},{8,4},{12,28},{16,0},{20,24},{24,20},{28,12},{1,17},{... | collective-permute-start | bytes 516104 | tf_op jit(solution)/shard_map/ppermute | solution.py:798
  11.4 4.4 %collective-permute-start.6 = (f32[21,8,256]{2,1,0:T(8,128)S(1)}, f32[21,8,256]{2,1,0:T(8,128)S(1)}, u32[]{:S(2)}, u32[]{:S(2)}) collective-permute-start(f32[21,8,256]{2,1,0:T(8,128)S(1)} %get-tuple-element.52), channel_id=1, source_target_pairs={{0,4},{4,0},{8,12},{12,8},{16,20},{20,16},{24,28},{28,24},{1,5},{5... | collective-permute-start | bytes 516104 | tf_op jit(solution)/shard_map/ppermute | solution.py:798
  12.9 4.4 %collective-permute-start.3 = (f32[9,8,256]{2,1,0:T(8,128)S(1)}, f32[9,8,256]{2,1,0:T(8,128)S(1)}, u32[]{:S(2)}, u32[]{:S(2)}) collective-permute-start(f32[9,8,256]{2,1,0:T(8,128)S(1)} %get-tuple-element.47), channel_id=1, source_target_pairs={{0,16},{4,8},{8,4},{12,28},{16,0},{20,24},{24,20},{28,12},{1,17},{... | collective-permute-start | bytes 221192 | tf_op jit(solution)/shard_map/ppermute | solution.py:798
  13.7 3.7 %collective-permute-start.4 = (f32[9,8,256]{2,1,0:T(8,128)S(1)}, f32[9,8,256]{2,1,0:T(8,128)S(1)}, u32[]{:S(2)}, u32[]{:S(2)}) collective-permute-start(f32[9,8,256]{2,1,0:T(8,128)S(1)} %get-tuple-element.48), channel_id=1, source_target_pairs={{0,4},{4,0},{8,12},{12,8},{16,20},{20,16},{24,28},{28,24},{1,5},{5... | collective-permute-start | bytes 221192 | tf_op jit(solution)/shard_map/ppermute | solution.py:798
  13.7 4.6 %collective-permute-start.7 = (f32[16,128]{1,0:T(8,128)S(1)}, f32[16,128]{1,0:T(8,128)S(1)}, u32[]{:S(2)}, u32[]{:S(2)}) collective-permute-start(f32[16,128]{1,0:T(8,128)S(1)} %get-tuple-element.60.refs_0_), channel_id=1, source_target_pairs={{0,2},{1,3},{2,0},{3,1},{4,6},{5,7},{6,4},{7,5},{8,10},{9,11},{10,... | collective-permute-start | bytes 24584 | tf_op jit(solution)/shard_map/ppermute | solution.py:762
  18.5 4.4 %collective-permute-start.10 = (f32[36,1,128]{2,1,0:T(1,128)S(1)}, f32[36,1,128]{2,1,0:T(1,128)S(1)}, u32[]{:S(2)}, u32[]{:S(2)}) collective-permute-start(f32[36,1,128]{2,1,0:T(1,128)S(1)} %get-tuple-element.66), channel_id=1, source_target_pairs={{0,1},{1,0},{2,3},{3,2},{4,5},{5,4},{6,7},{7,6},{8,9},{9,8},{10,11... | collective-permute-start | bytes 55304 | tf_op jit(solution)/shard_map/ppermute | solution.py:762
  19.2 5.6 %collective-permute-start.8 = (f32[36,1,128]{2,1,0:T(1,128)S(1)}, f32[36,1,128]{2,1,0:T(1,128)S(1)}, u32[]{:S(2)}, u32[]{:S(2)}) collective-permute-start(f32[36,1,128]{2,1,0:T(1,128)S(1)} %get-tuple-element.64), channel_id=1, source_target_pairs={{0,3},{1,2},{2,1},{3,0},{4,7},{5,6},{6,5},{7,4},{8,11},{9,10},{10,... | collective-permute-start | bytes 55304 | tf_op jit(solution)/shard_map/ppermute | solution.py:762
  21.5 4.7 %collective-permute-start.9 = (f32[36,1,128]{2,1,0:T(1,128)S(1)}, f32[36,1,128]{2,1,0:T(1,128)S(1)}, u32[]{:S(2)}, u32[]{:S(2)}) collective-permute-start(f32[36,1,128]{2,1,0:T(1,128)S(1)} %get-tuple-element.65), channel_id=1, source_target_pairs={{0,2},{1,3},{2,0},{3,1},{4,6},{5,7},{6,4},{7,5},{8,10},{9,11},{10,... | collective-permute-start | bytes 55304 | tf_op jit(solution)/shard_map/ppermute | solution.py:762

commit v17 on v12

--- a/solution.py
+++ b/solution.py
@@ -48,12 +48,18 @@
 VMEM_BYTES = 48 * 1024 * 1024
 
 
+def tree_sum(terms):
+    terms = list(terms)
+    while len(terms) > 1:
+        pairs = [terms[k] + terms[k + 1] for k in range(0, len(terms) - 1, 2)]
+        terms = pairs + terms[len(terms) - len(terms) % 2 :]
+    return terms[0]
+
+
 def moments(values):
     sums = [values[q] + values[q + 1] for q in range(1, Q, 2)]
     diffs = [values[q] - values[q + 1] for q in range(1, Q, 2)]
-    density = values[0]
-    for term in sums:
-        density = density + term
+    density = tree_sum([values[0]] + sums)
     flows = []
     for axis in range(3):
         total = None
@@ -193,7 +199,7 @@
         fixed[1, x] = rate[x]
         return carry
 
-    lax.fori_loop(0, planes, plane, 0)
+    lax.fori_loop(0, planes, plane, 0, unroll=2)
 
     def pack(out, sign, outside):
         def line(x, carry):
@@ -347,7 +353,7 @@
         store_plane(extended, walls, second, x + 1, fixed[1, x], fixed[0, x])
         return carry
 
-    lax.fori_loop(1, planes - 1, inside_plane, 0)
+    lax.fori_loop(1, planes - 1, inside_plane, 0, unroll=2)
 
 
 def second_kernel(
@@ -471,7 +477,7 @@
                 loads[x * half + piece, part] = parts[part][:, piece * BLK : (piece + 1) * BLK]
         return carry
 
-    lax.fori_loop(0, planes, plane_two, 0)
+    lax.fori_loop(0, planes, plane_two, 0, unroll=2)
 
     for copy in copies:
         copy.wait()
@@ -646,25 +652,30 @@
     wanted = keys[...]
     node_ids = lax.broadcasted_iota(jnp.int32, (node_blocks, BLK), 0)
     own_ids = (node_ids + inner * node_blocks).astype(F32)
-    external = [jnp.zeros((node_blocks, BLK), F32)] * 3
-    moved = [jnp.zeros((slots, BLK), F32)] * 3
-    for message in messages:
-        for k in range(slots):
-            key = key_of(message, k)
-            here = own_ids == key
-            same = wanted == key
-            for part in range(3):
-                row = message[3 * k + part]
-                external[part] = external[part] + jnp.where(here, row, 0.0)
-                moved[part] = moved[part] + jnp.where(same, row, 0.0)
+    external = [[] for _ in range(3)]
+    moved = [[] for _ in range(3)]
     for step, message in enumerate(messages):
         sender = partner_of(inner, step, count)
-        for b in range(node_blocks):
-            key = jnp.broadcast_to(sender * node_blocks + b, (1, BLK)).astype(F32)
-            same = wanted == key
-            for part in range(3):
-                at = 3 * slots + 1 + part * node_blocks + b
-                moved[part] = moved[part] - jnp.where(same, message[at], 0.0)
+        named = [key_of(message, k) for k in range(slots)]
+        here = [own_ids == key for key in named]
+        same = [wanted == key for key in named]
+        owned = [
+            wanted == (sender * node_blocks + b).astype(F32) for b in range(node_blocks)
+        ]
+        for part in range(3):
+            rows = [message[3 * k + part] for k in range(slots)]
+            external[part].append(
+                tree_sum([jnp.where(here[k], rows[k], 0.0) for k in range(slots)])
+            )
+            moved[part].append(
+                tree_sum([jnp.where(same[k], rows[k], 0.0) for k in range(slots)])
+            )
+            at = 3 * slots + 1 + part * node_blocks
+            moved[part].append(
+                -tree_sum([jnp.where(owned[b], message[at + b], 0.0) for b in range(node_blocks)])
+            )
+    external = [tree_sum(terms) for terms in external]
+    moved = [tree_sum(terms) for terms in moved]
     live = wanted >= 0.0
     for part in range(3):
         start = 3 * slots + 1 + part * node_blocks

time: 26.1 us -> 26.1 us (level)
  no operation moved by 1% of the time
where the time goes in v17:
time: 26.1 us; the launch traced here: 25.9 us
  starting transfers between devices  12.4 us (48%)
  Pallas kernels  8.76 us (34%)
  waiting for transfers between devices  3.36 us (13%)
  between operations  1.37 us (5%)
    pallas_call x10, Pallas kernels, call(): pl.pallas_call(kernel, out_shape=outs, in_specs=[spec(space) for space in...  8.76 us
    ppermute x3, starting transfers between devices, exchange(): lax.ppermute(block, axis, [(partner_of(i, step, count), i) for i in range...  4.45 us
    ppermute x3, starting transfers between devices, swap(): lax.ppermute(near, axes, routes[0])  3.14 us
    ppermute x1, starting transfers between devices, around(): lax.ppermute(block, axis, [(i, (i + step) % count) for i in range(count)])  2.46 us
    ppermute x3, starting transfers between devices, swap(): lax.ppermute(far, axes, routes[1])  2.37 us
    ppermute x3, waiting for transfers between devices, exchange(): lax.ppermute(block, axis, [(partner_of(i, step, count), i) for i in range...  1.78 us
    ppermute x3, waiting for transfers between devices, swap(): lax.ppermute(far, axes, routes[1])  1.57 us
  transfers between devices with their start and end apart: 10, of which 5 were waited for; matrix products, arithmetic and copies ran while one was open for 0% of the time, Pallas kernels for 27%

profile of v17, /device:TPU:0, one launch (start us, length us, event | category | flops | bytes accessed | tf_op | source)
XLA Modules:
  0.0 25.9 jit_solution(8527356496243007484)
XLA Ops:
  0.6 2.5 %collective-permute-start.2 = (f32[3,2048]{1,0:T(4,128)}, f32[3,2048]{1,0:T(4,128)S(1)}, u32[]{:S(2)}, u32[]{:S(2)}) collective-permute-start(f32[3,2048]{1,0:T(4,128)} %displacement_hbm.1), channel_id=1, source_target_pairs={{0,12},{4,0},{8,4},{12,8},{1,13},{5,1},{9,5},{13,9},{2,14},{6,2},{... | collective-permute-start | bytes 73736 | tf_op jit(solution)/shard_map/ppermute | solution.py:718
  3.1 1.7 %shard_map.130 = (f32[19,4,8,256]{3,2,1,0:T(8,128)S(1)}, f32[2,4,8,256]{3,2,1,0:T(8,128)S(1)}, f32[24,4,256]{2,1,0:T(4,128)S(1)}, f32[24,4,256]{2,1,0:T(4,128)S(...) custom-call(f32[19,4,8,256]{3,2,1,0:T(8,128)} %pops_hbm.1, ...), custom_call_target="tpu_custom_call" | custom-call | bytes 5400000 | tf_op jit(solution)/shard_map/pallas_call | solution.py:691
  4.8 0.1 collective-permute-start
  4.9 3.1 %collective-permute-start.1 = (f32[24,4,256]{2,1,0:T(4,128)S(1)}, f32[24,4,256]{2,1,0:T(4,128)S(1)}, u32[]{:S(2)}, u32[]{:S(2)}) collective-permute-start(f32[24,4,256]{2,1,0:T(4,128)S(1)} %get-tuple-element.28), channel_id=1, source_target_pairs={{0,1},{1,0},{2,3},{3,2},{4,5},{5,4},{6,7},{7,6},{8,9},{9,8},{10,11... | collective-permute-start | bytes 294920 | tf_op jit(solution)/shard_map/ppermute | solution.py:736
  8.0 0.0 collective-permute-done.2.next_nodes
  8.0 1.7 %shard_map.131 = (f32[3,32,128]{2,1,0:T(8,128)S(1)}, f32[3,32,128]{2,1,0:T(8,128)S(1)}, f32[6,3,32,128]{3,2,1,0:T(8,128)S(1)}) custom-call(s32[3,4096]{1,0:T(4,128)S(1)} %get-tuple-element.29.elements, f32[3,2048]{1,0:T(4,128)S(1)} %get-tuple-element.30.displacement, f32[3,2048]{1,0:T(4,128)S(1)} %collective-permute-done.2.next_nodes, ...), custom_call_target="tpu_custom_call" | custom-call | bytes 3600 | tf_op jit(solution)/shard_map/pallas_call | solution.py:691
  9.7 0.1 shard_map.134
  9.8 1.6 %collective-permute-start.5 = (f32[21,8,256]{2,1,0:T(8,128)S(1)}, f32[21,8,256]{2,1,0:T(8,128)S(1)}, u32[]{:S(2)}, u32[]{:S(2)}) collective-permute-start(f32[21,8,256]{2,1,0:T(8,128)S(1)} %get-tuple-element.40), channel_id=1, source_target_pairs={{0,16},{4,8},{8,4},{12,28},{16,0},{20,24},{24,20},{28,12},{1,17},{... | collective-permute-start | bytes 516104 | tf_op jit(solution)/shard_map/ppermute | solution.py:736
  11.4 0.0 collective-permute-start.6
  11.4 1.1 %shard_map.132.other = f32[3,8,256]{2,1,0:T(8,128)S(1)} custom-call(f32[3,32,128]{2,1,0:T(8,128)S(1)} %get-tuple-element.33.low_ids.numbers, f32[3,32,128]{2,1,0:T(8,128)S(1)} %get-tuple-element.34.high_ids, f32[6,3,32,128]{3,2,1,0:T(8,128)S(1)} %get-tuple-element.35.forces), custom_call_target="tpu_custom_call" | custom-call | bytes 3600 | tf_op jit(solution)/shard_map/pallas_call | solution.py:691
  12.5 0.0 collective-permute-done.far_y
  12.5 0.0 collective-permute-done.1.near_y
  12.5 0.1 shard_map.133
  12.6 0.7 %collective-permute-start.3 = (f32[9,8,256]{2,1,0:T(8,128)S(1)}, f32[9,8,256]{2,1,0:T(8,128)S(1)}, u32[]{:S(2)}, u32[]{:S(2)}) collective-permute-start(f32[9,8,256]{2,1,0:T(8,128)S(1)} %get-tuple-element.36), channel_id=1, source_target_pairs={{0,16},{4,8},{8,4},{12,28},{16,0},{20,24},{24,20},{28,12},{1,17},{... | collective-permute-start | bytes 221192 | tf_op jit(solution)/shard_map/ppermute | solution.py:736
  13.4 0.0 collective-permute-start.4
  14.0 1.1 %shard_map.136.internal_own = f32[3,8,256]{2,1,0:T(8,128)S(1)} custom-call(f32[3,32,128]{2,1,0:T(8,128)S(1)} %get-tuple-element.33.low_ids.numbers, f32[3,32,128]{2,1,0:T(8,128)S(1)} %get-tuple-element.34.high_ids, f32[6,3,32,128]{3,2,1,0:T(8,128)S(1)} %get-tuple-element.35.forces), custom_call_target="tpu_custom_call" | custom-call | bytes 2880000 | tf_op jit(solution)/shard_map/pallas_call | solution.py:691
  15.1 0.2 collective-permute-done.5.far_x
  15.3 0.0 collective-permute-done.6.near_x
  15.3 0.4 %shard_map.135 = (f32[19,8,8,256]{3,2,1,0:T(8,128)S(1)}, f32[2,21,8,256]{3,2,1,0:T(8,128)S(1)}, f32[2,5,8,256]{3,2,1,0:T(8,128)S(1)}, f32[19,6,8,256]{3,2,1,0:T(8,128)S(1)}, f32[2,2,8,256]{3,2,1,0:T(8,128)S(1)}) custom-call(f32[19,4,8,256]{3,2,1,0:T(8,128)S(1)} %get-tuple-element.39.c1, f32[2,4,8,256]{3,2,1,0:T(8,128)S(1)} %get-tuple-element.38.fixed, ...), custom_call_target="tpu_custom_call" | custom-call | bytes 2880000 | tf_op jit(solution)/shard_map/pallas_call | solution.py:691
  15.7 1.4 %collective-permute-done.3.far = f32[9,8,256]{2,1,0:T(8,128)S(1)} collective-permute-done((f32[9,8,256]{2,1,0:T(8,128)S(1)}, f32[9,8,256]{2,1,0:T(8,128)S(1)}, u32[]{:S(2)}, u32[]{:S(2)}) %collective-permute-start.3) | collective-permute-done | bytes 73760 | tf_op jit(solution)/shard_map/ppermute | solution.py:736
  17.0 0.0 collective-permute-done.4.near
  17.0 0.9 %shard_map.137 = (f32[19,4,8,256]{3,2,1,0:T(8,128)S(1)}, f32[73,1,128]{2,1,0:T(1,128)S(1)}, f32[2,21,8,256]{3,2,1,0:T(8,128)S(1)}, f32[19,6,8,256]{3,2,1,0:T(8,128)S(1)}) custom-call(s32[1,1,8]{2,1,0:T(1,128)} %block_source_hbm.1, s32[1,1,8]{2,1,0:T(1,128)} %block_target_hbm.1, ...), custom_call_target="tpu_custom_call", output_to_operand_aliasing={{2}: (11, {}), {3}: (12, {})} | custom-call | bytes 5400000 | tf_op jit(solution)/shard_map/pallas_call | solution.py:691
  17.9 1.4 %collective-permute-start.9 = (f32[73,1,128]{2,1,0:T(1,128)S(1)}, f32[73,1,128]{2,1,0:T(1,128)S(1)}, u32[]{:S(2)}, u32[]{:S(2)}) collective-permute-start(f32[73,1,128]{2,1,0:T(1,128)S(1)} %get-tuple-element.48.refs_0_), channel_id=1, source_target_pairs={{3,0},{2,1},{1,2},{0,3},{7,4},{6,5},{5,6},{4,7},{11,8},{10,9},{9,1... | collective-permute-start | bytes 112136 | tf_op jit(solution)/shard_map/ppermute | solution.py:713
  19.4 0.3 collective-permute-start.8
  19.6 2.8 %collective-permute-start.7 = (f32[73,1,128]{2,1,0:T(1,128)S(1)}, f32[73,1,128]{2,1,0:T(1,128)S(1)}, u32[]{:S(2)}, u32[]{:S(2)}) collective-permute-start(f32[73,1,128]{2,1,0:T(1,128)S(1)} %get-tuple-element.48.refs_0_), channel_id=1, source_target_pairs={{1,0},{0,1},{3,2},{2,3},{5,4},{4,5},{7,6},{6,7},{9,8},{8,9},{11,10... | collective-permute-start | bytes 112136 | tf_op jit(solution)/shard_map/ppermute | solution.py:713
  22.4 0.8 %shard_map.138 = f32[19,4,8,256]{3,2,1,0:T(8,128)} custom-call(f32[19,4,8,256]{3,2,1,0:T(8,128)S(1)} %get-tuple-element.47.values), custom_call_target="tpu_custom_call" | custom-call | bytes 3600000 | tf_op jit(solution)/shard_map/pallas_call | solution.py:691
  23.2 0.6 %collective-permute-done.9.refs_3_ = f32[73,1,128]{2,1,0:T(1,128)S(1)} collective-permute-done((f32[73,1,128]{2,1,0:T(1,128)S(1)}, f32[73,1,128]{2,1,0:T(1,128)S(1)}, u32[]{:S(2)}, u32[]{:S(2)}) %collective-permute-start.9) | collective-permute-done | bytes 37408 | tf_op jit(solution)/shard_map/ppermute | solution.py:713
  23.8 1.1 %collective-permute-done.8.refs_2_ = f32[73,1,128]{2,1,0:T(1,128)S(1)} collective-permute-done((f32[73,1,128]{2,1,0:T(1,128)S(1)}, f32[73,1,128]{2,1,0:T(1,128)S(1)}, u32[]{:S(2)}, u32[]{:S(2)}) %collective-permute-start.8) | collective-permute-done | bytes 37408 | tf_op jit(solution)/shard_map/ppermute | solution.py:713
  25.0 0.1 collective-permute-done.7.refs_1_
  25.0 0.9 %shard_map.139 = (f32[3,2048]{1,0:T(4,128)}, f32[3,8,128]{2,1,0:T(8,128)}) custom-call(f32[73,1,128]{2,1,0:T(1,128)S(1)} %get-tuple-element.48.refs_0_, f32[73,1,128]{2,1,0:T(1,128)S(1)} %collective-permute-done.7.refs_1_, f32[73,1,128]{2,1,0:T(1,128)S(1)} %collective-permute-done.8.refs_2_, f32[73,1,128]{2,1,0:T(1,128)S(1)} %collective-permute-done.9.refs_3_), custom_call_target="tpu_custom_call" | custom-call | bytes 2880000 | tf_op jit(solution)/shard_map/pallas_call | solution.py:691
Async XLA Ops:
  0.6 7.4 %collective-permute-start.2 = (f32[3,2048]{1,0:T(4,128)}, f32[3,2048]{1,0:T(4,128)S(1)}, u32[]{:S(2)}, u32[]{:S(2)}) collective-permute-start(f32[3,2048]{1,0:T(4,128)} %displacement_hbm.1), channel_id=1, source_target_pairs={{0,12},{4,0},{8,4},{12,8},{1,13},{5,1},{9,5},{13,9},{2,14},{6,2},{... | collective-permute-start | bytes 73736 | tf_op jit(solution)/shard_map/ppermute | solution.py:718
  4.8 7.7 %collective-permute-start = (f32[24,4,256]{2,1,0:T(4,128)S(1)}, f32[24,4,256]{2,1,0:T(4,128)S(1)}, u32[]{:S(2)}, u32[]{:S(2)}) collective-permute-start(f32[24,4,256]{2,1,0:T(4,128)S(1)} %get-tuple-element.27), channel_id=1, source_target_pairs={{0,4},{1,2},{2,1},{3,7},{4,0},{5,6},{6,5},{7,3},{8,12},{9,10},{10,... | collective-permute-start | bytes 294920 | tf_op jit(solution)/shard_map/ppermute | solution.py:736
  4.9 7.6 %collective-permute-start.1 = (f32[24,4,256]{2,1,0:T(4,128)S(1)}, f32[24,4,256]{2,1,0:T(4,128)S(1)}, u32[]{:S(2)}, u32[]{:S(2)}) collective-permute-start(f32[24,4,256]{2,1,0:T(4,128)S(1)} %get-tuple-element.28), channel_id=1, source_target_pairs={{0,1},{1,0},{2,3},{3,2},{4,5},{5,4},{6,7},{7,6},{8,9},{9,8},{10,11... | collective-permute-start | bytes 294920 | tf_op jit(solution)/shard_map/ppermute | solution.py:736
  9.8 5.5 %collective-permute-start.5 = (f32[21,8,256]{2,1,0:T(8,128)S(1)}, f32[21,8,256]{2,1,0:T(8,128)S(1)}, u32[]{:S(2)}, u32[]{:S(2)}) collective-permute-start(f32[21,8,256]{2,1,0:T(8,128)S(1)} %get-tuple-element.40), channel_id=1, source_target_pairs={{0,16},{4,8},{8,4},{12,28},{16,0},{20,24},{24,20},{28,12},{1,17},{... | collective-permute-start | bytes 516104 | tf_op jit(solution)/shard_map/ppermute | solution.py:736
  11.4 3.9 %collective-permute-start.6 = (f32[21,8,256]{2,1,0:T(8,128)S(1)}, f32[21,8,256]{2,1,0:T(8,128)S(1)}, u32[]{:S(2)}, u32[]{:S(2)}) collective-permute-start(f32[21,8,256]{2,1,0:T(8,128)S(1)} %get-tuple-element.41), channel_id=1, source_target_pairs={{0,4},{4,0},{8,12},{12,8},{16,20},{20,16},{24,28},{28,24},{1,5},{5... | collective-permute-start | bytes 516104 | tf_op jit(solution)/shard_map/ppermute | solution.py:736
  12.6 4.4 %collective-permute-start.3 = (f32[9,8,256]{2,1,0:T(8,128)S(1)}, f32[9,8,256]{2,1,0:T(8,128)S(1)}, u32[]{:S(2)}, u32[]{:S(2)}) collective-permute-start(f32[9,8,256]{2,1,0:T(8,128)S(1)} %get-tuple-element.36), channel_id=1, source_target_pairs={{0,16},{4,8},{8,4},{12,28},{16,0},{20,24},{24,20},{28,12},{1,17},{... | collective-permute-start | bytes 221192 | tf_op jit(solution)/shard_map/ppermute | solution.py:736
  13.4 3.7 %collective-permute-start.4 = (f32[9,8,256]{2,1,0:T(8,128)S(1)}, f32[9,8,256]{2,1,0:T(8,128)S(1)}, u32[]{:S(2)}, u32[]{:S(2)}) collective-permute-start(f32[9,8,256]{2,1,0:T(8,128)S(1)} %get-tuple-element.37), channel_id=1, source_target_pairs={{0,4},{4,0},{8,12},{12,8},{16,20},{20,16},{24,28},{28,24},{1,5},{5... | collective-permute-start | bytes 221192 | tf_op jit(solution)/shard_map/ppermute | solution.py:736
  17.9 5.9 %collective-permute-start.9 = (f32[73,1,128]{2,1,0:T(1,128)S(1)}, f32[73,1,128]{2,1,0:T(1,128)S(1)}, u32[]{:S(2)}, u32[]{:S(2)}) collective-permute-start(f32[73,1,128]{2,1,0:T(1,128)S(1)} %get-tuple-element.48.refs_0_), channel_id=1, source_target_pairs={{3,0},{2,1},{1,2},{0,3},{7,4},{6,5},{5,6},{4,7},{11,8},{10,9},{9,1... | collective-permute-start | bytes 112136 | tf_op jit(solution)/shard_map/ppermute | solution.py:713
  19.4 5.6 %collective-permute-start.8 = (f32[73,1,128]{2,1,0:T(1,128)S(1)}, f32[73,1,128]{2,1,0:T(1,128)S(1)}, u32[]{:S(2)}, u32[]{:S(2)}) collective-permute-start(f32[73,1,128]{2,1,0:T(1,128)S(1)} %get-tuple-element.48.refs_0_), channel_id=1, source_target_pairs={{2,0},{3,1},{0,2},{1,3},{6,4},{7,5},{4,6},{5,7},{10,8},{11,9},{8,1... | collective-permute-start | bytes 112136 | tf_op jit(solution)/shard_map/ppermute | solution.py:713
  19.6 5.4 %collective-permute-start.7 = (f32[73,1,128]{2,1,0:T(1,128)S(1)}, f32[73,1,128]{2,1,0:T(1,128)S(1)}, u32[]{:S(2)}, u32[]{:S(2)}) collective-permute-start(f32[73,1,128]{2,1,0:T(1,128)S(1)} %get-tuple-element.48.refs_0_), channel_id=1, source_target_pairs={{1,0},{0,1},{3,2},{2,3},{5,4},{4,5},{7,6},{6,7},{9,8},{8,9},{11,10... | collective-permute-start | bytes 112136 | tf_op jit(solution)/shard_map/ppermute | solution.py:713

commit v18 on v17

--- a/solution.py
+++ b/solution.py
@@ -153,8 +153,8 @@
     stiffness_hbm,
     c1,
     fixed,
+    near,
     far,
-    near,
     displacement,
     elements,
     shape_inverse,
@@ -243,7 +243,7 @@
         pack(far, 1, last)
 
 
-def slab_face_kernel(c1, fixed, numbers, far, near):
+def slab_face_kernel(c1, fixed, numbers, near, far):
     del numbers
     planes = c1.shape[1]
 
@@ -265,7 +265,7 @@
         both[odd, slot] = far[slot]
 
 
-def corner_kernel(far_y, near_y, other, far, near, both):
+def corner_kernel(near_y, far_y, other, near, far, both):
     planes = near_y.shape[1]
     gather_both(near_y, far_y, both, "inner")
 
@@ -308,10 +308,10 @@
 def inside_kernel(
     c1,
     fixed,
+    near_y,
     far_y,
-    near_y,
+    near_x,
     far_x,
-    near_x,
     extended,
     walls,
     crossing,
@@ -361,8 +361,8 @@
     block_target_hbm,
     block_node_hbm,
     block_count,
+    near,
     far,
-    near,
     fixed,
     extended,
     crossing,
@@ -635,54 +635,59 @@
     store.wait()
 
 
-def final_kernel(count, *refs):
-    messages = refs[:count]
-    residual, motion, keys = refs[count:]
-    slots = keys.shape[0]
-    node_blocks = residual.shape[1] // BLK
-    inner = lax.axis_index("inner")
-    width = BLK // slots
-
-    def key_of(message, k):
-        return jnp.broadcast_to(message[3 * slots][:, k * width : k * width + 1], (1, BLK))
-
-    mine = messages[0]
-    for k in range(slots):
-        keys[k : k + 1] = key_of(mine, k)
-    wanted = keys[...]
-    node_ids = lax.broadcasted_iota(jnp.int32, (node_blocks, BLK), 0)
-    own_ids = (node_ids + inner * node_blocks).astype(F32)
+def sum_messages(messages, senders, wanted, node_blocks):
+    slots = wanted.shape[0]
+    own_ids = lax.broadcasted_iota(jnp.int32, (node_blocks, BLK), 0)
+    own_ids = (own_ids + lax.axis_index("inner") * node_blocks).astype(F32)
     external = [[] for _ in range(3)]
     moved = [[] for _ in range(3)]
-    for step, message in enumerate(messages):
-        sender = partner_of(inner, step, count)
-        named = [key_of(message, k) for k in range(slots)]
+    for message, sender in zip(messages, senders):
+        named = [key_of(message, k, slots) for k in range(slots)]
         here = [own_ids == key for key in named]
         same = [wanted == key for key in named]
-        owned = [
-            wanted == (sender * node_blocks + b).astype(F32) for b in range(node_blocks)
-        ]
+        owned = [wanted == (sender * node_blocks + b).astype(F32) for b in range(node_blocks)]
         for part in range(3):
             rows = [message[3 * k + part] for k in range(slots)]
-            external[part].append(
-                tree_sum([jnp.where(here[k], rows[k], 0.0) for k in range(slots)])
-            )
-            moved[part].append(
-                tree_sum([jnp.where(same[k], rows[k], 0.0) for k in range(slots)])
-            )
             at = 3 * slots + 1 + part * node_blocks
-            moved[part].append(
-                -tree_sum([jnp.where(owned[b], message[at + b], 0.0) for b in range(node_blocks)])
-            )
-    external = [tree_sum(terms) for terms in external]
-    moved = [tree_sum(terms) for terms in moved]
+            inside = [message[at + b] for b in range(node_blocks)]
+            external[part].append(tree_sum([jnp.where(m, r, 0.0) for m, r in zip(here, rows)]))
+            moved[part].append(tree_sum([jnp.where(m, r, 0.0) for m, r in zip(same, rows)]))
+            moved[part].append(-tree_sum([jnp.where(m, r, 0.0) for m, r in zip(owned, inside)]))
+    return [tree_sum(terms) for terms in external], [tree_sum(terms) for terms in moved]
+
+
+def key_of(message, k, slots):
+    width = BLK // slots
+    return jnp.broadcast_to(message[3 * slots][:, k * width : k * width + 1], (1, BLK))
+
+
+def early_kernel(count, *refs):
+    messages = refs[:-3]
+    total, moved, keys = refs[-3:]
+    slots, node_blocks = keys.shape[0], total.shape[1]
+    inner = lax.axis_index("inner")
+    for k in range(slots):
+        keys[k : k + 1] = key_of(messages[0], k, slots)
+    steps = [0] + list(range(count - 1, 1, -1))
+    senders = [partner_of(inner, step, count) for step in steps]
+    external, forces = sum_messages(messages, senders, keys[...], node_blocks)
+    for part in range(3):
+        start = 3 * slots + 1 + part * node_blocks
+        total[part] = external[part] - messages[0][start : start + node_blocks, 0]
+        moved[part] = forces[part]
+
+
+def final_kernel(count, message, total, moved, keys, residual, motion):
+    node_blocks = total.shape[1]
+    wanted = keys[...]
+    sender = partner_of(lax.axis_index("inner"), 1, count)
+    external, forces = sum_messages([message], [sender], wanted, node_blocks)
     live = wanted >= 0.0
     for part in range(3):
-        start = 3 * slots + 1 + part * node_blocks
-        left = external[part] - mine[start : start + node_blocks, 0]
+        left = total[part] + external[part]
         for b in range(node_blocks):
             residual[part : part + 1, b * BLK : (b + 1) * BLK] = left[b : b + 1]
-        motion[part] = jnp.where(live, COMPLIANCE * moved[part], 0.0)
+        motion[part] = jnp.where(live, COMPLIANCE * (moved[part] + forces[part]), 0.0)
 
 
 def call(kernel, outs, operands, spaces, scratch=(), out_spaces=None, micros=1.0, aliases=None):
@@ -766,7 +771,7 @@
     pin = lambda block: pltpu.with_memory_space_constraint(block, hbm)
     whole_like = lambda block: jax.ShapeDtypeStruct(block.shape, block.dtype)
     shell = (displacement, elements, shape_inverse, stiffness.reshape(runs, BLK))
-    c1, fixed, far, near, own_nodes, corners, inverses, stiff = call(
+    c1, fixed, near, far, own_nodes, corners, inverses, stiff = call(
         first_kernel,
         (
             whole,
@@ -799,7 +804,7 @@
         ),
         micros=0.001,
     )
-    far, near = call(
+    near, far = call(
         slab_face_kernel, (face_x, face_x), (c1, fixed, low_ids), (vmem,) * 3, micros=0.001
     )
     near_x, far_x = swap(near, far, "slab", "group")
@@ -812,10 +817,10 @@
         micros=0.001,
     )
     corner = shape(CORNER_SLOTS, rows, length)
-    far, near = call(
+    near, far = call(
         corner_kernel,
         (corner, corner),
-        (far_y, near_y, other),
+        (near_y, far_y, other),
         (vmem,) * 3,
         scratch=(pltpu.VMEM((2, SLOTS, planes, length), F32),),
         micros=0.3,
@@ -840,7 +845,7 @@
             second_shape,
             shape(2, 2, rows, length),
         ),
-        (c1, fixed, far_y, near_y, far_x, near_x),
+        (c1, fixed, near_y, far_y, near_x, far_x),
         (vmem,) * 6,
         scratch=(
             pltpu.VMEM((2, SLOTS, planes, length), F32),
@@ -857,8 +862,8 @@
             pin(block_target),
             pin(block_node),
             block_count,
+            near_c,
             far_c,
-            near_c,
             fixed,
             extended,
             crossing,
@@ -890,13 +895,19 @@
         scratch=(pltpu.SemaphoreType.DMA(()),),
         micros=1.0,
     )
+    total, moved, keys = call(
+        functools.partial(early_kernel, count),
+        (shape(3, node_blocks, BLK), shape(3, slots, BLK), shape(slots, BLK)),
+        (messages[0], *messages[:1:-1]),
+        (vmem,) * (count - 1),
+        micros=0.4,
+    )
     residual, motion = call(
         functools.partial(final_kernel, count),
         (shape(3, node_dev), shape(3, slots, BLK)),
-        messages,
-        (vmem,) * count,
-        scratch=(pltpu.VMEM((slots, BLK), F32),),
-        micros=0.8,
+        (messages[1], total, moved, keys),
+        (vmem,) * 4,
+        micros=0.5,
     )
     return populations_out, residual, motion.transpose(1, 0, 2)[None, None]
 

time: 26.1 us -> 26.9 us (1.031)
  waiting for transfers between devices: 3.36 us -> 4.5 us
  starting transfers between devices: 12.4 us -> 12.1 us
    ppermute x3, waiting for transfers between devices: 1.78 us -> 2.89 us  [exchange(): lax.ppermute(block, axis, [(partner_of(i, step, count), i) for i in range...]
    ppermute x3, starting transfers between devices: 3.14 us -> 2.27 us  [swap(): lax.ppermute(near, axes, routes[0])]
    ppermute x3, starting transfers between devices: 4.45 us -> 5.18 us  [exchange(): lax.ppermute(block, axis, [(partner_of(i, step, count), i) for i in range...]
    pallas_call x10 -> x11, Pallas kernels: 8.76 us -> 8.79 us  [call(): pl.pallas_call(kernel, out_shape=outs, in_specs=[spec(space) for space in...]
  transfers between devices with their start and end apart: 10 -> 10, of which waited for: 5 -> 4; matrix products, arithmetic and copies ran while one was open for 0% -> 0% of each run, Pallas kernels for 27% -> 27%
where the time goes in v18:
time: 26.9 us; the launch traced here: 26.8 us
  starting transfers between devices  12.1 us (45%)
  Pallas kernels  8.79 us (33%)
  waiting for transfers between devices  4.5 us (17%)
  between operations  1.4 us (5%)
    pallas_call x11, Pallas kernels, call(): pl.pallas_call(kernel, out_shape=outs, in_specs=[spec(space) for space in...  8.79 us
    ppermute x3, starting transfers between devices, exchange(): lax.ppermute(block, axis, [(partner_of(i, step, count), i) for i in range...  5.18 us
    ppermute x3, waiting for transfers between devices, exchange(): lax.ppermute(block, axis, [(partner_of(i, step, count), i) for i in range...  2.89 us
    ppermute x1, starting transfers between devices, around(): lax.ppermute(block, axis, [(i, (i + step) % count) for i in range(count)])  2.46 us
    ppermute x3, starting transfers between devices, swap(): lax.ppermute(near, axes, routes[0])  2.27 us
    ppermute x3, starting transfers between devices, swap(): lax.ppermute(far, axes, routes[1])  2.18 us
    ppermute x3, waiting for transfers between devices, swap(): lax.ppermute(far, axes, routes[1])  1.57 us
  transfers between devices with their start and end apart: 10, of which 4 were waited for; matrix products, arithmetic and copies ran while one was open for 0% of the time, Pallas kernels for 27%

profile of v18, /device:TPU:0, one launch (start us, length us, event | category | flops | bytes accessed | tf_op | source)
XLA Modules:
  0.0 26.8 jit_solution(9072021084000309747)
XLA Ops:
  0.6 2.5 %collective-permute-start.2 = (f32[3,2048]{1,0:T(4,128)}, f32[3,2048]{1,0:T(4,128)S(1)}, u32[]{:S(2)}, u32[]{:S(2)}) collective-permute-start(f32[3,2048]{1,0:T(4,128)} %displacement_hbm.1), channel_id=1, source_target_pairs={{0,12},{4,0},{8,4},{12,8},{1,13},{5,1},{9,5},{13,9},{2,14},{6,2},{... | collective-permute-start | bytes 73736 | tf_op jit(solution)/shard_map/ppermute | solution.py:723
  3.1 1.7 %shard_map.130 = (f32[19,4,8,256]{3,2,1,0:T(8,128)S(1)}, f32[2,4,8,256]{3,2,1,0:T(8,128)S(1)}, f32[24,4,256]{2,1,0:T(4,128)S(1)}, f32[24,4,256]{2,1,0:T(4,128)S(...) custom-call(f32[19,4,8,256]{3,2,1,0:T(8,128)} %pops_hbm.1, ...), custom_call_target="tpu_custom_call" | custom-call | bytes 5400000 | tf_op jit(solution)/shard_map/pallas_call | solution.py:696
  4.8 1.6 %collective-permute-start = (f32[24,4,256]{2,1,0:T(4,128)S(1)}, f32[24,4,256]{2,1,0:T(4,128)S(1)}, u32[]{:S(2)}, u32[]{:S(2)}) collective-permute-start(f32[24,4,256]{2,1,0:T(4,128)S(1)} %get-tuple-element.30), channel_id=1, source_target_pairs={{0,1},{1,0},{2,3},{3,2},{4,5},{5,4},{6,7},{7,6},{8,9},{9,8},{10,11... | collective-permute-start | bytes 294920 | tf_op jit(solution)/shard_map/ppermute | solution.py:741
  6.5 0.0 collective-permute-start.1
  6.5 0.0 collective-permute-done.2.next_nodes
  6.5 1.7 %shard_map.131 = (f32[3,32,128]{2,1,0:T(8,128)S(1)}, f32[3,32,128]{2,1,0:T(8,128)S(1)}, f32[6,3,32,128]{3,2,1,0:T(8,128)S(1)}) custom-call(s32[3,4096]{1,0:T(4,128)S(1)} %get-tuple-element.32.elements, f32[3,2048]{1,0:T(4,128)S(1)} %get-tuple-element.33.displacement, f32[3,2048]{1,0:T(4,128)S(1)} %collective-permute-done.2.next_nodes, ...), custom_call_target="tpu_custom_call" | custom-call | bytes 3600 | tf_op jit(solution)/shard_map/pallas_call | solution.py:696
  8.2 0.1 shard_map.134
  8.2 0.6 %collective-permute-start.5 = (f32[21,8,256]{2,1,0:T(8,128)S(1)}, f32[21,8,256]{2,1,0:T(8,128)S(1)}, u32[]{:S(2)}, u32[]{:S(2)}) collective-permute-start(f32[21,8,256]{2,1,0:T(8,128)S(1)} %get-tuple-element.43), channel_id=1, source_target_pairs={{0,4},{4,0},{8,12},{12,8},{16,20},{20,16},{24,28},{28,24},{1,5},{5... | collective-permute-start | bytes 516104 | tf_op jit(solution)/shard_map/ppermute | solution.py:741
  8.8 1.5 %collective-permute-start.6 = (f32[21,8,256]{2,1,0:T(8,128)S(1)}, f32[21,8,256]{2,1,0:T(8,128)S(1)}, u32[]{:S(2)}, u32[]{:S(2)}) collective-permute-start(f32[21,8,256]{2,1,0:T(8,128)S(1)} %get-tuple-element.44), channel_id=1, source_target_pairs={{0,16},{4,8},{8,4},{12,28},{16,0},{20,24},{24,20},{28,12},{1,17},{... | collective-permute-start | bytes 516104 | tf_op jit(solution)/shard_map/ppermute | solution.py:741
  10.3 1.1 %shard_map.132.other = f32[3,8,256]{2,1,0:T(8,128)S(1)} custom-call(f32[3,32,128]{2,1,0:T(8,128)S(1)} %get-tuple-element.36.low_ids.numbers, f32[3,32,128]{2,1,0:T(8,128)S(1)} %get-tuple-element.37.high_ids, f32[6,3,32,128]{3,2,1,0:T(8,128)S(1)} %get-tuple-element.38.forces), custom_call_target="tpu_custom_call" | custom-call | bytes 3600 | tf_op jit(solution)/shard_map/pallas_call | solution.py:696
  11.4 0.0 collective-permute-done.near_y
  11.4 0.0 collective-permute-done.1.far_y
  11.4 0.1 shard_map.133
  11.5 0.1 collective-permute-start.3
  11.6 0.7 %collective-permute-start.4 = (f32[9,8,256]{2,1,0:T(8,128)S(1)}, f32[9,8,256]{2,1,0:T(8,128)S(1)}, u32[]{:S(2)}, u32[]{:S(2)}) collective-permute-start(f32[9,8,256]{2,1,0:T(8,128)S(1)} %get-tuple-element.40), channel_id=1, source_target_pairs={{0,16},{4,8},{8,4},{12,28},{16,0},{20,24},{24,20},{28,12},{1,17},{... | collective-permute-start | bytes 221192 | tf_op jit(solution)/shard_map/ppermute | solution.py:741
  12.9 1.1 %shard_map.136.internal_own = f32[3,8,256]{2,1,0:T(8,128)S(1)} custom-call(f32[3,32,128]{2,1,0:T(8,128)S(1)} %get-tuple-element.36.low_ids.numbers, f32[3,32,128]{2,1,0:T(8,128)S(1)} %get-tuple-element.37.high_ids, f32[6,3,32,128]{3,2,1,0:T(8,128)S(1)} %get-tuple-element.38.forces), custom_call_target="tpu_custom_call" | custom-call | bytes 2880000 | tf_op jit(solution)/shard_map/pallas_call | solution.py:696
  14.0 0.0 collective-permute-done.5.near_x
  14.1 0.1 collective-permute-done.6.far_x
  14.2 0.4 %shard_map.135 = (f32[19,8,8,256]{3,2,1,0:T(8,128)S(1)}, f32[2,21,8,256]{3,2,1,0:T(8,128)S(1)}, f32[2,5,8,256]{3,2,1,0:T(8,128)S(1)}, f32[19,6,8,256]{3,2,1,0:T(8,128)S(1)}, f32[2,2,8,256]{3,2,1,0:T(8,128)S(1)}) custom-call(f32[19,4,8,256]{3,2,1,0:T(8,128)S(1)} %get-tuple-element.42.c1, f32[2,4,8,256]{3,2,1,0:T(8,128)S(1)} %get-tuple-element.41.fixed, ...), custom_call_target="tpu_custom_call" | custom-call | bytes 2880000 | tf_op jit(solution)/shard_map/pallas_call | solution.py:696
  14.6 0.0 collective-permute-done.3.near
  14.6 1.4 %collective-permute-done.4.far = f32[9,8,256]{2,1,0:T(8,128)S(1)} collective-permute-done((f32[9,8,256]{2,1,0:T(8,128)S(1)}, f32[9,8,256]{2,1,0:T(8,128)S(1)}, u32[]{:S(2)}, u32[]{:S(2)}) %collective-permute-start.4) | collective-permute-done | bytes 73760 | tf_op jit(solution)/shard_map/ppermute | solution.py:741
  16.0 0.9 %shard_map.137 = (f32[19,4,8,256]{3,2,1,0:T(8,128)S(1)}, f32[73,1,128]{2,1,0:T(1,128)S(1)}, f32[2,21,8,256]{3,2,1,0:T(8,128)S(1)}, f32[19,6,8,256]{3,2,1,0:T(8,128)S(1)}) custom-call(s32[1,1,8]{2,1,0:T(1,128)} %block_source_hbm.1, s32[1,1,8]{2,1,0:T(1,128)} %block_target_hbm.1, ...), custom_call_target="tpu_custom_call", output_to_operand_aliasing={{2}: (11, {}), {3}: (12, {})} | custom-call | bytes 5400000 | tf_op jit(solution)/shard_map/pallas_call | solution.py:696
  16.9 2.3 %collective-permute-start.9 = (f32[73,1,128]{2,1,0:T(1,128)S(1)}, f32[73,1,128]{2,1,0:T(1,128)S(1)}, u32[]{:S(2)}, u32[]{:S(2)}) collective-permute-start(f32[73,1,128]{2,1,0:T(1,128)S(1)} %get-tuple-element.51.refs_0_), channel_id=1, source_target_pairs={{2,0},{3,1},{0,2},{1,3},{6,4},{7,5},{4,6},{5,7},{10,8},{11,9},{8,1... | collective-permute-start | bytes 112136 | tf_op jit(solution)/shard_map/ppermute | solution.py:718
  19.2 2.9 %collective-permute-start.8 = (f32[73,1,128]{2,1,0:T(1,128)S(1)}, f32[73,1,128]{2,1,0:T(1,128)S(1)}, u32[]{:S(2)}, u32[]{:S(2)}) collective-permute-start(f32[73,1,128]{2,1,0:T(1,128)S(1)} %get-tuple-element.51.refs_0_), channel_id=1, source_target_pairs={{3,0},{2,1},{1,2},{0,3},{7,4},{6,5},{5,6},{4,7},{11,8},{10,9},{9,1... | collective-permute-start | bytes 112136 | tf_op jit(solution)/shard_map/ppermute | solution.py:718
  22.1 0.0 collective-permute-start.7
  22.1 0.8 %shard_map.138 = f32[19,4,8,256]{3,2,1,0:T(8,128)} custom-call(f32[19,4,8,256]{3,2,1,0:T(8,128)S(1)} %get-tuple-element.50.values), custom_call_target="tpu_custom_call" | custom-call | bytes 3600000 | tf_op jit(solution)/shard_map/pallas_call | solution.py:696
  22.9 0.0 collective-permute-done.9.refs_2_
  23.0 2.1 %collective-permute-done.8.refs_1_ = f32[73,1,128]{2,1,0:T(1,128)S(1)} collective-permute-done((f32[73,1,128]{2,1,0:T(1,128)S(1)}, f32[73,1,128]{2,1,0:T(1,128)S(1)}, u32[]{:S(2)}, u32[]{:S(2)}) %collective-permute-start.8) | collective-permute-done | bytes 37408 | tf_op jit(solution)/shard_map/ppermute | solution.py:718
  25.1 0.2 shard_map.139
  25.3 0.8 %collective-permute-done.7.message = f32[73,1,128]{2,1,0:T(1,128)S(1)} collective-permute-done((f32[73,1,128]{2,1,0:T(1,128)S(1)}, f32[73,1,128]{2,1,0:T(1,128)S(1)}, u32[]{:S(2)}, u32[]{:S(2)}) %collective-permute-start.7) | collective-permute-done | bytes 37408 | tf_op jit(solution)/shard_map/ppermute | solution.py:718
  26.1 0.7 %shard_map.140 = (f32[3,2048]{1,0:T(4,128)}, f32[3,8,128]{2,1,0:T(8,128)}) custom-call(f32[73,1,128]{2,1,0:T(1,128)S(1)} %collective-permute-done.7.message, f32[3,16,128]{2,1,0:T(8,128)S(1)} %get-tuple-element.52.total, f32[3,8,128]{2,1,0:T(8,128)S(1)} %get-tuple-element.53.moved, f32[8,128]{1,0:T(8,128)S(1)} %get-tuple-element.54.keys), custom_call_target="tpu_custom_call" | custom-call | bytes 1800000 | tf_op jit(solution)/shard_map/pallas_call | solution.py:696
Async XLA Ops:
  0.6 5.8 %collective-permute-start.2 = (f32[3,2048]{1,0:T(4,128)}, f32[3,2048]{1,0:T(4,128)S(1)}, u32[]{:S(2)}, u32[]{:S(2)}) collective-permute-start(f32[3,2048]{1,0:T(4,128)} %displacement_hbm.1), channel_id=1, source_target_pairs={{0,12},{4,0},{8,4},{12,8},{1,13},{5,1},{9,5},{13,9},{2,14},{6,2},{... | collective-permute-start | bytes 73736 | tf_op jit(solution)/shard_map/ppermute | solution.py:723
  4.8 6.6 %collective-permute-start = (f32[24,4,256]{2,1,0:T(4,128)S(1)}, f32[24,4,256]{2,1,0:T(4,128)S(1)}, u32[]{:S(2)}, u32[]{:S(2)}) collective-permute-start(f32[24,4,256]{2,1,0:T(4,128)S(1)} %get-tuple-element.30), channel_id=1, source_target_pairs={{0,1},{1,0},{2,3},{3,2},{4,5},{5,4},{6,7},{7,6},{8,9},{9,8},{10,11... | collective-permute-start | bytes 294920 | tf_op jit(solution)/shard_map/ppermute | solution.py:741
  6.5 5.0 %collective-permute-start.1 = (f32[24,4,256]{2,1,0:T(4,128)S(1)}, f32[24,4,256]{2,1,0:T(4,128)S(1)}, u32[]{:S(2)}, u32[]{:S(2)}) collective-permute-start(f32[24,4,256]{2,1,0:T(4,128)S(1)} %get-tuple-element.31), channel_id=1, source_target_pairs={{0,4},{1,2},{2,1},{3,7},{4,0},{5,6},{6,5},{7,3},{8,12},{9,10},{10,... | collective-permute-start | bytes 294920 | tf_op jit(solution)/shard_map/ppermute | solution.py:741
  8.2 5.8 %collective-permute-start.5 = (f32[21,8,256]{2,1,0:T(8,128)S(1)}, f32[21,8,256]{2,1,0:T(8,128)S(1)}, u32[]{:S(2)}, u32[]{:S(2)}) collective-permute-start(f32[21,8,256]{2,1,0:T(8,128)S(1)} %get-tuple-element.43), channel_id=1, source_target_pairs={{0,4},{4,0},{8,12},{12,8},{16,20},{20,16},{24,28},{28,24},{1,5},{5... | collective-permute-start | bytes 516104 | tf_op jit(solution)/shard_map/ppermute | solution.py:741
  8.8 5.4 %collective-permute-start.6 = (f32[21,8,256]{2,1,0:T(8,128)S(1)}, f32[21,8,256]{2,1,0:T(8,128)S(1)}, u32[]{:S(2)}, u32[]{:S(2)}) collective-permute-start(f32[21,8,256]{2,1,0:T(8,128)S(1)} %get-tuple-element.44), channel_id=1, source_target_pairs={{0,16},{4,8},{8,4},{12,28},{16,0},{20,24},{24,20},{28,12},{1,17},{... | collective-permute-start | bytes 516104 | tf_op jit(solution)/shard_map/ppermute | solution.py:741
  11.5 3.1 %collective-permute-start.3 = (f32[9,8,256]{2,1,0:T(8,128)S(1)}, f32[9,8,256]{2,1,0:T(8,128)S(1)}, u32[]{:S(2)}, u32[]{:S(2)}) collective-permute-start(f32[9,8,256]{2,1,0:T(8,128)S(1)} %get-tuple-element.39), channel_id=1, source_target_pairs={{0,4},{4,0},{8,12},{12,8},{16,20},{20,16},{24,28},{28,24},{1,5},{5... | collective-permute-start | bytes 221192 | tf_op jit(solution)/shard_map/ppermute | solution.py:741
  11.6 4.4 %collective-permute-start.4 = (f32[9,8,256]{2,1,0:T(8,128)S(1)}, f32[9,8,256]{2,1,0:T(8,128)S(1)}, u32[]{:S(2)}, u32[]{:S(2)}) collective-permute-start(f32[9,8,256]{2,1,0:T(8,128)S(1)} %get-tuple-element.40), channel_id=1, source_target_pairs={{0,16},{4,8},{8,4},{12,28},{16,0},{20,24},{24,20},{28,12},{1,17},{... | collective-permute-start | bytes 221192 | tf_op jit(solution)/shard_map/ppermute | solution.py:741
  16.9 6.0 %collective-permute-start.9 = (f32[73,1,128]{2,1,0:T(1,128)S(1)}, f32[73,1,128]{2,1,0:T(1,128)S(1)}, u32[]{:S(2)}, u32[]{:S(2)}) collective-permute-start(f32[73,1,128]{2,1,0:T(1,128)S(1)} %get-tuple-element.51.refs_0_), channel_id=1, source_target_pairs={{2,0},{3,1},{0,2},{1,3},{6,4},{7,5},{4,6},{5,7},{10,8},{11,9},{8,1... | collective-permute-start | bytes 112136 | tf_op jit(solution)/shard_map/ppermute | solution.py:718
  19.2 5.8 %collective-permute-start.8 = (f32[73,1,128]{2,1,0:T(1,128)S(1)}, f32[73,1,128]{2,1,0:T(1,128)S(1)}, u32[]{:S(2)}, u32[]{:S(2)}) collective-permute-start(f32[73,1,128]{2,1,0:T(1,128)S(1)} %get-tuple-element.51.refs_0_), channel_id=1, source_target_pairs={{3,0},{2,1},{1,2},{0,3},{7,4},{6,5},{5,6},{4,7},{11,8},{10,9},{9,1... | collective-permute-start | bytes 112136 | tf_op jit(solution)/shard_map/ppermute | solution.py:718
  22.1 4.0 %collective-permute-start.7 = (f32[73,1,128]{2,1,0:T(1,128)S(1)}, f32[73,1,128]{2,1,0:T(1,128)S(1)}, u32[]{:S(2)}, u32[]{:S(2)}) collective-permute-start(f32[73,1,128]{2,1,0:T(1,128)S(1)} %get-tuple-element.51.refs_0_), channel_id=1, source_target_pairs={{1,0},{0,1},{3,2},{2,3},{5,4},{4,5},{7,6},{6,7},{9,8},{8,9},{11,10... | collective-permute-start | bytes 112136 | tf_op jit(solution)/shard_map/ppermute | solution.py:718

commit v19 on v18

--- a/solution.py
+++ b/solution.py
@@ -153,8 +153,8 @@
     stiffness_hbm,
     c1,
     fixed,
+    far,
     near,
-    far,
     displacement,
     elements,
     shape_inverse,
@@ -243,7 +243,7 @@
         pack(far, 1, last)
 
 
-def slab_face_kernel(c1, fixed, numbers, near, far):
+def slab_face_kernel(c1, fixed, numbers, far, near):
     del numbers
     planes = c1.shape[1]
 
@@ -265,7 +265,7 @@
         both[odd, slot] = far[slot]
 
 
-def corner_kernel(near_y, far_y, other, near, far, both):
+def corner_kernel(far_y, near_y, other, far, near, both):
     planes = near_y.shape[1]
     gather_both(near_y, far_y, both, "inner")
 
@@ -308,10 +308,10 @@
 def inside_kernel(
     c1,
     fixed,
+    far_y,
     near_y,
-    far_y,
+    far_x,
     near_x,
-    far_x,
     extended,
     walls,
     crossing,
@@ -361,8 +361,8 @@
     block_target_hbm,
     block_node_hbm,
     block_count,
+    far,
     near,
-    far,
     fixed,
     extended,
     crossing,
@@ -668,7 +668,7 @@
     inner = lax.axis_index("inner")
     for k in range(slots):
         keys[k : k + 1] = key_of(messages[0], k, slots)
-    steps = [0] + list(range(count - 1, 1, -1))
+    steps = [0] + list(range(2, count))
     senders = [partner_of(inner, step, count) for step in steps]
     external, forces = sum_messages(messages, senders, keys[...], node_blocks)
     for part in range(3):
@@ -771,7 +771,7 @@
     pin = lambda block: pltpu.with_memory_space_constraint(block, hbm)
     whole_like = lambda block: jax.ShapeDtypeStruct(block.shape, block.dtype)
     shell = (displacement, elements, shape_inverse, stiffness.reshape(runs, BLK))
-    c1, fixed, near, far, own_nodes, corners, inverses, stiff = call(
+    c1, fixed, far, near, own_nodes, corners, inverses, stiff = call(
         first_kernel,
         (
             whole,
@@ -804,7 +804,7 @@
         ),
         micros=0.001,
     )
-    near, far = call(
+    far, near = call(
         slab_face_kernel, (face_x, face_x), (c1, fixed, low_ids), (vmem,) * 3, micros=0.001
     )
     near_x, far_x = swap(near, far, "slab", "group")
@@ -817,10 +817,10 @@
         micros=0.001,
     )
     corner = shape(CORNER_SLOTS, rows, length)
-    near, far = call(
+    far, near = call(
         corner_kernel,
         (corner, corner),
-        (near_y, far_y, other),
+        (far_y, near_y, other),
         (vmem,) * 3,
         scratch=(pltpu.VMEM((2, SLOTS, planes, length), F32),),
         micros=0.3,
@@ -845,7 +845,7 @@
             second_shape,
             shape(2, 2, rows, length),
         ),
-        (c1, fixed, near_y, far_y, near_x, far_x),
+        (c1, fixed, far_y, near_y, far_x, near_x),
         (vmem,) * 6,
         scratch=(
             pltpu.VMEM((2, SLOTS, planes, length), F32),
@@ -862,8 +862,8 @@
             pin(block_target),
             pin(block_node),
             block_count,
+            far_c,
             near_c,
-            far_c,
             fixed,
             extended,
             crossing,
@@ -898,7 +898,7 @@
     total, moved, keys = call(
         functools.partial(early_kernel, count),
         (shape(3, node_blocks, BLK), shape(3, slots, BLK), shape(slots, BLK)),
-        (messages[0], *messages[:1:-1]),
+        (messages[0], *messages[2:]),
         (vmem,) * (count - 1),
         micros=0.4,
     )

time: 26.9 us -> 26.1 us (0.970)
  waiting for transfers between devices: 4.5 us -> 3.3 us
  starting transfers between devices: 12.1 us -> 12.4 us
    ppermute x3, waiting for transfers between devices: 2.89 us -> 1.72 us  [exchange(): lax.ppermute(block, axis, [(partner_of(i, step, count), i) for i in range...]
    ppermute x3, starting transfers between devices: 2.27 us -> 3.14 us  [swap(): lax.ppermute(near, axes, routes[0])]
    ppermute x3, starting transfers between devices: 5.18 us -> 4.45 us  [exchange(): lax.ppermute(block, axis, [(partner_of(i, step, count), i) for i in range...]
  transfers between devices with their start and end apart: 10 -> 10, of which waited for: 4 -> 4; matrix products, arithmetic and copies ran while one was open for 0% -> 0% of each run, Pallas kernels for 27% -> 28%
where the time goes in v19:
time: 26.1 us; the launch traced here: 25.9 us
  starting transfers between devices  12.4 us (48%)
  Pallas kernels  8.8 us (34%)
  waiting for transfers between devices  3.3 us (13%)
  between operations  1.39 us (5%)
    pallas_call x11, Pallas kernels, call(): pl.pallas_call(kernel, out_shape=outs, in_specs=[spec(space) for space in...  8.8 us
    ppermute x3, starting transfers between devices, exchange(): lax.ppermute(block, axis, [(partner_of(i, step, count), i) for i in range...  4.45 us
    ppermute x3, starting transfers between devices, swap(): lax.ppermute(near, axes, routes[0])  3.14 us
    ppermute x1, starting transfers between devices, around(): lax.ppermute(block, axis, [(i, (i + step) % count) for i in range(count)])  2.46 us
    ppermute x3, starting transfers between devices, swap(): lax.ppermute(far, axes, routes[1])  2.37 us
    ppermute x3, waiting for transfers between devices, exchange(): lax.ppermute(block, axis, [(partner_of(i, step, count), i) for i in range...  1.72 us
    ppermute x3, waiting for transfers between devices, swap(): lax.ppermute(far, axes, routes[1])  1.57 us
  transfers between devices with their start and end apart: 10, of which 4 were waited for; matrix products, arithmetic and copies ran while one was open for 0% of the time, Pallas kernels for 28%

profile of v19, /device:TPU:0, one launch (start us, length us, event | category | flops | bytes accessed | tf_op | source)
XLA Modules:
  0.0 25.9 jit_solution(6267416481296696543)
XLA Ops:
  0.6 2.5 %collective-permute-start.2 = (f32[3,2048]{1,0:T(4,128)}, f32[3,2048]{1,0:T(4,128)S(1)}, u32[]{:S(2)}, u32[]{:S(2)}) collective-permute-start(f32[3,2048]{1,0:T(4,128)} %displacement_hbm.1), channel_id=1, source_target_pairs={{0,12},{4,0},{8,4},{12,8},{1,13},{5,1},{9,5},{13,9},{2,14},{6,2},{... | collective-permute-start | bytes 73736 | tf_op jit(solution)/shard_map/ppermute | solution.py:723
  3.1 1.7 %shard_map.130 = (f32[19,4,8,256]{3,2,1,0:T(8,128)S(1)}, f32[2,4,8,256]{3,2,1,0:T(8,128)S(1)}, f32[24,4,256]{2,1,0:T(4,128)S(1)}, f32[24,4,256]{2,1,0:T(4,128)S(...) custom-call(f32[19,4,8,256]{3,2,1,0:T(8,128)} %pops_hbm.1, ...), custom_call_target="tpu_custom_call" | custom-call | bytes 5400000 | tf_op jit(solution)/shard_map/pallas_call | solution.py:696
  4.8 0.1 collective-permute-start
  4.9 3.1 %collective-permute-start.1 = (f32[24,4,256]{2,1,0:T(4,128)S(1)}, f32[24,4,256]{2,1,0:T(4,128)S(1)}, u32[]{:S(2)}, u32[]{:S(2)}) collective-permute-start(f32[24,4,256]{2,1,0:T(4,128)S(1)} %get-tuple-element.31), channel_id=1, source_target_pairs={{0,1},{1,0},{2,3},{3,2},{4,5},{5,4},{6,7},{7,6},{8,9},{9,8},{10,11... | collective-permute-start | bytes 294920 | tf_op jit(solution)/shard_map/ppermute | solution.py:741
  8.0 0.0 collective-permute-done.2.next_nodes
  8.0 1.7 %shard_map.131 = (f32[3,32,128]{2,1,0:T(8,128)S(1)}, f32[3,32,128]{2,1,0:T(8,128)S(1)}, f32[6,3,32,128]{3,2,1,0:T(8,128)S(1)}) custom-call(s32[3,4096]{1,0:T(4,128)S(1)} %get-tuple-element.32.elements, f32[3,2048]{1,0:T(4,128)S(1)} %get-tuple-element.33.displacement, f32[3,2048]{1,0:T(4,128)S(1)} %collective-permute-done.2.next_nodes, ...), custom_call_target="tpu_custom_call" | custom-call | bytes 3600 | tf_op jit(solution)/shard_map/pallas_call | solution.py:696
  9.7 0.1 shard_map.134
  9.8 1.6 %collective-permute-start.5 = (f32[21,8,256]{2,1,0:T(8,128)S(1)}, f32[21,8,256]{2,1,0:T(8,128)S(1)}, u32[]{:S(2)}, u32[]{:S(2)}) collective-permute-start(f32[21,8,256]{2,1,0:T(8,128)S(1)} %get-tuple-element.43), channel_id=1, source_target_pairs={{0,16},{4,8},{8,4},{12,28},{16,0},{20,24},{24,20},{28,12},{1,17},{... | collective-permute-start | bytes 516104 | tf_op jit(solution)/shard_map/ppermute | solution.py:741
  11.4 0.0 collective-permute-start.6
  11.4 1.1 %shard_map.132.other = f32[3,8,256]{2,1,0:T(8,128)S(1)} custom-call(f32[3,32,128]{2,1,0:T(8,128)S(1)} %get-tuple-element.36.low_ids.numbers, f32[3,32,128]{2,1,0:T(8,128)S(1)} %get-tuple-element.37.high_ids, f32[6,3,32,128]{3,2,1,0:T(8,128)S(1)} %get-tuple-element.38.forces), custom_call_target="tpu_custom_call" | custom-call | bytes 3600 | tf_op jit(solution)/shard_map/pallas_call | solution.py:696
  12.5 0.0 collective-permute-done.far_y
  12.5 0.0 collective-permute-done.1.near_y
  12.5 0.1 shard_map.133
  12.6 0.7 %collective-permute-start.3 = (f32[9,8,256]{2,1,0:T(8,128)S(1)}, f32[9,8,256]{2,1,0:T(8,128)S(1)}, u32[]{:S(2)}, u32[]{:S(2)}) collective-permute-start(f32[9,8,256]{2,1,0:T(8,128)S(1)} %get-tuple-element.39), channel_id=1, source_target_pairs={{0,16},{4,8},{8,4},{12,28},{16,0},{20,24},{24,20},{28,12},{1,17},{... | collective-permute-start | bytes 221192 | tf_op jit(solution)/shard_map/ppermute | solution.py:741
  13.4 0.0 collective-permute-start.4
  14.0 1.1 %shard_map.136.internal_own = f32[3,8,256]{2,1,0:T(8,128)S(1)} custom-call(f32[3,32,128]{2,1,0:T(8,128)S(1)} %get-tuple-element.36.low_ids.numbers, f32[3,32,128]{2,1,0:T(8,128)S(1)} %get-tuple-element.37.high_ids, f32[6,3,32,128]{3,2,1,0:T(8,128)S(1)} %get-tuple-element.38.forces), custom_call_target="tpu_custom_call" | custom-call | bytes 2880000 | tf_op jit(solution)/shard_map/pallas_call | solution.py:696
  15.1 0.2 collective-permute-done.5.far_x
  15.3 0.0 collective-permute-done.6.near_x
  15.3 0.4 %shard_map.135 = (f32[19,8,8,256]{3,2,1,0:T(8,128)S(1)}, f32[2,21,8,256]{3,2,1,0:T(8,128)S(1)}, f32[2,5,8,256]{3,2,1,0:T(8,128)S(1)}, f32[19,6,8,256]{3,2,1,0:T(8,128)S(1)}, f32[2,2,8,256]{3,2,1,0:T(8,128)S(1)}) custom-call(f32[19,4,8,256]{3,2,1,0:T(8,128)S(1)} %get-tuple-element.42.c1, f32[2,4,8,256]{3,2,1,0:T(8,128)S(1)} %get-tuple-element.41.fixed, ...), custom_call_target="tpu_custom_call" | custom-call | bytes 2880000 | tf_op jit(solution)/shard_map/pallas_call | solution.py:696
  15.7 1.4 %collective-permute-done.3.far = f32[9,8,256]{2,1,0:T(8,128)S(1)} collective-permute-done((f32[9,8,256]{2,1,0:T(8,128)S(1)}, f32[9,8,256]{2,1,0:T(8,128)S(1)}, u32[]{:S(2)}, u32[]{:S(2)}) %collective-permute-start.3) | collective-permute-done | bytes 73760 | tf_op jit(solution)/shard_map/ppermute | solution.py:741
  17.0 0.0 collective-permute-done.4.near
  17.0 0.9 %shard_map.137 = (f32[19,4,8,256]{3,2,1,0:T(8,128)S(1)}, f32[73,1,128]{2,1,0:T(1,128)S(1)}, f32[2,21,8,256]{3,2,1,0:T(8,128)S(1)}, f32[19,6,8,256]{3,2,1,0:T(8,128)S(1)}) custom-call(s32[1,1,8]{2,1,0:T(1,128)} %block_source_hbm.1, s32[1,1,8]{2,1,0:T(1,128)} %block_target_hbm.1, ...), custom_call_target="tpu_custom_call", output_to_operand_aliasing={{2}: (11, {}), {3}: (12, {})} | custom-call | bytes 5400000 | tf_op jit(solution)/shard_map/pallas_call | solution.py:696
  17.9 1.4 %collective-permute-start.9 = (f32[73,1,128]{2,1,0:T(1,128)S(1)}, f32[73,1,128]{2,1,0:T(1,128)S(1)}, u32[]{:S(2)}, u32[]{:S(2)}) collective-permute-start(f32[73,1,128]{2,1,0:T(1,128)S(1)} %get-tuple-element.51.refs_0_), channel_id=1, source_target_pairs={{3,0},{2,1},{1,2},{0,3},{7,4},{6,5},{5,6},{4,7},{11,8},{10,9},{9,1... | collective-permute-start | bytes 112136 | tf_op jit(solution)/shard_map/ppermute | solution.py:718
  19.4 0.3 collective-permute-start.8
  19.6 2.8 %collective-permute-start.7 = (f32[73,1,128]{2,1,0:T(1,128)S(1)}, f32[73,1,128]{2,1,0:T(1,128)S(1)}, u32[]{:S(2)}, u32[]{:S(2)}) collective-permute-start(f32[73,1,128]{2,1,0:T(1,128)S(1)} %get-tuple-element.51.refs_0_), channel_id=1, source_target_pairs={{1,0},{0,1},{3,2},{2,3},{5,4},{4,5},{7,6},{6,7},{9,8},{8,9},{11,10... | collective-permute-start | bytes 112136 | tf_op jit(solution)/shard_map/ppermute | solution.py:718
  22.4 0.8 %shard_map.138 = f32[19,4,8,256]{3,2,1,0:T(8,128)} custom-call(f32[19,4,8,256]{3,2,1,0:T(8,128)S(1)} %get-tuple-element.50.values), custom_call_target="tpu_custom_call" | custom-call | bytes 3600000 | tf_op jit(solution)/shard_map/pallas_call | solution.py:696
  23.2 0.6 %collective-permute-done.9.refs_2_ = f32[73,1,128]{2,1,0:T(1,128)S(1)} collective-permute-done((f32[73,1,128]{2,1,0:T(1,128)S(1)}, f32[73,1,128]{2,1,0:T(1,128)S(1)}, u32[]{:S(2)}, u32[]{:S(2)}) %collective-permute-start.9) | collective-permute-done | bytes 37408 | tf_op jit(solution)/shard_map/ppermute | solution.py:718
  23.8 1.1 %collective-permute-done.8.refs_1_ = f32[73,1,128]{2,1,0:T(1,128)S(1)} collective-permute-done((f32[73,1,128]{2,1,0:T(1,128)S(1)}, f32[73,1,128]{2,1,0:T(1,128)S(1)}, u32[]{:S(2)}, u32[]{:S(2)}) %collective-permute-start.8) | collective-permute-done | bytes 37408 | tf_op jit(solution)/shard_map/ppermute | solution.py:718
  25.0 0.2 shard_map.139
  25.2 0.0 collective-permute-done.7.message
  25.2 0.7 %shard_map.140 = (f32[3,2048]{1,0:T(4,128)}, f32[3,8,128]{2,1,0:T(8,128)}) custom-call(f32[73,1,128]{2,1,0:T(1,128)S(1)} %collective-permute-done.7.message, f32[3,16,128]{2,1,0:T(8,128)S(1)} %get-tuple-element.52.total, f32[3,8,128]{2,1,0:T(8,128)S(1)} %get-tuple-element.53.moved, f32[8,128]{1,0:T(8,128)S(1)} %get-tuple-element.54.keys), custom_call_target="tpu_custom_call" | custom-call | bytes 1800000 | tf_op jit(solution)/shard_map/pallas_call | solution.py:696
Async XLA Ops:
  0.6 7.4 %collective-permute-start.2 = (f32[3,2048]{1,0:T(4,128)}, f32[3,2048]{1,0:T(4,128)S(1)}, u32[]{:S(2)}, u32[]{:S(2)}) collective-permute-start(f32[3,2048]{1,0:T(4,128)} %displacement_hbm.1), channel_id=1, source_target_pairs={{0,12},{4,0},{8,4},{12,8},{1,13},{5,1},{9,5},{13,9},{2,14},{6,2},{... | collective-permute-start | bytes 73736 | tf_op jit(solution)/shard_map/ppermute | solution.py:723
  4.8 7.7 %collective-permute-start = (f32[24,4,256]{2,1,0:T(4,128)S(1)}, f32[24,4,256]{2,1,0:T(4,128)S(1)}, u32[]{:S(2)}, u32[]{:S(2)}) collective-permute-start(f32[24,4,256]{2,1,0:T(4,128)S(1)} %get-tuple-element.30), channel_id=1, source_target_pairs={{0,4},{1,2},{2,1},{3,7},{4,0},{5,6},{6,5},{7,3},{8,12},{9,10},{10,... | collective-permute-start | bytes 294920 | tf_op jit(solution)/shard_map/ppermute | solution.py:741
  4.9 7.6 %collective-permute-start.1 = (f32[24,4,256]{2,1,0:T(4,128)S(1)}, f32[24,4,256]{2,1,0:T(4,128)S(1)}, u32[]{:S(2)}, u32[]{:S(2)}) collective-permute-start(f32[24,4,256]{2,1,0:T(4,128)S(1)} %get-tuple-element.31), channel_id=1, source_target_pairs={{0,1},{1,0},{2,3},{3,2},{4,5},{5,4},{6,7},{7,6},{8,9},{9,8},{10,11... | collective-permute-start | bytes 294920 | tf_op jit(solution)/shard_map/ppermute | solution.py:741
  9.8 5.5 %collective-permute-start.5 = (f32[21,8,256]{2,1,0:T(8,128)S(1)}, f32[21,8,256]{2,1,0:T(8,128)S(1)}, u32[]{:S(2)}, u32[]{:S(2)}) collective-permute-start(f32[21,8,256]{2,1,0:T(8,128)S(1)} %get-tuple-element.43), channel_id=1, source_target_pairs={{0,16},{4,8},{8,4},{12,28},{16,0},{20,24},{24,20},{28,12},{1,17},{... | collective-permute-start | bytes 516104 | tf_op jit(solution)/shard_map/ppermute | solution.py:741
  11.4 3.9 %collective-permute-start.6 = (f32[21,8,256]{2,1,0:T(8,128)S(1)}, f32[21,8,256]{2,1,0:T(8,128)S(1)}, u32[]{:S(2)}, u32[]{:S(2)}) collective-permute-start(f32[21,8,256]{2,1,0:T(8,128)S(1)} %get-tuple-element.44), channel_id=1, source_target_pairs={{0,4},{4,0},{8,12},{12,8},{16,20},{20,16},{24,28},{28,24},{1,5},{5... | collective-permute-start | bytes 516104 | tf_op jit(solution)/shard_map/ppermute | solution.py:741
  12.6 4.4 %collective-permute-start.3 = (f32[9,8,256]{2,1,0:T(8,128)S(1)}, f32[9,8,256]{2,1,0:T(8,128)S(1)}, u32[]{:S(2)}, u32[]{:S(2)}) collective-permute-start(f32[9,8,256]{2,1,0:T(8,128)S(1)} %get-tuple-element.39), channel_id=1, source_target_pairs={{0,16},{4,8},{8,4},{12,28},{16,0},{20,24},{24,20},{28,12},{1,17},{... | collective-permute-start | bytes 221192 | tf_op jit(solution)/shard_map/ppermute | solution.py:741
  13.4 3.7 %collective-permute-start.4 = (f32[9,8,256]{2,1,0:T(8,128)S(1)}, f32[9,8,256]{2,1,0:T(8,128)S(1)}, u32[]{:S(2)}, u32[]{:S(2)}) collective-permute-start(f32[9,8,256]{2,1,0:T(8,128)S(1)} %get-tuple-element.40), channel_id=1, source_target_pairs={{0,4},{4,0},{8,12},{12,8},{16,20},{20,16},{24,28},{28,24},{1,5},{5... | collective-permute-start | bytes 221192 | tf_op jit(solution)/shard_map/ppermute | solution.py:741
  17.9 5.9 %collective-permute-start.9 = (f32[73,1,128]{2,1,0:T(1,128)S(1)}, f32[73,1,128]{2,1,0:T(1,128)S(1)}, u32[]{:S(2)}, u32[]{:S(2)}) collective-permute-start(f32[73,1,128]{2,1,0:T(1,128)S(1)} %get-tuple-element.51.refs_0_), channel_id=1, source_target_pairs={{3,0},{2,1},{1,2},{0,3},{7,4},{6,5},{5,6},{4,7},{11,8},{10,9},{9,1... | collective-permute-start | bytes 112136 | tf_op jit(solution)/shard_map/ppermute | solution.py:718
  19.4 5.6 %collective-permute-start.8 = (f32[73,1,128]{2,1,0:T(1,128)S(1)}, f32[73,1,128]{2,1,0:T(1,128)S(1)}, u32[]{:S(2)}, u32[]{:S(2)}) collective-permute-start(f32[73,1,128]{2,1,0:T(1,128)S(1)} %get-tuple-element.51.refs_0_), channel_id=1, source_target_pairs={{2,0},{3,1},{0,2},{1,3},{6,4},{7,5},{4,6},{5,7},{10,8},{11,9},{8,1... | collective-permute-start | bytes 112136 | tf_op jit(solution)/shard_map/ppermute | solution.py:718
  19.6 5.6 %collective-permute-start.7 = (f32[73,1,128]{2,1,0:T(1,128)S(1)}, f32[73,1,128]{2,1,0:T(1,128)S(1)}, u32[]{:S(2)}, u32[]{:S(2)}) collective-permute-start(f32[73,1,128]{2,1,0:T(1,128)S(1)} %get-tuple-element.51.refs_0_), channel_id=1, source_target_pairs={{1,0},{0,1},{3,2},{2,3},{5,4},{4,5},{7,6},{6,7},{9,8},{8,9},{11,10... | collective-permute-start | bytes 112136 | tf_op jit(solution)/shard_map/ppermute | solution.py:718

commit v20 on v12

--- a/solution.py
+++ b/solution.py
@@ -539,7 +539,7 @@
                 corners[corner, part, rows] = nodes[part]
         return carry
 
-    lax.fori_loop(0, runs // 8, gather, 0)
+    lax.fori_loop(0, runs // 8, gather, 0, unroll=2)
 
     first, second, third = [[corners[c, p] for p in range(3)] for c in range(3)]
     diag_a = shapes[0]

time: 26.1 us -> 25.9 us (level)
  no operation moved by 1% of the time
where the time goes in v20:
time: 25.9 us; the launch traced here: 25.8 us
  starting transfers between devices  12.4 us (48%)
  Pallas kernels  8.72 us (34%)
  waiting for transfers between devices  3.25 us (13%)
  between operations  1.37 us (5%)
    pallas_call x10, Pallas kernels, call(): pl.pallas_call(kernel, out_shape=outs, in_specs=[spec(space) for space in...  8.72 us
    ppermute x3, starting transfers between devices, exchange(): lax.ppermute(block, axis, [(partner_of(i, step, count), i) for i in range...  4.45 us
    ppermute x3, starting transfers between devices, swap(): lax.ppermute(near, axes, routes[0])  3.14 us
    ppermute x1, starting transfers between devices, around(): lax.ppermute(block, axis, [(i, (i + step) % count) for i in range(count)])  2.46 us
    ppermute x3, starting transfers between devices, swap(): lax.ppermute(far, axes, routes[1])  2.38 us
    ppermute x3, waiting for transfers between devices, exchange(): lax.ppermute(block, axis, [(partner_of(i, step, count), i) for i in range...  1.78 us
    ppermute x3, waiting for transfers between devices, swap(): lax.ppermute(far, axes, routes[1])  1.46 us
  transfers between devices with their start and end apart: 10, of which 5 were waited for; matrix products, arithmetic and copies ran while one was open for 0% of the time, Pallas kernels for 27%

profile of v20, /device:TPU:0, one launch (start us, length us, event | category | flops | bytes accessed | tf_op | source)
XLA Modules:
  0.0 25.8 jit_solution(1743639604616957555)
XLA Ops:
  0.6 2.5 %collective-permute-start.2 = (f32[3,2048]{1,0:T(4,128)}, f32[3,2048]{1,0:T(4,128)S(1)}, u32[]{:S(2)}, u32[]{:S(2)}) collective-permute-start(f32[3,2048]{1,0:T(4,128)} %displacement_hbm.1), channel_id=1, source_target_pairs={{0,12},{4,0},{8,4},{12,8},{1,13},{5,1},{9,5},{13,9},{2,14},{6,2},{... | collective-permute-start | bytes 73736 | tf_op jit(solution)/shard_map/ppermute | solution.py:707
  3.1 1.7 %shard_map.130 = (f32[19,4,8,256]{3,2,1,0:T(8,128)S(1)}, f32[2,4,8,256]{3,2,1,0:T(8,128)S(1)}, f32[24,4,256]{2,1,0:T(4,128)S(1)}, f32[24,4,256]{2,1,0:T(4,128)S(...) custom-call(f32[19,4,8,256]{3,2,1,0:T(8,128)} %pops_hbm.1, ...), custom_call_target="tpu_custom_call" | custom-call | bytes 5400000 | tf_op jit(solution)/shard_map/pallas_call | solution.py:680
  4.8 0.1 collective-permute-start
  4.9 3.1 %collective-permute-start.1 = (f32[24,4,256]{2,1,0:T(4,128)S(1)}, f32[24,4,256]{2,1,0:T(4,128)S(1)}, u32[]{:S(2)}, u32[]{:S(2)}) collective-permute-start(f32[24,4,256]{2,1,0:T(4,128)S(1)} %get-tuple-element.28), channel_id=1, source_target_pairs={{0,1},{1,0},{2,3},{3,2},{4,5},{5,4},{6,7},{7,6},{8,9},{9,8},{10,11... | collective-permute-start | bytes 294920 | tf_op jit(solution)/shard_map/ppermute | solution.py:725
  8.0 0.0 collective-permute-done.2.next_nodes
  8.0 1.6 %shard_map.131 = (f32[3,32,128]{2,1,0:T(8,128)S(1)}, f32[3,32,128]{2,1,0:T(8,128)S(1)}, f32[6,3,32,128]{3,2,1,0:T(8,128)S(1)}) custom-call(s32[3,4096]{1,0:T(4,128)S(1)} %get-tuple-element.29.elements, f32[3,2048]{1,0:T(4,128)S(1)} %get-tuple-element.30.displacement, f32[3,2048]{1,0:T(4,128)S(1)} %collective-permute-done.2.next_nodes, ...), custom_call_target="tpu_custom_call" | custom-call | bytes 3600 | tf_op jit(solution)/shard_map/pallas_call | solution.py:680
  9.6 0.1 shard_map.134
  9.7 1.6 %collective-permute-start.5 = (f32[21,8,256]{2,1,0:T(8,128)S(1)}, f32[21,8,256]{2,1,0:T(8,128)S(1)}, u32[]{:S(2)}, u32[]{:S(2)}) collective-permute-start(f32[21,8,256]{2,1,0:T(8,128)S(1)} %get-tuple-element.40), channel_id=1, source_target_pairs={{0,16},{4,8},{8,4},{12,28},{16,0},{20,24},{24,20},{28,12},{1,17},{... | collective-permute-start | bytes 516104 | tf_op jit(solution)/shard_map/ppermute | solution.py:725
  11.2 0.0 collective-permute-start.6
  11.2 1.1 %shard_map.132.other = f32[3,8,256]{2,1,0:T(8,128)S(1)} custom-call(f32[3,32,128]{2,1,0:T(8,128)S(1)} %get-tuple-element.33.low_ids.numbers, f32[3,32,128]{2,1,0:T(8,128)S(1)} %get-tuple-element.34.high_ids, f32[6,3,32,128]{3,2,1,0:T(8,128)S(1)} %get-tuple-element.35.forces), custom_call_target="tpu_custom_call" | custom-call | bytes 3600 | tf_op jit(solution)/shard_map/pallas_call | solution.py:680
  12.3 0.0 collective-permute-done.far_y
  12.4 0.0 collective-permute-done.1.near_y
  12.4 0.1 shard_map.133
  12.5 0.8 %collective-permute-start.3 = (f32[9,8,256]{2,1,0:T(8,128)S(1)}, f32[9,8,256]{2,1,0:T(8,128)S(1)}, u32[]{:S(2)}, u32[]{:S(2)}) collective-permute-start(f32[9,8,256]{2,1,0:T(8,128)S(1)} %get-tuple-element.36), channel_id=1, source_target_pairs={{0,16},{4,8},{8,4},{12,28},{16,0},{20,24},{24,20},{28,12},{1,17},{... | collective-permute-start | bytes 221192 | tf_op jit(solution)/shard_map/ppermute | solution.py:725
  13.2 0.0 collective-permute-start.4
  13.9 1.1 %shard_map.136.internal_own = f32[3,8,256]{2,1,0:T(8,128)S(1)} custom-call(f32[3,32,128]{2,1,0:T(8,128)S(1)} %get-tuple-element.33.low_ids.numbers, f32[3,32,128]{2,1,0:T(8,128)S(1)} %get-tuple-element.34.high_ids, f32[6,3,32,128]{3,2,1,0:T(8,128)S(1)} %get-tuple-element.35.forces), custom_call_target="tpu_custom_call" | custom-call | bytes 2880000 | tf_op jit(solution)/shard_map/pallas_call | solution.py:680
  15.0 0.2 collective-permute-done.5.far_x
  15.1 0.0 collective-permute-done.6.near_x
  15.1 0.5 %shard_map.135 = (f32[19,8,8,256]{3,2,1,0:T(8,128)S(1)}, f32[2,21,8,256]{3,2,1,0:T(8,128)S(1)}, f32[2,5,8,256]{3,2,1,0:T(8,128)S(1)}, f32[19,6,8,256]{3,2,1,0:T(8,128)S(1)}, f32[2,2,8,256]{3,2,1,0:T(8,128)S(1)}) custom-call(f32[19,4,8,256]{3,2,1,0:T(8,128)S(1)} %get-tuple-element.39.c1, f32[2,4,8,256]{3,2,1,0:T(8,128)S(1)} %get-tuple-element.38.fixed, ...), custom_call_target="tpu_custom_call" | custom-call | bytes 2880000 | tf_op jit(solution)/shard_map/pallas_call | solution.py:680
  15.6 1.2 %collective-permute-done.3.far = f32[9,8,256]{2,1,0:T(8,128)S(1)} collective-permute-done((f32[9,8,256]{2,1,0:T(8,128)S(1)}, f32[9,8,256]{2,1,0:T(8,128)S(1)}, u32[]{:S(2)}, u32[]{:S(2)}) %collective-permute-start.3) | collective-permute-done | bytes 73760 | tf_op jit(solution)/shard_map/ppermute | solution.py:725
  16.9 0.0 collective-permute-done.4.near
  16.9 0.9 %shard_map.137 = (f32[19,4,8,256]{3,2,1,0:T(8,128)S(1)}, f32[73,1,128]{2,1,0:T(1,128)S(1)}, f32[2,21,8,256]{3,2,1,0:T(8,128)S(1)}, f32[19,6,8,256]{3,2,1,0:T(8,128)S(1)}) custom-call(s32[1,1,8]{2,1,0:T(1,128)} %block_source_hbm.1, s32[1,1,8]{2,1,0:T(1,128)} %block_target_hbm.1, ...), custom_call_target="tpu_custom_call", output_to_operand_aliasing={{2}: (11, {}), {3}: (12, {})} | custom-call | bytes 5400000 | tf_op jit(solution)/shard_map/pallas_call | solution.py:680
  17.8 1.4 %collective-permute-start.9 = (f32[73,1,128]{2,1,0:T(1,128)S(1)}, f32[73,1,128]{2,1,0:T(1,128)S(1)}, u32[]{:S(2)}, u32[]{:S(2)}) collective-permute-start(f32[73,1,128]{2,1,0:T(1,128)S(1)} %get-tuple-element.48.refs_0_), channel_id=1, source_target_pairs={{3,0},{2,1},{1,2},{0,3},{7,4},{6,5},{5,6},{4,7},{11,8},{10,9},{9,1... | collective-permute-start | bytes 112136 | tf_op jit(solution)/shard_map/ppermute | solution.py:702
  19.2 0.4 %collective-permute-start.8 = (f32[73,1,128]{2,1,0:T(1,128)S(1)}, f32[73,1,128]{2,1,0:T(1,128)S(1)}, u32[]{:S(2)}, u32[]{:S(2)}) collective-permute-start(f32[73,1,128]{2,1,0:T(1,128)S(1)} %get-tuple-element.48.refs_0_), channel_id=1, source_target_pairs={{2,0},{3,1},{0,2},{1,3},{6,4},{7,5},{4,6},{5,7},{10,8},{11,9},{8,1... | collective-permute-start | bytes 112136 | tf_op jit(solution)/shard_map/ppermute | solution.py:702
  19.6 2.6 %collective-permute-start.7 = (f32[73,1,128]{2,1,0:T(1,128)S(1)}, f32[73,1,128]{2,1,0:T(1,128)S(1)}, u32[]{:S(2)}, u32[]{:S(2)}) collective-permute-start(f32[73,1,128]{2,1,0:T(1,128)S(1)} %get-tuple-element.48.refs_0_), channel_id=1, source_target_pairs={{1,0},{0,1},{3,2},{2,3},{5,4},{4,5},{7,6},{6,7},{9,8},{8,9},{11,10... | collective-permute-start | bytes 112136 | tf_op jit(solution)/shard_map/ppermute | solution.py:702
  22.3 0.8 %shard_map.138 = f32[19,4,8,256]{3,2,1,0:T(8,128)} custom-call(f32[19,4,8,256]{3,2,1,0:T(8,128)S(1)} %get-tuple-element.47.values), custom_call_target="tpu_custom_call" | custom-call | bytes 3600000 | tf_op jit(solution)/shard_map/pallas_call | solution.py:680
  23.1 0.6 %collective-permute-done.9.refs_3_ = f32[73,1,128]{2,1,0:T(1,128)S(1)} collective-permute-done((f32[73,1,128]{2,1,0:T(1,128)S(1)}, f32[73,1,128]{2,1,0:T(1,128)S(1)}, u32[]{:S(2)}, u32[]{:S(2)}) %collective-permute-start.9) | collective-permute-done | bytes 37408 | tf_op jit(solution)/shard_map/ppermute | solution.py:702
  23.7 1.1 %collective-permute-done.8.refs_2_ = f32[73,1,128]{2,1,0:T(1,128)S(1)} collective-permute-done((f32[73,1,128]{2,1,0:T(1,128)S(1)}, f32[73,1,128]{2,1,0:T(1,128)S(1)}, u32[]{:S(2)}, u32[]{:S(2)}) %collective-permute-start.8) | collective-permute-done | bytes 37408 | tf_op jit(solution)/shard_map/ppermute | solution.py:702
  24.8 0.1 collective-permute-done.7.refs_1_
  24.9 0.9 %shard_map.139 = (f32[3,2048]{1,0:T(4,128)}, f32[3,8,128]{2,1,0:T(8,128)}) custom-call(f32[73,1,128]{2,1,0:T(1,128)S(1)} %get-tuple-element.48.refs_0_, f32[73,1,128]{2,1,0:T(1,128)S(1)} %collective-permute-done.7.refs_1_, f32[73,1,128]{2,1,0:T(1,128)S(1)} %collective-permute-done.8.refs_2_, f32[73,1,128]{2,1,0:T(1,128)S(1)} %collective-permute-done.9.refs_3_), custom_call_target="tpu_custom_call" | custom-call | bytes 2880000 | tf_op jit(solution)/shard_map/pallas_call | solution.py:680
Async XLA Ops:
  0.6 7.4 %collective-permute-start.2 = (f32[3,2048]{1,0:T(4,128)}, f32[3,2048]{1,0:T(4,128)S(1)}, u32[]{:S(2)}, u32[]{:S(2)}) collective-permute-start(f32[3,2048]{1,0:T(4,128)} %displacement_hbm.1), channel_id=1, source_target_pairs={{0,12},{4,0},{8,4},{12,8},{1,13},{5,1},{9,5},{13,9},{2,14},{6,2},{... | collective-permute-start | bytes 73736 | tf_op jit(solution)/shard_map/ppermute | solution.py:707
  4.8 7.5 %collective-permute-start = (f32[24,4,256]{2,1,0:T(4,128)S(1)}, f32[24,4,256]{2,1,0:T(4,128)S(1)}, u32[]{:S(2)}, u32[]{:S(2)}) collective-permute-start(f32[24,4,256]{2,1,0:T(4,128)S(1)} %get-tuple-element.27), channel_id=1, source_target_pairs={{0,4},{1,2},{2,1},{3,7},{4,0},{5,6},{6,5},{7,3},{8,12},{9,10},{10,... | collective-permute-start | bytes 294920 | tf_op jit(solution)/shard_map/ppermute | solution.py:725
  4.9 7.4 %collective-permute-start.1 = (f32[24,4,256]{2,1,0:T(4,128)S(1)}, f32[24,4,256]{2,1,0:T(4,128)S(1)}, u32[]{:S(2)}, u32[]{:S(2)}) collective-permute-start(f32[24,4,256]{2,1,0:T(4,128)S(1)} %get-tuple-element.28), channel_id=1, source_target_pairs={{0,1},{1,0},{2,3},{3,2},{4,5},{5,4},{6,7},{7,6},{8,9},{9,8},{10,11... | collective-permute-start | bytes 294920 | tf_op jit(solution)/shard_map/ppermute | solution.py:725
  9.7 5.5 %collective-permute-start.5 = (f32[21,8,256]{2,1,0:T(8,128)S(1)}, f32[21,8,256]{2,1,0:T(8,128)S(1)}, u32[]{:S(2)}, u32[]{:S(2)}) collective-permute-start(f32[21,8,256]{2,1,0:T(8,128)S(1)} %get-tuple-element.40), channel_id=1, source_target_pairs={{0,16},{4,8},{8,4},{12,28},{16,0},{20,24},{24,20},{28,12},{1,17},{... | collective-permute-start | bytes 516104 | tf_op jit(solution)/shard_map/ppermute | solution.py:725
  11.2 3.9 %collective-permute-start.6 = (f32[21,8,256]{2,1,0:T(8,128)S(1)}, f32[21,8,256]{2,1,0:T(8,128)S(1)}, u32[]{:S(2)}, u32[]{:S(2)}) collective-permute-start(f32[21,8,256]{2,1,0:T(8,128)S(1)} %get-tuple-element.41), channel_id=1, source_target_pairs={{0,4},{4,0},{8,12},{12,8},{16,20},{20,16},{24,28},{28,24},{1,5},{5... | collective-permute-start | bytes 516104 | tf_op jit(solution)/shard_map/ppermute | solution.py:725
  12.5 4.4 %collective-permute-start.3 = (f32[9,8,256]{2,1,0:T(8,128)S(1)}, f32[9,8,256]{2,1,0:T(8,128)S(1)}, u32[]{:S(2)}, u32[]{:S(2)}) collective-permute-start(f32[9,8,256]{2,1,0:T(8,128)S(1)} %get-tuple-element.36), channel_id=1, source_target_pairs={{0,16},{4,8},{8,4},{12,28},{16,0},{20,24},{24,20},{28,12},{1,17},{... | collective-permute-start | bytes 221192 | tf_op jit(solution)/shard_map/ppermute | solution.py:725
  13.2 3.7 %collective-permute-start.4 = (f32[9,8,256]{2,1,0:T(8,128)S(1)}, f32[9,8,256]{2,1,0:T(8,128)S(1)}, u32[]{:S(2)}, u32[]{:S(2)}) collective-permute-start(f32[9,8,256]{2,1,0:T(8,128)S(1)} %get-tuple-element.37), channel_id=1, source_target_pairs={{0,4},{4,0},{8,12},{12,8},{16,20},{20,16},{24,28},{28,24},{1,5},{5... | collective-permute-start | bytes 221192 | tf_op jit(solution)/shard_map/ppermute | solution.py:725
  17.8 5.9 %collective-permute-start.9 = (f32[73,1,128]{2,1,0:T(1,128)S(1)}, f32[73,1,128]{2,1,0:T(1,128)S(1)}, u32[]{:S(2)}, u32[]{:S(2)}) collective-permute-start(f32[73,1,128]{2,1,0:T(1,128)S(1)} %get-tuple-element.48.refs_0_), channel_id=1, source_target_pairs={{3,0},{2,1},{1,2},{0,3},{7,4},{6,5},{5,6},{4,7},{11,8},{10,9},{9,1... | collective-permute-start | bytes 112136 | tf_op jit(solution)/shard_map/ppermute | solution.py:702
  19.2 5.6 %collective-permute-start.8 = (f32[73,1,128]{2,1,0:T(1,128)S(1)}, f32[73,1,128]{2,1,0:T(1,128)S(1)}, u32[]{:S(2)}, u32[]{:S(2)}) collective-permute-start(f32[73,1,128]{2,1,0:T(1,128)S(1)} %get-tuple-element.48.refs_0_), channel_id=1, source_target_pairs={{2,0},{3,1},{0,2},{1,3},{6,4},{7,5},{4,6},{5,7},{10,8},{11,9},{8,1... | collective-permute-start | bytes 112136 | tf_op jit(solution)/shard_map/ppermute | solution.py:702
  19.6 5.3 %collective-permute-start.7 = (f32[73,1,128]{2,1,0:T(1,128)S(1)}, f32[73,1,128]{2,1,0:T(1,128)S(1)}, u32[]{:S(2)}, u32[]{:S(2)}) collective-permute-start(f32[73,1,128]{2,1,0:T(1,128)S(1)} %get-tuple-element.48.refs_0_), channel_id=1, source_target_pairs={{1,0},{0,1},{3,2},{2,3},{5,4},{4,5},{7,6},{6,7},{9,8},{8,9},{11,10... | collective-permute-start | bytes 112136 | tf_op jit(solution)/shard_map/ppermute | solution.py:702

commit v21 on v20

--- a/solution.py
+++ b/solution.py
@@ -539,7 +539,7 @@
                 corners[corner, part, rows] = nodes[part]
         return carry
 
-    lax.fori_loop(0, runs // 8, gather, 0, unroll=2)
+    lax.fori_loop(0, runs // 8, gather, 0, unroll=4)
 
     first, second, third = [[corners[c, p] for p in range(3)] for c in range(3)]
     diag_a = shapes[0]

time: 25.9 us -> 25.8 us (level)
  transfers between devices with their start and end apart: 10 -> 10, of which waited for: 5 -> 5; matrix products, arithmetic and copies ran while one was open for 0% -> 0% of each run, Pallas kernels for 27% -> 26%
where the time goes in v21:
time: 25.8 us; the launch traced here: 25.7 us
  starting transfers between devices  12.4 us (48%)
  Pallas kernels  8.59 us (33%)
  waiting for transfers between devices  3.27 us (13%)
  between operations  1.37 us (5%)
    pallas_call x10, Pallas kernels, call(): pl.pallas_call(kernel, out_shape=outs, in_specs=[spec(space) for space in...  8.59 us
    ppermute x3, starting transfers between devices, exchange(): lax.ppermute(block, axis, [(partner_of(i, step, count), i) for i in range...  4.45 us
    ppermute x3, starting transfers between devices, swap(): lax.ppermute(near, axes, routes[0])  3.14 us
    ppermute x1, starting transfers between devices, around(): lax.ppermute(block, axis, [(i, (i + step) % count) for i in range(count)])  2.46 us
    ppermute x3, starting transfers between devices, swap(): lax.ppermute(far, axes, routes[1])  2.37 us
    ppermute x3, waiting for transfers between devices, exchange(): lax.ppermute(block, axis, [(partner_of(i, step, count), i) for i in range...  1.8 us
    ppermute x3, waiting for transfers between devices, swap(): lax.ppermute(far, axes, routes[1])  1.46 us
  transfers between devices with their start and end apart: 10, of which 5 were waited for; matrix products, arithmetic and copies ran while one was open for 0% of the time, Pallas kernels for 26%

profile of v21, /device:TPU:0, one launch (start us, length us, event | category | flops | bytes accessed | tf_op | source)
XLA Modules:
  0.0 25.7 jit_solution(17893290952655897678)
XLA Ops:
  0.6 2.5 %collective-permute-start.2 = (f32[3,2048]{1,0:T(4,128)}, f32[3,2048]{1,0:T(4,128)S(1)}, u32[]{:S(2)}, u32[]{:S(2)}) collective-permute-start(f32[3,2048]{1,0:T(4,128)} %displacement_hbm.1), channel_id=1, source_target_pairs={{0,12},{4,0},{8,4},{12,8},{1,13},{5,1},{9,5},{13,9},{2,14},{6,2},{... | collective-permute-start | bytes 73736 | tf_op jit(solution)/shard_map/ppermute | solution.py:707
  3.1 1.7 %shard_map.130 = (f32[19,4,8,256]{3,2,1,0:T(8,128)S(1)}, f32[2,4,8,256]{3,2,1,0:T(8,128)S(1)}, f32[24,4,256]{2,1,0:T(4,128)S(1)}, f32[24,4,256]{2,1,0:T(4,128)S(...) custom-call(f32[19,4,8,256]{3,2,1,0:T(8,128)} %pops_hbm.1, ...), custom_call_target="tpu_custom_call" | custom-call | bytes 5400000 | tf_op jit(solution)/shard_map/pallas_call | solution.py:680
  4.8 0.1 collective-permute-start
  4.9 3.1 %collective-permute-start.1 = (f32[24,4,256]{2,1,0:T(4,128)S(1)}, f32[24,4,256]{2,1,0:T(4,128)S(1)}, u32[]{:S(2)}, u32[]{:S(2)}) collective-permute-start(f32[24,4,256]{2,1,0:T(4,128)S(1)} %get-tuple-element.28), channel_id=1, source_target_pairs={{0,1},{1,0},{2,3},{3,2},{4,5},{5,4},{6,7},{7,6},{8,9},{9,8},{10,11... | collective-permute-start | bytes 294920 | tf_op jit(solution)/shard_map/ppermute | solution.py:725
  8.0 0.0 collective-permute-done.2.next_nodes
  8.0 1.4 %shard_map.131 = (f32[3,32,128]{2,1,0:T(8,128)S(1)}, f32[3,32,128]{2,1,0:T(8,128)S(1)}, f32[6,3,32,128]{3,2,1,0:T(8,128)S(1)}) custom-call(s32[3,4096]{1,0:T(4,128)S(1)} %get-tuple-element.29.elements, f32[3,2048]{1,0:T(4,128)S(1)} %get-tuple-element.30.displacement, f32[3,2048]{1,0:T(4,128)S(1)} %collective-permute-done.2.next_nodes, ...), custom_call_target="tpu_custom_call" | custom-call | bytes 3600 | tf_op jit(solution)/shard_map/pallas_call | solution.py:680
  9.5 0.1 shard_map.134
  9.5 1.6 %collective-permute-start.5 = (f32[21,8,256]{2,1,0:T(8,128)S(1)}, f32[21,8,256]{2,1,0:T(8,128)S(1)}, u32[]{:S(2)}, u32[]{:S(2)}) collective-permute-start(f32[21,8,256]{2,1,0:T(8,128)S(1)} %get-tuple-element.40), channel_id=1, source_target_pairs={{0,16},{4,8},{8,4},{12,28},{16,0},{20,24},{24,20},{28,12},{1,17},{... | collective-permute-start | bytes 516104 | tf_op jit(solution)/shard_map/ppermute | solution.py:725
  11.1 0.0 collective-permute-start.6
  11.1 1.1 %shard_map.132.other = f32[3,8,256]{2,1,0:T(8,128)S(1)} custom-call(f32[3,32,128]{2,1,0:T(8,128)S(1)} %get-tuple-element.33.low_ids.numbers, f32[3,32,128]{2,1,0:T(8,128)S(1)} %get-tuple-element.34.high_ids, f32[6,3,32,128]{3,2,1,0:T(8,128)S(1)} %get-tuple-element.35.forces), custom_call_target="tpu_custom_call" | custom-call | bytes 3600 | tf_op jit(solution)/shard_map/pallas_call | solution.py:680
  12.2 0.0 collective-permute-done.far_y
  12.2 0.0 collective-permute-done.1.near_y
  12.2 0.1 shard_map.133
  12.3 0.7 %collective-permute-start.3 = (f32[9,8,256]{2,1,0:T(8,128)S(1)}, f32[9,8,256]{2,1,0:T(8,128)S(1)}, u32[]{:S(2)}, u32[]{:S(2)}) collective-permute-start(f32[9,8,256]{2,1,0:T(8,128)S(1)} %get-tuple-element.36), channel_id=1, source_target_pairs={{0,16},{4,8},{8,4},{12,28},{16,0},{20,24},{24,20},{28,12},{1,17},{... | collective-permute-start | bytes 221192 | tf_op jit(solution)/shard_map/ppermute | solution.py:725
  13.1 0.0 collective-permute-start.4
  13.7 1.1 %shard_map.136.internal_own = f32[3,8,256]{2,1,0:T(8,128)S(1)} custom-call(f32[3,32,128]{2,1,0:T(8,128)S(1)} %get-tuple-element.33.low_ids.numbers, f32[3,32,128]{2,1,0:T(8,128)S(1)} %get-tuple-element.34.high_ids, f32[6,3,32,128]{3,2,1,0:T(8,128)S(1)} %get-tuple-element.35.forces), custom_call_target="tpu_custom_call" | custom-call | bytes 2880000 | tf_op jit(solution)/shard_map/pallas_call | solution.py:680
  14.8 0.2 collective-permute-done.5.far_x
  15.0 0.0 collective-permute-done.6.near_x
  15.0 0.5 %shard_map.135 = (f32[19,8,8,256]{3,2,1,0:T(8,128)S(1)}, f32[2,21,8,256]{3,2,1,0:T(8,128)S(1)}, f32[2,5,8,256]{3,2,1,0:T(8,128)S(1)}, f32[19,6,8,256]{3,2,1,0:T(8,128)S(1)}, f32[2,2,8,256]{3,2,1,0:T(8,128)S(1)}) custom-call(f32[19,4,8,256]{3,2,1,0:T(8,128)S(1)} %get-tuple-element.39.c1, f32[2,4,8,256]{3,2,1,0:T(8,128)S(1)} %get-tuple-element.38.fixed, ...), custom_call_target="tpu_custom_call" | custom-call | bytes 2880000 | tf_op jit(solution)/shard_map/pallas_call | solution.py:680
  15.5 1.3 %collective-permute-done.3.far = f32[9,8,256]{2,1,0:T(8,128)S(1)} collective-permute-done((f32[9,8,256]{2,1,0:T(8,128)S(1)}, f32[9,8,256]{2,1,0:T(8,128)S(1)}, u32[]{:S(2)}, u32[]{:S(2)}) %collective-permute-start.3) | collective-permute-done | bytes 73760 | tf_op jit(solution)/shard_map/ppermute | solution.py:725
  16.7 0.0 collective-permute-done.4.near
  16.7 0.9 %shard_map.137 = (f32[19,4,8,256]{3,2,1,0:T(8,128)S(1)}, f32[73,1,128]{2,1,0:T(1,128)S(1)}, f32[2,21,8,256]{3,2,1,0:T(8,128)S(1)}, f32[19,6,8,256]{3,2,1,0:T(8,128)S(1)}) custom-call(s32[1,1,8]{2,1,0:T(1,128)} %block_source_hbm.1, s32[1,1,8]{2,1,0:T(1,128)} %block_target_hbm.1, ...), custom_call_target="tpu_custom_call", output_to_operand_aliasing={{2}: (11, {}), {3}: (12, {})} | custom-call | bytes 5400000 | tf_op jit(solution)/shard_map/pallas_call | solution.py:680
  17.7 1.6 %collective-permute-start.9 = (f32[73,1,128]{2,1,0:T(1,128)S(1)}, f32[73,1,128]{2,1,0:T(1,128)S(1)}, u32[]{:S(2)}, u32[]{:S(2)}) collective-permute-start(f32[73,1,128]{2,1,0:T(1,128)S(1)} %get-tuple-element.48.refs_0_), channel_id=1, source_target_pairs={{3,0},{2,1},{1,2},{0,3},{7,4},{6,5},{5,6},{4,7},{11,8},{10,9},{9,1... | collective-permute-start | bytes 112136 | tf_op jit(solution)/shard_map/ppermute | solution.py:702
  19.2 0.4 %collective-permute-start.8 = (f32[73,1,128]{2,1,0:T(1,128)S(1)}, f32[73,1,128]{2,1,0:T(1,128)S(1)}, u32[]{:S(2)}, u32[]{:S(2)}) collective-permute-start(f32[73,1,128]{2,1,0:T(1,128)S(1)} %get-tuple-element.48.refs_0_), channel_id=1, source_target_pairs={{2,0},{3,1},{0,2},{1,3},{6,4},{7,5},{4,6},{5,7},{10,8},{11,9},{8,1... | collective-permute-start | bytes 112136 | tf_op jit(solution)/shard_map/ppermute | solution.py:702
  19.6 2.5 %collective-permute-start.7 = (f32[73,1,128]{2,1,0:T(1,128)S(1)}, f32[73,1,128]{2,1,0:T(1,128)S(1)}, u32[]{:S(2)}, u32[]{:S(2)}) collective-permute-start(f32[73,1,128]{2,1,0:T(1,128)S(1)} %get-tuple-element.48.refs_0_), channel_id=1, source_target_pairs={{1,0},{0,1},{3,2},{2,3},{5,4},{4,5},{7,6},{6,7},{9,8},{8,9},{11,10... | collective-permute-start | bytes 112136 | tf_op jit(solution)/shard_map/ppermute | solution.py:702
  22.1 0.8 %shard_map.138 = f32[19,4,8,256]{3,2,1,0:T(8,128)} custom-call(f32[19,4,8,256]{3,2,1,0:T(8,128)S(1)} %get-tuple-element.47.values), custom_call_target="tpu_custom_call" | custom-call | bytes 3600000 | tf_op jit(solution)/shard_map/pallas_call | solution.py:680
  23.0 0.6 %collective-permute-done.9.refs_3_ = f32[73,1,128]{2,1,0:T(1,128)S(1)} collective-permute-done((f32[73,1,128]{2,1,0:T(1,128)S(1)}, f32[73,1,128]{2,1,0:T(1,128)S(1)}, u32[]{:S(2)}, u32[]{:S(2)}) %collective-permute-start.9) | collective-permute-done | bytes 37408 | tf_op jit(solution)/shard_map/ppermute | solution.py:702
  23.5 1.2 %collective-permute-done.8.refs_2_ = f32[73,1,128]{2,1,0:T(1,128)S(1)} collective-permute-done((f32[73,1,128]{2,1,0:T(1,128)S(1)}, f32[73,1,128]{2,1,0:T(1,128)S(1)}, u32[]{:S(2)}, u32[]{:S(2)}) %collective-permute-start.8) | collective-permute-done | bytes 37408 | tf_op jit(solution)/shard_map/ppermute | solution.py:702
  24.7 0.1 collective-permute-done.7.refs_1_
  24.8 0.9 %shard_map.139 = (f32[3,2048]{1,0:T(4,128)}, f32[3,8,128]{2,1,0:T(8,128)}) custom-call(f32[73,1,128]{2,1,0:T(1,128)S(1)} %get-tuple-element.48.refs_0_, f32[73,1,128]{2,1,0:T(1,128)S(1)} %collective-permute-done.7.refs_1_, f32[73,1,128]{2,1,0:T(1,128)S(1)} %collective-permute-done.8.refs_2_, f32[73,1,128]{2,1,0:T(1,128)S(1)} %collective-permute-done.9.refs_3_), custom_call_target="tpu_custom_call" | custom-call | bytes 2880000 | tf_op jit(solution)/shard_map/pallas_call | solution.py:680
Async XLA Ops:
  0.6 7.4 %collective-permute-start.2 = (f32[3,2048]{1,0:T(4,128)}, f32[3,2048]{1,0:T(4,128)S(1)}, u32[]{:S(2)}, u32[]{:S(2)}) collective-permute-start(f32[3,2048]{1,0:T(4,128)} %displacement_hbm.1), channel_id=1, source_target_pairs={{0,12},{4,0},{8,4},{12,8},{1,13},{5,1},{9,5},{13,9},{2,14},{6,2},{... | collective-permute-start | bytes 73736 | tf_op jit(solution)/shard_map/ppermute | solution.py:707
  4.8 7.4 %collective-permute-start = (f32[24,4,256]{2,1,0:T(4,128)S(1)}, f32[24,4,256]{2,1,0:T(4,128)S(1)}, u32[]{:S(2)}, u32[]{:S(2)}) collective-permute-start(f32[24,4,256]{2,1,0:T(4,128)S(1)} %get-tuple-element.27), channel_id=1, source_target_pairs={{0,4},{1,2},{2,1},{3,7},{4,0},{5,6},{6,5},{7,3},{8,12},{9,10},{10,... | collective-permute-start | bytes 294920 | tf_op jit(solution)/shard_map/ppermute | solution.py:725
  4.9 7.3 %collective-permute-start.1 = (f32[24,4,256]{2,1,0:T(4,128)S(1)}, f32[24,4,256]{2,1,0:T(4,128)S(1)}, u32[]{:S(2)}, u32[]{:S(2)}) collective-permute-start(f32[24,4,256]{2,1,0:T(4,128)S(1)} %get-tuple-element.28), channel_id=1, source_target_pairs={{0,1},{1,0},{2,3},{3,2},{4,5},{5,4},{6,7},{7,6},{8,9},{9,8},{10,11... | collective-permute-start | bytes 294920 | tf_op jit(solution)/shard_map/ppermute | solution.py:725
  9.5 5.5 %collective-permute-start.5 = (f32[21,8,256]{2,1,0:T(8,128)S(1)}, f32[21,8,256]{2,1,0:T(8,128)S(1)}, u32[]{:S(2)}, u32[]{:S(2)}) collective-permute-start(f32[21,8,256]{2,1,0:T(8,128)S(1)} %get-tuple-element.40), channel_id=1, source_target_pairs={{0,16},{4,8},{8,4},{12,28},{16,0},{20,24},{24,20},{28,12},{1,17},{... | collective-permute-start | bytes 516104 | tf_op jit(solution)/shard_map/ppermute | solution.py:725
  11.1 3.9 %collective-permute-start.6 = (f32[21,8,256]{2,1,0:T(8,128)S(1)}, f32[21,8,256]{2,1,0:T(8,128)S(1)}, u32[]{:S(2)}, u32[]{:S(2)}) collective-permute-start(f32[21,8,256]{2,1,0:T(8,128)S(1)} %get-tuple-element.41), channel_id=1, source_target_pairs={{0,4},{4,0},{8,12},{12,8},{16,20},{20,16},{24,28},{28,24},{1,5},{5... | collective-permute-start | bytes 516104 | tf_op jit(solution)/shard_map/ppermute | solution.py:725
  12.3 4.4 %collective-permute-start.3 = (f32[9,8,256]{2,1,0:T(8,128)S(1)}, f32[9,8,256]{2,1,0:T(8,128)S(1)}, u32[]{:S(2)}, u32[]{:S(2)}) collective-permute-start(f32[9,8,256]{2,1,0:T(8,128)S(1)} %get-tuple-element.36), channel_id=1, source_target_pairs={{0,16},{4,8},{8,4},{12,28},{16,0},{20,24},{24,20},{28,12},{1,17},{... | collective-permute-start | bytes 221192 | tf_op jit(solution)/shard_map/ppermute | solution.py:725
  13.1 3.7 %collective-permute-start.4 = (f32[9,8,256]{2,1,0:T(8,128)S(1)}, f32[9,8,256]{2,1,0:T(8,128)S(1)}, u32[]{:S(2)}, u32[]{:S(2)}) collective-permute-start(f32[9,8,256]{2,1,0:T(8,128)S(1)} %get-tuple-element.37), channel_id=1, source_target_pairs={{0,4},{4,0},{8,12},{12,8},{16,20},{20,16},{24,28},{28,24},{1,5},{5... | collective-permute-start | bytes 221192 | tf_op jit(solution)/shard_map/ppermute | solution.py:725
  17.7 5.9 %collective-permute-start.9 = (f32[73,1,128]{2,1,0:T(1,128)S(1)}, f32[73,1,128]{2,1,0:T(1,128)S(1)}, u32[]{:S(2)}, u32[]{:S(2)}) collective-permute-start(f32[73,1,128]{2,1,0:T(1,128)S(1)} %get-tuple-element.48.refs_0_), channel_id=1, source_target_pairs={{3,0},{2,1},{1,2},{0,3},{7,4},{6,5},{5,6},{4,7},{11,8},{10,9},{9,1... | collective-permute-start | bytes 112136 | tf_op jit(solution)/shard_map/ppermute | solution.py:702
  19.2 5.5 %collective-permute-start.8 = (f32[73,1,128]{2,1,0:T(1,128)S(1)}, f32[73,1,128]{2,1,0:T(1,128)S(1)}, u32[]{:S(2)}, u32[]{:S(2)}) collective-permute-start(f32[73,1,128]{2,1,0:T(1,128)S(1)} %get-tuple-element.48.refs_0_), channel_id=1, source_target_pairs={{2,0},{3,1},{0,2},{1,3},{6,4},{7,5},{4,6},{5,7},{10,8},{11,9},{8,1... | collective-permute-start | bytes 112136 | tf_op jit(solution)/shard_map/ppermute | solution.py:702
  19.6 5.1 %collective-permute-start.7 = (f32[73,1,128]{2,1,0:T(1,128)S(1)}, f32[73,1,128]{2,1,0:T(1,128)S(1)}, u32[]{:S(2)}, u32[]{:S(2)}) collective-permute-start(f32[73,1,128]{2,1,0:T(1,128)S(1)} %get-tuple-element.48.refs_0_), channel_id=1, source_target_pairs={{1,0},{0,1},{3,2},{2,3},{5,4},{4,5},{7,6},{6,7},{9,8},{8,9},{11,10... | collective-permute-start | bytes 112136 | tf_op jit(solution)/shard_map/ppermute | solution.py:702
